TPU v7x, 32 devices: a whole 2x2x4 slice. The times are simulated.
32 devices in a mesh: wide: 8 (over z, x), narrow: 4 (over y, core).
Axes of the slice: x: 2, y: 2, z: 4, core: 2. Of those that a mesh axis runs over, the one named last changes fastest.
Arguments:
- activations: bfloat16 [64, 512, 512], P('wide', 'narrow'), may hold values from -6 to 6
- cotangent: bfloat16 [64, 512, 512], P('wide', 'narrow'), may hold values from -6 to 6
- doc_lengths: int32 [64, 5], P('wide'), may hold values from 1 to 508, as said below
- expand_weight: float32 [512, 3072], P('wide'), may hold values from -0.25 to 0.25
- expand_momentum: float32 [512, 3072], P('wide'), may hold values from -0.0009765625 to 0.0009765625
- expand_variance: float32 [512, 3072], P('wide'), may hold values from 1.9054879e-10 to 1.5243903e-09
- expand_average: float32 [512, 3072], P('wide'), may hold values from -0.25 to 0.25
- shrink_weight: float32 [1536, 512], P('wide'), may hold values from -0.3125 to 0.3125
- shrink_momentum: float32 [1536, 512], P('wide'), may hold values from -0.0009765625 to 0.0009765625
- shrink_variance: float32 [1536, 512], P('wide'), may hold values from 1.9054879e-10 to 1.5243903e-09
- shrink_average: float32 [1536, 512], P('wide'), may hold values from -0.3125 to 0.3125
- spatial_weight: float32 [512, 512], P('wide'), may hold values from -0.5 to 0.5
- spatial_momentum: float32 [512, 512], P('wide'), may hold values from -0.0009765625 to 0.0009765625
- spatial_variance: float32 [512, 512], P('wide'), may hold values from 1.9054879e-10 to 1.5243903e-09
- spatial_average: float32 [512, 512], P('wide'), may hold values from -0.5 to 0.5
- norm_gains: float32 [2048], P('wide'), may hold values from 0.3 to 3.5
- gains_momentum: float32 [2048], P('wide'), may hold values from -0.0029296875 to 0.0029296875
- gains_variance: float32 [2048], P('wide'), may hold values from 1.1432927e-09 to 9.527439e-09
- gains_average: float32 [2048], P('wide'), may hold values from 0.5 to 1.5
- spatial_bias: float32 [512], P('wide'), may hold values from 0.5 to 1.5
- bias_momentum: float32 [512], P('wide'), may hold values from -0.0029296875 to 0.0029296875
- bias_variance: float32 [512], P('wide'), may hold values from 1.1432927e-09 to 9.527439e-09
- bias_average: float32 [512], P('wide'), may hold values from 0.5 to 1.5
Outputs:
- layer_out: bfloat16 [64, 512, 512], P('wide', 'narrow')
- input_grad: float32 [64, 512, 512], P('wide', 'narrow')
- grad_norm: float32 [], replicated
- expand_grad: float32 [512, 3072], P('wide')
- expand_moment: float32 [512, 3072], P('wide')
- expand_square: float32 [512, 3072], P('wide')
- expand_updated: float32 [512, 3072], P('wide')
- expand_smoothed: float32 [512, 3072], P('wide')
- shrink_grad: float32 [1536, 512], P('wide')
- shrink_moment: float32 [1536, 512], P('wide')
- shrink_square: float32 [1536, 512], P('wide')
- shrink_updated: float32 [1536, 512], P('wide')
- shrink_smoothed: float32 [1536, 512], P('wide')
- spatial_grad: float32 [512, 512], P('wide')
- spatial_moment: float32 [512, 512], P('wide')
- spatial_square: float32 [512, 512], P('wide')
- spatial_updated: float32 [512, 512], P('wide')
- spatial_smoothed: float32 [512, 512], P('wide')
- gains_grad: float32 [2048], P('wide')
- gains_moment: float32 [2048], P('wide')
- gains_square: float32 [2048], P('wide')
- gains_updated: float32 [2048], P('wide')
- gains_smoothed: float32 [2048], P('wide')
- bias_grad: float32 [512], P('wide')
- bias_moment: float32 [512], P('wide')
- bias_square: float32 [512], P('wide')
- bias_updated: float32 [512], P('wide')
- bias_smoothed: float32 [512], P('wide')
Inputs may be any that keep to these rules, and one draw needn't show every extreme that they name: `doc_lengths`: every row's entries sum to 512 and its last entry is 1 or more. In each aligned block of 8 rows one row has a document from slot 1 to slot 508.
All inputs are finite; a program needn't handle non-finite values.
Results may differ from a plain program's by a relative error of at most 0.012.
Values may be sent and summed in bfloat16 or wider, within the bound.
No kernel may reach another device: no remote copies, remote signals or barrier semaphores. Data moves between devices by JAX's collectives and lax.ppermute only.
A program may use at most 128 MiB of HBM per device.

v0:
```python
import jax
import jax.numpy as jnp
from jax import lax
from jax.sharding import PartitionSpec as P

D = 512
ROW = 512
DOCS = 5
STEP = 10
HALF = 1536


LAYER_EPS = 1e-05
CLIP_LIMIT = 1.0
BETA_FIRST = 0.9
BETA_SECOND = 0.999
ADAM_EPS = 1e-08
RATE_MATRIX = 0.03
RATE_VECTOR = 0.2
DECAY_MATRIX = 0.1
EMA_DECAY = 0.9999


def layer_normal(values, scales):
    centre = jnp.mean(values, axis=-1, keepdims=True)
    shifted = values - centre
    spread = jnp.mean(shifted * shifted, axis=-1, keepdims=True)
    return shifted * lax.rsqrt(spread + LAYER_EPS) * scales


def row_masks(lengths):
    bounds = jnp.cumsum(lengths, axis=1, dtype=jnp.int32)
    places = jnp.arange(ROW, dtype=jnp.int32)
    doc_ids = jnp.sum(
        (places[None, :, None] >= bounds[:, None, :]).astype(jnp.int32), axis=2, dtype=jnp.int32
    )
    live_slots = places[None, :] < bounds[:, DOCS - 2][:, None]
    same_doc = (
        (doc_ids[:, :, None] == doc_ids[:, None, :])
        & live_slots[:, :, None]
        & live_slots[:, None, :]
    )
    return (same_doc.astype(jnp.float32), live_slots.astype(jnp.float32))


def adam_update(weight, gradient, momentum, variance, average, clip_scale, step_rate, decay_rate):
    ema_rate = min(EMA_DECAY, (1.0 + STEP) / (10.0 + STEP))
    clipped = clip_scale * gradient
    moment = BETA_FIRST * momentum + (1.0 - BETA_FIRST) * clipped
    square = BETA_SECOND * variance + (1.0 - BETA_SECOND) * clipped * clipped
    first_hat = moment / (1.0 - BETA_FIRST**STEP)
    second_hat = square / (1.0 - BETA_SECOND**STEP)
    updated = weight - step_rate * (
        first_hat / (jnp.sqrt(second_hat) + ADAM_EPS) + decay_rate * weight
    )
    smoothed = ema_rate * average + (1.0 - ema_rate) * updated
    return (clipped, moment, square, updated, smoothed)


def front_pass(acts_float, first_gain, second_gain, expand_low):
    normed, first_back = jax.vjp(layer_normal, acts_float, first_gain)
    normed_low = normed.astype(jnp.bfloat16)
    hidden = jnp.einsum("rpd,df->rpf", normed_low, expand_low, preferred_element_type=jnp.float32)
    active, gelu_back = jax.vjp(jax.nn.gelu, hidden)
    content = active[..., :HALF]
    gating = active[..., HALF:]
    gate_normed, second_back = jax.vjp(layer_normal, gating, second_gain)
    return (
        normed_low,
        first_back,
        gelu_back,
        second_back,
        content,
        gate_normed.astype(jnp.bfloat16),
    )


def rear_pass(
    cots, normed_low, first_back, gelu_back, second_back, grad_content, grad_gate_vals, expand_low
):
    grad_gating, second_raw = second_back(grad_gate_vals)
    (grad_hidden,) = gelu_back(jnp.concatenate([grad_content, grad_gating], axis=-1))
    grad_hidden_low = grad_hidden.astype(jnp.bfloat16)
    expand_raw = jnp.einsum(
        "rpd,rpf->df", normed_low, grad_hidden_low, preferred_element_type=jnp.float32
    )
    grad_normed = jnp.einsum(
        "rpf,df->rpd", grad_hidden_low, expand_low, preferred_element_type=jnp.float32
    )
    grad_input, first_raw = first_back(grad_normed)
    input_grad = cots.astype(jnp.float32) + grad_input
    return (input_grad, expand_raw, jnp.concatenate([first_raw, second_raw]))


def on_device(
    activations,
    cotangent,
    doc_lengths,
    expand_weight,
    expand_momentum,
    expand_variance,
    expand_average,
    shrink_weight,
    shrink_momentum,
    shrink_variance,
    shrink_average,
    spatial_weight,
    spatial_momentum,
    spatial_variance,
    spatial_average,
    norm_gains,
    gains_momentum,
    gains_variance,
    gains_average,
    spatial_bias,
    bias_momentum,
    bias_variance,
    bias_average,
):
    narrow_count = lax.axis_size("narrow")
    group_rows, quarter = (activations.shape[0], activations.shape[1])
    channels = HALF // narrow_count
    gathered = (
        lax.all_gather(expand_weight.astype(jnp.bfloat16), "wide", axis=0, tiled=True),
        lax.all_gather(shrink_weight.astype(jnp.bfloat16), "wide", axis=0, tiled=True),
        lax.all_gather(spatial_weight.astype(jnp.bfloat16), "wide", axis=0, tiled=True),
        lax.all_gather(norm_gains.astype(jnp.bfloat16), "wide", axis=0, tiled=True),
        lax.all_gather(spatial_bias.astype(jnp.bfloat16), "wide", axis=0, tiled=True),
    )
    expand_low, shrink_low, spatial_low, gains_low, bias_low = gathered
    gains_full = gains_low.astype(jnp.float32)
    first_gain = gains_full[:D]
    second_gain = gains_full[D:]
    same_doc, live_slots = row_masks(doc_lengths)
    masked_spatial = same_doc.astype(jnp.bfloat16) * spatial_low[None]
    bias_term = live_slots[:, :, None] * bias_low.astype(jnp.float32)[None, :, None]
    acts_float = activations.astype(jnp.float32)
    normed_low, first_back, gelu_back, second_back, content, gate_flat = front_pass(
        acts_float, first_gain, second_gain, expand_low
    )
    gate_low = gate_flat.reshape(group_rows, quarter, narrow_count, channels)
    received = lax.all_to_all(gate_low, "narrow", split_axis=2, concat_axis=1, tiled=True)
    block_vals = received[:, :, 0, :]
    mixed_raw = (
        jnp.einsum("rij,rjc->ric", masked_spatial, block_vals, preferred_element_type=jnp.float32)
        + bias_term
    )
    mixed_low = mixed_raw.astype(jnp.bfloat16)[:, :, None, :]
    returned = lax.all_to_all(mixed_low, "narrow", split_axis=1, concat_axis=2, tiled=True)
    mixed_tokens = returned
    gate_channels = received
    mixed_vals = mixed_tokens.reshape(group_rows, quarter, HALF).astype(jnp.float32)
    gated_low = (content * mixed_vals).astype(jnp.bfloat16)
    layer_out = (
        acts_float
        + jnp.einsum("rph,hd->rpd", gated_low, shrink_low, preferred_element_type=jnp.float32)
    ).astype(jnp.bfloat16)
    grad_gated = jnp.einsum(
        "rpd,hd->rph", cotangent, shrink_low, preferred_element_type=jnp.float32
    )
    shrink_raw = jnp.einsum("rph,rpd->hd", gated_low, cotangent, preferred_element_type=jnp.float32)
    grad_content = grad_gated * mixed_vals
    grad_mixed = (
        (grad_gated * content)
        .astype(jnp.bfloat16)
        .reshape(group_rows, quarter, narrow_count, channels)
    )
    received = lax.all_to_all(grad_mixed, "narrow", split_axis=2, concat_axis=1, tiled=True)
    block_vals = received[:, :, 0, :]
    grad_gate = jnp.einsum(
        "rij,ric->rjc", masked_spatial, block_vals, preferred_element_type=jnp.float32
    )
    grad_gate_low = grad_gate.astype(jnp.bfloat16)[:, :, None, :]
    returned = lax.all_to_all(grad_gate_low, "narrow", split_axis=1, concat_axis=2, tiled=True)
    mixed_grads = received[:, :, 0, :]
    gate_vals = gate_channels[:, :, 0, :]
    spatial_raw = jnp.sum(
        same_doc
        * jnp.einsum("ric,rjc->rij", mixed_grads, gate_vals, preferred_element_type=jnp.float32),
        axis=0,
    )
    bias_raw = jnp.sum(live_slots * jnp.sum(mixed_grads, axis=2, dtype=jnp.float32), axis=0)
    grad_gate_vals = returned.reshape(group_rows, quarter, HALF).astype(jnp.float32)
    input_grad, expand_raw, gains_raw = rear_pass(
        cotangent,
        normed_low,
        first_back,
        gelu_back,
        second_back,
        grad_content,
        grad_gate_vals,
        expand_low,
    )
    local_grads = (expand_raw, shrink_raw, spatial_raw, gains_raw, bias_raw)
    totals = lax.psum(
        (local_grads[0], local_grads[1], local_grads[2], local_grads[3], local_grads[4]), "narrow"
    )
    shards = (
        lax.psum_scatter(totals[0], "wide", scatter_dimension=0, tiled=True),
        lax.psum_scatter(totals[1], "wide", scatter_dimension=0, tiled=True),
        lax.psum_scatter(totals[2], "wide", scatter_dimension=0, tiled=True),
        lax.psum_scatter(totals[3], "wide", scatter_dimension=0, tiled=True),
        lax.psum_scatter(totals[4], "wide", scatter_dimension=0, tiled=True),
    )
    expand_shard, shrink_shard, spatial_shard, gains_shard, bias_shard = shards
    local_squares = (
        jnp.sum(expand_shard * expand_shard)
        + jnp.sum(shrink_shard * shrink_shard)
        + jnp.sum(spatial_shard * spatial_shard)
        + jnp.sum(gains_shard * gains_shard)
        + jnp.sum(bias_shard * bias_shard)
    )
    square_total = lax.psum(local_squares, "wide")
    grad_norm = jnp.sqrt(square_total)
    clip_scale = CLIP_LIMIT / jnp.maximum(grad_norm, CLIP_LIMIT)
    expand_grad, expand_moment, expand_square, expand_updated, expand_smoothed = adam_update(
        expand_weight,
        expand_shard,
        expand_momentum,
        expand_variance,
        expand_average,
        clip_scale,
        RATE_MATRIX,
        DECAY_MATRIX,
    )
    shrink_grad, shrink_moment, shrink_square, shrink_updated, shrink_smoothed = adam_update(
        shrink_weight,
        shrink_shard,
        shrink_momentum,
        shrink_variance,
        shrink_average,
        clip_scale,
        RATE_MATRIX,
        DECAY_MATRIX,
    )
    spatial_grad, spatial_moment, spatial_square, spatial_updated, spatial_smoothed = adam_update(
        spatial_weight,
        spatial_shard,
        spatial_momentum,
        spatial_variance,
        spatial_average,
        clip_scale,
        RATE_MATRIX,
        DECAY_MATRIX,
    )
    gains_grad, gains_moment, gains_square, gains_updated, gains_smoothed = adam_update(
        norm_gains,
        gains_shard,
        gains_momentum,
        gains_variance,
        gains_average,
        clip_scale,
        RATE_VECTOR,
        0.0,
    )
    bias_grad, bias_moment, bias_square, bias_updated, bias_smoothed = adam_update(
        spatial_bias,
        bias_shard,
        bias_momentum,
        bias_variance,
        bias_average,
        clip_scale,
        RATE_VECTOR,
        0.0,
    )
    return (
        layer_out,
        input_grad,
        grad_norm,
        expand_grad,
        expand_moment,
        expand_square,
        expand_updated,
        expand_smoothed,
        shrink_grad,
        shrink_moment,
        shrink_square,
        shrink_updated,
        shrink_smoothed,
        spatial_grad,
        spatial_moment,
        spatial_square,
        spatial_updated,
        spatial_smoothed,
        gains_grad,
        gains_moment,
        gains_square,
        gains_updated,
        gains_smoothed,
        bias_grad,
        bias_moment,
        bias_square,
        bias_updated,
        bias_smoothed,
    )


def solution(mesh):
    placed = (
        P("wide", "narrow", None),
        P("wide", "narrow", None),
        P("wide", None),
        P("wide", None),
        P("wide", None),
        P("wide", None),
        P("wide", None),
        P("wide", None),
        P("wide", None),
        P("wide", None),
        P("wide", None),
        P("wide", None),
        P("wide", None),
        P("wide", None),
        P("wide", None),
        P("wide"),
        P("wide"),
        P("wide"),
        P("wide"),
        P("wide"),
        P("wide"),
        P("wide"),
        P("wide"),
    )
    return jax.shard_map(
        on_device,
        mesh=mesh,
        in_specs=placed,
        out_specs=(
            P("wide", "narrow", None),
            P("wide", "narrow", None),
            P(),
            P("wide", None),
            P("wide", None),
            P("wide", None),
            P("wide", None),
            P("wide", None),
            P("wide", None),
            P("wide", None),
            P("wide", None),
            P("wide", None),
            P("wide", None),
            P("wide", None),
            P("wide", None),
            P("wide", None),
            P("wide", None),
            P("wide", None),
            P("wide"),
            P("wide"),
            P("wide"),
            P("wide"),
            P("wide"),
            P("wide"),
            P("wide"),
            P("wide"),
            P("wide"),
            P("wide"),
        ),
        check_vma=False,
    )
```

profile of v0, /device:TPU:0, one launch (start us, length us, event | category | flops | bytes accessed | tf_op | source)
XLA Modules:
  0.0 678.1 jit_solution(678104147840212410)
XLA Ops:
  7.2 1.9 convert_element_type.94
  9.2 1.7 convert_element_type.108
  11.0 0.7 convert_element_type.91
  11.7 22.2 %all-gather = bf16[8,1,256]{2,1,0:T(2,128)(2,1)S(1)} all-gather(bf16[1,1,256]{2,1,0:T(2,128)(2,1)S(1)} %reshape.236), channel_id=1, replica_groups=mesh['wide'=8,'narrow'=4] {'wide'}, dimensions={0}, use_global_device_ids=true | all-gather | bytes 4608 | tf_op jit(solution)/shard_map/all_gather | solution.py:127
  33.9 1.4 convert_reduce_fusion.1
  35.4 1.7 fusion.37
  37.0 37.0 %all-gather.4.cloned.1.call-done = bf16[512,3072]{1,0:T(8,128)(2,1)} async-done(((bf16[64,3072]{1,0:T(8,128)(2,1)}), bf16[512,3072]{1,0:T(8,128)(2,1)}) %all-gather.4.cloned.1.call-update) | async-done | bytes 3145744 | tf_op jit(solution)/shard_map/all_gather | solution.py:124
  74.0 13.5 %multiply_multiply_fusion.2 = (f32[8,128,3072]{2,1,0:T(8,128)}, f32[8,128,3072]{2,1,0:T(8,128)}) fusion(bf16[512,3072]{1,0:T(8,128)(2,1)} %all-gather.4.cloned.1.call-done, bf16[8,128,512]{2,1,0:T(8,128)(2,1)} %param.23, f32[512]{0:T(512)S(1)} %bitcast.82, f32[8,128]{1,0:T(8,128)S(1)} %fusion.55, f32[8,128]{1,0:T(8,128)S(1)} %broadcast_multiply_fusion.4), kind=kOutput, calls=%fused_computation.10 | convolution fusion | flops 3249012736 | bytes 29370368 | tf_op jit(solution)/shard_map/rpd,df->rpf/dot_general | solution.py:63
  87.5 32.1 %all-gather.6.cloned.1.call-done = bf16[1536,512]{1,0:T(8,128)(2,1)} async-done(((bf16[192,512]{1,0:T(8,128)(2,1)}), bf16[1536,512]{1,0:T(8,128)(2,1)}) %all-gather.6.cloned.1.call-update) | async-done | bytes 1572880 | tf_op jit(solution)/shard_map/all_gather | solution.py:125
  119.6 10.0 %slice_reduce_fusion = (f32[8,128]{1,0:T(8,128)S(1)}, bf16[8,128,1536]{2,1,0:T(8,128)(2,1)S(1)}, f32[8,128,1536]{2,1,0:T(8,128)}) fusion(f32[8,128,3072]{2,1,0:T(8,128)} %get-tuple-element.76, bf16[8,128,512]{2,1,0:T(8,128)(2,1)} %param.24, bf16[1536,512]{1,0:T(8,128)(2,1)} %all-gather.6.cloned.1.call-done), kind=kOutput, calls=%fused_computation.26 | convolution fusion | flops 1615330304 | bytes 24645632 | tf_op jit(solution)/shard_map/rpd,hd->rph/dot_general | solution.py:158
  129.7 2.2 copy.121
  131.9 3.7 all-to-all-start.2
  136.2 33.6 %all_gather.17 = bf16[512,512]{1,0:T(8,128)(2,1)} all-gather(bf16[64,512]{1,0:T(8,128)(2,1)S(1)} %convert_element_type.98), channel_id=1, replica_groups=mesh['wide'=8,'narrow'=4] {'wide'}, dimensions={0}, use_global_device_ids=true | all-gather | bytes 589824 | tf_op jit(solution)/shard_map/all_gather | solution.py:126
  169.7 2.7 all-to-all-done.2
  173.5 4.7 convert_bitcast_fusion
  178.2 3.5 copy.103
  181.7 4.8 all-to-all-start.3
  186.6 36.9 %all-to-all-done.3 = bf16[8,512,1,384]{3,0,2,1:T(8,128)(2,1)} async-done(((bf16[8,512,1,384]{3,0,2,1:T(8,128)(2,1)}), bf16[8,512,1,384]{3,0,2,1:T(8,128)(2,1)}, u32[]{:S(2)}, u32[]{:S(2)}) %all-to-all-start.3) | async-done | bytes 3145760 | tf_op jit(solution)/shard_map/all_to_all | solution.py:174
  223.6 7.0 %copy.119 = f32[8,4,128,1,384]{4,1,2,0,3:T(4,128)} copy(bf16[8,4,128,1,384]{4,0,2,1,3:T(8,128)(2,1)} %bitcast.22) | data formatting | bytes 9437184 | tf_op jit(solution)/shard_map/convert_element_type | solution.py:183
  230.6 8.0 %reshape.230 = f32[8,128,1536]{2,1,0:T(8,128)} reshape(f32[8,128,4,1,384]{4,2,1,0,3:T(4,128)} %bitcast.72) | data formatting | bytes 12582912 | tf_op jit(solution)/shard_map/convert_element_type | solution.py:183
  238.6 5.6 multiply_reduce_fusion.1
  244.2 0.8 copy-done
  245.0 4.5 multiply_reduce_fusion
  249.5 6.4 broadcast_add_fusion
  255.9 2.2 copy.122
  258.1 4.7 all-to-all-start
  262.8 0.6 fusion.65
  264.3 19.2 %all-reduce = bf16[512]{0:T(512)(128)(2,1)S(1)} all-reduce(bf16[512]{0:T(512)(128)(2,1)S(1)} %dynamic-update-slice), channel_id=1, replica_groups=mesh['wide'=8,'narrow'=4] {'wide'}, use_global_device_ids=true, to_apply=%add | all-reduce | flops 512 | bytes 2048
  283.7 16.1 %all-to-all-done = bf16[8,128,4,384]{3,1,0,2:T(8,128)(2,1)} async-done(((bf16[8,128,4,384]{3,1,0,2:T(8,128)(2,1)}), bf16[8,128,4,384]{3,1,0,2:T(8,128)(2,1)}, u32[]{:S(2)}, u32[]{:S(2)}) %all-to-all-start) | async-done | bytes 3145760 | tf_op jit(solution)/shard_map/all_to_all | solution.py:142
  299.8 2.5 copy.97
  302.3 4.7 fusion.20
  307.0 3.5 copy.98
  310.5 4.7 all-to-all-start.1
  315.4 6.0 select_reduce_fusion
  321.5 30.7 %all-to-all-done.1 = bf16[8,512,1,384]{3,0,2,1:T(8,128)(2,1)} async-done(((bf16[8,512,1,384]{3,0,2,1:T(8,128)(2,1)}), bf16[8,512,1,384]{3,0,2,1:T(8,128)(2,1)}, u32[]{:S(2)}, u32[]{:S(2)}) %all-to-all-start.1) | async-done | bytes 3145760 | tf_op jit(solution)/shard_map/all_to_all | solution.py:149
  352.2 7.0 %copy.120 = f32[8,4,128,1,384]{4,1,2,0,3:T(4,128)} copy(bf16[8,4,128,1,384]{4,0,2,1,3:T(8,128)(2,1)} %bitcast.21) | data formatting | bytes 9437184 | tf_op jit(solution)/shard_map/convert_element_type | solution.py:152
  359.1 8.0 %reshape.229 = f32[8,128,1536]{2,1,0:T(8,128)} reshape(f32[8,128,4,1,384]{4,2,1,0,3:T(4,128)} %bitcast.73) | data formatting | bytes 12582912 | tf_op jit(solution)/shard_map/convert_element_type | solution.py:152
  367.1 12.1 %fusion.64 = (f32[8,128,1536]{2,1,0:T(8,128)}, bf16[8,128,1536]{2,1,0:T(8,128)(2,1)}) fusion(f32[8,128,1536]{2,1,0:T(8,128)} %get-tuple-element.78, f32[8,128,1536]{2,1,0:T(8,128)} %reshape.229, f32[8,128,3072]{2,1,0:T(8,128)} %get-tuple-element.76), kind=kLoop, calls=%fused_computation.127 | loop fusion | flops 4718592 | bytes 28311552 | tf_op jit(solution)/shard_map/mul | solution.py:162
  379.2 5.7 convolution_bitcast_fusion.1
  385.2 12.4 %fusion.6 = bf16[8,128,3072]{2,1,0:T(8,128)(2,1)S(1)} fusion(f32[8,128,3072]{2,1,0:T(8,128)} %get-tuple-element.77, f32[8,128,1536]{2,1,0:T(8,128)} %get-tuple-element.66, f32[8,128,1536]{2,1,0:T(8,128)} %get-tuple-element.70), kind=kLoop, calls=%fused_computation.8 | loop fusion | flops 66060288 | bytes 31457280 | tf_op jit(solution)/shard_map/convert_element_type | solution.py:83
  397.7 2.6 copy-done.3
  400.3 5.8 convolution_bitcast_fusion
  407.5 0.6 convert_reduce_fusion
  408.5 7.9 %fusion.38 = (f32[8,128]{1,0:T(8,128)S(1)}, f32[8,128,512]{2,1,0:T(8,128)S(1)}) fusion(bf16[8,128,512]{2,1,0:T(8,128)(2,1)} %param.23, f32[512]{0:T(512)S(1)} %bitcast.84, f32[8,128]{1,0:T(8,128)S(1)} %broadcast_multiply_fusion.4, bf16[8,128,3072]{2,1,0:T(8,128)(2,1)} %copy-done.3, bf16[512,3072]{1,0:T(8,128)(2,1)} %all-gather.4.cloned.1.call-done), kind=kOutput, calls=%fused_computation.62 | convolution fusion | flops 3223845888 | bytes 12593152 | tf_op jit(solution)/shard_map/rpf,df->rpd/dot_general | solution.py:87
  416.5 1.2 fusion.36
  417.7 35.0 %all-reduce.3 = (f32[2048]{0:T(1024)S(1)}, f32[512]{0:T(512)S(1)}) all-reduce(f32[2048]{0:T(1024)S(1)} %pad_maximum_fusion.1, f32[512]{0:T(512)S(1)} %bitcast.87), channel_id=5, replica_groups=mesh['wide'=8,'narrow'=4] {'wide'}, use_global_device_ids=true, to_apply=%region_23.24.clone | all-reduce | flops 2560 | bytes 20480
  452.8 6.0 all-reduce.4
  458.9 0.6 multiply_reduce_fusion.6
  459.5 0.6 negate_multiply_fusion
  460.1 1.9 reduce-scatter.6.cloned.1.call-done
  461.9 121.2 %reduce-scatter.4.cloned.1.call-done = f32[64,3072]{1,0:T(8,128)} async-done(((f32[512,3072]{1,0:T(8,128)}), f32[64,3072]{1,0:T(8,128)}) %reduce-scatter.4.cloned.1.call-update) | async-done | bytes 786448 | tf_op jit(solution)/shard_map/reduce_scatter | solution.py:199
  583.1 0.6 multiply_reduce_fusion.7
  583.7 5.1 fusion.39
  588.8 35.3 %all-reduce.8.cloned.1.call-done = (f32[64,3072]{1,0:T(8,128)}, f32[192,512]{1,0:T(8,128)}, f32[64,512]{1,0:T(8,128)}) async-done(((f32[64,3072]{1,0:T(8,128)}, f32[192,512]{1,0:T(8,128)}, f32[64,512]{1,0:T(8,128)}), (f32[64,3072]{1,0:T(8,128)}, f32[192,512]{1,0:T(8,128)}, f32[64,512]{1,0:T(8,128)})) %all-reduce.8.cloned.1.call-update) | async-done | bytes 1310736 | tf_op jit(solution)/shard_map/psum | solution.py:195
  624.1 1.5 multiply_reduce_fusion.5
  625.7 1.7 multiply_reduce_fusion.4
  627.4 1.9 multiply_reduce_fusion.3
  632.6 2.9 add_add_fusion.2
  635.5 21.8 %psum.47 = f32[]{:T(128)} all-reduce(f32[]{:T(128)S(6)} %add.180), channel_id=1, replica_groups=mesh['wide'=8,'narrow'=4] {'wide'}, use_global_device_ids=true, to_apply=%region_30.31 | all-reduce | flops 1 | bytes 8 | tf_op jit(solution)/shard_map/psum | solution.py:213
  658.0 1.3 multiply_add_fusion.11
  659.3 1.3 multiply_add_fusion.9
  660.6 2.0 multiply_add_fusion.4
  662.7 2.8 multiply_add_fusion.2
  665.4 4.3 multiply_add_fusion
  (71 shorter events, 3.5 us)
Async XLA Ops:
  7.2 66.8 %all-gather.4.cloned.1.call-start = ((), (), s32[]{:S(2)}) async-start(), calls=%async_computation.7 | async-start | bytes 3538944 | tf_op jit(solution)/shard_map/all_gather | solution.py:124
  9.2 110.4 %all-gather.6.cloned.1.call-start = ((), (), s32[]{:S(2)}) async-start(), calls=%async_computation.8 | async-start | bytes 1769472 | tf_op jit(solution)/shard_map/all_gather | solution.py:125
  129.7 5.9 copy-start.10
  129.7 6.2 copy-start.7
  131.9 40.6 %all-to-all-start.2 = ((bf16[8,128,4,384]{3,1,0,2:T(8,128)(2,1)}), bf16[8,128,4,384]{3,1,0,2:T(8,128)(2,1)S(1)}, u32[]{:S(2)}, u32[]{:S(2)}) async-start(bf16[8,128,4,384]{3,1,0,2:T(8,128)(2,1)} %bitcast.76), calls=%async_computation.2 | async-start | bytes 6291456 | tf_op jit(solution)/shard_map/all_to_all | solution.py:168
  172.5 1.0 copy-start.8
  173.0 5.3 copy-start.4
  181.7 41.8 %all-to-all-start.3 = ((bf16[8,512,1,384]{3,0,2,1:T(8,128)(2,1)}), bf16[8,512,1,384]{3,0,2,1:T(8,128)(2,1)}, u32[]{:S(2)}, u32[]{:S(2)}) async-start(bf16[8,512,1,384]{3,0,2,1:T(8,128)(2,1)} %copy.103), calls=%async_computation.3 | async-start | bytes 6291456 | tf_op jit(solution)/shard_map/all_to_all | solution.py:174
  238.6 6.4 copy-start
  255.9 6.9 %copy-start.13 = (f32[64]{0:T(128)S(1)}, f32[64]{0:T(128)}, u32[]{:S(2)}) copy-start(f32[64]{0:T(128)} %param.42) | copy-start | bytes 772
  255.9 6.9 %copy-start.11 = (u32[32]{0:T(128)S(1)}, u32[32]{0:T(128)}, u32[]{:S(2)}) copy-start(u32[32]{0:T(128)} %constant.51) | copy-start | bytes 388
  258.1 41.7 %all-to-all-start = ((bf16[8,128,4,384]{3,1,0,2:T(8,128)(2,1)}), bf16[8,128,4,384]{3,1,0,2:T(8,128)(2,1)}, u32[]{:S(2)}, u32[]{:S(2)}) async-start(bf16[8,128,4,384]{3,1,0,2:T(8,128)(2,1)} %bitcast.75), calls=%async_computation | async-start | bytes 6291456 | tf_op jit(solution)/shard_map/all_to_all | solution.py:142
  299.8 2.5 copy-start.9
  302.2 4.8 copy-start.5
  310.5 41.7 %all-to-all-start.1 = ((bf16[8,512,1,384]{3,0,2,1:T(8,128)(2,1)}), bf16[8,512,1,384]{3,0,2,1:T(8,128)(2,1)}, u32[]{:S(2)}, u32[]{:S(2)}) async-start(bf16[8,512,1,384]{3,0,2,1:T(8,128)(2,1)} %copy.98), calls=%async_computation.1 | async-start | bytes 6291456 | tf_op jit(solution)/shard_map/all_to_all | solution.py:149
  315.2 144.9 %reduce-scatter.8.cloned.1.call-start = ((), (), s32[]{:S(2)}) async-start(), calls=%async_computation.11 | async-start | bytes 1179648 | tf_op jit(solution)/shard_map/reduce_scatter | solution.py:201
  321.4 140.5 %reduce-scatter.6.cloned.1.call-start = ((), (), s32[]{:S(2)}) async-start(), calls=%async_computation.10 | async-start | bytes 3538944 | tf_op jit(solution)/shard_map/reduce_scatter | solution.py:200
  384.9 198.2 %reduce-scatter.4.cloned.1.call-start = ((), (), s32[]{:S(2)}) async-start(), calls=%async_computation.9 | async-start | bytes 7077888 | tf_op jit(solution)/shard_map/reduce_scatter | solution.py:199
  385.2 15.1 %copy-start.1 = (bf16[8,128,512]{2,1,0:T(8,128)(2,1)S(1)}, bf16[8,128,512]{2,1,0:T(8,128)(2,1)}, u32[]{:S(2)}) copy-start(bf16[8,128,512]{2,1,0:T(8,128)(2,1)} %param.23) | copy-start | bytes 3145732
  397.7 2.7 copy-start.3
  406.1 218.0 %all-reduce.8.cloned.1.call-start = ((), (), s32[]{:S(2)}) async-start(), calls=%async_computation.12 | async-start | bytes 2621440 | tf_op jit(solution)/shard_map/psum | solution.py:195
  408.5 8.0 %copy-start.2 = (bf16[8,128,512]{2,1,0:T(8,128)(2,1)S(1)}, bf16[8,128,512]{2,1,0:T(8,128)(2,1)}, u32[]{:S(2)}) copy-start(bf16[8,128,512]{2,1,0:T(8,128)(2,1)} %param.23) | copy-start | bytes 3145732
  458.9 124.9 %copy-start.12 = (f32[256]{0:T(256)}, f32[256]{0:T(256)S(1)}, u32[]{:S(2)}) copy-start(f32[256]{0:T(256)S(1)} %get-tuple-element.36) | copy-start | bytes 3076
  458.9 124.9 %copy-start.14 = (f32[64]{0:T(128)}, f32[64]{0:T(128)S(1)}, u32[]{:S(2)}) copy-start(f32[64]{0:T(128)S(1)} %get-tuple-element.37) | copy-start | bytes 772
  588.8 73.8 %copy-start.6 = (f32[192,512]{1,0:T(8,128)S(1)}, f32[192,512]{1,0:T(8,128)}, u32[]{:S(2)}) copy-start(f32[192,512]{1,0:T(8,128)} %param.30) | copy-start | bytes 1179652
Sparse Core Ops, SparseCore 0:
  10.8 63.1 all-gather.3
  76.8 42.7 all-gather.5
  321.5 62.7 reduce-scatter.7
  388.2 73.6 reduce-scatter.5
  465.8 117.2 reduce-scatter.3
  585.6 38.4 all-reduce.7
where the time goes:
time: 686 us; the launch traced here: 678 us
  waiting for transfers between devices  314 us (46%)
  blocking collectives  138 us (20%)
  other arithmetic  72.3 us (11%)
  matrix products  63.5 us (9%)
  local copies, waits for them, and re-layouts  49.9 us (7%)
  between operations  22 us (3%)
  starting transfers between devices  18.6 us (3%)
    reduce_scatter x1, waiting for transfers between devices, on_device(): lax.psum_scatter(totals[0], 'wide', scatter_dimension=0, tiled=True)  121 us
    unnamed x2, blocking collectives  54.2 us
    all_gather x1, waiting for transfers between devices, on_device(): lax.all_gather(expand_weight.astype(jnp.bfloat16), 'wide', axis=0, tiled=...  37 us
    all_to_all x1, waiting for transfers between devices, on_device(): lax.all_to_all(grad_gate_low, 'narrow', split_axis=1, concat_axis=2, tile...  36.9 us
    psum x1, waiting for transfers between devices, on_device(): lax.psum((local_grads[0], local_grads[1], local_grads[2], local_grads[3],...  35.3 us
    all_gather x1, blocking collectives, on_device(): lax.all_gather(spatial_weight.astype(jnp.bfloat16), 'wide', axis=0, tiled...  33.6 us
    all_gather x1, waiting for transfers between devices, on_device(): lax.all_gather(shrink_weight.astype(jnp.bfloat16), 'wide', axis=0, tiled=...  32.1 us
    all_to_all x1, waiting for transfers between devices, on_device(): lax.all_to_all(mixed_low, 'narrow', split_axis=1, concat_axis=2, tiled=True)  30.7 us
  transfers between devices with their start and end apart: 10, of which 9 were waited for; matrix products, arithmetic and copies ran while one was open for 14% of the time, Pallas kernels for 0%

commit v1 on v0

v1 whole, which is shorter than its diff:
```python
import functools

import jax
import jax.numpy as jnp
from jax import lax
from jax.experimental import pallas as pl
from jax.experimental.pallas import tpu as pltpu
from jax.sharding import PartitionSpec as P

D = 512
FF = 3072
ROW = 512
DOCS = 5
STEP = 10
HALF = 1536

LAYER_EPS = 1e-05
CLIP_LIMIT = 1.0
BETA_FIRST = 0.9
BETA_SECOND = 0.999
ADAM_EPS = 1e-08
RATE_MATRIX = 0.03
RATE_VECTOR = 0.2
DECAY_MATRIX = 0.1
EMA_DECAY = 0.9999

F32 = jnp.float32
BF16 = jnp.bfloat16
GELU_A = 0.7978845608028654
GELU_B = GELU_A * 0.044715
LANES = 128
CHUNK = 64
BLOCK = 16
VMEM_LIMIT = 16 * 1024 * 1024

PIECES = ((0, 0), (1, 0), (0, 1), (1, 1))
WIDTH = 256
SPLIT = 1024
VECTOR_LANES = 128


def gelu_gate(hidden):
    squares = hidden * hidden
    gate = 0.5 * jnp.tanh(hidden * (GELU_A + GELU_B * squares)) + 0.5
    return squares, gate


def gelu_slope(hidden, squares, gate):
    return gate * (1.0 + hidden * (1.0 - gate) * (2.0 * GELU_A + 6.0 * GELU_B * squares))


def doc_ids(places, lens_ref, row):
    bound = jnp.int32(0)
    ids = jnp.zeros(places.shape, jnp.int32)
    for k in range(DOCS - 1):
        bound = bound + lens_ref[row, k]
        ids = ids + (places >= bound).astype(jnp.int32)
    return ids


def doc_mask(start, rows, lens_ref, row):
    across = doc_ids(lax.broadcasted_iota(jnp.int32, (1, ROW), 1), lens_ref, row)
    down = doc_ids(lax.broadcasted_iota(jnp.int32, (rows, 1), 0) + start, lens_ref, row)
    live = down != DOCS - 1
    return jnp.where(live, down, -1) == across, live


def dot(left, right, dims=((1,), (0,))):
    return lax.dot_general(left, right, (dims, ((), ())), preferred_element_type=F32)


def run(start, size):
    return pl.ds(pl.multiple_of(start, size), size)


def fetch_weights(sources, moves, tree):
    if not tree:
        for source, (_, _, _, target, _, _, _, sem) in zip(sources, moves):
            pltpu.make_async_copy(source, target, sem).start()
        return
    wide, core = lax.axis_index("wide"), lax.axis_index("narrow") & 1
    for base, first, count, target, height, unit, shift, sem in moves:
        for i, (x_off, core_off) in enumerate(PIECES):
            for step in range(4):
                start = (wide ^ (2 * step + x_off)) * height + (core ^ core_off) * unit + shift
                pltpu.make_async_copy(
                    sources[base + i].at[step, :, pl.ds(first, count)], target.at[run(start, 32), :], sem
                ).start()


def wait_weights(targets):
    for target, sem in targets:
        pltpu.make_async_copy(target, target, sem).wait()


def cut_kernel(acts_ref, cots_ref, core_out, pair_out, sems):
    rows_here = core_out.shape[1]
    narrow = lax.axis_index("narrow")
    copies = []
    for i, ref in enumerate((acts_ref, cots_ref)):
        for j, target in ((1, core_out.at[i]), (2, pair_out.at[0, i]), (3, pair_out.at[1, i])):
            source = ref.at[pl.ds((narrow ^ j) * rows_here, rows_here)]
            copies.append(pltpu.make_async_copy(source, target, sems.at[len(copies)]))
    for copy in copies:
        copy.start()
    for copy in copies:
        copy.wait()


def pack_first_kernel(expand_ref, spatial_ref, gains_ref, bias_ref, out_ref, expand, spatial, gains, bias, sems):
    rows = run((lax.axis_index("narrow") & 1) * 32, 32)
    copies = [
        pltpu.make_async_copy(expand_ref.at[rows, pl.ds(HALF, HALF)], expand, sems.at[0]),
        pltpu.make_async_copy(spatial_ref.at[rows, :], spatial, sems.at[1]),
        pltpu.make_async_copy(gains_ref, gains, sems.at[2]),
        pltpu.make_async_copy(bias_ref, bias, sems.at[3]),
    ]
    for copy in copies:
        copy.start()
    for copy in copies:
        copy.wait()
    vectors = jnp.concatenate(
        [
            gains[...],
            jnp.concatenate([bias[...], jnp.zeros((1, LANES - 64), F32)], axis=1),
            jnp.zeros((29, LANES), F32),
        ],
        axis=0,
    )
    out_ref[:, HALF + ROW :] = vectors.astype(BF16)
    out_ref[:, :HALF] = expand[...].astype(BF16)
    out_ref[:, HALF : HALF + ROW] = spatial[...].astype(BF16)


def pack_second_kernel(expand_ref, shrink_ref, expand_out, shrink_out, expand, shrink, sems):
    core = lax.axis_index("narrow") & 1
    copies = [
        pltpu.make_async_copy(expand_ref.at[run(core * 32, 32), pl.ds(0, HALF)], expand, sems.at[0]),
        pltpu.make_async_copy(shrink_ref.at[run(core * 96, 32 * 3), :], shrink, sems.at[1]),
    ]
    for copy in copies:
        copy.start()
    for copy in copies:
        copy.wait()
    expand_out[...] = expand[...].astype(BF16)
    for k in range(3):
        shrink_out[:, k * D : (k + 1) * D] = shrink[k * 32 : (k + 1) * 32, :].astype(BF16)


def stack_kernel(*refs):
    for i, ref in enumerate(refs[:-1]):
        refs[-1][i] = ref[...]


def add_kernel(*refs):
    total = refs[0][...] + refs[1][...]
    if len(refs) == 5:
        total = total + (refs[2][...] + refs[3][...])
    refs[-1][...] = total


def fetch_kernel(*refs):
    count = (len(refs) - 1) // 2
    copies = [pltpu.make_async_copy(refs[i], refs[count + i], refs[-1].at[i]) for i in range(count)]
    for copy in copies:
        copy.start()
    for copy in copies:
        copy.wait()


def gating_kernel(tree, count, members, lens_ref, own_ref, core_ref, side_ref, forward_ref, *refs):
    parts = [core_ref.at[0], side_ref.at[0, 0], forward_ref.at[1, 0]]
    sources, small_sources = refs[:count], refs[count : count + 2]
    (
        normed_ref, xhat_ref, scale_ref, gate_ref, slope_ref, rstd_ref, mixed_ref, spatial_ref, gains_ref, weight,
        small, acts, active, sums, bias_col, sems,
    ) = refs[count + 2 :]
    wide, narrow = lax.axis_index("wide"), lax.axis_index("narrow")
    rows_here, quarter = acts.shape[1:3]

    pltpu.make_async_copy(own_ref.at[pl.ds(narrow * rows_here, rows_here)], acts.at[narrow], sems.at[3]).start()
    for j, part in enumerate(parts):
        pltpu.make_async_copy(part, acts.at[narrow ^ (j + 1)], sems.at[3]).start()
    fetch_weights(
        sources,
        [
            (0, 0, HALF, weight, 64, 32, 0, sems.at[0]),
            (0, HALF, ROW, spatial_ref, 64, 32, 0, sems.at[1]),
        ],
        tree,
    )
    if tree:
        for x_off in range(2):
            for step in range(4):
                pltpu.make_async_copy(
                    small_sources[x_off].at[step, pl.ds(0, BLOCK), pl.ds(HALF + ROW, 128)],
                    small.at[wide ^ (2 * step + x_off)],
                    sems.at[2],
                ).start()
    else:
        pltpu.make_async_copy(small_sources[0], small, sems.at[2]).start()
    wait_weights([(weight, sems.at[0]), (spatial_ref, sems.at[1]), (small, sems.at[2]), (acts, sems.at[3])])
    diagonal = lax.broadcasted_iota(jnp.int32, (64, 128), 0) == lax.broadcasted_iota(jnp.int32, (64, 128), 1)
    for owner in range(8):
        values = small[owner].astype(F32)
        for k in range(2):
            gains_ref[:, owner * 256 + k * 128 : owner * 256 + (k + 1) * 128] = jnp.broadcast_to(
                values[k : k + 1, :], (8, 128)
            )
        column = jnp.sum(jnp.where(diagonal, values[2:3, :], 0.0), axis=1, keepdims=True)
        bias_col[owner * 64 : (owner + 1) * 64, :] = jnp.broadcast_to(column, (64, 128))

    def do_row(row, carry):
        for member in range(members):
            here = slice(member * quarter, (member + 1) * quarter)
            values = acts[member, row].astype(F32)
            shifted = values - jnp.mean(values, axis=1, keepdims=True)
            scale = lax.rsqrt(jnp.mean(shifted * shifted, axis=1, keepdims=True) + LAYER_EPS)
            xhat = shifted * scale
            scale_ref[row, here, :] = jnp.broadcast_to(scale, (quarter, 128))
            xhat_ref[row, here, :] = xhat.astype(BF16)
            normed_ref[row, here, :] = (xhat * gains_ref[0:1, :D]).astype(BF16)

        normed = normed_ref[row]
        for c in range(0, HALF, WIDTH):
            hidden = dot(normed, weight[:, c : c + WIDTH])
            for p in range(0, ROW, CHUNK):
                here = slice(p, p + CHUNK)
                values = hidden[here]
                squares, gate = gelu_gate(values)
                slope_ref[row, here, c : c + WIDTH] = gelu_slope(values, squares, gate).astype(BF16)
                result = values * gate
                active[here, c : c + WIDTH] = result
                total = result[:, :LANES] + result[:, LANES:]
                sums[here, :] = total if c == 0 else sums[here, :] + total
        for p in range(0, ROW, CHUNK):
            here = slice(p, p + CHUNK)
            centre = jnp.sum(sums[here, :], axis=1, keepdims=True) * (1.0 / HALF)
            total = jnp.zeros((CHUNK, LANES), F32)
            for c in range(0, HALF, LANES):
                shifted = active[here, c : c + LANES] - centre
                total = total + shifted * shifted
            scale = lax.rsqrt(jnp.sum(total, axis=1, keepdims=True) * (1.0 / HALF) + LAYER_EPS)
            rstd_ref[row, here, :] = jnp.broadcast_to(scale, (CHUNK, 128))
            for c in range(0, HALF, LANES):
                vhat = (active[here, c : c + LANES] - centre) * scale
                gate_ref[row, here, c : c + LANES] = (vhat * gains_ref[0:1, D + c : D + c + LANES]).astype(BF16)

        same, live = doc_mask(0, ROW, lens_ref, narrow * rows_here + row)
        masked = jnp.where(same, spatial_ref[...], jnp.zeros((), BF16))
        bias = jnp.where(live, bias_col[:, 0:1], 0.0)
        for c in range(0, HALF, WIDTH):
            mixed_ref[row, :, c : c + WIDTH] = (dot(masked, gate_ref[row, :, c : c + WIDTH]) + bias).astype(BF16)
        return carry

    lax.fori_loop(0, rows_here, do_row, 0)


def emit_blocks(order, read, columns, first, keep_near, keep_far, send):
    wide, narrow = lax.axis_index("wide"), lax.axis_index("narrow")
    for core in range(2):
        for one in range(2):
            for two in range(2):
                for step in range(4):
                    x_off, y_off = (one, two) if order == "x" else (two, one)
                    values = read(wide ^ (2 * step + x_off), narrow ^ (2 * y_off + core)).astype(BF16)
                    place = pl.ds(first, columns)
                    if core == 1:
                        send[one, two, step, :, place] = values
                    elif one == 1:
                        keep_far[two, step, :, place] = values
                    else:
                        keep_near[two, step, :, place] = values


def reader(matrix, height, part, shift, columns):
    def read(owner, member):
        return matrix[run(owner * height + member * part + shift, BLOCK), columns]

    return read


def content_up_kernel(tree, normed_ref, *refs):
    sources, (content_ref, slope_ref, weight, sem) = refs[:-4], refs[-4:]
    tokens = normed_ref.shape[0] * normed_ref.shape[1]
    if tree:
        fetch_weights(sources, [(0, 0, HALF, weight, 64, 32, 0, sem)], tree)
    else:
        pltpu.make_async_copy(sources[0], weight, sem).start()
    wait_weights([(weight, sem)])

    def do_channels(k, carry):
        channels = run(k * WIDTH, WIDTH)
        hidden = dot(normed_ref[...].reshape(tokens, D), weight[:, channels])
        for p in range(0, tokens, CHUNK):
            r, here = p // ROW, slice(p % ROW, p % ROW + CHUNK)
            values = hidden[p : p + CHUNK]
            squares, gate = gelu_gate(values)
            content_ref[r, here, channels] = (values * gate).astype(BF16)
            slope_ref[r, here, channels] = gelu_slope(values, squares, gate).astype(BF16)
        return carry

    lax.fori_loop(0, HALF // WIDTH, do_channels, 0)


def content_down_kernel(
    tree, count, members, lens_ref, content_ref, slope_ref, mixed_ref, own_ref, core_ref, side_ref, forward_ref, *refs
):
    parts = [core_ref.at[1], side_ref.at[0, 1], forward_ref.at[1, 1]]
    sources = refs[:count]
    gated_ref, grad_ref, grad_mixed_ref, bias_ref, shrink = refs[count : count + 5]
    raws = refs[count + 5 : count + (8 if tree else 6)]
    cots, sums, tall_sum, sems = refs[count + 5 + len(raws) :]
    narrow = lax.axis_index("narrow")
    rows_here, quarter = core_ref.shape[1:3]
    tokens = rows_here * ROW

    if tree:
        fetch_weights(sources, [(0, k * D, D, shrink, 192, 96, k * 32, sems.at[0]) for k in range(3)], tree)
    else:
        pltpu.make_async_copy(sources[0], shrink, sems.at[0]).start()
    for r in range(rows_here):
        for j in range(members):
            source = own_ref.at[narrow * rows_here + r] if j == 0 else parts[j - 1].at[r]
            place = run(r * ROW + (narrow ^ j) * quarter, quarter)
            pltpu.make_async_copy(source, cots.at[place, :], sems.at[1]).start()
    sums[...] = jnp.zeros_like(sums)
    wait_weights([(shrink, sems.at[0]), (cots, sems.at[1])])

    def do_channels(k, carry):
        channels = run(k * WIDTH, WIDTH)
        grad_gated = dot(cots[...], shrink[channels, :], ((1,), (1,)))
        for p in range(0, tokens, CHUNK):
            r, here = p // ROW, slice(p % ROW, p % ROW + CHUNK)
            grads = grad_gated[p : p + CHUNK]
            content = content_ref[r, here, channels].astype(F32)
            mixed = mixed_ref[r, here, channels].astype(F32)
            slope = slope_ref[r, here, channels].astype(F32)
            gated_ref[r, here, channels] = (content * mixed).astype(BF16)
            grad_ref[r, here, channels] = (grads * mixed * slope).astype(BF16)
            grad_mixed = (grads * content).astype(BF16)
            grad_mixed_ref[r, here, channels] = grad_mixed
            total = grad_mixed.astype(F32)
            sums[p : p + CHUNK, :] += total[:, :LANES] + total[:, LANES:]
        tall_sum[channels, :] = dot(gated_ref[:, :, channels].reshape(tokens, WIDTH), cots[...], ((0,), (0,)))
        return carry

    lax.fori_loop(0, HALF // WIDTH, do_channels, 0)
    for r in range(rows_here):
        _, live = doc_mask(0, ROW, lens_ref, narrow * rows_here + r)
        part = jnp.where(live, sums[r * ROW : (r + 1) * ROW, :], 0.0)
        bias_ref[...] = part if r == 0 else bias_ref[...] + part
    if tree:
        for j in range(3):
            emit_blocks("y", reader(tall_sum, 192, 48, j * BLOCK, slice(0, D)), D, j * D, *raws)
    else:
        raws[0][...] = tall_sum[...]


def content_sum_kernel(tree, normed_ref, grad_ref, *refs):
    raws, normed_turned, wide_sum = refs[:-2], refs[-2], refs[-1]
    tokens = normed_ref.shape[0] * normed_ref.shape[1]
    normed_turned[...] = normed_ref[...].reshape(tokens, D).T
    for c in range(0, HALF, D):
        wide_sum[...] = dot(normed_turned[...], grad_ref[:, :, c : c + D].reshape(tokens, D))
        if tree:
            emit_blocks("x", reader(wide_sum, 64, 16, 0, slice(0, D)), D, c, *raws)
        else:
            raws[0][:, c : c + D] = wide_sum[...]


def spatial_sum_kernel(lens_ref, grad_mixed_ref, gate_ref, square_ref):
    rows_here = grad_mixed_ref.shape[0]
    narrow = lax.axis_index("narrow")
    for row in range(rows_here):
        same, _ = doc_mask(0, ROW, lens_ref, narrow * rows_here + row)
        products = jnp.where(same, dot(grad_mixed_ref[row], gate_ref[row], ((1,), (1,))), 0.0)
        square_ref[...] = products if row == 0 else square_ref[...] + products


def gate_back_kernel(
    lens_ref, grad_mixed_ref, gate_ref, slope_ref, rstd_ref, spatial_ref, gains_ref, bias_ref,
    grad_ref, vectors_ref, turned, grad_gate, first_sums, second_sums, second, inverse,
):
    rows_here = grad_mixed_ref.shape[0]
    narrow = lax.axis_index("narrow")
    turned[...] = spatial_ref[...].T
    second[...] = jnp.zeros_like(second)
    inverse[...] = 1.0 / gains_ref[:, D:]

    def do_row(row, carry):
        same, _ = doc_mask(0, ROW, lens_ref, narrow * rows_here + row)
        masked = jnp.where(same, turned[...], jnp.zeros((), BF16))
        for c in range(0, HALF, WIDTH):
            grads_all = dot(masked, grad_mixed_ref[row, :, c : c + WIDTH])
            vector = jnp.zeros((8, WIDTH), F32)
            for p in range(0, ROW, CHUNK):
                here = slice(p, p + CHUNK)
                low = grads_all[here].astype(BF16)
                grad_gate[here, c : c + WIDTH] = low
                grads = low.astype(F32)
                products = grads * gate_ref[row, here, c : c + WIDTH].astype(F32)
                vector = vector + jnp.sum(products.reshape(CHUNK // 8, 8, WIDTH), axis=0)
                scaled = grads * gains_ref[0:1, D + c : D + c + WIDTH]
                first = scaled[:, :LANES] + scaled[:, LANES:]
                other = products[:, :LANES] + products[:, LANES:]
                first_sums[here, :] = first if c == 0 else first_sums[here, :] + first
                second_sums[here, :] = other if c == 0 else second_sums[here, :] + other
            second[:, c : c + WIDTH] += vector
        for p in range(0, ROW, CHUNK):
            here = slice(p, p + CHUNK)
            scale = rstd_ref[row, here, 0:1]
            first_mean = jnp.sum(first_sums[here, :], axis=1, keepdims=True) * (1.0 / HALF) * scale
            second_mean = jnp.sum(second_sums[here, :], axis=1, keepdims=True) * (1.0 / HALF) * scale
            for c in range(0, HALF, LANES):
                place = slice(c, c + LANES)
                scaled = grad_gate[here, place].astype(F32) * gains_ref[0:1, D + c : D + c + LANES] * scale
                vhat = gate_ref[row, here, place].astype(F32) * inverse[0:1, place]
                slope = slope_ref[row, here, place].astype(F32)
                grad_ref[row, here, place] = ((scaled - first_mean - vhat * second_mean) * slope).astype(BF16)
        return carry

    lax.fori_loop(0, rows_here, do_row, 0)
    vectors_ref[...] = jnp.zeros_like(vectors_ref)
    diagonal = lax.broadcasted_iota(jnp.int32, (64, 128), 0) == lax.broadcasted_iota(jnp.int32, (64, 128), 1)
    for owner in range(8):
        for k in range(2 if owner >= 2 else 0):
            c = (owner - 2) * 256 + k * 128
            total = jnp.sum(second[:, c : c + 128], axis=0, keepdims=True)
            vectors_ref[owner, k : k + 1, :] = total * inverse[0:1, c : c + 128]
        column = jnp.sum(bias_ref[owner * 64 : (owner + 1) * 64, :], axis=1, keepdims=True)
        vectors_ref[owner, 2:3, :] = jnp.sum(jnp.where(diagonal, column, 0.0), axis=0, keepdims=True)


def gate_sum_kernel(tree, normed_ref, grad_ref, square_ref, vectors_ref, *refs):
    raws, normed_turned, wide_sum = refs[:-2], refs[-2], refs[-1]
    tokens = normed_ref.shape[0] * normed_ref.shape[1]
    rest = HALF - SPLIT
    normed_turned[...] = normed_ref[...].reshape(tokens, D).T
    if tree:
        emit_blocks("y", reader(square_ref, 64, 16, 0, slice(0, ROW)), ROW, rest, *raws[3:])
        emit_blocks("y", lambda owner, member: vectors_ref[owner], VECTOR_LANES, rest + ROW, *raws[3:])
    else:
        raws[1][...] = square_ref[...]
        raws[2][...] = vectors_ref[...]
    for c in range(0, HALF, D):
        wide_sum[...] = dot(normed_turned[...], grad_ref[:, :, c : c + D].reshape(tokens, D))
        if not tree:
            raws[0][:, c : c + D] = wide_sum[...]
        elif c < SPLIT:
            emit_blocks("x", reader(wide_sum, 64, 16, 0, slice(0, D)), D, c, *raws[:3])
        else:
            emit_blocks("y", reader(wide_sum, 64, 16, 0, slice(0, D)), D, c - SPLIT, *raws[3:])


def layer_kernel(gated_ref, shrink, own_ref, core_ref, pair_ref, total):
    members, rows_here, quarter = total.shape[:3]
    narrow = lax.axis_index("narrow")
    for row in range(rows_here):
        added = dot(gated_ref[row], shrink[...])
        for member in range(members):
            total[member ^ narrow, row] = added[member * quarter : (member + 1) * quarter].astype(BF16)
    own_ref[...] = total[0]
    core_ref[...] = total[1]
    pair_ref[0] = total[2]
    pair_ref[1] = total[3]


def back_kernel(
    gate_grad_ref, content_grad_ref, gate_weight, weight, xhat_ref, scale_ref, gains_ref, layer_core, layer_pair,
    own_ref, core_ref, pair_ref, total,
):
    members, rows_here, quarter = total.shape[:3]
    narrow = lax.axis_index("narrow")
    for row in range(rows_here):
        grad_normed = dot(gate_grad_ref[row], gate_weight[...], ((1,), (1,))) + dot(
            content_grad_ref[row], weight[...], ((1,), (1,))
        )
        for member in range(members):
            here = slice(member * quarter, (member + 1) * quarter)
            xhat = xhat_ref[row, here, :].astype(F32)
            scaled = grad_normed[here] * gains_ref[0:1, :D]
            first_mean = jnp.mean(scaled, axis=1, keepdims=True)
            second_mean = jnp.mean(scaled * xhat, axis=1, keepdims=True)
            scale = scale_ref[row, here, 0:1]
            total[member ^ narrow, row] = ((scaled - first_mean - xhat * second_mean) * scale).astype(BF16)
    own_ref[...] = total[0]
    core_ref[0] = total[1]
    core_ref[1] = layer_core[...]
    for j in range(2):
        pair_ref[j, 0] = total[2 + j]
        pair_ref[j, 1] = layer_pair[j]


def give_kernel(
    cots_ref, acts_ref, grad_own, layer_own, core_ref, side_ref, forward_ref, grad_out, layer_out, grads, layers, sems
):
    rows_here = grad_own.shape[0]
    narrow = lax.axis_index("narrow")
    stores = []
    for kind, (base, own, total, out) in enumerate(
        ((cots_ref, grad_own, grads, grad_out), (acts_ref, layer_own, layers, layer_out))
    ):
        parts = [own, core_ref.at[kind], side_ref.at[0, kind], forward_ref.at[1, kind]]
        for j, part in enumerate(parts):
            rows = pl.ds((narrow ^ j) * rows_here, rows_here)
            total[j] = (base[rows].astype(F32) + part[...].astype(F32)).astype(total.dtype)
            stores.append(pltpu.make_async_copy(total.at[j], out.at[rows], sems.at[kind, j]))
            stores[-1].start()
    for store in stores:
        store.wait()


def sum_three(near_ref, came_ref, far_ref, half, columns):
    values = near_ref[half, :, :, columns].astype(F32) + came_ref[0, half, :, :, columns].astype(F32)
    return values + far_ref[half, :, :, columns].astype(F32)


def side_kernel(*refs):
    inputs, outputs = refs[:12], refs[12:]
    for i, out_ref in enumerate(outputs):
        first = 0
        for group in range(2):
            near, came, far = inputs[6 * i + 3 * group : 6 * i + 3 * group + 3]
            width = near.shape[3]
            for c in range(0, width, LANES):
                out_ref[:, :, first + c : first + c + LANES] = sum_three(
                    near, came, far, 1, slice(c, c + LANES)
                ).astype(BF16)
            first += width


def fold_kernel(*refs):
    inputs, sides, outputs = refs[:12], refs[12:14], refs[14:]
    base = 0
    for i in range(2):
        first = 0
        for group in range(2):
            near, came, far = inputs[6 * i + 3 * group : 6 * i + 3 * group + 3]
            width = near.shape[3]
            for c in range(0, width, LANES):
                place = slice(first + c, first + c + LANES)
                total = sum_three(near, came, far, 0, slice(c, c + LANES)) + sides[i][:, :, place].astype(F32)
                there = slice(base + first + c, base + first + c + LANES)
                outputs[0][:, there] = total[0]
                for step in range(1, 4):
                    outputs[step][:, there] = total[step].astype(BF16)
            first += width
        base += first


def norm_kernel(mine_ref, one_ref, two_ref, three_ref, weight_ref, gains_ref, low_ref, message_ref):
    wide, narrow = lax.axis_index("wide"), lax.axis_index("narrow")
    columns = mine_ref.shape[1]
    squares = jnp.zeros((BLOCK, LANES), F32)
    products = jnp.zeros((BLOCK, LANES), F32)
    here = run(narrow * BLOCK, BLOCK)
    for c in range(0, columns, LANES):
        place = slice(c, c + LANES)
        total = mine_ref[:, place]
        for ref in (one_ref, two_ref, three_ref):
            total = total + ref[:, place].astype(F32)
        low = total.astype(BF16)
        low_ref[:, place] = low
        value = low.astype(F32)
        square = value * value
        squares = squares + (square if c < columns - LANES else jnp.where(narrow == 0, square, 0.0))
        at = expand_column(c)
        if at is not None:
            weight = weight_ref[here, at : at + LANES].astype(BF16).astype(F32)
            products = products + value * weight
    first = wide * 64 + narrow * BLOCK
    lanes = lax.broadcasted_iota(jnp.int32, (BLOCK, D), 1)
    diagonal = lanes == lax.broadcasted_iota(jnp.int32, (BLOCK, D), 0) + first
    gain = jnp.sum(jnp.where(diagonal, gains_ref[0:1, :D], 0.0), axis=1, keepdims=True)
    first_raw = jnp.sum(products, axis=1, keepdims=True) / gain
    total = jnp.sum(squares) + jnp.sum(first_raw * first_raw)
    places = jnp.sum(jnp.where(diagonal, first_raw, 0.0), axis=0, keepdims=True)
    message_ref[...] = jnp.full(message_ref.shape, total, F32)
    for k in range(D // LANES):
        message_ref[k : k + 1, :] = places[:, k * LANES : (k + 1) * LANES]


def expand_column(c):
    right = HALF + SPLIT
    turn = right + HALF
    if c < right:
        return c
    if turn <= c < turn + HALF - SPLIT:
        return c - HALF
    return None


def adam_kernel(message_ref, own_ref, side_ref, other_ref, *refs):
    states, vectors, outputs, vector_outputs, norm_ref = refs[:12], refs[12:20], refs[20:35], refs[35:45], refs[45]
    results, blocks, sem = refs[46:61], refs[61], refs[62]
    wide, narrow = lax.axis_index("wide"), lax.axis_index("narrow")
    norm = jnp.sqrt(message_ref[4:5, :])
    norm_ref[0, 0] = jnp.max(norm)
    clip = CLIP_LIMIT / jnp.maximum(norm, CLIP_LIMIT)
    right = HALF + SPLIT
    turn = right + HALF
    blocks[narrow] = own_ref[...]
    blocks[narrow ^ 1] = other_ref[0]
    blocks[narrow ^ 2] = side_ref[...]
    blocks[narrow ^ 3] = other_ref[1]

    def update(which, gradient, rows, place):
        weight, momentum, variance, average = [ref[rows, place] for ref in states[4 * which : 4 * which + 4]]
        updates = adam_update(
            weight, gradient.astype(F32), momentum, variance, average, clip, RATE_MATRIX, DECAY_MATRIX
        )
        for ref, value in zip(results[5 * which : 5 * which + 5], updates):
            ref[rows, place] = value

    def do_member(member, carry):
        thin = run(member * BLOCK, BLOCK)
        for c in range(0, turn + HALF - SPLIT + ROW, LANES):
            gradient = blocks[member, :, c : c + LANES]
            at = expand_column(c)
            if at is not None:
                update(0, gradient, thin, slice(at, at + LANES))
            elif c < turn:
                k, at = (c - right) // D, (c - right) % D
                update(1, gradient, run(member * 48 + k * BLOCK, BLOCK), slice(at, at + LANES))
            else:
                at = c - turn - (HALF - SPLIT)
                update(2, gradient, thin, slice(at, at + LANES))
        for i in range(15):
            rows = run(member * 48, 48) if 5 <= i < 10 else thin
            pltpu.make_async_copy(results[i].at[rows, :], outputs[i].at[rows, :], sem.at[i]).start()
        return carry

    lax.fori_loop(0, 4, do_member, 0)
    own = blocks[0, :, turn + HALF - SPLIT + ROW :].astype(F32)
    gains = jnp.where(wide == 0, message_ref[0:2, :], jnp.where(wide == 1, message_ref[2:4, :], own[0:2, :]))
    for which, gradient in ((0, gains), (1, own[2:3, :64])):
        weight, momentum, variance, average = [ref[...] for ref in vectors[4 * which : 4 * which + 4]]
        updates = adam_update(
            weight, gradient, momentum, variance, average, clip[:, : gradient.shape[1]], RATE_VECTOR, 0.0
        )
        for ref, value in zip(vector_outputs[5 * which : 5 * which + 5], updates):
            ref[...] = value
    for i in range(15):
        pltpu.make_async_copy(results[i], outputs[i], sem.at[i]).wait()


def call_kernel(kernel, name, args, in_specs, out_types, scratch, flops, limit=VMEM_LIMIT):
    vmem = pl.BlockSpec(memory_space=pltpu.VMEM)
    specs = [kind[1] if isinstance(kind, tuple) else vmem for kind in out_types]
    types = [
        kind[0] if isinstance(kind, tuple) else pltpu.VMEM(kind.shape, kind.dtype) for kind in out_types
    ]
    in_specs = [vmem if spec is None else spec for spec in in_specs]
    args = [
        pltpu.with_memory_space_constraint(value, pltpu.HBM) if spec.memory_space == pltpu.HBM else value
        for value, spec in zip(args, in_specs)
    ]
    results = pl.pallas_call(
        kernel,
        name=name,
        in_specs=in_specs,
        out_specs=specs,
        out_shape=types,
        scratch_shapes=scratch,
        compiler_params=pltpu.CompilerParams(vmem_limit_bytes=limit),
        cost_estimate=pl.CostEstimate(flops=int(flops), bytes_accessed=int(flops / 500), transcendentals=0),
    )(*args)
    return list(results)


def swap_with(value, axis, size, bit):
    return lax.ppermute(value, axis, [(i, i ^ bit) for i in range(size)])


def after(value, *others):
    return lax.optimization_barrier((value,) + others)[0]


def sum_core(keep_far, came):
    return (keep_far.astype(F32) + came[1].astype(F32)).astype(BF16)


def adam_update(weight, gradient, momentum, variance, average, clip_scale, step_rate, decay_rate):
    ema_rate = min(EMA_DECAY, (1.0 + STEP) / (10.0 + STEP))
    clipped = clip_scale * gradient
    moment = BETA_FIRST * momentum + (1.0 - BETA_FIRST) * clipped
    square = BETA_SECOND * variance + (1.0 - BETA_SECOND) * clipped * clipped
    first_hat = moment / (1.0 - BETA_FIRST**STEP)
    second_hat = square / (1.0 - BETA_SECOND**STEP)
    updated = weight - step_rate * (
        first_hat / (jnp.sqrt(second_hat) + ADAM_EPS) + decay_rate * weight
    )
    smoothed = ema_rate * average + (1.0 - ema_rate) * updated
    return (clipped, moment, square, updated, smoothed)


def on_device(
    activations,
    cotangent,
    doc_lengths,
    expand_weight,
    expand_momentum,
    expand_variance,
    expand_average,
    shrink_weight,
    shrink_momentum,
    shrink_variance,
    shrink_average,
    spatial_weight,
    spatial_momentum,
    spatial_variance,
    spatial_average,
    norm_gains,
    gains_momentum,
    gains_variance,
    gains_average,
    spatial_bias,
    bias_momentum,
    bias_variance,
    bias_average,
):
    narrow_size, wide_size = lax.axis_size("narrow"), lax.axis_size("wide")
    wide, narrow = lax.axis_index("wide"), lax.axis_index("narrow")
    group_rows, quarter = activations.shape[0], activations.shape[1]
    rows = group_rows // narrow_size
    tokens = rows * ROW
    tree = (wide_size, narrow_size) == (8, 4)
    smem = pl.BlockSpec(memory_space=pltpu.SMEM)
    anywhere = pl.BlockSpec(memory_space=pl.ANY)
    stored = pl.BlockSpec(memory_space=pltpu.HBM)
    shape = jax.ShapeDtypeStruct
    dma = pltpu.SemaphoreType.DMA
    part = shape((rows, quarter, D), BF16)
    product = 2 * tokens * HALF * D
    cross_x = lambda value: swap_with(value, "wide", wide_size, 1)
    cross_y = lambda value: swap_with(value, "narrow", narrow_size, 2)
    cross_core = lambda value: swap_with(value, "narrow", narrow_size, 1)

    def trade(core_part, pair):
        side = cross_y(pair)
        return [cross_core(core_part), side, cross_core(side)]

    def stack(values):
        kind = shape((len(values), *values[0].shape), values[0].dtype)
        return call_kernel(stack_kernel, "stack", values, [None] * len(values), [kind], [], product // 64)[0]

    def add(*values):
        kind = shape(values[0].shape, values[0].dtype)
        return call_kernel(add_kernel, "add", values, [None] * len(values), [kind], [], product // 64)[0]

    pair = shape((2, *part.shape), BF16)

    def cut(acts, cots):
        return call_kernel(
            cut_kernel,
            "cut",
            [acts, cots],
            [stored] * 2,
            [(pair, stored), (shape((2, *pair.shape), BF16), stored)],
            [dma((6,))],
            product // 64,
        )

    if tree:
        first_own = call_kernel(
            pack_first_kernel,
            "pack_first",
            [expand_weight, spatial_weight, norm_gains.reshape(2, LANES), spatial_bias.reshape(1, 64)],
            [stored] * 4,
            [shape((32, HALF + ROW + VECTOR_LANES), BF16)],
            [pltpu.VMEM((32, HALF), F32), pltpu.VMEM((32, ROW), F32), pltpu.VMEM((2, LANES), F32)]
            + [pltpu.VMEM((1, 64), F32), dma((4,))],
            product // 64,
        )[0]
        over_z = lambda own: [swap_with(own, "wide", wide_size, 2 * s) for s in range(1, 4)]
        came_z = over_z(first_own)
        core_cut, pair_cut = cut(after(activations, first_own), cotangent)
        side_came = cross_y(pair_cut)
        expand_own, shrink_own = call_kernel(
            pack_second_kernel,
            "pack_second",
            [expand_weight, shrink_weight],
            [stored, stored],
            [shape((32, HALF), BF16)] * 2,
            [pltpu.VMEM((32, HALF), F32), pltpu.VMEM((96, D), F32), dma((2,))],
            product // 64,
        )
        *came_z, core_came, _, expand_own = lax.optimization_barrier(
            (*came_z, cross_core(core_cut), pair_cut, expand_own)
        )
        first_near = stack([first_own, *came_z])
        first_across = cross_x(first_near)
        expand_own = after(expand_own, first_near)
        *came_z, side_came = lax.optimization_barrier((*over_z(expand_own), side_came))
        expand_near = stack([expand_own, *came_z])
        expand_across = cross_x(after(expand_near, first_across))
        shrink_own = after(shrink_own, expand_near)
        shrink_came = over_z(shrink_own)
        near_core = cross_core(after(first_near, expand_near))
        across_core = cross_core(after(first_across, expand_near))
        forward_came = cross_core(after(side_came, expand_near))
        first_pieces = [after(first_near, expand_near), first_across, near_core, across_core]
        small_pieces = first_pieces[:2]
        near_other = cross_core(expand_near)
        count = len(PIECES)
    else:
        gather = lambda value: lax.all_gather(value.astype(BF16), "wide", axis=0, tiled=True)
        expand_low = gather(expand_weight)
        gains_low, bias_low = gather(norm_gains), gather(spatial_bias)
        small = jnp.concatenate(
            [
                gains_low.reshape(8, 2, 128),
                jnp.pad(bias_low.reshape(8, 1, 64), ((0, 0), (0, 0), (0, 64))),
                jnp.zeros((8, 13, 128), BF16),
            ],
            axis=1,
        )
        first_pieces = [expand_low[:, HALF:], gather(spatial_weight)]
        small_pieces = [small, small]
        expand_pieces, shrink_pieces = [expand_low[:, :HALF]], [gather(shrink_weight)]
        core_came, side_came, forward_came = trade(*cut(activations, cotangent))
        count = 2

    low_d, low_half = shape((rows, ROW, D), BF16), shape((rows, ROW, HALF), BF16)
    thin = shape((rows, ROW, 128), F32)
    weight_type = shape((D, HALF), BF16)

    normed, xhat, scale, gate_normed, slope, rstd, mixed, spatial_low, gains, gate_weight = call_kernel(
        functools.partial(gating_kernel, tree, count, narrow_size),
        "gating",
        [doc_lengths, activations, core_came, side_came, forward_came] + list(first_pieces) + list(small_pieces),
        [smem, stored] + [anywhere] * (narrow_size - 1 + count + 2),
        [low_d, low_d, thin, low_half, low_half, thin, low_half]
        + [shape((ROW, ROW), BF16), shape((8, D + HALF), F32), weight_type],
        [
            pltpu.VMEM((8, BLOCK, 128), BF16),
            pltpu.VMEM((narrow_size, *part.shape), BF16),
            pltpu.VMEM((ROW, HALF), F32),
            pltpu.VMEM((ROW, 128), F32),
            pltpu.VMEM((ROW, 128), F32),
            dma((4,)),
        ],
        product // 64,
    )

    if tree:
        *shrink_came, expand_across, _ = lax.optimization_barrier((*shrink_came, expand_across, normed))
        shrink_near = stack([shrink_own, *shrink_came])
        shrink_across = cross_x(shrink_near)
        expand_pieces = [expand_near, expand_across, near_other, cross_core(expand_across)]
    content, content_slope, content_weight = call_kernel(
        functools.partial(content_up_kernel, tree),
        "content_up",
        [normed, *expand_pieces],
        [None] + [anywhere] * len(expand_pieces),
        [low_half, low_half, weight_type],
        [dma(())],
        product // 64,
    )
    if tree:
        shrink_across, _ = lax.optimization_barrier((shrink_across, content))
        shrink_pieces = [shrink_near, shrink_across, cross_core(shrink_near), cross_core(shrink_across)]

    def raw_outputs(column_list, plain):
        if tree:
            return [
                shape(size, BF16)
                for columns in column_list
                for size in ((2, 4, BLOCK, columns), (2, 4, BLOCK, columns), (2, 2, 4, BLOCK, columns))
            ]
        return [shape(size, F32) for size in plain]

    gated, content_grad, grad_mixed, bias_part, shrink_low, *shrink_raws = call_kernel(
        functools.partial(content_down_kernel, tree, len(shrink_pieces), narrow_size),
        "content_down",
        [doc_lengths, content, content_slope, mixed, cotangent, core_came, side_came, forward_came, *shrink_pieces],
        [smem, None, None, None, stored] + [anywhere] * (narrow_size - 1 + len(shrink_pieces)),
        [low_half, low_half, low_half, shape((ROW, 128), F32), shape((HALF, D), BF16)]
        + raw_outputs((HALF,), ((HALF, D),)),
        [
            pltpu.VMEM((tokens, D), BF16),
            pltpu.VMEM((tokens, 128), F32),
            pltpu.VMEM((HALF, D), F32),
            dma((2,)),
        ],
        product // 64,
    )
    if tree:
        came = {"shrink": cross_core(shrink_raws[2])}
    sum_scratch = [pltpu.VMEM((D, tokens), BF16), pltpu.VMEM((D, D), F32)]
    content_raws = call_kernel(
        functools.partial(content_sum_kernel, tree),
        "content_sum",
        [normed, content_grad],
        [None] * 2,
        raw_outputs((HALF,), ((D, HALF),)),
        sum_scratch,
        product // 64,
    )
    mixed_late = grad_mixed
    if tree:
        came["shrink"], content_raws[0] = lax.optimization_barrier((came["shrink"], content_raws[0]))
        came["content"] = cross_core(content_raws[2])
        far = {"shrink": sum_core(shrink_raws[1], came["shrink"])}
        came_far = {"shrink": cross_y(far["shrink"])}
        mixed_late = after(grad_mixed, far["shrink"])
    square_sum = call_kernel(
        spatial_sum_kernel,
        "spatial_sum",
        [doc_lengths, mixed_late, gate_normed],
        [smem, None, None],
        [shape((ROW, ROW), F32)],
        [],
        product // 64,
    )[0]
    if tree:
        came["content"], square_sum = lax.optimization_barrier((came["content"], square_sum))
        far["content"] = sum_core(content_raws[1], came["content"])
        came_far["content"] = cross_x(far["content"])
        mixed_late = after(grad_mixed, far["content"])

    gate_grad, vectors = call_kernel(
        gate_back_kernel,
        "gate_back",
        [doc_lengths, mixed_late, gate_normed, slope, rstd, spatial_low, gains, bias_part],
        [smem] + [None] * 7,
        [low_half, shape((8, BLOCK, 128), F32)],
        [
            pltpu.VMEM((ROW, ROW), BF16),
            pltpu.VMEM((ROW, HALF), BF16),
            pltpu.VMEM((ROW, 128), F32),
            pltpu.VMEM((ROW, 128), F32),
            pltpu.VMEM((8, HALF), F32),
            pltpu.VMEM((8, HALF), F32),
        ],
        product // 64,
    )
    normed_late = normed
    if tree:
        came_far["shrink"], normed_late = lax.optimization_barrier((came_far["shrink"], normed))
    second_raws = call_kernel(
        functools.partial(gate_sum_kernel, tree),
        "gate_sum",
        [normed_late, gate_grad, square_sum, vectors],
        [None] * 4,
        raw_outputs((SPLIT, HALF - SPLIT + ROW + VECTOR_LANES), ((D, HALF), (ROW, ROW), (8, BLOCK, 128))),
        sum_scratch,
        product // 64,
    )
    gated_late = gated
    if tree:
        second_raws[2], second_raws[5], came_far["content"] = lax.optimization_barrier(
            (second_raws[2], second_raws[5], came_far["content"])
        )
        second_came = [cross_core(second_raws[i]) for i in (2, 5)]
        gated_late = after(gated, second_raws[0], came_far["content"])
    part_scratch = pltpu.VMEM((narrow_size, *part.shape), BF16)
    layer_own, layer_core, layer_pair = call_kernel(
        layer_kernel,
        "layer",
        [gated_late, shrink_low],
        [None] * 2,
        [part, part, pair],
        [part_scratch],
        product // 64,
    )
    grad_late = gate_grad
    if tree:
        *second_came, layer_own = lax.optimization_barrier((*second_came, layer_own))
        second_far = [sum_core(second_raws[1], second_came[0]), sum_core(second_raws[4], second_came[1])]
        second_came_far = [cross_x(second_far[0]), cross_y(second_far[1])]
        grad_late = after(gate_grad, *second_far)
    grad_own, core_back, pair_back = call_kernel(
        back_kernel,
        "back",
        [grad_late, content_grad, gate_weight, content_weight, xhat, scale, gains, layer_core, layer_pair],
        [None] * 9,
        [part, pair, shape((2, *pair.shape), BF16)],
        [part_scratch],
        product // 64,
    )

    def give(cots_base, acts_base, returned):
        whole = (group_rows, quarter, D)
        return call_kernel(
            give_kernel,
            "give",
            [cots_base, acts_base, grad_own, layer_own, *returned],
            [None] * 7,
            [(shape(whole, F32), stored), (shape(whole, BF16), stored)],
            [
                pltpu.VMEM((narrow_size, *part.shape), F32),
                pltpu.VMEM((narrow_size, *part.shape), BF16),
                dma((2, narrow_size)),
            ],
            product // 64,
        )

    if tree:
        columns = HALF + HALF + SPLIT + (HALF - SPLIT) + ROW + VECTOR_LANES
        half_columns = HALF + SPLIT
        (*all_far, grad_own) = lax.optimization_barrier(
            (came_far["content"], second_came_far[0], came_far["shrink"], second_came_far[1], grad_own)
        )
        terms = []
        for near, near_came, far_came in zip(
            (content_raws[0], second_raws[0], shrink_raws[0], second_raws[3]),
            (came["content"], second_came[0], came["shrink"], second_came[1]),
            all_far,
        ):
            terms += [near, near_came, far_came]
        sides = call_kernel(
            side_kernel,
            "side",
            terms,
            [None] * 12,
            [shape((4, BLOCK, half_columns), BF16), shape((4, BLOCK, columns - half_columns), BF16)],
            [],
            product // 64,
        )
        came_side = [cross_y(sides[0]), cross_x(sides[1])]
        *came_side, core_back = lax.optimization_barrier((*came_side, cross_core(core_back)))
        mine, *sent = call_kernel(
            fold_kernel,
            "fold",
            terms + came_side,
            [None] * 14,
            [shape((BLOCK, columns), F32)] + [shape((BLOCK, columns), BF16)] * 3,
            [],
            product // 64,
        )
        came_z = [swap_with(sent[s - 1], "wide", wide_size, 2 * s) for s in range(1, 4)]
        matrices = [expand_weight, expand_momentum, expand_variance, expand_average]
        matrices += [shrink_weight, shrink_momentum, shrink_variance, shrink_average]
        matrices += [spatial_weight, spatial_momentum, spatial_variance, spatial_average]
        fetched = [*matrices, cotangent, activations]
        states = call_kernel(
            fetch_kernel,
            "fetch",
            list(lax.optimization_barrier((*fetched, sent[0]))[:14]),
            [stored] * 14,
            [shape(value.shape, value.dtype) for value in fetched],
            [dma((14,))],
            product // 64,
        )
        states, bases = states[:12], states[12:]
        side_back = cross_y(after(pair_back, sent[0]))
        *came_z, first_state = lax.optimization_barrier((*came_z, states[0]))
        low, message = call_kernel(
            norm_kernel,
            "norm",
            [mine, *came_z, first_state, gains],
            [None] * 6,
            [shape((BLOCK, columns), BF16), shape((8, LANES), F32)],
            [],
            product // 64,
        )
        side = cross_y(low)
        message = add(message, cross_core(message))
        message = add(message, cross_x(message))
        *arrived, side, side_back = lax.optimization_barrier((*over_z(message), side, side_back))
        message = add(message, *arrived)
        other = cross_core(stack([low, side]))
        returned = [core_back, side_back, cross_core(side_back)]
        input_grad, layer_out = give(*bases, returned)
        arrived, layer_out, input_grad = lax.optimization_barrier((cross_y(message), layer_out, input_grad))
        message = add(message, arrived)
        as_rows = lambda value: value.reshape(-1, min(value.shape[0], LANES))
        vector_states = [norm_gains, gains_momentum, gains_variance, gains_average]
        vector_states += [spatial_bias, bias_momentum, bias_variance, bias_average]
        vector_kinds = [shape((2, LANES), F32)] * 5 + [shape((1, 64), F32)] * 5
        *updates, norm_row = call_kernel(
            adam_kernel,
            "adam",
            [message, low, side, other, *states] + [as_rows(value) for value in vector_states],
            [None] * 24,
            [(shape(value.shape, F32), stored) for value in (matrices[0], matrices[4], matrices[8]) for _ in range(5)]
            + [(kind, pl.BlockSpec(memory_space=pltpu.VMEM)) for kind in vector_kinds]
            + [(shape((1, 1), F32), smem)],
            [pltpu.VMEM(value.shape, F32) for value in (matrices[0], matrices[4], matrices[8]) for _ in range(5)]
            + [pltpu.VMEM((4, BLOCK, columns), BF16), dma((15,))],
            product // 64,
        )
        grad_norm = norm_row[0, 0]
        results = [layer_out, input_grad, grad_norm, *updates[:15]]
        return tuple(results + [value.reshape(-1) for value in updates[15:]])

    returned = trade(core_back, pair_back)
    input_grad, layer_out = give(cotangent, activations, returned)
    gains_size, bias_size = norm_gains.shape[0], spatial_bias.shape[0]
    vectors = lax.psum(second_raws[2], ("narrow", "wide"))
    totals = lax.psum(
        (jnp.concatenate([content_raws[0], second_raws[0]], axis=1), shrink_raws[0], second_raws[1]), "narrow"
    )
    expand_shard, shrink_shard, spatial_shard = [
        lax.psum_scatter(total, "wide", scatter_dimension=0, tiled=True) for total in totals
    ]
    second_shard = lax.dynamic_slice_in_dim(vectors[:, :2].reshape(-1), wide * gains_size, gains_size)
    bias_shard = lax.dynamic_slice_in_dim(vectors[:, 2, :64].reshape(-1), wide * bias_size, bias_size)
    low_weight = expand_weight.astype(BF16).astype(F32)
    height = expand_weight.shape[0]
    first_gain = lax.dynamic_slice_in_dim(gains[0], wide * height, height)
    first_raw = jnp.sum(low_weight * expand_shard, axis=1) / first_gain
    squares = [expand_shard, shrink_shard, spatial_shard, second_shard, bias_shard, first_raw]
    square_total = lax.psum(sum(jnp.sum(value * value) for value in squares), "wide")
    first_all = lax.all_gather(first_raw, "wide", axis=0, tiled=True)
    first_all = jnp.concatenate([first_all, jnp.zeros((HALF,), F32)])
    gains_shard = second_shard + lax.dynamic_slice_in_dim(first_all, wide * gains_size, gains_size)
    grad_norm = jnp.sqrt(square_total)
    clip_scale = CLIP_LIMIT / jnp.maximum(grad_norm, CLIP_LIMIT)
    results = [layer_out, input_grad, grad_norm]
    for weight, shard, momentum, variance, average, rate, decay in (
        (expand_weight, expand_shard, expand_momentum, expand_variance, expand_average, RATE_MATRIX, DECAY_MATRIX),
        (shrink_weight, shrink_shard, shrink_momentum, shrink_variance, shrink_average, RATE_MATRIX, DECAY_MATRIX),
        (spatial_weight, spatial_shard, spatial_momentum, spatial_variance, spatial_average, RATE_MATRIX, DECAY_MATRIX),
        (norm_gains, gains_shard, gains_momentum, gains_variance, gains_average, RATE_VECTOR, 0.0),
        (spatial_bias, bias_shard, bias_momentum, bias_variance, bias_average, RATE_VECTOR, 0.0),
    ):
        results += adam_update(weight, shard, momentum, variance, average, clip_scale, rate, decay)
    return tuple(results)


def solution(mesh):
    tokens, matrix, vector = P("wide", "narrow", None), P("wide", None), P("wide")
    return jax.shard_map(
        on_device,
        mesh=mesh,
        in_specs=(tokens, tokens) + (matrix,) * 13 + (vector,) * 8,
        out_specs=(tokens, tokens, P()) + (matrix,) * 15 + (vector,) * 10,
        check_vma=False,
    )
```

time: 686 us -> 151 us (0.22); the launches traced: 678 us -> 151 us
  waiting for transfers between devices: 314 us -> 51.8 us
  blocking collectives: 138 us -> 0 us
  other arithmetic: 72.3 us -> 0.33 us
  matrix products: 63.5 us -> 0 us
  Pallas kernels: 0 us -> 57.4 us
  local copies, waits for them, and re-layouts: 49.9 us -> 0.04 us
  starting transfers between devices: 18.6 us -> 39.9 us
  between operations: 22 us -> 1.25 us
    reduce_scatter x3 -> x0, waiting for transfers between devices: 123 us -> none  [the longest x1 121 us: on_device(): lax.psum_scatter(totals[0], 'wide', scatter_dimension=0, tiled=True)]
    all_to_all x4 -> x0, waiting for transfers between devices: 86.5 us -> none  [the longest x1 36.9 us: on_device(): lax.all_to_all(grad_gate_low, 'narrow', split_axis=1, concat_axis=2, tile...]
    all_gather x2 -> x0, waiting for transfers between devices: 69.1 us -> none  [the longest x1 37 us: on_device(): lax.all_gather(expand_weight.astype(jnp.bfloat16), 'wide', axis=0, tiled=...]
    dot_general x9 -> x0, matrix products: 63.5 us -> none  [the longest x1 13.5 us: front_pass(): jnp.einsum('rpd,df->rpf', normed_low, expand_low, preferred_element_type=...]
    pallas_call x0 -> x26, Pallas kernels: none -> 57.4 us  [call_kernel(): pl.pallas_call(kernel, name=name, in_specs=in_specs, out_specs=specs, out...]
    all_gather x2 -> x0, blocking collectives: 55.8 us -> none  [the longest x1 33.6 us: on_device(): lax.all_gather(spatial_weight.astype(jnp.bfloat16), 'wide', axis=0, tiled...]
    unnamed x2 -> x0, blocking collectives: 54.2 us -> none
    ppermute x0 -> x45, waiting for transfers between devices: none -> 51.8 us  [swap_with(): return lax.ppermute(value, axis, [(i, i ^ bit) for i in range(size)])]
  transfers between devices with their start and end apart: 10 -> 45, of which waited for: 9 -> 22; matrix products, arithmetic and copies ran while one was open for 14% -> 0% of each run, Pallas kernels for 0% -> 28%
where the time goes in v1:
time: 151 us
  Pallas kernels  57.4 us (38%)
  waiting for transfers between devices  51.8 us (34%)
  starting transfers between devices  39.9 us (26%)
    pallas_call x26, Pallas kernels, call_kernel(): pl.pallas_call(kernel, name=name, in_specs=in_specs, out_specs=specs, out...  57.4 us
    ppermute x45, waiting for transfers between devices, swap_with(): return lax.ppermute(value, axis, [(i, i ^ bit) for i in range(size)])  51.8 us
    ppermute x45, starting transfers between devices, swap_with(): return lax.ppermute(value, axis, [(i, i ^ bit) for i in range(size)])  39.9 us
  transfers between devices with their start and end apart: 45, of which 22 were waited for; matrix products, arithmetic and copies ran while one was open for 0% of the time, Pallas kernels for 28%

profile of v1, /device:TPU:0, one launch (start us, length us, event | category | flops | bytes accessed | tf_op | source)
XLA Modules:
  0.0 150.7 jit_solution(11185329633242971996)
XLA Ops:
  0.7 1.0 pack_first.1.refs_0_
  1.7 1.4 cut.1
  3.1 3.0 %collective-permute-start.7 = (bf16[2,2,2,128,512]{4,3,2,1,0:T(8,128)(2,1)S(1)}, bf16[2,2,2,128,512]{4,3,2,1,0:T(8,128)(2,1)S(1)}, u32[]{:S(2)}, u32[]{:S(2)}) collective-permute-start(bf16[2,2,2,128,512]{4,3,2,1,0:T(8,128)(2,1)S(1)} %get-tuple-element.194), channel_id=1, source_target_pairs={{0,2},{1,3},{2,0},{3,1},{4,6},{5,7},{6,4},{7,5},{8,10},{9,11},{10,... | collective-permute-start | bytes 3145736 | tf_op jit(solution)/shard_map/ppermute | solution.py:673
  6.1 3.6 %collective-permute-start.2 = (bf16[32,2176]{1,0:T(8,128)(2,1)S(1)}, bf16[32,2176]{1,0:T(8,128)(2,1)S(1)}, u32[]{:S(2)}, u32[]{:S(2)}) collective-permute-start(bf16[32,2176]{1,0:T(8,128)(2,1)S(1)} %pack_first.1.refs_0_), channel_id=1, source_target_pairs={{0,24},{4,28},{8,16},{12,20},{16,8},{20,12},{24,0},{28,4},{1,25},{... | collective-permute-start | bytes 417800 | tf_op jit(solution)/shard_map/ppermute | solution.py:673
  9.7 0.8 collective-permute-start
  10.5 1.1 pack_second.1
  11.6 2.9 %collective-permute-done.2.refs_3_ = bf16[32,2176]{1,0:T(8,128)(2,1)S(1)} collective-permute-done((bf16[32,2176]{1,0:T(8,128)(2,1)S(1)}, bf16[32,2176]{1,0:T(8,128)(2,1)S(1)}, u32[]{:S(2)}, u32[]{:S(2)}) %collective-permute-start.2) | collective-permute-done | bytes 139296 | tf_op jit(solution)/shard_map/ppermute | solution.py:673
  14.5 7.7 %collective-permute-done.1.refs_2_ = bf16[32,2176]{1,0:T(8,128)(2,1)S(1)} collective-permute-done((bf16[32,2176]{1,0:T(8,128)(2,1)S(1)}, bf16[32,2176]{1,0:T(8,128)(2,1)S(1)}, u32[]{:S(2)}, u32[]{:S(2)}) %collective-permute-start.1) | collective-permute-done | bytes 139296 | tf_op jit(solution)/shard_map/ppermute | solution.py:673
  22.2 1.6 %collective-permute-start.9 = (bf16[4,32,2176]{2,1,0:T(8,128)(2,1)S(1)}, bf16[4,32,2176]{2,1,0:T(8,128)(2,1)S(1)}, u32[]{:S(2)}, u32[]{:S(2)}) collective-permute-start(bf16[4,32,2176]{2,1,0:T(8,128)(2,1)S(1)} %stack.4.refs_0_.refs_4_), channel_id=1, source_target_pairs={{0,4},{4,0},{8,12},{12,8},{16,20},{20,16},{24,28},{28,24},{1,5},{5... | collective-permute-start | bytes 1671176 | tf_op jit(solution)/shard_map/ppermute | solution.py:673
  23.8 2.5 %collective-permute-start.6 = (bf16[32,1536]{1,0:T(8,128)(2,1)S(1)}, bf16[32,1536]{1,0:T(8,128)(2,1)S(1)}, u32[]{:S(2)}, u32[]{:S(2)}) collective-permute-start(bf16[32,1536]{1,0:T(8,128)(2,1)S(1)} %get-tuple-element.201.refs_0_), channel_id=1, source_target_pairs={{0,24},{4,28},{8,16},{12,20},{16,8},{20,12},{24,0},{28,4},{1,25},{... | collective-permute-start | bytes 294920 | tf_op jit(solution)/shard_map/ppermute | solution.py:673
  26.3 1.9 %collective-permute-start.4 = (bf16[32,1536]{1,0:T(8,128)(2,1)S(1)}, bf16[32,1536]{1,0:T(8,128)(2,1)S(1)}, u32[]{:S(2)}, u32[]{:S(2)}) collective-permute-start(bf16[32,1536]{1,0:T(8,128)(2,1)S(1)} %get-tuple-element.201.refs_0_), channel_id=1, source_target_pairs={{0,8},{4,12},{8,0},{12,4},{16,24},{20,28},{24,16},{28,20},{1,9},{5... | collective-permute-start | bytes 294920 | tf_op jit(solution)/shard_map/ppermute | solution.py:673
  28.2 3.2 %collective-permute-done.6.refs_3_ = bf16[32,1536]{1,0:T(8,128)(2,1)S(1)} collective-permute-done((bf16[32,1536]{1,0:T(8,128)(2,1)S(1)}, bf16[32,1536]{1,0:T(8,128)(2,1)S(1)}, u32[]{:S(2)}, u32[]{:S(2)}) %collective-permute-start.6) | collective-permute-done | bytes 98336 | tf_op jit(solution)/shard_map/ppermute | solution.py:673
  31.4 2.6 %collective-permute-done.5.refs_2_ = bf16[32,1536]{1,0:T(8,128)(2,1)S(1)} collective-permute-done((bf16[32,1536]{1,0:T(8,128)(2,1)S(1)}, bf16[32,1536]{1,0:T(8,128)(2,1)S(1)}, u32[]{:S(2)}, u32[]{:S(2)}) %collective-permute-start.5) | collective-permute-done | bytes 98336 | tf_op jit(solution)/shard_map/ppermute | solution.py:673
  34.1 0.5 collective-permute-start.10
  34.6 2.0 %collective-permute-done.9.refs_1_.refs_5_ = bf16[4,32,2176]{2,1,0:T(8,128)(2,1)S(1)} collective-permute-done((bf16[4,32,2176]{2,1,0:T(8,128)(2,1)S(1)}, bf16[4,32,2176]{2,1,0:T(8,128)(2,1)S(1)}, u32[]{:S(2)}, u32[]{:S(2)}) %collective-permute-start.9) | collective-permute-done | bytes 557088 | tf_op jit(solution)/shard_map/ppermute | solution.py:673
  36.6 1.5 collective-permute-start.15
  38.1 2.5 %collective-permute-start.14 = (bf16[32,1536]{1,0:T(8,128)(2,1)S(1)}, bf16[32,1536]{1,0:T(8,128)(2,1)S(1)}, u32[]{:S(2)}, u32[]{:S(2)}) collective-permute-start(bf16[32,1536]{1,0:T(8,128)(2,1)S(1)} %get-tuple-element.211.refs_0_), channel_id=1, source_target_pairs={{0,24},{4,28},{8,16},{12,20},{16,8},{20,12},{24,0},{28,4},{1,25},{... | collective-permute-start | bytes 294920 | tf_op jit(solution)/shard_map/ppermute | solution.py:673
  40.5 1.9 %collective-permute-start.12 = (bf16[32,1536]{1,0:T(8,128)(2,1)S(1)}, bf16[32,1536]{1,0:T(8,128)(2,1)S(1)}, u32[]{:S(2)}, u32[]{:S(2)}) collective-permute-start(bf16[32,1536]{1,0:T(8,128)(2,1)S(1)} %get-tuple-element.211.refs_0_), channel_id=1, source_target_pairs={{0,8},{4,12},{8,0},{12,4},{16,24},{20,28},{24,16},{28,20},{1,9},{5... | collective-permute-start | bytes 294920 | tf_op jit(solution)/shard_map/ppermute | solution.py:673
  42.5 10.4 %gating.1 = (bf16[2,512,512]{2,1,0:T(8,128)(2,1)S(1)}, bf16[2,512,512]{2,1,0:T(8,128)(2,1)S(1)}, f32[2,512,128]{2,1,0:T(8,128)S(1)}, bf16[2,512,1536]{2,1,0:T(8,...) custom-call(s32[8,5]{1,0:T(8,128)S(1)} %copy-done, ...), custom_call_target="tpu_custom_call" | custom-call | flops 25165824 | bytes 50331 | tf_op jit(solution)/shard_map/gating/pallas_call | solution.py:659
  52.9 0.5 collective-permute-start.17
  53.5 0.6 collective-permute-start.18
  54.1 0.7 collective-permute-done.17.refs_3_
  54.8 6.6 %content_up.1 = (bf16[2,512,1536]{2,1,0:T(8,128)(2,1)S(1)}, bf16[2,512,1536]{2,1,0:T(8,128)(2,1)S(1)}, bf16[512,1536]{1,0:T(8,128)(2,1)S(1)}) custom-call(bf16[2,512,512]{2,1,0:T(8,128)(2,1)S(1)} %get-tuple-element.232.normed_ref, bf16[4,32,1536]{2,1,0:T(8,128)(2,1)S(1)} %stack.5.refs_0_, bf16[4,32,1536]{2,1,0:T(8,128)(2,1)S(1)} %collective-permute-done.15.refs_1_, ...), custom_call_target="tpu_custom_call" | custom-call | flops 25165824 | bytes 50331 | tf_op jit(solution)/shard_map/content_up/pallas_call | solution.py:659
  61.4 3.2 %collective-permute-done.18.refs_1_ = bf16[4,32,1536]{2,1,0:T(8,128)(2,1)S(1)} collective-permute-done((bf16[4,32,1536]{2,1,0:T(8,128)(2,1)S(1)}, bf16[4,32,1536]{2,1,0:T(8,128)(2,1)S(1)}, u32[]{:S(2)}, u32[]{:S(2)}) %collective-permute-start.18) | collective-permute-done | bytes 393248 | tf_op jit(solution)/shard_map/ppermute | solution.py:673
  64.6 1.7 %collective-permute-done.20.refs_3_ = bf16[4,32,1536]{2,1,0:T(8,128)(2,1)S(1)} collective-permute-done((bf16[4,32,1536]{2,1,0:T(8,128)(2,1)S(1)}, bf16[4,32,1536]{2,1,0:T(8,128)(2,1)S(1)}, u32[]{:S(2)}, u32[]{:S(2)}) %collective-permute-start.20) | collective-permute-done | bytes 393248 | tf_op jit(solution)/shard_map/ppermute | solution.py:673
  66.3 8.3 %content_down.1 = (bf16[2,512,1536]{2,1,0:T(8,128)(2,1)S(1)}, bf16[2,512,1536]{2,1,0:T(8,128)(2,1)S(1)}, bf16[2,512,1536]{2,1,0:T(8,128)(2,1)S(1)}, f32[512,128]...) custom-call(s32[8,5]{1,0:T(8,128)S(1)} %copy-done, ...), custom_call_target="tpu_custom_call" | custom-call | flops 25165824 | bytes 50331 | tf_op jit(solution)/shard_map/content_down/pallas_call | solution.py:659
  74.9 1.9 %content_sum.1 = (bf16[2,4,16,1536]{3,2,1,0:T(8,128)(2,1)S(1)}, bf16[2,4,16,1536]{3,2,1,0:T(8,128)(2,1)S(1)}, bf16[2,2,4,16,1536]{4,3,2,1,0:T(8,128)(2,1)S(1)}) custom-call(bf16[2,512,512]{2,1,0:T(8,128)(2,1)S(1)} %get-tuple-element.232.normed_ref, bf16[2,512,1536]{2,1,0:T(8,128)(2,1)S(1)} %get-tuple-element.222.grad_ref.content_grad_ref), custom_call_target="tpu_custom_call" | custom-call | flops 25165824 | bytes 50331 | tf_op jit(solution)/shard_map/content_sum/pallas_call | solution.py:659
  77.3 0.6 collective-permute-start.23
  77.9 2.5 %spatial_sum.1.square_ref = f32[512,512]{1,0:T(8,128)S(1)} custom-call(s32[8,5]{1,0:T(8,128)S(1)} %copy-done, bf16[2,512,1536]{2,1,0:T(8,128)(2,1)S(1)} %get-tuple-element.234.grad_mixed_ref, bf16[2,512,1536]{2,1,0:T(8,128)(2,1)S(1)} %get-tuple-element.230.gate_ref), custom_call_target="tpu_custom_call" | custom-call | flops 25165824 | bytes 50331 | tf_op jit(solution)/shard_map/spatial_sum/pallas_call | solution.py:659
  80.5 0.6 collective-permute-start.24
  81.1 6.7 %gate_back.1 = (bf16[2,512,1536]{2,1,0:T(8,128)(2,1)S(1)}, f32[8,16,128]{2,1,0:T(8,128)S(1)}) custom-call(s32[8,5]{1,0:T(8,128)S(1)} %copy-done, bf16[2,512,1536]{2,1,0:T(8,128)(2,1)S(1)} %get-tuple-element.234.grad_mixed_ref, bf16[2,512,1536]{2,1,0:T(8,128)(2,1)S(1)} %get-tuple-element.230.gate_ref, bf16[2,512,1536]{2,1,0:T(8,128)(2,1)S(1)} %get-tuple-element.235.slope_ref, ...), custom_call_target="tpu_custom_call" | custom-call | flops 25165824 | bytes 50331 | tf_op jit(solution)/shard_map/gate_back/pallas_call | solution.py:659
  87.8 0.7 collective-permute-done.23.refs_8_
  88.6 2.0 %gate_sum.1 = (bf16[2,4,16,1024]{3,2,1,0:T(8,128)(2,1)S(1)}, bf16[2,4,16,1024]{3,2,1,0:T(8,128)(2,1)S(1)}, bf16[2,2,4,16,1024]{4,3,2,1,0:T(8,128)(2,1)S(1)}, bf1...) custom-call(bf16[2,512,512]{2,1,0:T(8,128)(2,1)S(1)} %get-tuple-elem, ...), custom_call_target="tpu_custom_call" | custom-call | flops 25165824 | bytes 50331 | tf_op jit(solution)/shard_map/gate_sum/pallas_call | solution.py:659
  90.6 0.9 collective-permute-done.24.refs_2_
  91.5 0.5 collective-permute-start.25
  92.0 1.9 %layer.1 = (bf16[2,128,512]{2,1,0:T(8,128)(2,1)S(1)}, bf16[2,128,512]{2,1,0:T(8,128)(2,1)S(1)}, bf16[2,2,128,512]{3,2,1,0:T(8,128)(2,1)S(1)}) custom-call(bf16[2,512,1536]{2,1,0:T(8,128)(2,1)S(1)} %get-tuple-element.251.gated_ref, bf16[1536,512]{1,0:T(8,128)(2,1)S(1)} %get-tuple-element.252.shrink), custom_call_target="tpu_custom_call" | custom-call | flops 25165824 | bytes 50331 | tf_op jit(solution)/shard_map/layer/pallas_call | solution.py:659
  94.3 1.6 %collective-permute-start.28 = (bf16[2,4,16,1152]{3,2,1,0:T(8,128)(2,1)S(1)}, bf16[2,4,16,1152]{3,2,1,0:T(8,128)(2,1)S(1)}, u32[]{:S(2)}, u32[]{:S(2)}) collective-permute-start(bf16[2,4,16,1152]{3,2,1,0:T(8,128)(2,1)S(1)} %fusion.2), channel_id=1, source_target_pairs={{0,2},{1,3},{2,0},{3,1},{4,6},{5,7},{6,4},{7,5},{8,10},{9,11},{10,... | collective-permute-start | bytes 884744 | tf_op jit(solution)/shard_map/ppermute | solution.py:673
  96.0 0.6 collective-permute-start.27
  96.6 3.9 %back.1 = (bf16[2,128,512]{2,1,0:T(8,128)(2,1)S(1)}, bf16[2,2,128,512]{3,2,1,0:T(8,128)(2,1)S(1)}, bf16[2,2,2,128,512]{4,3,2,1,0:T(8,128)(2,1)S(1)}) custom-call(bf16[2,512,1536]{2,1,0:T(8,128)(2,1)S(1)} %get-tuple-element.258.grad_ref.gate_grad_ref, bf16[2,512,1536]{2,1,0:T(8,128)(2,1)S(1)} %get-tuple-element.222.grad_ref.content_grad_ref, ...), custom_call_target="tpu_custom_call" | custom-call | flops 25165824 | bytes 50331 | tf_op jit(solution)/shard_map/back/pallas_call | solution.py:659
  100.5 3.6 %collective-permute-done.27.refs_5_ = bf16[2,4,16,1024]{3,2,1,0:T(8,128)(2,1)S(1)} collective-permute-done((bf16[2,4,16,1024]{3,2,1,0:T(8,128)(2,1)S(1)}, bf16[2,4,16,1024]{3,2,1,0:T(8,128)(2,1)S(1)}, u32[]{:S(2)}, u32[]{:S(2)}) %collective-permute-start.27) | collective-permute-done | bytes 262176 | tf_op jit(solution)/shard_map/ppermute | solution.py:673
  104.4 0.6 collective-permute-start.30
  105.0 0.8 collective-permute-start.29
  105.8 7.5 %collective-permute-done.29.refs_12_ = bf16[4,16,2560]{2,1,0:T(8,128)(2,1)S(1)} collective-permute-done((bf16[4,16,2560]{2,1,0:T(8,128)(2,1)S(1)}, bf16[4,16,2560]{2,1,0:T(8,128)(2,1)S(1)}, u32[]{:S(2)}, u32[]{:S(2)}) %collective-permute-start.29) | collective-permute-done | bytes 327712 | tf_op jit(solution)/shard_map/ppermute | solution.py:673
  113.7 1.2 collective-permute-start.41
  115.0 1.1 collective-permute-start.33
  116.1 1.4 collective-permute-start.34
  117.5 1.0 collective-permute-start.32
  118.5 3.2 %fetch.1 = (f32[64,3072]{1,0:T(8,128)S(1)}, f32[64,3072]{1,0:T(8,128)S(1)}, f32[64,3072]{1,0:T(8,128)S(1)}, f32[64,3072]{1,0:T(8,128)S(1)}, f32[192,512]{1,0:T(8...) custom-call(f32[64,3072]{1,0:T(8,128)} %refs_0_, ...), custom_call_target="tpu_custom_call" | custom-call | flops 25165824 | bytes 50331 | tf_op jit(solution)/shard_map/fetch/pallas_call | solution.py:659
  121.7 5.6 %collective-permute-done.33.two_ref = bf16[16,5248]{1,0:T(8,128)(2,1)S(1)} collective-permute-done((bf16[16,5248]{1,0:T(8,128)(2,1)S(1)}, bf16[16,5248]{1,0:T(8,128)(2,1)S(1)}, u32[]{:S(2)}, u32[]{:S(2)}) %collective-permute-start.33) | collective-permute-done | bytes 167968 | tf_op jit(solution)/shard_map/ppermute | solution.py:673
  127.3 1.3 collective-permute-done.32.one_ref
  128.8 0.6 collective-permute-start.40
  129.6 1.2 collective-permute-done.35.refs_1_
  130.7 1.1 collective-permute-start.36
  131.9 2.5 %collective-permute-done.36.refs_1_ = f32[8,128]{1,0:T(8,128)S(1)} collective-permute-done((f32[8,128]{1,0:T(8,128)S(1)}, f32[8,128]{1,0:T(8,128)S(1)}, u32[]{:S(2)}, u32[]{:S(2)}) %collective-permute-start.36) | collective-permute-done | bytes 4128 | tf_op jit(solution)/shard_map/ppermute | solution.py:673
  134.4 2.2 %collective-permute-start.39 = (f32[8,128]{1,0:T(8,128)S(1)}, f32[8,128]{1,0:T(8,128)S(1)}, u32[]{:S(2)}, u32[]{:S(2)}) collective-permute-start(f32[8,128]{1,0:T(8,128)S(1)} %add.33.refs_0_), channel_id=1, source_target_pairs={{0,24},{4,28},{8,16},{12,20},{16,8},{20,12},{24,0},{28,4},{1,25},{... | collective-permute-start | bytes 12296 | tf_op jit(solution)/shard_map/ppermute | solution.py:673
  136.5 2.1 %collective-permute-start.38 = (f32[8,128]{1,0:T(8,128)S(1)}, f32[8,128]{1,0:T(8,128)S(1)}, u32[]{:S(2)}, u32[]{:S(2)}) collective-permute-start(f32[8,128]{1,0:T(8,128)S(1)} %add.33.refs_0_), channel_id=1, source_target_pairs={{0,16},{4,20},{8,24},{12,28},{16,0},{20,4},{24,8},{28,12},{1,17},{... | collective-permute-start | bytes 12296 | tf_op jit(solution)/shard_map/ppermute | solution.py:673
  138.7 1.0 collective-permute-done.39.refs_3_
  139.8 1.3 collective-permute-done.38.refs_2_
  141.0 1.2 collective-permute-done.37.refs_1_
  142.3 0.6 collective-permute-start.44
  142.9 1.4 collective-permute-start.42
  144.3 0.6 collective-permute-done.43.forward_ref
  144.9 1.8 %give.1 = (f32[8,128,512]{2,1,0:T(8,128)}, bf16[8,128,512]{2,1,0:T(8,128)(2,1)}) custom-call(bf16[8,128,512]{2,1,0:T(8,128)(2,1)S(1)} %get-tuple-element.307.cots_ref, bf16[8,128,512]{2,1,0:T(8,128)(2,1)S(1)} %get-tuple-element.308.acts_ref, bf16[2,128,512]{2,1,0:T(8,128)(2,1)S(1)} %get-tuple-element.309.grad_own, ...), custom_call_target="tpu_custom_call" | custom-call | flops 25165824 | bytes 50331 | tf_op jit(solution)/shard_map/give/pallas_call | solution.py:659
  146.8 3.7 %adam.1 = (f32[64,3072]{1,0:T(8,128)}, f32[64,3072]{1,0:T(8,128)}, f32[64,3072]{1,0:T(8,128)}, f32[64,3072]{1,0:T(8,128)}, f32[64,3072]{1,0:T(8,128)}, /*index=5...) custom-call(f32[8,128]{1,0:T(8,128)S(1)} %add.35.message_ref, ...), custom_call_target="tpu_custom_call" | custom-call | flops 25165824 | bytes 50331 | tf_op jit(solution)/shard_map/adam/pallas_call | solution.py:659
  (74 shorter events, 2.9 us)
Async XLA Ops:
  0.7 41.8 %copy-start = (s32[8,5]{1,0:T(8,128)S(1)}, s32[8,5]{1,0:T(8,128)}, u32[]{:S(2)}) copy-start(s32[8,5]{1,0:T(8,128)} %lens_ref.7) | copy-start | bytes 484
  3.1 30.9 %collective-permute-start.7 = (bf16[2,2,2,128,512]{4,3,2,1,0:T(8,128)(2,1)S(1)}, bf16[2,2,2,128,512]{4,3,2,1,0:T(8,128)(2,1)S(1)}, u32[]{:S(2)}, u32[]{:S(2)}) collective-permute-start(bf16[2,2,2,128,512]{4,3,2,1,0:T(8,128)(2,1)S(1)} %get-tuple-element.194), channel_id=1, source_target_pairs={{0,2},{1,3},{2,0},{3,1},{4,6},{5,7},{6,4},{7,5},{8,10},{9,11},{10,... | collective-permute-start | bytes 3145736 | tf_op jit(solution)/shard_map/ppermute | solution.py:673
  6.1 16.1 %collective-permute-start.3 = (bf16[2,2,128,512]{3,2,1,0:T(8,128)(2,1)S(1)}, bf16[2,2,128,512]{3,2,1,0:T(8,128)(2,1)S(1)}, u32[]{:S(2)}, u32[]{:S(2)}) collective-permute-start(bf16[2,2,128,512]{3,2,1,0:T(8,128)(2,1)S(1)} %get-tuple-element.193), channel_id=1, source_target_pairs={{0,1},{1,0},{2,3},{3,2},{4,5},{5,4},{6,7},{7,6},{8,9},{9,8},{10,11... | collective-permute-start | bytes 1572872 | tf_op jit(solution)/shard_map/ppermute | solution.py:673
  6.1 8.4 %collective-permute-start.2 = (bf16[32,2176]{1,0:T(8,128)(2,1)S(1)}, bf16[32,2176]{1,0:T(8,128)(2,1)S(1)}, u32[]{:S(2)}, u32[]{:S(2)}) collective-permute-start(bf16[32,2176]{1,0:T(8,128)(2,1)S(1)} %pack_first.1.refs_0_), channel_id=1, source_target_pairs={{0,24},{4,28},{8,16},{12,20},{16,8},{20,12},{24,0},{28,4},{1,25},{... | collective-permute-start | bytes 417800 | tf_op jit(solution)/shard_map/ppermute | solution.py:673
  9.7 12.4 %collective-permute-start.1 = (bf16[32,2176]{1,0:T(8,128)(2,1)S(1)}, bf16[32,2176]{1,0:T(8,128)(2,1)S(1)}, u32[]{:S(2)}, u32[]{:S(2)}) collective-permute-start(bf16[32,2176]{1,0:T(8,128)(2,1)S(1)} %pack_first.1.refs_0_), channel_id=1, source_target_pairs={{0,16},{4,20},{8,24},{12,28},{16,0},{20,4},{24,8},{28,12},{1,17},{... | collective-permute-start | bytes 417800 | tf_op jit(solution)/shard_map/ppermute | solution.py:673
  9.7 12.4 %collective-permute-start = (bf16[32,2176]{1,0:T(8,128)(2,1)S(1)}, bf16[32,2176]{1,0:T(8,128)(2,1)S(1)}, u32[]{:S(2)}, u32[]{:S(2)}) collective-permute-start(bf16[32,2176]{1,0:T(8,128)(2,1)S(1)} %pack_first.1.refs_0_), channel_id=1, source_target_pairs={{0,8},{4,12},{8,0},{12,4},{16,24},{20,28},{24,16},{28,20},{1,9},{5... | collective-permute-start | bytes 417800 | tf_op jit(solution)/shard_map/ppermute | solution.py:673
  22.2 14.3 %collective-permute-start.9 = (bf16[4,32,2176]{2,1,0:T(8,128)(2,1)S(1)}, bf16[4,32,2176]{2,1,0:T(8,128)(2,1)S(1)}, u32[]{:S(2)}, u32[]{:S(2)}) collective-permute-start(bf16[4,32,2176]{2,1,0:T(8,128)(2,1)S(1)} %stack.4.refs_0_.refs_4_), channel_id=1, source_target_pairs={{0,4},{4,0},{8,12},{12,8},{16,20},{20,16},{24,28},{28,24},{1,5},{5... | collective-permute-start | bytes 1671176 | tf_op jit(solution)/shard_map/ppermute | solution.py:673
  23.8 7.6 %collective-permute-start.6 = (bf16[32,1536]{1,0:T(8,128)(2,1)S(1)}, bf16[32,1536]{1,0:T(8,128)(2,1)S(1)}, u32[]{:S(2)}, u32[]{:S(2)}) collective-permute-start(bf16[32,1536]{1,0:T(8,128)(2,1)S(1)} %get-tuple-element.201.refs_0_), channel_id=1, source_target_pairs={{0,24},{4,28},{8,16},{12,20},{16,8},{20,12},{24,0},{28,4},{1,25},{... | collective-permute-start | bytes 294920 | tf_op jit(solution)/shard_map/ppermute | solution.py:673
  26.3 7.7 %collective-permute-start.5 = (bf16[32,1536]{1,0:T(8,128)(2,1)S(1)}, bf16[32,1536]{1,0:T(8,128)(2,1)S(1)}, u32[]{:S(2)}, u32[]{:S(2)}) collective-permute-start(bf16[32,1536]{1,0:T(8,128)(2,1)S(1)} %get-tuple-element.201.refs_0_), channel_id=1, source_target_pairs={{0,16},{4,20},{8,24},{12,28},{16,0},{20,4},{24,8},{28,12},{1,17},{... | collective-permute-start | bytes 294920 | tf_op jit(solution)/shard_map/ppermute | solution.py:673
  26.3 7.7 %collective-permute-start.4 = (bf16[32,1536]{1,0:T(8,128)(2,1)S(1)}, bf16[32,1536]{1,0:T(8,128)(2,1)S(1)}, u32[]{:S(2)}, u32[]{:S(2)}) collective-permute-start(bf16[32,1536]{1,0:T(8,128)(2,1)S(1)} %get-tuple-element.201.refs_0_), channel_id=1, source_target_pairs={{0,8},{4,12},{8,0},{12,4},{16,24},{20,28},{24,16},{28,20},{1,9},{5... | collective-permute-start | bytes 294920 | tf_op jit(solution)/shard_map/ppermute | solution.py:673
  34.0 8.5 %collective-permute-start.8 = (bf16[2,2,2,128,512]{4,3,2,1,0:T(8,128)(2,1)S(1)}, bf16[2,2,2,128,512]{4,3,2,1,0:T(8,128)(2,1)S(1)}, u32[]{:S(2)}, u32[]{:S(2)}) collective-permute-start(bf16[2,2,2,128,512]{4,3,2,1,0:T(8,128)(2,1)S(1)} %collective-permute-done.7.side_ref), channel_id=1, source_target_pairs={{0,1},{1,0},{2,3},{3,2},{4,5},{5,4},{6,7},{7,6},{8,9},{9,8},{10,11... | collective-permute-start | bytes 3145736 | tf_op jit(solution)/shard_map/ppermute | solution.py:673
  34.1 6.5 %collective-permute-start.10 = (bf16[4,32,2176]{2,1,0:T(8,128)(2,1)S(1)}, bf16[4,32,2176]{2,1,0:T(8,128)(2,1)S(1)}, u32[]{:S(2)}, u32[]{:S(2)}) collective-permute-start(bf16[4,32,2176]{2,1,0:T(8,128)(2,1)S(1)} %stack.4.refs_0_.refs_4_), channel_id=1, source_target_pairs={{0,1},{1,0},{2,3},{3,2},{4,5},{5,4},{6,7},{7,6},{8,9},{9,8},{10,11... | collective-permute-start | bytes 1671176 | tf_op jit(solution)/shard_map/ppermute | solution.py:673
  36.6 4.0 %collective-permute-start.11 = (bf16[4,32,2176]{2,1,0:T(8,128)(2,1)S(1)}, bf16[4,32,2176]{2,1,0:T(8,128)(2,1)S(1)}, u32[]{:S(2)}, u32[]{:S(2)}) collective-permute-start(bf16[4,32,2176]{2,1,0:T(8,128)(2,1)S(1)} %collective-permute-done.9.refs_1_.refs_5_), channel_id=1, source_target_pairs={{0,1},{1,0},{2,3},{3,2},{4,5},{5,4},{6,7},{7,6},{8,9},{9,8},{10,11... | collective-permute-start | bytes 1671176 | tf_op jit(solution)/shard_map/ppermute | solution.py:673
  36.6 16.3 %collective-permute-start.15 = (bf16[4,32,1536]{2,1,0:T(8,128)(2,1)S(1)}, bf16[4,32,1536]{2,1,0:T(8,128)(2,1)S(1)}, u32[]{:S(2)}, u32[]{:S(2)}) collective-permute-start(bf16[4,32,1536]{2,1,0:T(8,128)(2,1)S(1)} %stack.5.refs_0_), channel_id=1, source_target_pairs={{0,4},{4,0},{8,12},{12,8},{16,20},{20,16},{24,28},{28,24},{1,5},{5... | collective-permute-start | bytes 1179656 | tf_op jit(solution)/shard_map/ppermute | solution.py:673
  38.1 14.8 %collective-permute-start.14 = (bf16[32,1536]{1,0:T(8,128)(2,1)S(1)}, bf16[32,1536]{1,0:T(8,128)(2,1)S(1)}, u32[]{:S(2)}, u32[]{:S(2)}) collective-permute-start(bf16[32,1536]{1,0:T(8,128)(2,1)S(1)} %get-tuple-element.211.refs_0_), channel_id=1, source_target_pairs={{0,24},{4,28},{8,16},{12,20},{16,8},{20,12},{24,0},{28,4},{1,25},{... | collective-permute-start | bytes 294920 | tf_op jit(solution)/shard_map/ppermute | solution.py:673
  40.5 12.3 %collective-permute-start.13 = (bf16[32,1536]{1,0:T(8,128)(2,1)S(1)}, bf16[32,1536]{1,0:T(8,128)(2,1)S(1)}, u32[]{:S(2)}, u32[]{:S(2)}) collective-permute-start(bf16[32,1536]{1,0:T(8,128)(2,1)S(1)} %get-tuple-element.211.refs_0_), channel_id=1, source_target_pairs={{0,16},{4,20},{8,24},{12,28},{16,0},{20,4},{24,8},{28,12},{1,17},{... | collective-permute-start | bytes 294920 | tf_op jit(solution)/shard_map/ppermute | solution.py:673
  40.5 12.3 %collective-permute-start.12 = (bf16[32,1536]{1,0:T(8,128)(2,1)S(1)}, bf16[32,1536]{1,0:T(8,128)(2,1)S(1)}, u32[]{:S(2)}, u32[]{:S(2)}) collective-permute-start(bf16[32,1536]{1,0:T(8,128)(2,1)S(1)} %get-tuple-element.211.refs_0_), channel_id=1, source_target_pairs={{0,8},{4,12},{8,0},{12,4},{16,24},{20,28},{24,16},{28,20},{1,9},{5... | collective-permute-start | bytes 294920 | tf_op jit(solution)/shard_map/ppermute | solution.py:673
  42.5 11.6 %collective-permute-start.16 = (bf16[4,32,1536]{2,1,0:T(8,128)(2,1)S(1)}, bf16[4,32,1536]{2,1,0:T(8,128)(2,1)S(1)}, u32[]{:S(2)}, u32[]{:S(2)}) collective-permute-start(bf16[4,32,1536]{2,1,0:T(8,128)(2,1)S(1)} %stack.5.refs_0_), channel_id=1, source_target_pairs={{0,1},{1,0},{2,3},{3,2},{4,5},{5,4},{6,7},{7,6},{8,9},{9,8},{10,11... | collective-permute-start | bytes 1179656 | tf_op jit(solution)/shard_map/ppermute | solution.py:673
  52.9 1.9 %collective-permute-start.17 = (bf16[4,32,1536]{2,1,0:T(8,128)(2,1)S(1)}, bf16[4,32,1536]{2,1,0:T(8,128)(2,1)S(1)}, u32[]{:S(2)}, u32[]{:S(2)}) collective-permute-start(bf16[4,32,1536]{2,1,0:T(8,128)(2,1)S(1)} %collective-permute-done.15.refs_1_), channel_id=1, source_target_pairs={{0,1},{1,0},{2,3},{3,2},{4,5},{5,4},{6,7},{7,6},{8,9},{9,8},{10,11... | collective-permute-start | bytes 1179656 | tf_op jit(solution)/shard_map/ppermute | solution.py:673
  53.5 11.1 %collective-permute-start.18 = (bf16[4,32,1536]{2,1,0:T(8,128)(2,1)S(1)}, bf16[4,32,1536]{2,1,0:T(8,128)(2,1)S(1)}, u32[]{:S(2)}, u32[]{:S(2)}) collective-permute-start(bf16[4,32,1536]{2,1,0:T(8,128)(2,1)S(1)} %stack.6.refs_0_), channel_id=1, source_target_pairs={{0,4},{4,0},{8,12},{12,8},{16,20},{20,16},{24,28},{28,24},{1,5},{5... | collective-permute-start | bytes 1179656 | tf_op jit(solution)/shard_map/ppermute | solution.py:673
  54.1 10.5 %collective-permute-start.19 = (bf16[4,32,1536]{2,1,0:T(8,128)(2,1)S(1)}, bf16[4,32,1536]{2,1,0:T(8,128)(2,1)S(1)}, u32[]{:S(2)}, u32[]{:S(2)}) collective-permute-start(bf16[4,32,1536]{2,1,0:T(8,128)(2,1)S(1)} %stack.6.refs_0_), channel_id=1, source_target_pairs={{0,1},{1,0},{2,3},{3,2},{4,5},{5,4},{6,7},{7,6},{8,9},{9,8},{10,11... | collective-permute-start | bytes 1179656 | tf_op jit(solution)/shard_map/ppermute | solution.py:673
  64.6 1.7 %collective-permute-start.20 = (bf16[4,32,1536]{2,1,0:T(8,128)(2,1)S(1)}, bf16[4,32,1536]{2,1,0:T(8,128)(2,1)S(1)}, u32[]{:S(2)}, u32[]{:S(2)}) collective-permute-start(bf16[4,32,1536]{2,1,0:T(8,128)(2,1)S(1)} %collective-permute-done.18.refs_1_), channel_id=1, source_target_pairs={{0,1},{1,0},{2,3},{3,2},{4,5},{5,4},{6,7},{7,6},{8,9},{9,8},{10,11... | collective-permute-start | bytes 1179656 | tf_op jit(solution)/shard_map/ppermute | solution.py:673
  74.7 2.6 %collective-permute-start.21 = (bf16[2,2,4,16,1536]{4,3,2,1,0:T(8,128)(2,1)S(1)}, bf16[2,2,4,16,1536]{4,3,2,1,0:T(8,128)(2,1)S(1)}, u32[]{:S(2)}, u32[]{:S(2)}) collective-permute-start(bf16[2,2,4,16,1536]{4,3,2,1,0:T(8,128)(2,1)S(1)} %get-tuple-element.221), channel_id=1, source_target_pairs={{0,1},{1,0},{2,3},{3,2},{4,5},{5,4},{6,7},{7,6},{8,9},{9,8},{10,11... | collective-permute-start | bytes 2359304 | tf_op jit(solution)/shard_map/ppermute | solution.py:673
  76.8 3.6 %collective-permute-start.22 = (bf16[2,2,4,16,1536]{4,3,2,1,0:T(8,128)(2,1)S(1)}, bf16[2,2,4,16,1536]{4,3,2,1,0:T(8,128)(2,1)S(1)}, u32[]{:S(2)}, u32[]{:S(2)}) collective-permute-start(bf16[2,2,4,16,1536]{4,3,2,1,0:T(8,128)(2,1)S(1)} %get-tuple-element.225), channel_id=1, source_target_pairs={{0,1},{1,0},{2,3},{3,2},{4,5},{5,4},{6,7},{7,6},{8,9},{9,8},{10,11... | collective-permute-start | bytes 2359304 | tf_op jit(solution)/shard_map/ppermute | solution.py:673
  77.3 11.2 %collective-permute-start.23 = (bf16[2,4,16,1536]{3,2,1,0:T(8,128)(2,1)S(1)}, bf16[2,4,16,1536]{3,2,1,0:T(8,128)(2,1)S(1)}, u32[]{:S(2)}, u32[]{:S(2)}) collective-permute-start(bf16[2,4,16,1536]{3,2,1,0:T(8,128)(2,1)S(1)} %fusion.1), channel_id=1, source_target_pairs={{0,2},{1,3},{2,0},{3,1},{4,6},{5,7},{6,4},{7,5},{8,10},{9,11},{10,... | collective-permute-start | bytes 1179656 | tf_op jit(solution)/shard_map/ppermute | solution.py:673
  80.5 10.9 %collective-permute-start.24 = (bf16[2,4,16,1536]{3,2,1,0:T(8,128)(2,1)S(1)}, bf16[2,4,16,1536]{3,2,1,0:T(8,128)(2,1)S(1)}, u32[]{:S(2)}, u32[]{:S(2)}) collective-permute-start(bf16[2,4,16,1536]{3,2,1,0:T(8,128)(2,1)S(1)} %fusion), channel_id=1, source_target_pairs={{0,4},{4,0},{8,12},{12,8},{16,20},{20,16},{24,28},{28,24},{1,5},{5... | collective-permute-start | bytes 1179656 | tf_op jit(solution)/shard_map/ppermute | solution.py:673
  91.5 2.8 %collective-permute-start.26 = (bf16[2,2,4,16,1152]{4,3,2,1,0:T(8,128)(2,1)S(1)}, bf16[2,2,4,16,1152]{4,3,2,1,0:T(8,128)(2,1)S(1)}, u32[]{:S(2)}, u32[]{:S(2)}) collective-permute-start(bf16[2,2,4,16,1152]{4,3,2,1,0:T(8,128)(2,1)S(1)} %get-tuple-element.248), channel_id=1, source_target_pairs={{0,1},{1,0},{2,3},{3,2},{4,5},{5,4},{6,7},{7,6},{8,9},{9,8},{10,11... | collective-permute-start | bytes 1769480 | tf_op jit(solution)/shard_map/ppermute | solution.py:673
  91.5 2.8 %collective-permute-start.25 = (bf16[2,2,4,16,1024]{4,3,2,1,0:T(8,128)(2,1)S(1)}, bf16[2,2,4,16,1024]{4,3,2,1,0:T(8,128)(2,1)S(1)}, u32[]{:S(2)}, u32[]{:S(2)}) collective-permute-start(bf16[2,2,4,16,1024]{4,3,2,1,0:T(8,128)(2,1)S(1)} %get-tuple-element.247), channel_id=1, source_target_pairs={{0,1},{1,0},{2,3},{3,2},{4,5},{5,4},{6,7},{7,6},{8,9},{9,8},{10,11... | collective-permute-start | bytes 1572872 | tf_op jit(solution)/shard_map/ppermute | solution.py:673
  94.3 9.8 %collective-permute-start.28 = (bf16[2,4,16,1152]{3,2,1,0:T(8,128)(2,1)S(1)}, bf16[2,4,16,1152]{3,2,1,0:T(8,128)(2,1)S(1)}, u32[]{:S(2)}, u32[]{:S(2)}) collective-permute-start(bf16[2,4,16,1152]{3,2,1,0:T(8,128)(2,1)S(1)} %fusion.2), channel_id=1, source_target_pairs={{0,2},{1,3},{2,0},{3,1},{4,6},{5,7},{6,4},{7,5},{8,10},{9,11},{10,... | collective-permute-start | bytes 884744 | tf_op jit(solution)/shard_map/ppermute | solution.py:673
  96.0 8.1 %collective-permute-start.27 = (bf16[2,4,16,1024]{3,2,1,0:T(8,128)(2,1)S(1)}, bf16[2,4,16,1024]{3,2,1,0:T(8,128)(2,1)S(1)}, u32[]{:S(2)}, u32[]{:S(2)}) collective-permute-start(bf16[2,4,16,1024]{3,2,1,0:T(8,128)(2,1)S(1)} %fusion.3), channel_id=1, source_target_pairs={{0,4},{4,0},{8,12},{12,8},{16,20},{20,16},{24,28},{28,24},{1,5},{5... | collective-permute-start | bytes 786440 | tf_op jit(solution)/shard_map/ppermute | solution.py:673
  100.5 5.3 %collective-permute-start.31 = (bf16[2,2,128,512]{3,2,1,0:T(8,128)(2,1)S(1)}, bf16[2,2,128,512]{3,2,1,0:T(8,128)(2,1)S(1)}, u32[]{:S(2)}, u32[]{:S(2)}) collective-permute-start(bf16[2,2,128,512]{3,2,1,0:T(8,128)(2,1)S(1)} %get-tuple-element.274), channel_id=1, source_target_pairs={{0,1},{1,0},{2,3},{3,2},{4,5},{5,4},{6,7},{7,6},{8,9},{9,8},{10,11... | collective-permute-start | bytes 1572872 | tf_op jit(solution)/shard_map/ppermute | solution.py:673
  104.4 9.0 %collective-permute-start.30 = (bf16[4,16,2688]{2,1,0:T(8,128)(2,1)S(1)}, bf16[4,16,2688]{2,1,0:T(8,128)(2,1)S(1)}, u32[]{:S(2)}, u32[]{:S(2)}) collective-permute-start(bf16[4,16,2688]{2,1,0:T(8,128)(2,1)S(1)} %get-tuple-element.273), channel_id=1, source_target_pairs={{0,4},{4,0},{8,12},{12,8},{16,20},{20,16},{24,28},{28,24},{1,5},{5... | collective-permute-start | bytes 1032200 | tf_op jit(solution)/shard_map/ppermute | solution.py:673
  105.0 8.3 %collective-permute-start.29 = (bf16[4,16,2560]{2,1,0:T(8,128)(2,1)S(1)}, bf16[4,16,2560]{2,1,0:T(8,128)(2,1)S(1)}, u32[]{:S(2)}, u32[]{:S(2)}) collective-permute-start(bf16[4,16,2560]{2,1,0:T(8,128)(2,1)S(1)} %get-tuple-element.272), channel_id=1, source_target_pairs={{0,2},{1,3},{2,0},{3,1},{4,6},{5,7},{6,4},{7,5},{8,10},{9,11},{10,... | collective-permute-start | bytes 983048 | tf_op jit(solution)/shard_map/ppermute | solution.py:673
  113.7 28.5 %collective-permute-start.41 = (bf16[2,2,2,128,512]{4,3,2,1,0:T(8,128)(2,1)S(1)}, bf16[2,2,2,128,512]{4,3,2,1,0:T(8,128)(2,1)S(1)}, u32[]{:S(2)}, u32[]{:S(2)}) collective-permute-start(bf16[2,2,2,128,512]{4,3,2,1,0:T(8,128)(2,1)S(1)} %get-tuple-element.303), channel_id=1, source_target_pairs={{0,2},{1,3},{2,0},{3,1},{4,6},{5,7},{6,4},{7,5},{8,10},{9,11},{10,... | collective-permute-start | bytes 3145736 | tf_op jit(solution)/shard_map/ppermute | solution.py:673
  115.0 12.3 %collective-permute-start.33 = (bf16[16,5248]{1,0:T(8,128)(2,1)S(1)}, bf16[16,5248]{1,0:T(8,128)(2,1)S(1)}, u32[]{:S(2)}, u32[]{:S(2)}) collective-permute-start(bf16[16,5248]{1,0:T(8,128)(2,1)S(1)} %get-tuple-element.279), channel_id=1, source_target_pairs={{0,16},{4,20},{8,24},{12,28},{16,0},{20,4},{24,8},{28,12},{1,17},{... | collective-permute-start | bytes 503816 | tf_op jit(solution)/shard_map/ppermute | solution.py:673
  116.1 11.2 %collective-permute-start.34 = (bf16[16,5248]{1,0:T(8,128)(2,1)S(1)}, bf16[16,5248]{1,0:T(8,128)(2,1)S(1)}, u32[]{:S(2)}, u32[]{:S(2)}) collective-permute-start(bf16[16,5248]{1,0:T(8,128)(2,1)S(1)} %get-tuple-element.280), channel_id=1, source_target_pairs={{0,24},{4,28},{8,16},{12,20},{16,8},{20,12},{24,0},{28,4},{1,25},{... | collective-permute-start | bytes 503816 | tf_op jit(solution)/shard_map/ppermute | solution.py:673
  117.5 11.1 %collective-permute-start.32 = (bf16[16,5248]{1,0:T(8,128)(2,1)S(1)}, bf16[16,5248]{1,0:T(8,128)(2,1)S(1)}, u32[]{:S(2)}, u32[]{:S(2)}) collective-permute-start(bf16[16,5248]{1,0:T(8,128)(2,1)S(1)} %get-tuple-element.278), channel_id=1, source_target_pairs={{0,8},{4,12},{8,0},{12,4},{16,24},{20,28},{24,16},{28,20},{1,9},{5... | collective-permute-start | bytes 503816 | tf_op jit(solution)/shard_map/ppermute | solution.py:673
  128.8 13.4 %collective-permute-start.40 = (bf16[16,5248]{1,0:T(8,128)(2,1)S(1)}, bf16[16,5248]{1,0:T(8,128)(2,1)S(1)}, u32[]{:S(2)}, u32[]{:S(2)}) collective-permute-start(bf16[16,5248]{1,0:T(8,128)(2,1)S(1)} %get-tuple-element.301.refs_0_.own_ref), channel_id=1, source_target_pairs={{0,2},{1,3},{2,0},{3,1},{4,6},{5,7},{6,4},{7,5},{8,10},{9,11},{10,... | collective-permute-start | bytes 503816 | tf_op jit(solution)/shard_map/ppermute | solution.py:673
  129.4 17.3 %copy-start.1 = (f32[256]{0:T(256)S(1)}, f32[256]{0:T(256)}, u32[]{:S(2)}) copy-start(f32[256]{0:T(256)} %param.38) | copy-start | bytes 3076
  129.5 17.3 %copy-start.2 = (f32[64]{0:T(128)S(1)}, f32[64]{0:T(128)}, u32[]{:S(2)}) copy-start(f32[64]{0:T(128)} %param.42) | copy-start | bytes 772
  129.5 17.3 %copy-start.3 = (f32[256]{0:T(256)S(1)}, f32[256]{0:T(256)}, u32[]{:S(2)}) copy-start(f32[256]{0:T(256)} %param.39) | copy-start | bytes 3076
  129.5 17.3 %copy-start.4 = (f32[256]{0:T(256)S(1)}, f32[256]{0:T(256)}, u32[]{:S(2)}) copy-start(f32[256]{0:T(256)} %param.40) | copy-start | bytes 3076
  129.5 17.3 %copy-start.5 = (f32[256]{0:T(256)S(1)}, f32[256]{0:T(256)}, u32[]{:S(2)}) copy-start(f32[256]{0:T(256)} %param.41) | copy-start | bytes 3076
  129.5 17.3 %copy-start.6 = (f32[64]{0:T(128)S(1)}, f32[64]{0:T(128)}, u32[]{:S(2)}) copy-start(f32[64]{0:T(128)} %param.43) | copy-start | bytes 772
  129.5 17.3 %copy-start.7 = (f32[64]{0:T(128)S(1)}, f32[64]{0:T(128)}, u32[]{:S(2)}) copy-start(f32[64]{0:T(128)} %param.44) | copy-start | bytes 772
  129.5 17.3 %copy-start.8 = (f32[64]{0:T(128)S(1)}, f32[64]{0:T(128)}, u32[]{:S(2)}) copy-start(f32[64]{0:T(128)} %param.45) | copy-start | bytes 772
  129.5 1.2 collective-permute-start.35
  130.7 3.6 %collective-permute-start.36 = (f32[8,128]{1,0:T(8,128)S(1)}, f32[8,128]{1,0:T(8,128)S(1)}, u32[]{:S(2)}, u32[]{:S(2)}) collective-permute-start(f32[8,128]{1,0:T(8,128)S(1)} %add.32.refs_0_), channel_id=1, source_target_pairs={{0,4},{4,0},{8,12},{12,8},{16,20},{20,16},{24,28},{28,24},{1,5},{5... | collective-permute-start | bytes 12296 | tf_op jit(solution)/shard_map/ppermute | solution.py:673
  134.4 5.4 %collective-permute-start.39 = (f32[8,128]{1,0:T(8,128)S(1)}, f32[8,128]{1,0:T(8,128)S(1)}, u32[]{:S(2)}, u32[]{:S(2)}) collective-permute-start(f32[8,128]{1,0:T(8,128)S(1)} %add.33.refs_0_), channel_id=1, source_target_pairs={{0,24},{4,28},{8,16},{12,20},{16,8},{20,12},{24,0},{28,4},{1,25},{... | collective-permute-start | bytes 12296 | tf_op jit(solution)/shard_map/ppermute | solution.py:673
  136.5 4.5 %collective-permute-start.38 = (f32[8,128]{1,0:T(8,128)S(1)}, f32[8,128]{1,0:T(8,128)S(1)}, u32[]{:S(2)}, u32[]{:S(2)}) collective-permute-start(f32[8,128]{1,0:T(8,128)S(1)} %add.33.refs_0_), channel_id=1, source_target_pairs={{0,16},{4,20},{8,24},{12,28},{16,0},{20,4},{24,8},{28,12},{1,17},{... | collective-permute-start | bytes 12296 | tf_op jit(solution)/shard_map/ppermute | solution.py:673
  138.7 3.6 %collective-permute-start.37 = (f32[8,128]{1,0:T(8,128)S(1)}, f32[8,128]{1,0:T(8,128)S(1)}, u32[]{:S(2)}, u32[]{:S(2)}) collective-permute-start(f32[8,128]{1,0:T(8,128)S(1)} %add.33.refs_0_), channel_id=1, source_target_pairs={{0,8},{4,12},{8,0},{12,4},{16,24},{20,28},{24,16},{28,20},{1,9},{5... | collective-permute-start | bytes 12296 | tf_op jit(solution)/shard_map/ppermute | solution.py:673
  142.3 2.7 %collective-permute-start.43 = (bf16[2,2,2,128,512]{4,3,2,1,0:T(8,128)(2,1)S(1)}, bf16[2,2,2,128,512]{4,3,2,1,0:T(8,128)(2,1)S(1)}, u32[]{:S(2)}, u32[]{:S(2)}) collective-permute-start(bf16[2,2,2,128,512]{4,3,2,1,0:T(8,128)(2,1)S(1)} %collective-permute-done.41.side_ref), channel_id=1, source_target_pairs={{0,1},{1,0},{2,3},{3,2},{4,5},{5,4},{6,7},{7,6},{8,9},{9,8},{10,11... | collective-permute-start | bytes 3145736 | tf_op jit(solution)/shard_map/ppermute | solution.py:673
  142.3 4.4 %collective-permute-start.44 = (bf16[2,16,5248]{2,1,0:T(8,128)(2,1)S(1)}, bf16[2,16,5248]{2,1,0:T(8,128)(2,1)S(1)}, u32[]{:S(2)}, u32[]{:S(2)}) collective-permute-start(bf16[2,16,5248]{2,1,0:T(8,128)(2,1)S(1)} %stack.7), channel_id=1, source_target_pairs={{0,1},{1,0},{2,3},{3,2},{4,5},{5,4},{6,7},{7,6},{8,9},{9,8},{10,11... | collective-permute-start | bytes 1007624 | tf_op jit(solution)/shard_map/ppermute | solution.py:673
  142.9 3.8 %collective-permute-start.42 = (f32[8,128]{1,0:T(8,128)S(1)}, f32[8,128]{1,0:T(8,128)S(1)}, u32[]{:S(2)}, u32[]{:S(2)}) collective-permute-start(f32[8,128]{1,0:T(8,128)S(1)} %add.34.refs_0_), channel_id=1, source_target_pairs={{0,2},{1,3},{2,0},{3,1},{4,6},{5,7},{6,4},{7,5},{8,10},{9,11},{10,... | collective-permute-start | bytes 12296 | tf_op jit(solution)/shard_map/ppermute | solution.py:673

commit v2 on v1

--- a/solution.py
+++ b/solution.py
@@ -168,12 +168,12 @@
         copy.wait()
 
 
-def gating_kernel(tree, count, members, lens_ref, own_ref, core_ref, side_ref, forward_ref, *refs):
+def gating_kernel(tree, count, members, own_ref, core_ref, side_ref, forward_ref, *refs):
     parts = [core_ref.at[0], side_ref.at[0, 0], forward_ref.at[1, 0]]
     sources, small_sources = refs[:count], refs[count : count + 2]
     (
-        normed_ref, xhat_ref, scale_ref, gate_ref, slope_ref, rstd_ref, mixed_ref, spatial_ref, gains_ref, weight,
-        small, acts, active, sums, bias_col, sems,
+        normed_ref, xhat_ref, scale_ref, gate_ref, slope_ref, rstd_ref, spatial_ref, gains_ref, bias_col, weight,
+        small, acts, active, sums, sems,
     ) = refs[count + 2 :]
     wide, narrow = lax.axis_index("wide"), lax.axis_index("narrow")
     rows_here, quarter = acts.shape[1:3]
@@ -246,14 +246,20 @@
                 vhat = (active[here, c : c + LANES] - centre) * scale
                 gate_ref[row, here, c : c + LANES] = (vhat * gains_ref[0:1, D + c : D + c + LANES]).astype(BF16)
 
+        return carry
+
+    lax.fori_loop(0, rows_here, do_row, 0)
+
+
+def mixing_kernel(lens_ref, spatial_ref, gate_ref, bias_col, mixed_ref):
+    rows_here = gate_ref.shape[0]
+    narrow = lax.axis_index("narrow")
+    for row in range(rows_here):
         same, live = doc_mask(0, ROW, lens_ref, narrow * rows_here + row)
         masked = jnp.where(same, spatial_ref[...], jnp.zeros((), BF16))
         bias = jnp.where(live, bias_col[:, 0:1], 0.0)
-        for c in range(0, HALF, WIDTH):
-            mixed_ref[row, :, c : c + WIDTH] = (dot(masked, gate_ref[row, :, c : c + WIDTH]) + bias).astype(BF16)
-        return carry
-
-    lax.fori_loop(0, rows_here, do_row, 0)
+        for c in range(0, HALF, D):
+            mixed_ref[row, :, c : c + D] = (dot(masked, gate_ref[row, :, c : c + D]) + bias).astype(BF16)
 
 
 def emit_blocks(order, read, columns, first, keep_near, keep_far, send):
@@ -517,36 +523,25 @@
 
 
 def side_kernel(*refs):
-    inputs, outputs = refs[:12], refs[12:]
-    for i, out_ref in enumerate(outputs):
-        first = 0
-        for group in range(2):
-            near, came, far = inputs[6 * i + 3 * group : 6 * i + 3 * group + 3]
-            width = near.shape[3]
-            for c in range(0, width, LANES):
-                out_ref[:, :, first + c : first + c + LANES] = sum_three(
-                    near, came, far, 1, slice(c, c + LANES)
-                ).astype(BF16)
-            first += width
+    for i, out_ref in enumerate(refs[6:]):
+        near, came, far = refs[3 * i : 3 * i + 3]
+        for c in range(0, near.shape[3], LANES):
+            out_ref[:, :, c : c + LANES] = sum_three(near, came, far, 1, slice(c, c + LANES)).astype(BF16)
 
 
 def fold_kernel(*refs):
-    inputs, sides, outputs = refs[:12], refs[12:14], refs[14:]
-    base = 0
-    for i in range(2):
-        first = 0
-        for group in range(2):
-            near, came, far = inputs[6 * i + 3 * group : 6 * i + 3 * group + 3]
-            width = near.shape[3]
-            for c in range(0, width, LANES):
-                place = slice(first + c, first + c + LANES)
-                total = sum_three(near, came, far, 0, slice(c, c + LANES)) + sides[i][:, :, place].astype(F32)
-                there = slice(base + first + c, base + first + c + LANES)
-                outputs[0][:, there] = total[0]
-                for step in range(1, 4):
-                    outputs[step][:, there] = total[step].astype(BF16)
-            first += width
-        base += first
+    sides, outputs = refs[12:16], refs[16:]
+    first = 0
+    for i in range(4):
+        near, came, far = refs[3 * i : 3 * i + 3]
+        for c in range(0, near.shape[3], LANES):
+            place = slice(c, c + LANES)
+            total = sum_three(near, came, far, 0, place) + sides[i][:, :, place].astype(F32)
+            there = slice(first + c, first + c + LANES)
+            outputs[0][:, there] = total[0]
+            for step in range(1, 4):
+                outputs[step][:, there] = total[step].astype(BF16)
+        first += near.shape[3]
 
 
 def norm_kernel(mine_ref, one_ref, two_ref, three_ref, weight_ref, gains_ref, low_ref, message_ref):
@@ -826,33 +821,46 @@
     thin = shape((rows, ROW, 128), F32)
     weight_type = shape((D, HALF), BF16)
 
-    normed, xhat, scale, gate_normed, slope, rstd, mixed, spatial_low, gains, gate_weight = call_kernel(
+    normed, xhat, scale, gate_normed, slope, rstd, spatial_low, gains, bias_col, gate_weight = call_kernel(
         functools.partial(gating_kernel, tree, count, narrow_size),
         "gating",
-        [doc_lengths, activations, core_came, side_came, forward_came] + list(first_pieces) + list(small_pieces),
-        [smem, stored] + [anywhere] * (narrow_size - 1 + count + 2),
-        [low_d, low_d, thin, low_half, low_half, thin, low_half]
-        + [shape((ROW, ROW), BF16), shape((8, D + HALF), F32), weight_type],
+        [activations, core_came, side_came, forward_came] + list(first_pieces) + list(small_pieces),
+        [stored] + [anywhere] * (narrow_size - 1 + count + 2),
+        [low_d, low_d, thin, low_half, low_half, thin]
+        + [shape((ROW, ROW), BF16), shape((8, D + HALF), F32), shape((ROW, 128), F32), weight_type],
         [
             pltpu.VMEM((8, BLOCK, 128), BF16),
             pltpu.VMEM((narrow_size, *part.shape), BF16),
             pltpu.VMEM((ROW, HALF), F32),
             pltpu.VMEM((ROW, 128), F32),
-            pltpu.VMEM((ROW, 128), F32),
             dma((4,)),
         ],
         product // 64,
     )
 
+    bias_late = bias_col
     if tree:
         *shrink_came, expand_across, _ = lax.optimization_barrier((*shrink_came, expand_across, normed))
         shrink_near = stack([shrink_own, *shrink_came])
         shrink_across = cross_x(shrink_near)
         expand_pieces = [expand_near, expand_across, near_other, cross_core(expand_across)]
+        bias_late = after(bias_col, shrink_near)
+    mixed = call_kernel(
+        mixing_kernel,
+        "mixing",
+        [doc_lengths, spatial_low, gate_normed, bias_late],
+        [smem] + [None] * 3,
+        [low_half],
+        [],
+        product // 64,
+    )[0]
+    normed_late = normed
+    if tree:
+        expand_pieces[3], normed_late, _ = lax.optimization_barrier((expand_pieces[3], normed, mixed))
     content, content_slope, content_weight = call_kernel(
         functools.partial(content_up_kernel, tree),
         "content_up",
-        [normed, *expand_pieces],
+        [normed_late, *expand_pieces],
         [None] + [anywhere] * len(expand_pieces),
         [low_half, low_half, weight_type],
         [dma(())],
@@ -948,13 +956,21 @@
         sum_scratch,
         product // 64,
     )
+    def side_step(terms, widths):
+        kinds = [shape((4, BLOCK, width), BF16) for width in widths]
+        return call_kernel(side_kernel, "side", terms, [None] * 6, kinds, [], product // 64)
+
     gated_late = gated
     if tree:
         second_raws[2], second_raws[5], came_far["content"] = lax.optimization_barrier(
             (second_raws[2], second_raws[5], came_far["content"])
         )
         second_came = [cross_core(second_raws[i]) for i in (2, 5)]
-        gated_late = after(gated, second_raws[0], came_far["content"])
+        first_terms = [content_raws[0], came["content"], came_far["content"]]
+        first_terms += [shrink_raws[0], came["shrink"], came_far["shrink"]]
+        first_sides = side_step(first_terms, (HALF, HALF))
+        first_came_side = [cross_y(first_sides[0]), cross_x(first_sides[1])]
+        gated_late = after(gated, second_raws[0], *first_sides)
     part_scratch = pltpu.VMEM((narrow_size, *part.shape), BF16)
     layer_own, layer_core, layer_pair = call_kernel(
         layer_kernel,
@@ -999,33 +1015,19 @@
 
     if tree:
         columns = HALF + HALF + SPLIT + (HALF - SPLIT) + ROW + VECTOR_LANES
-        half_columns = HALF + SPLIT
-        (*all_far, grad_own) = lax.optimization_barrier(
-            (came_far["content"], second_came_far[0], came_far["shrink"], second_came_far[1], grad_own)
-        )
-        terms = []
-        for near, near_came, far_came in zip(
-            (content_raws[0], second_raws[0], shrink_raws[0], second_raws[3]),
-            (came["content"], second_came[0], came["shrink"], second_came[1]),
-            all_far,
-        ):
-            terms += [near, near_came, far_came]
-        sides = call_kernel(
-            side_kernel,
-            "side",
-            terms,
-            [None] * 12,
-            [shape((4, BLOCK, half_columns), BF16), shape((4, BLOCK, columns - half_columns), BF16)],
-            [],
-            product // 64,
-        )
-        came_side = [cross_y(sides[0]), cross_x(sides[1])]
-        *came_side, core_back = lax.optimization_barrier((*came_side, cross_core(core_back)))
+        tied = lax.optimization_barrier((*second_came_far, *first_came_side, grad_own))
+        second_came_far, first_came_side, grad_own = tied[:2], tied[2:4], tied[4]
+        second_terms = [second_raws[0], second_came[0], second_came_far[0]]
+        second_terms += [second_raws[3], second_came[1], second_came_far[1]]
+        second_sides = side_step(second_terms, (SPLIT, HALF - SPLIT + ROW + VECTOR_LANES))
+        second_came_side = [cross_y(second_sides[0]), cross_x(second_sides[1])]
+        terms = first_terms[:3] + second_terms[:3] + first_terms[3:] + second_terms[3:]
+        came_side = [first_came_side[0], second_came_side[0], first_came_side[1], second_came_side[1]]
         mine, *sent = call_kernel(
             fold_kernel,
             "fold",
             terms + came_side,
-            [None] * 14,
+            [None] * 16,
             [shape((BLOCK, columns), F32)] + [shape((BLOCK, columns), BF16)] * 3,
             [],
             product // 64,
@@ -1046,6 +1048,7 @@
         )
         states, bases = states[:12], states[12:]
         side_back = cross_y(after(pair_back, sent[0]))
+        core_back = cross_core(after(core_back, sent[0]))
         *came_z, first_state = lax.optimization_barrier((*came_z, states[0]))
         low, message = call_kernel(
             norm_kernel,

time: 151 us -> 149 us (0.987)
  waiting for transfers between devices: 51.8 us -> 47.7 us
  starting transfers between devices: 39.9 us -> 42.3 us
    ppermute x45 -> x47, waiting for transfers between devices: 51.8 us -> 47.7 us  [swap_with(): return lax.ppermute(value, axis, [(i, i ^ bit) for i in range(size)])]
    ppermute x45 -> x47, starting transfers between devices: 39.9 us -> 42.3 us  [swap_with(): return lax.ppermute(value, axis, [(i, i ^ bit) for i in range(size)])]
    pallas_call x26 -> x28, Pallas kernels: 57.4 us -> 57.3 us  [call_kernel(): pl.pallas_call(kernel, name=name, in_specs=in_specs, out_specs=specs, out...]
  transfers between devices with their start and end apart: 45 -> 47, of which waited for: 22 -> 21; matrix products, arithmetic and copies ran while one was open for 0% -> 0% of each run, Pallas kernels for 28% -> 28%
where the time goes in v2:
time: 149 us
  Pallas kernels  57.3 us (38%)
  waiting for transfers between devices  47.7 us (32%)
  starting transfers between devices  42.3 us (28%)
    pallas_call x28, Pallas kernels, call_kernel(): pl.pallas_call(kernel, name=name, in_specs=in_specs, out_specs=specs, out...  57.3 us
    ppermute x47, waiting for transfers between devices, swap_with(): return lax.ppermute(value, axis, [(i, i ^ bit) for i in range(size)])  47.7 us
    ppermute x47, starting transfers between devices, swap_with(): return lax.ppermute(value, axis, [(i, i ^ bit) for i in range(size)])  42.3 us
  transfers between devices with their start and end apart: 47, of which 21 were waited for; matrix products, arithmetic and copies ran while one was open for 0% of the time, Pallas kernels for 28%

profile of v2, /device:TPU:0, one launch (start us, length us, event | category | flops | bytes accessed | tf_op | source)
XLA Modules:
  0.0 149.0 jit_solution(4096490086312491289)
XLA Ops:
  0.7 1.0 pack_first.1.refs_0_
  1.7 1.4 cut.1
  3.1 3.0 %collective-permute-start.7 = (bf16[2,2,2,128,512]{4,3,2,1,0:T(8,128)(2,1)S(1)}, bf16[2,2,2,128,512]{4,3,2,1,0:T(8,128)(2,1)S(1)}, u32[]{:S(2)}, u32[]{:S(2)}) collective-permute-start(bf16[2,2,2,128,512]{4,3,2,1,0:T(8,128)(2,1)S(1)} %get-tuple-element.198), channel_id=1, source_target_pairs={{0,2},{1,3},{2,0},{3,1},{4,6},{5,7},{6,4},{7,5},{8,10},{9,11},{10,... | collective-permute-start | bytes 3145736 | tf_op jit(solution)/shard_map/ppermute | solution.py:668
  6.1 3.6 %collective-permute-start.2 = (bf16[32,2176]{1,0:T(8,128)(2,1)S(1)}, bf16[32,2176]{1,0:T(8,128)(2,1)S(1)}, u32[]{:S(2)}, u32[]{:S(2)}) collective-permute-start(bf16[32,2176]{1,0:T(8,128)(2,1)S(1)} %pack_first.1.refs_0_), channel_id=1, source_target_pairs={{0,24},{4,28},{8,16},{12,20},{16,8},{20,12},{24,0},{28,4},{1,25},{... | collective-permute-start | bytes 417800 | tf_op jit(solution)/shard_map/ppermute | solution.py:668
  9.7 0.8 collective-permute-start
  10.5 1.1 pack_second.1
  11.6 2.9 %collective-permute-done.2.refs_3_ = bf16[32,2176]{1,0:T(8,128)(2,1)S(1)} collective-permute-done((bf16[32,2176]{1,0:T(8,128)(2,1)S(1)}, bf16[32,2176]{1,0:T(8,128)(2,1)S(1)}, u32[]{:S(2)}, u32[]{:S(2)}) %collective-permute-start.2) | collective-permute-done | bytes 139296 | tf_op jit(solution)/shard_map/ppermute | solution.py:668
  14.5 7.7 %collective-permute-done.1.refs_2_ = bf16[32,2176]{1,0:T(8,128)(2,1)S(1)} collective-permute-done((bf16[32,2176]{1,0:T(8,128)(2,1)S(1)}, bf16[32,2176]{1,0:T(8,128)(2,1)S(1)}, u32[]{:S(2)}, u32[]{:S(2)}) %collective-permute-start.1) | collective-permute-done | bytes 139296 | tf_op jit(solution)/shard_map/ppermute | solution.py:668
  22.2 1.6 %collective-permute-start.11 = (bf16[4,32,2176]{2,1,0:T(8,128)(2,1)S(1)}, bf16[4,32,2176]{2,1,0:T(8,128)(2,1)S(1)}, u32[]{:S(2)}, u32[]{:S(2)}) collective-permute-start(bf16[4,32,2176]{2,1,0:T(8,128)(2,1)S(1)} %stack.4.refs_0_.refs_4_), channel_id=1, source_target_pairs={{0,4},{4,0},{8,12},{12,8},{16,20},{20,16},{24,28},{28,24},{1,5},{5... | collective-permute-start | bytes 1671176 | tf_op jit(solution)/shard_map/ppermute | solution.py:668
  23.8 2.5 %collective-permute-start.6 = (bf16[32,1536]{1,0:T(8,128)(2,1)S(1)}, bf16[32,1536]{1,0:T(8,128)(2,1)S(1)}, u32[]{:S(2)}, u32[]{:S(2)}) collective-permute-start(bf16[32,1536]{1,0:T(8,128)(2,1)S(1)} %get-tuple-element.204.refs_0_), channel_id=1, source_target_pairs={{0,24},{4,28},{8,16},{12,20},{16,8},{20,12},{24,0},{28,4},{1,25},{... | collective-permute-start | bytes 294920 | tf_op jit(solution)/shard_map/ppermute | solution.py:668
  26.3 1.9 %collective-permute-start.4 = (bf16[32,1536]{1,0:T(8,128)(2,1)S(1)}, bf16[32,1536]{1,0:T(8,128)(2,1)S(1)}, u32[]{:S(2)}, u32[]{:S(2)}) collective-permute-start(bf16[32,1536]{1,0:T(8,128)(2,1)S(1)} %get-tuple-element.204.refs_0_), channel_id=1, source_target_pairs={{0,8},{4,12},{8,0},{12,4},{16,24},{20,28},{24,16},{28,20},{1,9},{5... | collective-permute-start | bytes 294920 | tf_op jit(solution)/shard_map/ppermute | solution.py:668
  28.2 3.2 %collective-permute-done.6.refs_3_ = bf16[32,1536]{1,0:T(8,128)(2,1)S(1)} collective-permute-done((bf16[32,1536]{1,0:T(8,128)(2,1)S(1)}, bf16[32,1536]{1,0:T(8,128)(2,1)S(1)}, u32[]{:S(2)}, u32[]{:S(2)}) %collective-permute-start.6) | collective-permute-done | bytes 98336 | tf_op jit(solution)/shard_map/ppermute | solution.py:668
  31.4 2.6 %collective-permute-done.5.refs_2_ = bf16[32,1536]{1,0:T(8,128)(2,1)S(1)} collective-permute-done((bf16[32,1536]{1,0:T(8,128)(2,1)S(1)}, bf16[32,1536]{1,0:T(8,128)(2,1)S(1)}, u32[]{:S(2)}, u32[]{:S(2)}) %collective-permute-start.5) | collective-permute-done | bytes 98336 | tf_op jit(solution)/shard_map/ppermute | solution.py:668
  34.6 2.0 %collective-permute-done.11.refs_1_.refs_5_ = bf16[4,32,2176]{2,1,0:T(8,128)(2,1)S(1)} collective-permute-done((bf16[4,32,2176]{2,1,0:T(8,128)(2,1)S(1)}, bf16[4,32,2176]{2,1,0:T(8,128)(2,1)S(1)}, u32[]{:S(2)}, u32[]{:S(2)}) %collective-permute-start.11) | collective-permute-done | bytes 557088 | tf_op jit(solution)/shard_map/ppermute | solution.py:668
  36.6 1.5 %collective-permute-start.12 = (bf16[4,32,1536]{2,1,0:T(8,128)(2,1)S(1)}, bf16[4,32,1536]{2,1,0:T(8,128)(2,1)S(1)}, u32[]{:S(2)}, u32[]{:S(2)}) collective-permute-start(bf16[4,32,1536]{2,1,0:T(8,128)(2,1)S(1)} %stack.5.refs_0_), channel_id=1, source_target_pairs={{0,4},{4,0},{8,12},{12,8},{16,20},{20,16},{24,28},{28,24},{1,5},{5... | collective-permute-start | bytes 1179656 | tf_op jit(solution)/shard_map/ppermute | solution.py:668
  38.0 2.5 %collective-permute-start.10 = (bf16[32,1536]{1,0:T(8,128)(2,1)S(1)}, bf16[32,1536]{1,0:T(8,128)(2,1)S(1)}, u32[]{:S(2)}, u32[]{:S(2)}) collective-permute-start(bf16[32,1536]{1,0:T(8,128)(2,1)S(1)} %get-tuple-element.208.refs_0_), channel_id=1, source_target_pairs={{0,24},{4,28},{8,16},{12,20},{16,8},{20,12},{24,0},{28,4},{1,25},{... | collective-permute-start | bytes 294920 | tf_op jit(solution)/shard_map/ppermute | solution.py:668
  40.5 1.9 %collective-permute-start.8 = (bf16[32,1536]{1,0:T(8,128)(2,1)S(1)}, bf16[32,1536]{1,0:T(8,128)(2,1)S(1)}, u32[]{:S(2)}, u32[]{:S(2)}) collective-permute-start(bf16[32,1536]{1,0:T(8,128)(2,1)S(1)} %get-tuple-element.208.refs_0_), channel_id=1, source_target_pairs={{0,8},{4,12},{8,0},{12,4},{16,24},{20,28},{24,16},{28,20},{1,9},{5... | collective-permute-start | bytes 294920 | tf_op jit(solution)/shard_map/ppermute | solution.py:668
  42.4 7.7 %gating.1 = (bf16[2,512,512]{2,1,0:T(8,128)(2,1)S(1)}, bf16[2,512,512]{2,1,0:T(8,128)(2,1)S(1)}, f32[2,512,128]{2,1,0:T(8,128)S(1)}, bf16[2,512,1536]{2,1,0:T(8,...) custom-call(bf16[8,128,512]{2,1,0:T(8,128)(2,1)} %refs_13_, ...), custom_call_target="tpu_custom_call" | custom-call | flops 25165824 | bytes 50331 | tf_op jit(solution)/shard_map/gating/pallas_call | solution.py:654
  50.8 0.6 collective-permute-start.18
  51.4 2.5 %mixing.1.mixed_ref = bf16[2,512,1536]{2,1,0:T(8,128)(2,1)S(1)} custom-call(s32[8,5]{1,0:T(8,128)S(1)} %copy-done, bf16[512,512]{1,0:T(8,128)(2,1)S(1)} %get-tuple-element.217.spatial_ref, bf16[2,512,1536]{2,1,0:T(8,128)(2,1)S(1)} %get-tuple-element.218.gate_ref, f32[512,128]{1,0:T(8,128)S(1)} %get-tuple-element.223.bias_col), custom_call_target="tpu_custom_call" | custom-call | flops 25165824 | bytes 50331 | tf_op jit(solution)/shard_map/mixing/pallas_call | solution.py:654
  53.9 6.7 %content_up.1 = (bf16[2,512,1536]{2,1,0:T(8,128)(2,1)S(1)}, bf16[2,512,1536]{2,1,0:T(8,128)(2,1)S(1)}, bf16[512,1536]{1,0:T(8,128)(2,1)S(1)}) custom-call(bf16[2,512,512]{2,1,0:T(8,128)(2,1)S(1)} %get-tuple-element.239.normed_ref, bf16[4,32,1536]{2,1,0:T(8,128)(2,1)S(1)} %stack.5.refs_0_, bf16[4,32,1536]{2,1,0:T(8,128)(2,1)S(1)} %collective-permute-done.12.refs_1_, ...), custom_call_target="tpu_custom_call" | custom-call | flops 25165824 | bytes 50331 | tf_op jit(solution)/shard_map/content_up/pallas_call | solution.py:654
  60.6 1.4 collective-permute-done.18.refs_1_
  61.9 1.7 %collective-permute-done.20.refs_3_ = bf16[4,32,1536]{2,1,0:T(8,128)(2,1)S(1)} collective-permute-done((bf16[4,32,1536]{2,1,0:T(8,128)(2,1)S(1)}, bf16[4,32,1536]{2,1,0:T(8,128)(2,1)S(1)}, u32[]{:S(2)}, u32[]{:S(2)}) %collective-permute-start.20) | collective-permute-done | bytes 393248 | tf_op jit(solution)/shard_map/ppermute | solution.py:668
  63.7 8.4 %content_down.1 = (bf16[2,512,1536]{2,1,0:T(8,128)(2,1)S(1)}, bf16[2,512,1536]{2,1,0:T(8,128)(2,1)S(1)}, bf16[2,512,1536]{2,1,0:T(8,128)(2,1)S(1)}, f32[512,128]...) custom-call(s32[8,5]{1,0:T(8,128)S(1)} %copy-done, ...), custom_call_target="tpu_custom_call" | custom-call | flops 25165824 | bytes 50331 | tf_op jit(solution)/shard_map/content_down/pallas_call | solution.py:654
  72.2 1.9 %content_sum.1 = (bf16[2,4,16,1536]{3,2,1,0:T(8,128)(2,1)S(1)}, bf16[2,4,16,1536]{3,2,1,0:T(8,128)(2,1)S(1)}, bf16[2,2,4,16,1536]{4,3,2,1,0:T(8,128)(2,1)S(1)}) custom-call(bf16[2,512,512]{2,1,0:T(8,128)(2,1)S(1)} %get-tuple-element.239.normed_ref, bf16[2,512,1536]{2,1,0:T(8,128)(2,1)S(1)} %get-tuple-element.230.grad_ref.content_grad_ref), custom_call_target="tpu_custom_call" | custom-call | flops 25165824 | bytes 50331 | tf_op jit(solution)/shard_map/content_sum/pallas_call | solution.py:654
  74.7 0.6 collective-permute-start.23
  75.3 2.5 %spatial_sum.1.square_ref = f32[512,512]{1,0:T(8,128)S(1)} custom-call(s32[8,5]{1,0:T(8,128)S(1)} %copy-done, bf16[2,512,1536]{2,1,0:T(8,128)(2,1)S(1)} %get-tuple-element.241.grad_mixed_ref, bf16[2,512,1536]{2,1,0:T(8,128)(2,1)S(1)} %get-tuple-element.218.gate_ref), custom_call_target="tpu_custom_call" | custom-call | flops 25165824 | bytes 50331 | tf_op jit(solution)/shard_map/spatial_sum/pallas_call | solution.py:654
  77.9 0.6 collective-permute-start.24
  78.5 6.7 %gate_back.1 = (bf16[2,512,1536]{2,1,0:T(8,128)(2,1)S(1)}, f32[8,16,128]{2,1,0:T(8,128)S(1)}) custom-call(s32[8,5]{1,0:T(8,128)S(1)} %copy-done, bf16[2,512,1536]{2,1,0:T(8,128)(2,1)S(1)} %get-tuple-element.241.grad_mixed_ref, bf16[2,512,1536]{2,1,0:T(8,128)(2,1)S(1)} %get-tuple-element.218.gate_ref, bf16[2,512,1536]{2,1,0:T(8,128)(2,1)S(1)} %get-tuple-element.242.slope_ref, ...), custom_call_target="tpu_custom_call" | custom-call | flops 25165824 | bytes 50331 | tf_op jit(solution)/shard_map/gate_back/pallas_call | solution.py:654
  85.2 0.7 collective-permute-done.23.refs_5_.refs_8_
  85.9 2.0 %gate_sum.1 = (bf16[2,4,16,1024]{3,2,1,0:T(8,128)(2,1)S(1)}, bf16[2,4,16,1024]{3,2,1,0:T(8,128)(2,1)S(1)}, bf16[2,2,4,16,1024]{4,3,2,1,0:T(8,128)(2,1)S(1)}, bf1...) custom-call(bf16[2,512,512]{2,1,0:T(8,128)(2,1)S(1)} %get-tuple-elem, ...), custom_call_target="tpu_custom_call" | custom-call | flops 25165824 | bytes 50331 | tf_op jit(solution)/shard_map/gate_sum/pallas_call | solution.py:654
  87.9 0.9 collective-permute-done.24.refs_2_
  88.8 0.5 collective-permute-start.25
  89.5 1.9 %layer.1 = (bf16[2,128,512]{2,1,0:T(8,128)(2,1)S(1)}, bf16[2,128,512]{2,1,0:T(8,128)(2,1)S(1)}, bf16[2,2,128,512]{3,2,1,0:T(8,128)(2,1)S(1)}) custom-call(bf16[2,512,1536]{2,1,0:T(8,128)(2,1)S(1)} %get-tuple-element.260.gated_ref, bf16[1536,512]{1,0:T(8,128)(2,1)S(1)} %get-tuple-element.261.shrink), custom_call_target="tpu_custom_call" | custom-call | flops 25165824 | bytes 50331 | tf_op jit(solution)/shard_map/layer/pallas_call | solution.py:654
  91.7 1.6 %collective-permute-start.28 = (bf16[2,4,16,1152]{3,2,1,0:T(8,128)(2,1)S(1)}, bf16[2,4,16,1152]{3,2,1,0:T(8,128)(2,1)S(1)}, u32[]{:S(2)}, u32[]{:S(2)}) collective-permute-start(bf16[2,4,16,1152]{3,2,1,0:T(8,128)(2,1)S(1)} %fusion.2), channel_id=1, source_target_pairs={{0,2},{1,3},{2,0},{3,1},{4,6},{5,7},{6,4},{7,5},{8,10},{9,11},{10,... | collective-permute-start | bytes 884744 | tf_op jit(solution)/shard_map/ppermute | solution.py:668
  93.3 0.7 collective-permute-start.27
  94.5 1.4 collective-permute-start.30
  95.9 3.9 %back.1 = (bf16[2,128,512]{2,1,0:T(8,128)(2,1)S(1)}, bf16[2,2,128,512]{3,2,1,0:T(8,128)(2,1)S(1)}, bf16[2,2,2,128,512]{4,3,2,1,0:T(8,128)(2,1)S(1)}) custom-call(bf16[2,512,1536]{2,1,0:T(8,128)(2,1)S(1)} %get-tuple-element.267.grad_ref.gate_grad_ref, bf16[2,512,1536]{2,1,0:T(8,128)(2,1)S(1)} %get-tuple-element.230.grad_ref.content_grad_ref, ...), custom_call_target="tpu_custom_call" | custom-call | flops 25165824 | bytes 50331 | tf_op jit(solution)/shard_map/back/pallas_call | solution.py:654
  99.8 5.2 %collective-permute-done.29.refs_12_ = bf16[4,16,1536]{2,1,0:T(8,128)(2,1)S(1)} collective-permute-done((bf16[4,16,1536]{2,1,0:T(8,128)(2,1)S(1)}, bf16[4,16,1536]{2,1,0:T(8,128)(2,1)S(1)}, u32[]{:S(2)}, u32[]{:S(2)}) %collective-permute-start.29) | collective-permute-done | bytes 196640 | tf_op jit(solution)/shard_map/ppermute | solution.py:668
  105.0 0.7 collective-permute-done.30.refs_14_
  105.8 0.7 collective-permute-start.32
  106.4 0.9 collective-permute-start.31
  107.3 4.1 %collective-permute-done.31.refs_13_ = bf16[4,16,1024]{2,1,0:T(8,128)(2,1)S(1)} collective-permute-done((bf16[4,16,1024]{2,1,0:T(8,128)(2,1)S(1)}, bf16[4,16,1024]{2,1,0:T(8,128)(2,1)S(1)}, u32[]{:S(2)}, u32[]{:S(2)}) %collective-permute-start.31) | collective-permute-done | bytes 131104 | tf_op jit(solution)/shard_map/ppermute | solution.py:668
  111.8 0.9 collective-permute-start.42
  112.7 1.0 collective-permute-start.34
  113.7 1.5 %collective-permute-start.35 = (bf16[16,5248]{1,0:T(8,128)(2,1)S(1)}, bf16[16,5248]{1,0:T(8,128)(2,1)S(1)}, u32[]{:S(2)}, u32[]{:S(2)}) collective-permute-start(bf16[16,5248]{1,0:T(8,128)(2,1)S(1)} %get-tuple-element.285), channel_id=1, source_target_pairs={{0,24},{4,28},{8,16},{12,20},{16,8},{20,12},{24,0},{28,4},{1,25},{... | collective-permute-start | bytes 503816 | tf_op jit(solution)/shard_map/ppermute | solution.py:668
  115.2 1.0 collective-permute-start.33
  116.2 3.2 %fetch.1 = (f32[64,3072]{1,0:T(8,128)S(1)}, f32[64,3072]{1,0:T(8,128)S(1)}, f32[64,3072]{1,0:T(8,128)S(1)}, f32[64,3072]{1,0:T(8,128)S(1)}, f32[192,512]{1,0:T(8...) custom-call(f32[64,3072]{1,0:T(8,128)} %refs_0_, ...), custom_call_target="tpu_custom_call" | custom-call | flops 25165824 | bytes 50331 | tf_op jit(solution)/shard_map/fetch/pallas_call | solution.py:654
  119.4 5.4 %collective-permute-done.34.two_ref = bf16[16,5248]{1,0:T(8,128)(2,1)S(1)} collective-permute-done((bf16[16,5248]{1,0:T(8,128)(2,1)S(1)}, bf16[16,5248]{1,0:T(8,128)(2,1)S(1)}, u32[]{:S(2)}, u32[]{:S(2)}) %collective-permute-start.34) | collective-permute-done | bytes 167968 | tf_op jit(solution)/shard_map/ppermute | solution.py:668
  124.8 1.2 collective-permute-done.33.one_ref
  126.3 0.6 collective-permute-start.41
  127.1 1.2 collective-permute-done.36.refs_1_
  128.3 1.7 %collective-permute-start.37 = (f32[8,128]{1,0:T(8,128)S(1)}, f32[8,128]{1,0:T(8,128)S(1)}, u32[]{:S(2)}, u32[]{:S(2)}) collective-permute-start(f32[8,128]{1,0:T(8,128)S(1)} %add.32.refs_0_), channel_id=1, source_target_pairs={{0,4},{4,0},{8,12},{12,8},{16,20},{20,16},{24,28},{28,24},{1,5},{5... | collective-permute-start | bytes 12296 | tf_op jit(solution)/shard_map/ppermute | solution.py:668
  130.0 1.9 %collective-permute-done.37.refs_1_ = f32[8,128]{1,0:T(8,128)S(1)} collective-permute-done((f32[8,128]{1,0:T(8,128)S(1)}, f32[8,128]{1,0:T(8,128)S(1)}, u32[]{:S(2)}, u32[]{:S(2)}) %collective-permute-start.37) | collective-permute-done | bytes 4128 | tf_op jit(solution)/shard_map/ppermute | solution.py:668
  131.9 2.1 %collective-permute-start.40 = (f32[8,128]{1,0:T(8,128)S(1)}, f32[8,128]{1,0:T(8,128)S(1)}, u32[]{:S(2)}, u32[]{:S(2)}) collective-permute-start(f32[8,128]{1,0:T(8,128)S(1)} %add.33.refs_0_), channel_id=1, source_target_pairs={{0,24},{4,28},{8,16},{12,20},{16,8},{20,12},{24,0},{28,4},{1,25},{... | collective-permute-start | bytes 12296 | tf_op jit(solution)/shard_map/ppermute | solution.py:668
  134.0 2.2 %collective-permute-start.39 = (f32[8,128]{1,0:T(8,128)S(1)}, f32[8,128]{1,0:T(8,128)S(1)}, u32[]{:S(2)}, u32[]{:S(2)}) collective-permute-start(f32[8,128]{1,0:T(8,128)S(1)} %add.33.refs_0_), channel_id=1, source_target_pairs={{0,16},{4,20},{8,24},{12,28},{16,0},{20,4},{24,8},{28,12},{1,17},{... | collective-permute-start | bytes 12296 | tf_op jit(solution)/shard_map/ppermute | solution.py:668
  136.3 1.0 collective-permute-done.40.refs_3_
  137.3 1.2 collective-permute-done.39.refs_2_
  138.5 1.3 collective-permute-done.38.refs_1_
  139.8 0.5 collective-permute-start.44
  140.5 1.5 collective-permute-start.43
  142.0 1.2 collective-permute-done.44.core_ref
  143.2 1.8 %give.1 = (f32[8,128,512]{2,1,0:T(8,128)}, bf16[8,128,512]{2,1,0:T(8,128)(2,1)}) custom-call(bf16[8,128,512]{2,1,0:T(8,128)(2,1)S(1)} %get-tuple-element.312.cots_ref, bf16[8,128,512]{2,1,0:T(8,128)(2,1)S(1)} %get-tuple-element.313.acts_ref, bf16[2,128,512]{2,1,0:T(8,128)(2,1)S(1)} %get-tuple-element.314.grad_own, ...), custom_call_target="tpu_custom_call" | custom-call | flops 25165824 | bytes 50331 | tf_op jit(solution)/shard_map/give/pallas_call | solution.py:654
  145.1 3.7 %adam.1 = (f32[64,3072]{1,0:T(8,128)}, f32[64,3072]{1,0:T(8,128)}, f32[64,3072]{1,0:T(8,128)}, f32[64,3072]{1,0:T(8,128)}, f32[64,3072]{1,0:T(8,128)}, /*index=5...) custom-call(f32[8,128]{1,0:T(8,128)S(1)} %add.35.message_ref, ...), custom_call_target="tpu_custom_call" | custom-call | flops 25165824 | bytes 50331 | tf_op jit(solution)/shard_map/adam/pallas_call | solution.py:654
  (80 shorter events, 4.3 us)
Async XLA Ops:
  3.1 30.9 %collective-permute-start.7 = (bf16[2,2,2,128,512]{4,3,2,1,0:T(8,128)(2,1)S(1)}, bf16[2,2,2,128,512]{4,3,2,1,0:T(8,128)(2,1)S(1)}, u32[]{:S(2)}, u32[]{:S(2)}) collective-permute-start(bf16[2,2,2,128,512]{4,3,2,1,0:T(8,128)(2,1)S(1)} %get-tuple-element.198), channel_id=1, source_target_pairs={{0,2},{1,3},{2,0},{3,1},{4,6},{5,7},{6,4},{7,5},{8,10},{9,11},{10,... | collective-permute-start | bytes 3145736 | tf_op jit(solution)/shard_map/ppermute | solution.py:668
  6.1 16.1 %collective-permute-start.3 = (bf16[2,2,128,512]{3,2,1,0:T(8,128)(2,1)S(1)}, bf16[2,2,128,512]{3,2,1,0:T(8,128)(2,1)S(1)}, u32[]{:S(2)}, u32[]{:S(2)}) collective-permute-start(bf16[2,2,128,512]{3,2,1,0:T(8,128)(2,1)S(1)} %get-tuple-element.197), channel_id=1, source_target_pairs={{0,1},{1,0},{2,3},{3,2},{4,5},{5,4},{6,7},{7,6},{8,9},{9,8},{10,11... | collective-permute-start | bytes 1572872 | tf_op jit(solution)/shard_map/ppermute | solution.py:668
  6.1 8.4 %collective-permute-start.2 = (bf16[32,2176]{1,0:T(8,128)(2,1)S(1)}, bf16[32,2176]{1,0:T(8,128)(2,1)S(1)}, u32[]{:S(2)}, u32[]{:S(2)}) collective-permute-start(bf16[32,2176]{1,0:T(8,128)(2,1)S(1)} %pack_first.1.refs_0_), channel_id=1, source_target_pairs={{0,24},{4,28},{8,16},{12,20},{16,8},{20,12},{24,0},{28,4},{1,25},{... | collective-permute-start | bytes 417800 | tf_op jit(solution)/shard_map/ppermute | solution.py:668
  9.7 12.4 %collective-permute-start.1 = (bf16[32,2176]{1,0:T(8,128)(2,1)S(1)}, bf16[32,2176]{1,0:T(8,128)(2,1)S(1)}, u32[]{:S(2)}, u32[]{:S(2)}) collective-permute-start(bf16[32,2176]{1,0:T(8,128)(2,1)S(1)} %pack_first.1.refs_0_), channel_id=1, source_target_pairs={{0,16},{4,20},{8,24},{12,28},{16,0},{20,4},{24,8},{28,12},{1,17},{... | collective-permute-start | bytes 417800 | tf_op jit(solution)/shard_map/ppermute | solution.py:668
  9.7 12.4 %collective-permute-start = (bf16[32,2176]{1,0:T(8,128)(2,1)S(1)}, bf16[32,2176]{1,0:T(8,128)(2,1)S(1)}, u32[]{:S(2)}, u32[]{:S(2)}) collective-permute-start(bf16[32,2176]{1,0:T(8,128)(2,1)S(1)} %pack_first.1.refs_0_), channel_id=1, source_target_pairs={{0,8},{4,12},{8,0},{12,4},{16,24},{20,28},{24,16},{28,20},{1,9},{5... | collective-permute-start | bytes 417800 | tf_op jit(solution)/shard_map/ppermute | solution.py:668
  22.2 14.3 %collective-permute-start.11 = (bf16[4,32,2176]{2,1,0:T(8,128)(2,1)S(1)}, bf16[4,32,2176]{2,1,0:T(8,128)(2,1)S(1)}, u32[]{:S(2)}, u32[]{:S(2)}) collective-permute-start(bf16[4,32,2176]{2,1,0:T(8,128)(2,1)S(1)} %stack.4.refs_0_.refs_4_), channel_id=1, source_target_pairs={{0,4},{4,0},{8,12},{12,8},{16,20},{20,16},{24,28},{28,24},{1,5},{5... | collective-permute-start | bytes 1671176 | tf_op jit(solution)/shard_map/ppermute | solution.py:668
  23.8 7.6 %collective-permute-start.6 = (bf16[32,1536]{1,0:T(8,128)(2,1)S(1)}, bf16[32,1536]{1,0:T(8,128)(2,1)S(1)}, u32[]{:S(2)}, u32[]{:S(2)}) collective-permute-start(bf16[32,1536]{1,0:T(8,128)(2,1)S(1)} %get-tuple-element.204.refs_0_), channel_id=1, source_target_pairs={{0,24},{4,28},{8,16},{12,20},{16,8},{20,12},{24,0},{28,4},{1,25},{... | collective-permute-start | bytes 294920 | tf_op jit(solution)/shard_map/ppermute | solution.py:668
  26.3 7.7 %collective-permute-start.5 = (bf16[32,1536]{1,0:T(8,128)(2,1)S(1)}, bf16[32,1536]{1,0:T(8,128)(2,1)S(1)}, u32[]{:S(2)}, u32[]{:S(2)}) collective-permute-start(bf16[32,1536]{1,0:T(8,128)(2,1)S(1)} %get-tuple-element.204.refs_0_), channel_id=1, source_target_pairs={{0,16},{4,20},{8,24},{12,28},{16,0},{20,4},{24,8},{28,12},{1,17},{... | collective-permute-start | bytes 294920 | tf_op jit(solution)/shard_map/ppermute | solution.py:668
  26.3 7.7 %collective-permute-start.4 = (bf16[32,1536]{1,0:T(8,128)(2,1)S(1)}, bf16[32,1536]{1,0:T(8,128)(2,1)S(1)}, u32[]{:S(2)}, u32[]{:S(2)}) collective-permute-start(bf16[32,1536]{1,0:T(8,128)(2,1)S(1)} %get-tuple-element.204.refs_0_), channel_id=1, source_target_pairs={{0,8},{4,12},{8,0},{12,4},{16,24},{20,28},{24,16},{28,20},{1,9},{5... | collective-permute-start | bytes 294920 | tf_op jit(solution)/shard_map/ppermute | solution.py:668
  34.0 8.5 %collective-permute-start.13 = (bf16[2,2,2,128,512]{4,3,2,1,0:T(8,128)(2,1)S(1)}, bf16[2,2,2,128,512]{4,3,2,1,0:T(8,128)(2,1)S(1)}, u32[]{:S(2)}, u32[]{:S(2)}) collective-permute-start(bf16[2,2,2,128,512]{4,3,2,1,0:T(8,128)(2,1)S(1)} %collective-permute-done.7.side_ref), channel_id=1, source_target_pairs={{0,1},{1,0},{2,3},{3,2},{4,5},{5,4},{6,7},{7,6},{8,9},{9,8},{10,11... | collective-permute-start | bytes 3145736 | tf_op jit(solution)/shard_map/ppermute | solution.py:668
  34.1 6.5 %collective-permute-start.14 = (bf16[4,32,2176]{2,1,0:T(8,128)(2,1)S(1)}, bf16[4,32,2176]{2,1,0:T(8,128)(2,1)S(1)}, u32[]{:S(2)}, u32[]{:S(2)}) collective-permute-start(bf16[4,32,2176]{2,1,0:T(8,128)(2,1)S(1)} %stack.4.refs_0_.refs_4_), channel_id=1, source_target_pairs={{0,1},{1,0},{2,3},{3,2},{4,5},{5,4},{6,7},{7,6},{8,9},{9,8},{10,11... | collective-permute-start | bytes 1671176 | tf_op jit(solution)/shard_map/ppermute | solution.py:668
  36.5 4.0 %collective-permute-start.15 = (bf16[4,32,2176]{2,1,0:T(8,128)(2,1)S(1)}, bf16[4,32,2176]{2,1,0:T(8,128)(2,1)S(1)}, u32[]{:S(2)}, u32[]{:S(2)}) collective-permute-start(bf16[4,32,2176]{2,1,0:T(8,128)(2,1)S(1)} %collective-permute-done.11.refs_1_.refs_5_), channel_id=1, source_target_pairs={{0,1},{1,0},{2,3},{3,2},{4,5},{5,4},{6,7},{7,6},{8,9},{9,8},{10,11... | collective-permute-start | bytes 1671176 | tf_op jit(solution)/shard_map/ppermute | solution.py:668
  36.6 13.6 %collective-permute-start.12 = (bf16[4,32,1536]{2,1,0:T(8,128)(2,1)S(1)}, bf16[4,32,1536]{2,1,0:T(8,128)(2,1)S(1)}, u32[]{:S(2)}, u32[]{:S(2)}) collective-permute-start(bf16[4,32,1536]{2,1,0:T(8,128)(2,1)S(1)} %stack.5.refs_0_), channel_id=1, source_target_pairs={{0,4},{4,0},{8,12},{12,8},{16,20},{20,16},{24,28},{28,24},{1,5},{5... | collective-permute-start | bytes 1179656 | tf_op jit(solution)/shard_map/ppermute | solution.py:668
  38.0 13.3 %copy-start = (s32[8,5]{1,0:T(8,128)S(1)}, s32[8,5]{1,0:T(8,128)}, u32[]{:S(2)}) copy-start(s32[8,5]{1,0:T(8,128)} %lens_ref.7) | copy-start | bytes 484
  38.0 12.1 %collective-permute-start.10 = (bf16[32,1536]{1,0:T(8,128)(2,1)S(1)}, bf16[32,1536]{1,0:T(8,128)(2,1)S(1)}, u32[]{:S(2)}, u32[]{:S(2)}) collective-permute-start(bf16[32,1536]{1,0:T(8,128)(2,1)S(1)} %get-tuple-element.208.refs_0_), channel_id=1, source_target_pairs={{0,24},{4,28},{8,16},{12,20},{16,8},{20,12},{24,0},{28,4},{1,25},{... | collective-permute-start | bytes 294920 | tf_op jit(solution)/shard_map/ppermute | solution.py:668
  40.5 9.6 %collective-permute-start.9 = (bf16[32,1536]{1,0:T(8,128)(2,1)S(1)}, bf16[32,1536]{1,0:T(8,128)(2,1)S(1)}, u32[]{:S(2)}, u32[]{:S(2)}) collective-permute-start(bf16[32,1536]{1,0:T(8,128)(2,1)S(1)} %get-tuple-element.208.refs_0_), channel_id=1, source_target_pairs={{0,16},{4,20},{8,24},{12,28},{16,0},{20,4},{24,8},{28,12},{1,17},{... | collective-permute-start | bytes 294920 | tf_op jit(solution)/shard_map/ppermute | solution.py:668
  40.5 9.6 %collective-permute-start.8 = (bf16[32,1536]{1,0:T(8,128)(2,1)S(1)}, bf16[32,1536]{1,0:T(8,128)(2,1)S(1)}, u32[]{:S(2)}, u32[]{:S(2)}) collective-permute-start(bf16[32,1536]{1,0:T(8,128)(2,1)S(1)} %get-tuple-element.208.refs_0_), channel_id=1, source_target_pairs={{0,8},{4,12},{8,0},{12,4},{16,24},{20,28},{24,16},{28,20},{1,9},{5... | collective-permute-start | bytes 294920 | tf_op jit(solution)/shard_map/ppermute | solution.py:668
  50.2 3.7 %collective-permute-start.16 = (bf16[4,32,1536]{2,1,0:T(8,128)(2,1)S(1)}, bf16[4,32,1536]{2,1,0:T(8,128)(2,1)S(1)}, u32[]{:S(2)}, u32[]{:S(2)}) collective-permute-start(bf16[4,32,1536]{2,1,0:T(8,128)(2,1)S(1)} %collective-permute-done.12.refs_1_), channel_id=1, source_target_pairs={{0,1},{1,0},{2,3},{3,2},{4,5},{5,4},{6,7},{7,6},{8,9},{9,8},{10,11... | collective-permute-start | bytes 1179656 | tf_op jit(solution)/shard_map/ppermute | solution.py:668
  50.3 3.7 %collective-permute-start.17 = (bf16[4,32,1536]{2,1,0:T(8,128)(2,1)S(1)}, bf16[4,32,1536]{2,1,0:T(8,128)(2,1)S(1)}, u32[]{:S(2)}, u32[]{:S(2)}) collective-permute-start(bf16[4,32,1536]{2,1,0:T(8,128)(2,1)S(1)} %stack.5.refs_0_), channel_id=1, source_target_pairs={{0,1},{1,0},{2,3},{3,2},{4,5},{5,4},{6,7},{7,6},{8,9},{9,8},{10,11... | collective-permute-start | bytes 1179656 | tf_op jit(solution)/shard_map/ppermute | solution.py:668
  50.8 11.2 %collective-permute-start.18 = (bf16[4,32,1536]{2,1,0:T(8,128)(2,1)S(1)}, bf16[4,32,1536]{2,1,0:T(8,128)(2,1)S(1)}, u32[]{:S(2)}, u32[]{:S(2)}) collective-permute-start(bf16[4,32,1536]{2,1,0:T(8,128)(2,1)S(1)} %stack.6.refs_0_), channel_id=1, source_target_pairs={{0,4},{4,0},{8,12},{12,8},{16,20},{20,16},{24,28},{28,24},{1,5},{5... | collective-permute-start | bytes 1179656 | tf_op jit(solution)/shard_map/ppermute | solution.py:668
  51.4 10.6 %collective-permute-start.19 = (bf16[4,32,1536]{2,1,0:T(8,128)(2,1)S(1)}, bf16[4,32,1536]{2,1,0:T(8,128)(2,1)S(1)}, u32[]{:S(2)}, u32[]{:S(2)}) collective-permute-start(bf16[4,32,1536]{2,1,0:T(8,128)(2,1)S(1)} %stack.6.refs_0_), channel_id=1, source_target_pairs={{0,1},{1,0},{2,3},{3,2},{4,5},{5,4},{6,7},{7,6},{8,9},{9,8},{10,11... | collective-permute-start | bytes 1179656 | tf_op jit(solution)/shard_map/ppermute | solution.py:668
  61.9 1.7 %collective-permute-start.20 = (bf16[4,32,1536]{2,1,0:T(8,128)(2,1)S(1)}, bf16[4,32,1536]{2,1,0:T(8,128)(2,1)S(1)}, u32[]{:S(2)}, u32[]{:S(2)}) collective-permute-start(bf16[4,32,1536]{2,1,0:T(8,128)(2,1)S(1)} %collective-permute-done.18.refs_1_), channel_id=1, source_target_pairs={{0,1},{1,0},{2,3},{3,2},{4,5},{5,4},{6,7},{7,6},{8,9},{9,8},{10,11... | collective-permute-start | bytes 1179656 | tf_op jit(solution)/shard_map/ppermute | solution.py:668
  72.0 2.6 %collective-permute-start.21 = (bf16[2,2,4,16,1536]{4,3,2,1,0:T(8,128)(2,1)S(1)}, bf16[2,2,4,16,1536]{4,3,2,1,0:T(8,128)(2,1)S(1)}, u32[]{:S(2)}, u32[]{:S(2)}) collective-permute-start(bf16[2,2,4,16,1536]{4,3,2,1,0:T(8,128)(2,1)S(1)} %get-tuple-element.229), channel_id=1, source_target_pairs={{0,1},{1,0},{2,3},{3,2},{4,5},{5,4},{6,7},{7,6},{8,9},{9,8},{10,11... | collective-permute-start | bytes 2359304 | tf_op jit(solution)/shard_map/ppermute | solution.py:668
  74.2 3.6 %collective-permute-start.22 = (bf16[2,2,4,16,1536]{4,3,2,1,0:T(8,128)(2,1)S(1)}, bf16[2,2,4,16,1536]{4,3,2,1,0:T(8,128)(2,1)S(1)}, u32[]{:S(2)}, u32[]{:S(2)}) collective-permute-start(bf16[2,2,4,16,1536]{4,3,2,1,0:T(8,128)(2,1)S(1)} %get-tuple-element.233), channel_id=1, source_target_pairs={{0,1},{1,0},{2,3},{3,2},{4,5},{5,4},{6,7},{7,6},{8,9},{9,8},{10,11... | collective-permute-start | bytes 2359304 | tf_op jit(solution)/shard_map/ppermute | solution.py:668
  74.7 11.2 %collective-permute-start.23 = (bf16[2,4,16,1536]{3,2,1,0:T(8,128)(2,1)S(1)}, bf16[2,4,16,1536]{3,2,1,0:T(8,128)(2,1)S(1)}, u32[]{:S(2)}, u32[]{:S(2)}) collective-permute-start(bf16[2,4,16,1536]{3,2,1,0:T(8,128)(2,1)S(1)} %fusion.1), channel_id=1, source_target_pairs={{0,2},{1,3},{2,0},{3,1},{4,6},{5,7},{6,4},{7,5},{8,10},{9,11},{10,... | collective-permute-start | bytes 1179656 | tf_op jit(solution)/shard_map/ppermute | solution.py:668
  77.9 10.9 %collective-permute-start.24 = (bf16[2,4,16,1536]{3,2,1,0:T(8,128)(2,1)S(1)}, bf16[2,4,16,1536]{3,2,1,0:T(8,128)(2,1)S(1)}, u32[]{:S(2)}, u32[]{:S(2)}) collective-permute-start(bf16[2,4,16,1536]{3,2,1,0:T(8,128)(2,1)S(1)} %fusion), channel_id=1, source_target_pairs={{0,4},{4,0},{8,12},{12,8},{16,20},{20,16},{24,28},{28,24},{1,5},{5... | collective-permute-start | bytes 1179656 | tf_op jit(solution)/shard_map/ppermute | solution.py:668
  88.8 2.8 %collective-permute-start.26 = (bf16[2,2,4,16,1152]{4,3,2,1,0:T(8,128)(2,1)S(1)}, bf16[2,2,4,16,1152]{4,3,2,1,0:T(8,128)(2,1)S(1)}, u32[]{:S(2)}, u32[]{:S(2)}) collective-permute-start(bf16[2,2,4,16,1152]{4,3,2,1,0:T(8,128)(2,1)S(1)} %get-tuple-element.254), channel_id=1, source_target_pairs={{0,1},{1,0},{2,3},{3,2},{4,5},{5,4},{6,7},{7,6},{8,9},{9,8},{10,11... | collective-permute-start | bytes 1769480 | tf_op jit(solution)/shard_map/ppermute | solution.py:668
  88.8 2.8 %collective-permute-start.25 = (bf16[2,2,4,16,1024]{4,3,2,1,0:T(8,128)(2,1)S(1)}, bf16[2,2,4,16,1024]{4,3,2,1,0:T(8,128)(2,1)S(1)}, u32[]{:S(2)}, u32[]{:S(2)}) collective-permute-start(bf16[2,2,4,16,1024]{4,3,2,1,0:T(8,128)(2,1)S(1)} %get-tuple-element.253), channel_id=1, source_target_pairs={{0,1},{1,0},{2,3},{3,2},{4,5},{5,4},{6,7},{7,6},{8,9},{9,8},{10,11... | collective-permute-start | bytes 1572872 | tf_op jit(solution)/shard_map/ppermute | solution.py:668
  91.7 14.0 %collective-permute-start.28 = (bf16[2,4,16,1152]{3,2,1,0:T(8,128)(2,1)S(1)}, bf16[2,4,16,1152]{3,2,1,0:T(8,128)(2,1)S(1)}, u32[]{:S(2)}, u32[]{:S(2)}) collective-permute-start(bf16[2,4,16,1152]{3,2,1,0:T(8,128)(2,1)S(1)} %fusion.2), channel_id=1, source_target_pairs={{0,2},{1,3},{2,0},{3,1},{4,6},{5,7},{6,4},{7,5},{8,10},{9,11},{10,... | collective-permute-start | bytes 884744 | tf_op jit(solution)/shard_map/ppermute | solution.py:668
  93.3 12.3 %collective-permute-start.27 = (bf16[2,4,16,1024]{3,2,1,0:T(8,128)(2,1)S(1)}, bf16[2,4,16,1024]{3,2,1,0:T(8,128)(2,1)S(1)}, u32[]{:S(2)}, u32[]{:S(2)}) collective-permute-start(bf16[2,4,16,1024]{3,2,1,0:T(8,128)(2,1)S(1)} %fusion.3), channel_id=1, source_target_pairs={{0,4},{4,0},{8,12},{12,8},{16,20},{20,16},{24,28},{28,24},{1,5},{5... | collective-permute-start | bytes 786440 | tf_op jit(solution)/shard_map/ppermute | solution.py:668
  94.0 11.0 %collective-permute-start.29 = (bf16[4,16,1536]{2,1,0:T(8,128)(2,1)S(1)}, bf16[4,16,1536]{2,1,0:T(8,128)(2,1)S(1)}, u32[]{:S(2)}, u32[]{:S(2)}) collective-permute-start(bf16[4,16,1536]{2,1,0:T(8,128)(2,1)S(1)} %get-tuple-element.258), channel_id=1, source_target_pairs={{0,2},{1,3},{2,0},{3,1},{4,6},{5,7},{6,4},{7,5},{8,10},{9,11},{10,... | collective-permute-start | bytes 589832 | tf_op jit(solution)/shard_map/ppermute | solution.py:668
  94.5 11.2 %collective-permute-start.30 = (bf16[4,16,1536]{2,1,0:T(8,128)(2,1)S(1)}, bf16[4,16,1536]{2,1,0:T(8,128)(2,1)S(1)}, u32[]{:S(2)}, u32[]{:S(2)}) collective-permute-start(bf16[4,16,1536]{2,1,0:T(8,128)(2,1)S(1)} %get-tuple-element.259), channel_id=1, source_target_pairs={{0,4},{4,0},{8,12},{12,8},{16,20},{20,16},{24,28},{28,24},{1,5},{5... | collective-permute-start | bytes 589832 | tf_op jit(solution)/shard_map/ppermute | solution.py:668
  105.8 5.6 %collective-permute-start.32 = (bf16[4,16,1152]{2,1,0:T(8,128)(2,1)S(1)}, bf16[4,16,1152]{2,1,0:T(8,128)(2,1)S(1)}, u32[]{:S(2)}, u32[]{:S(2)}) collective-permute-start(bf16[4,16,1152]{2,1,0:T(8,128)(2,1)S(1)} %get-tuple-element.281), channel_id=1, source_target_pairs={{0,4},{4,0},{8,12},{12,8},{16,20},{20,16},{24,28},{28,24},{1,5},{5... | collective-permute-start | bytes 442376 | tf_op jit(solution)/shard_map/ppermute | solution.py:668
  106.4 5.0 %collective-permute-start.31 = (bf16[4,16,1024]{2,1,0:T(8,128)(2,1)S(1)}, bf16[4,16,1024]{2,1,0:T(8,128)(2,1)S(1)}, u32[]{:S(2)}, u32[]{:S(2)}) collective-permute-start(bf16[4,16,1024]{2,1,0:T(8,128)(2,1)S(1)} %get-tuple-element.279), channel_id=1, source_target_pairs={{0,2},{1,3},{2,0},{3,1},{4,6},{5,7},{6,4},{7,5},{8,10},{9,11},{10,... | collective-permute-start | bytes 393224 | tf_op jit(solution)/shard_map/ppermute | solution.py:668
  111.8 28.0 %collective-permute-start.42 = (bf16[2,2,2,128,512]{4,3,2,1,0:T(8,128)(2,1)S(1)}, bf16[2,2,2,128,512]{4,3,2,1,0:T(8,128)(2,1)S(1)}, u32[]{:S(2)}, u32[]{:S(2)}) collective-permute-start(bf16[2,2,2,128,512]{4,3,2,1,0:T(8,128)(2,1)S(1)} %get-tuple-element.308), channel_id=1, source_target_pairs={{0,2},{1,3},{2,0},{3,1},{4,6},{5,7},{6,4},{7,5},{8,10},{9,11},{10,... | collective-permute-start | bytes 3145736 | tf_op jit(solution)/shard_map/ppermute | solution.py:668
  112.7 12.1 %collective-permute-start.34 = (bf16[16,5248]{1,0:T(8,128)(2,1)S(1)}, bf16[16,5248]{1,0:T(8,128)(2,1)S(1)}, u32[]{:S(2)}, u32[]{:S(2)}) collective-permute-start(bf16[16,5248]{1,0:T(8,128)(2,1)S(1)} %get-tuple-element.284), channel_id=1, source_target_pairs={{0,16},{4,20},{8,24},{12,28},{16,0},{20,4},{24,8},{28,12},{1,17},{... | collective-permute-start | bytes 503816 | tf_op jit(solution)/shard_map/ppermute | solution.py:668
  113.7 11.1 %collective-permute-start.35 = (bf16[16,5248]{1,0:T(8,128)(2,1)S(1)}, bf16[16,5248]{1,0:T(8,128)(2,1)S(1)}, u32[]{:S(2)}, u32[]{:S(2)}) collective-permute-start(bf16[16,5248]{1,0:T(8,128)(2,1)S(1)} %get-tuple-element.285), channel_id=1, source_target_pairs={{0,24},{4,28},{8,16},{12,20},{16,8},{20,12},{24,0},{28,4},{1,25},{... | collective-permute-start | bytes 503816 | tf_op jit(solution)/shard_map/ppermute | solution.py:668
  115.2 10.8 %collective-permute-start.33 = (bf16[16,5248]{1,0:T(8,128)(2,1)S(1)}, bf16[16,5248]{1,0:T(8,128)(2,1)S(1)}, u32[]{:S(2)}, u32[]{:S(2)}) collective-permute-start(bf16[16,5248]{1,0:T(8,128)(2,1)S(1)} %get-tuple-element.283), channel_id=1, source_target_pairs={{0,8},{4,12},{8,0},{12,4},{16,24},{20,28},{24,16},{28,20},{1,9},{5... | collective-permute-start | bytes 503816 | tf_op jit(solution)/shard_map/ppermute | solution.py:668
  126.3 13.4 %collective-permute-start.41 = (bf16[16,5248]{1,0:T(8,128)(2,1)S(1)}, bf16[16,5248]{1,0:T(8,128)(2,1)S(1)}, u32[]{:S(2)}, u32[]{:S(2)}) collective-permute-start(bf16[16,5248]{1,0:T(8,128)(2,1)S(1)} %get-tuple-element.306.refs_0_.own_ref), channel_id=1, source_target_pairs={{0,2},{1,3},{2,0},{3,1},{4,6},{5,7},{6,4},{7,5},{8,10},{9,11},{10,... | collective-permute-start | bytes 503816 | tf_op jit(solution)/shard_map/ppermute | solution.py:668
  127.0 18.1 %copy-start.1 = (f32[256]{0:T(256)S(1)}, f32[256]{0:T(256)}, u32[]{:S(2)}) copy-start(f32[256]{0:T(256)} %param.38) | copy-start | bytes 3076
  127.0 18.1 %copy-start.2 = (f32[64]{0:T(128)S(1)}, f32[64]{0:T(128)}, u32[]{:S(2)}) copy-start(f32[64]{0:T(128)} %param.42) | copy-start | bytes 772
  127.0 18.1 %copy-start.3 = (f32[256]{0:T(256)S(1)}, f32[256]{0:T(256)}, u32[]{:S(2)}) copy-start(f32[256]{0:T(256)} %param.39) | copy-start | bytes 3076
  127.0 18.1 %copy-start.4 = (f32[256]{0:T(256)S(1)}, f32[256]{0:T(256)}, u32[]{:S(2)}) copy-start(f32[256]{0:T(256)} %param.40) | copy-start | bytes 3076
  127.0 18.1 %copy-start.5 = (f32[256]{0:T(256)S(1)}, f32[256]{0:T(256)}, u32[]{:S(2)}) copy-start(f32[256]{0:T(256)} %param.41) | copy-start | bytes 3076
  127.0 18.1 %copy-start.6 = (f32[64]{0:T(128)S(1)}, f32[64]{0:T(128)}, u32[]{:S(2)}) copy-start(f32[64]{0:T(128)} %param.43) | copy-start | bytes 772
  127.0 18.1 %copy-start.7 = (f32[64]{0:T(128)S(1)}, f32[64]{0:T(128)}, u32[]{:S(2)}) copy-start(f32[64]{0:T(128)} %param.44) | copy-start | bytes 772
  127.0 18.1 %copy-start.8 = (f32[64]{0:T(128)S(1)}, f32[64]{0:T(128)}, u32[]{:S(2)}) copy-start(f32[64]{0:T(128)} %param.45) | copy-start | bytes 772
  127.0 1.2 collective-permute-start.36
  128.3 3.6 %collective-permute-start.37 = (f32[8,128]{1,0:T(8,128)S(1)}, f32[8,128]{1,0:T(8,128)S(1)}, u32[]{:S(2)}, u32[]{:S(2)}) collective-permute-start(f32[8,128]{1,0:T(8,128)S(1)} %add.32.refs_0_), channel_id=1, source_target_pairs={{0,4},{4,0},{8,12},{12,8},{16,20},{20,16},{24,28},{28,24},{1,5},{5... | collective-permute-start | bytes 12296 | tf_op jit(solution)/shard_map/ppermute | solution.py:668
  131.9 5.4 %collective-permute-start.40 = (f32[8,128]{1,0:T(8,128)S(1)}, f32[8,128]{1,0:T(8,128)S(1)}, u32[]{:S(2)}, u32[]{:S(2)}) collective-permute-start(f32[8,128]{1,0:T(8,128)S(1)} %add.33.refs_0_), channel_id=1, source_target_pairs={{0,24},{4,28},{8,16},{12,20},{16,8},{20,12},{24,0},{28,4},{1,25},{... | collective-permute-start | bytes 12296 | tf_op jit(solution)/shard_map/ppermute | solution.py:668
  134.0 4.5 %collective-permute-start.39 = (f32[8,128]{1,0:T(8,128)S(1)}, f32[8,128]{1,0:T(8,128)S(1)}, u32[]{:S(2)}, u32[]{:S(2)}) collective-permute-start(f32[8,128]{1,0:T(8,128)S(1)} %add.33.refs_0_), channel_id=1, source_target_pairs={{0,16},{4,20},{8,24},{12,28},{16,0},{20,4},{24,8},{28,12},{1,17},{... | collective-permute-start | bytes 12296 | tf_op jit(solution)/shard_map/ppermute | solution.py:668
  136.2 3.6 %collective-permute-start.38 = (f32[8,128]{1,0:T(8,128)S(1)}, f32[8,128]{1,0:T(8,128)S(1)}, u32[]{:S(2)}, u32[]{:S(2)}) collective-permute-start(f32[8,128]{1,0:T(8,128)S(1)} %add.33.refs_0_), channel_id=1, source_target_pairs={{0,8},{4,12},{8,0},{12,4},{16,24},{20,28},{24,16},{28,20},{1,9},{5... | collective-permute-start | bytes 12296 | tf_op jit(solution)/shard_map/ppermute | solution.py:668
  139.8 3.4 %collective-permute-start.45 = (bf16[2,2,2,128,512]{4,3,2,1,0:T(8,128)(2,1)S(1)}, bf16[2,2,2,128,512]{4,3,2,1,0:T(8,128)(2,1)S(1)}, u32[]{:S(2)}, u32[]{:S(2)}) collective-permute-start(bf16[2,2,2,128,512]{4,3,2,1,0:T(8,128)(2,1)S(1)} %collective-permute-done.42.side_ref), channel_id=1, source_target_pairs={{0,1},{1,0},{2,3},{3,2},{4,5},{5,4},{6,7},{7,6},{8,9},{9,8},{10,11... | collective-permute-start | bytes 3145736 | tf_op jit(solution)/shard_map/ppermute | solution.py:668
  139.8 3.4 %collective-permute-start.44 = (bf16[2,2,128,512]{3,2,1,0:T(8,128)(2,1)S(1)}, bf16[2,2,128,512]{3,2,1,0:T(8,128)(2,1)S(1)}, u32[]{:S(2)}, u32[]{:S(2)}) collective-permute-start(bf16[2,2,128,512]{3,2,1,0:T(8,128)(2,1)S(1)} %get-tuple-element.317), channel_id=1, source_target_pairs={{0,1},{1,0},{2,3},{3,2},{4,5},{5,4},{6,7},{7,6},{8,9},{9,8},{10,11... | collective-permute-start | bytes 1572872 | tf_op jit(solution)/shard_map/ppermute | solution.py:668
  140.3 4.7 %collective-permute-start.46 = (bf16[2,16,5248]{2,1,0:T(8,128)(2,1)S(1)}, bf16[2,16,5248]{2,1,0:T(8,128)(2,1)S(1)}, u32[]{:S(2)}, u32[]{:S(2)}) collective-permute-start(bf16[2,16,5248]{2,1,0:T(8,128)(2,1)S(1)} %stack.7), channel_id=1, source_target_pairs={{0,1},{1,0},{2,3},{3,2},{4,5},{5,4},{6,7},{7,6},{8,9},{9,8},{10,11... | collective-permute-start | bytes 1007624 | tf_op jit(solution)/shard_map/ppermute | solution.py:668
  140.5 4.5 %collective-permute-start.43 = (f32[8,128]{1,0:T(8,128)S(1)}, f32[8,128]{1,0:T(8,128)S(1)}, u32[]{:S(2)}, u32[]{:S(2)}) collective-permute-start(f32[8,128]{1,0:T(8,128)S(1)} %add.34.refs_0_), channel_id=1, source_target_pairs={{0,2},{1,3},{2,0},{3,1},{4,6},{5,7},{6,4},{7,5},{8,10},{9,11},{10,... | collective-permute-start | bytes 12296 | tf_op jit(solution)/shard_map/ppermute | solution.py:668

commit v3 on v2

--- a/solution.py
+++ b/solution.py
@@ -310,7 +310,7 @@
 
 
 def content_down_kernel(
-    tree, count, members, lens_ref, content_ref, slope_ref, mixed_ref, own_ref, core_ref, side_ref, forward_ref, *refs
+    tree, count, members, lens_ref, content_ref, content_slope_ref, mixed_ref, own_ref, core_ref, side_ref, forward_ref, *refs
 ):
     parts = [core_ref.at[1], side_ref.at[0, 1], forward_ref.at[1, 1]]
     sources = refs[:count]
@@ -338,13 +338,12 @@
         grad_gated = dot(cots[...], shrink[channels, :], ((1,), (1,)))
         for p in range(0, tokens, CHUNK):
             r, here = p // ROW, slice(p % ROW, p % ROW + CHUNK)
-            grads = grad_gated[p : p + CHUNK]
-            content = content_ref[r, here, channels].astype(F32)
-            mixed = mixed_ref[r, here, channels].astype(F32)
-            slope = slope_ref[r, here, channels].astype(F32)
-            gated_ref[r, here, channels] = (content * mixed).astype(BF16)
-            grad_ref[r, here, channels] = (grads * mixed * slope).astype(BF16)
-            grad_mixed = (grads * content).astype(BF16)
+            grads = grad_gated[p : p + CHUNK].astype(BF16)
+            content = content_ref[r, here, channels]
+            mixed = mixed_ref[r, here, channels]
+            gated_ref[r, here, channels] = content * mixed
+            grad_ref[r, here, channels] = grads * (mixed * content_slope_ref[r, here, channels])
+            grad_mixed = grads * content
             grad_mixed_ref[r, here, channels] = grad_mixed
             total = grad_mixed.astype(F32)
             sums[p : p + CHUNK, :] += total[:, :LANES] + total[:, LANES:]
@@ -386,13 +385,15 @@
 
 def gate_back_kernel(
     lens_ref, grad_mixed_ref, gate_ref, slope_ref, rstd_ref, spatial_ref, gains_ref, bias_ref,
-    grad_ref, vectors_ref, turned, grad_gate, first_sums, second_sums, second, inverse,
+    grad_ref, vectors_ref, turned, grad_gate, first_sums, second_sums, second, inverse, gains_low, inverse_low,
 ):
     rows_here = grad_mixed_ref.shape[0]
     narrow = lax.axis_index("narrow")
     turned[...] = spatial_ref[...].T
     second[...] = jnp.zeros_like(second)
     inverse[...] = 1.0 / gains_ref[:, D:]
+    gains_low[...] = jnp.broadcast_to(gains_ref[0:1, D:], (BLOCK, HALF)).astype(BF16)
+    inverse_low[...] = jnp.broadcast_to(inverse[0:1, :], (BLOCK, HALF)).astype(BF16)
 
     def do_row(row, carry):
         same, _ = doc_mask(0, ROW, lens_ref, narrow * rows_here + row)
@@ -404,10 +405,9 @@
                 here = slice(p, p + CHUNK)
                 low = grads_all[here].astype(BF16)
                 grad_gate[here, c : c + WIDTH] = low
-                grads = low.astype(F32)
-                products = grads * gate_ref[row, here, c : c + WIDTH].astype(F32)
+                products = (low * gate_ref[row, here, c : c + WIDTH]).astype(F32)
                 vector = vector + jnp.sum(products.reshape(CHUNK // 8, 8, WIDTH), axis=0)
-                scaled = grads * gains_ref[0:1, D + c : D + c + WIDTH]
+                scaled = (low * gains_low[0:1, c : c + WIDTH]).astype(F32)
                 first = scaled[:, :LANES] + scaled[:, LANES:]
                 other = products[:, :LANES] + products[:, LANES:]
                 first_sums[here, :] = first if c == 0 else first_sums[here, :] + first
@@ -418,12 +418,13 @@
             scale = rstd_ref[row, here, 0:1]
             first_mean = jnp.sum(first_sums[here, :], axis=1, keepdims=True) * (1.0 / HALF) * scale
             second_mean = jnp.sum(second_sums[here, :], axis=1, keepdims=True) * (1.0 / HALF) * scale
+            wide_row = lambda value: jnp.broadcast_to(value, (CHUNK, LANES)).astype(BF16)
+            scale, first_mean, second_mean = wide_row(scale), wide_row(first_mean), wide_row(second_mean)
             for c in range(0, HALF, LANES):
                 place = slice(c, c + LANES)
-                scaled = grad_gate[here, place].astype(F32) * gains_ref[0:1, D + c : D + c + LANES] * scale
-                vhat = gate_ref[row, here, place].astype(F32) * inverse[0:1, place]
-                slope = slope_ref[row, here, place].astype(F32)
-                grad_ref[row, here, place] = ((scaled - first_mean - vhat * second_mean) * slope).astype(BF16)
+                scaled = grad_gate[here, place] * gains_low[0:1, place] * scale
+                vhat = gate_ref[row, here, place] * inverse_low[0:1, place]
+                grad_ref[row, here, place] = (scaled - first_mean - vhat * second_mean) * slope_ref[row, here, place]
         return carry
 
     lax.fori_loop(0, rows_here, do_row, 0)
@@ -681,8 +682,8 @@
     clipped = clip_scale * gradient
     moment = BETA_FIRST * momentum + (1.0 - BETA_FIRST) * clipped
     square = BETA_SECOND * variance + (1.0 - BETA_SECOND) * clipped * clipped
-    first_hat = moment / (1.0 - BETA_FIRST**STEP)
-    second_hat = square / (1.0 - BETA_SECOND**STEP)
+    first_hat = moment * (1.0 / (1.0 - BETA_FIRST**STEP))
+    second_hat = square * (1.0 / (1.0 - BETA_SECOND**STEP))
     updated = weight - step_rate * (
         first_hat / (jnp.sqrt(second_hat) + ADAM_EPS) + decay_rate * weight
     )
@@ -941,6 +942,8 @@
             pltpu.VMEM((ROW, 128), F32),
             pltpu.VMEM((8, HALF), F32),
             pltpu.VMEM((8, HALF), F32),
+            pltpu.VMEM((BLOCK, HALF), BF16),
+            pltpu.VMEM((BLOCK, HALF), BF16),
         ],
         product // 64,
     )

time: 149 us -> 149 us (level)
  no operation moved by 1% of the time
where the time goes in v3:
time: 149 us
  Pallas kernels  56.7 us (38%)
  waiting for transfers between devices  48 us (32%)
  starting transfers between devices  42.3 us (28%)
    pallas_call x28, Pallas kernels, call_kernel(): pl.pallas_call(kernel, name=name, in_specs=in_specs, out_specs=specs, out...  56.7 us
    ppermute x47, waiting for transfers between devices, swap_with(): return lax.ppermute(value, axis, [(i, i ^ bit) for i in range(size)])  48 us
    ppermute x47, starting transfers between devices, swap_with(): return lax.ppermute(value, axis, [(i, i ^ bit) for i in range(size)])  42.3 us
  transfers between devices with their start and end apart: 47, of which 21 were waited for; matrix products, arithmetic and copies ran while one was open for 0% of the time, Pallas kernels for 28%

profile of v3, /device:TPU:0, one launch (start us, length us, event | category | flops | bytes accessed | tf_op | source)
XLA Modules:
  0.0 148.7 jit_solution(11401528991854238934)
XLA Ops:
  0.7 1.0 pack_first.1.refs_0_
  1.7 1.4 cut.1
  3.1 3.0 %collective-permute-start.7 = (bf16[2,2,2,128,512]{4,3,2,1,0:T(8,128)(2,1)S(1)}, bf16[2,2,2,128,512]{4,3,2,1,0:T(8,128)(2,1)S(1)}, u32[]{:S(2)}, u32[]{:S(2)}) collective-permute-start(bf16[2,2,2,128,512]{4,3,2,1,0:T(8,128)(2,1)S(1)} %get-tuple-element.198), channel_id=1, source_target_pairs={{0,2},{1,3},{2,0},{3,1},{4,6},{5,7},{6,4},{7,5},{8,10},{9,11},{10,... | collective-permute-start | bytes 3145736 | tf_op jit(solution)/shard_map/ppermute | solution.py:669
  6.1 3.6 %collective-permute-start.2 = (bf16[32,2176]{1,0:T(8,128)(2,1)S(1)}, bf16[32,2176]{1,0:T(8,128)(2,1)S(1)}, u32[]{:S(2)}, u32[]{:S(2)}) collective-permute-start(bf16[32,2176]{1,0:T(8,128)(2,1)S(1)} %pack_first.1.refs_0_), channel_id=1, source_target_pairs={{0,24},{4,28},{8,16},{12,20},{16,8},{20,12},{24,0},{28,4},{1,25},{... | collective-permute-start | bytes 417800 | tf_op jit(solution)/shard_map/ppermute | solution.py:669
  9.7 0.8 collective-permute-start
  10.5 1.1 pack_second.1
  11.6 2.9 %collective-permute-done.2.refs_3_ = bf16[32,2176]{1,0:T(8,128)(2,1)S(1)} collective-permute-done((bf16[32,2176]{1,0:T(8,128)(2,1)S(1)}, bf16[32,2176]{1,0:T(8,128)(2,1)S(1)}, u32[]{:S(2)}, u32[]{:S(2)}) %collective-permute-start.2) | collective-permute-done | bytes 139296 | tf_op jit(solution)/shard_map/ppermute | solution.py:669
  14.5 7.7 %collective-permute-done.1.refs_2_ = bf16[32,2176]{1,0:T(8,128)(2,1)S(1)} collective-permute-done((bf16[32,2176]{1,0:T(8,128)(2,1)S(1)}, bf16[32,2176]{1,0:T(8,128)(2,1)S(1)}, u32[]{:S(2)}, u32[]{:S(2)}) %collective-permute-start.1) | collective-permute-done | bytes 139296 | tf_op jit(solution)/shard_map/ppermute | solution.py:669
  22.2 1.6 %collective-permute-start.11 = (bf16[4,32,2176]{2,1,0:T(8,128)(2,1)S(1)}, bf16[4,32,2176]{2,1,0:T(8,128)(2,1)S(1)}, u32[]{:S(2)}, u32[]{:S(2)}) collective-permute-start(bf16[4,32,2176]{2,1,0:T(8,128)(2,1)S(1)} %stack.4.refs_0_.refs_4_), channel_id=1, source_target_pairs={{0,4},{4,0},{8,12},{12,8},{16,20},{20,16},{24,28},{28,24},{1,5},{5... | collective-permute-start | bytes 1671176 | tf_op jit(solution)/shard_map/ppermute | solution.py:669
  23.8 2.5 %collective-permute-start.6 = (bf16[32,1536]{1,0:T(8,128)(2,1)S(1)}, bf16[32,1536]{1,0:T(8,128)(2,1)S(1)}, u32[]{:S(2)}, u32[]{:S(2)}) collective-permute-start(bf16[32,1536]{1,0:T(8,128)(2,1)S(1)} %get-tuple-element.204.refs_0_), channel_id=1, source_target_pairs={{0,24},{4,28},{8,16},{12,20},{16,8},{20,12},{24,0},{28,4},{1,25},{... | collective-permute-start | bytes 294920 | tf_op jit(solution)/shard_map/ppermute | solution.py:669
  26.3 1.9 %collective-permute-start.4 = (bf16[32,1536]{1,0:T(8,128)(2,1)S(1)}, bf16[32,1536]{1,0:T(8,128)(2,1)S(1)}, u32[]{:S(2)}, u32[]{:S(2)}) collective-permute-start(bf16[32,1536]{1,0:T(8,128)(2,1)S(1)} %get-tuple-element.204.refs_0_), channel_id=1, source_target_pairs={{0,8},{4,12},{8,0},{12,4},{16,24},{20,28},{24,16},{28,20},{1,9},{5... | collective-permute-start | bytes 294920 | tf_op jit(solution)/shard_map/ppermute | solution.py:669
  28.2 3.2 %collective-permute-done.6.refs_3_ = bf16[32,1536]{1,0:T(8,128)(2,1)S(1)} collective-permute-done((bf16[32,1536]{1,0:T(8,128)(2,1)S(1)}, bf16[32,1536]{1,0:T(8,128)(2,1)S(1)}, u32[]{:S(2)}, u32[]{:S(2)}) %collective-permute-start.6) | collective-permute-done | bytes 98336 | tf_op jit(solution)/shard_map/ppermute | solution.py:669
  31.4 2.6 %collective-permute-done.5.refs_2_ = bf16[32,1536]{1,0:T(8,128)(2,1)S(1)} collective-permute-done((bf16[32,1536]{1,0:T(8,128)(2,1)S(1)}, bf16[32,1536]{1,0:T(8,128)(2,1)S(1)}, u32[]{:S(2)}, u32[]{:S(2)}) %collective-permute-start.5) | collective-permute-done | bytes 98336 | tf_op jit(solution)/shard_map/ppermute | solution.py:669
  34.6 2.0 %collective-permute-done.11.refs_1_.refs_5_ = bf16[4,32,2176]{2,1,0:T(8,128)(2,1)S(1)} collective-permute-done((bf16[4,32,2176]{2,1,0:T(8,128)(2,1)S(1)}, bf16[4,32,2176]{2,1,0:T(8,128)(2,1)S(1)}, u32[]{:S(2)}, u32[]{:S(2)}) %collective-permute-start.11) | collective-permute-done | bytes 557088 | tf_op jit(solution)/shard_map/ppermute | solution.py:669
  36.6 1.5 %collective-permute-start.12 = (bf16[4,32,1536]{2,1,0:T(8,128)(2,1)S(1)}, bf16[4,32,1536]{2,1,0:T(8,128)(2,1)S(1)}, u32[]{:S(2)}, u32[]{:S(2)}) collective-permute-start(bf16[4,32,1536]{2,1,0:T(8,128)(2,1)S(1)} %stack.5.refs_0_), channel_id=1, source_target_pairs={{0,4},{4,0},{8,12},{12,8},{16,20},{20,16},{24,28},{28,24},{1,5},{5... | collective-permute-start | bytes 1179656 | tf_op jit(solution)/shard_map/ppermute | solution.py:669
  38.0 2.5 %collective-permute-start.10 = (bf16[32,1536]{1,0:T(8,128)(2,1)S(1)}, bf16[32,1536]{1,0:T(8,128)(2,1)S(1)}, u32[]{:S(2)}, u32[]{:S(2)}) collective-permute-start(bf16[32,1536]{1,0:T(8,128)(2,1)S(1)} %get-tuple-element.208.refs_0_), channel_id=1, source_target_pairs={{0,24},{4,28},{8,16},{12,20},{16,8},{20,12},{24,0},{28,4},{1,25},{... | collective-permute-start | bytes 294920 | tf_op jit(solution)/shard_map/ppermute | solution.py:669
  40.5 1.9 %collective-permute-start.8 = (bf16[32,1536]{1,0:T(8,128)(2,1)S(1)}, bf16[32,1536]{1,0:T(8,128)(2,1)S(1)}, u32[]{:S(2)}, u32[]{:S(2)}) collective-permute-start(bf16[32,1536]{1,0:T(8,128)(2,1)S(1)} %get-tuple-element.208.refs_0_), channel_id=1, source_target_pairs={{0,8},{4,12},{8,0},{12,4},{16,24},{20,28},{24,16},{28,20},{1,9},{5... | collective-permute-start | bytes 294920 | tf_op jit(solution)/shard_map/ppermute | solution.py:669
  42.4 7.7 %gating.1 = (bf16[2,512,512]{2,1,0:T(8,128)(2,1)S(1)}, bf16[2,512,512]{2,1,0:T(8,128)(2,1)S(1)}, f32[2,512,128]{2,1,0:T(8,128)S(1)}, bf16[2,512,1536]{2,1,0:T(8,...) custom-call(bf16[8,128,512]{2,1,0:T(8,128)(2,1)} %refs_13_, ...), custom_call_target="tpu_custom_call" | custom-call | flops 25165824 | bytes 50331 | tf_op jit(solution)/shard_map/gating/pallas_call | solution.py:655
  50.8 0.6 collective-permute-start.18
  51.4 2.5 %mixing.1.mixed_ref = bf16[2,512,1536]{2,1,0:T(8,128)(2,1)S(1)} custom-call(s32[8,5]{1,0:T(8,128)S(1)} %copy-done, bf16[512,512]{1,0:T(8,128)(2,1)S(1)} %get-tuple-element.217.spatial_ref, bf16[2,512,1536]{2,1,0:T(8,128)(2,1)S(1)} %get-tuple-element.218.gate_ref, f32[512,128]{1,0:T(8,128)S(1)} %get-tuple-element.223.bias_col), custom_call_target="tpu_custom_call" | custom-call | flops 25165824 | bytes 50331 | tf_op jit(solution)/shard_map/mixing/pallas_call | solution.py:655
  53.9 6.7 %content_up.1 = (bf16[2,512,1536]{2,1,0:T(8,128)(2,1)S(1)}, bf16[2,512,1536]{2,1,0:T(8,128)(2,1)S(1)}, bf16[512,1536]{1,0:T(8,128)(2,1)S(1)}) custom-call(bf16[2,512,512]{2,1,0:T(8,128)(2,1)S(1)} %get-tuple-element.239.normed_ref, bf16[4,32,1536]{2,1,0:T(8,128)(2,1)S(1)} %stack.5.refs_0_, bf16[4,32,1536]{2,1,0:T(8,128)(2,1)S(1)} %collective-permute-done.12.refs_1_, ...), custom_call_target="tpu_custom_call" | custom-call | flops 25165824 | bytes 50331 | tf_op jit(solution)/shard_map/content_up/pallas_call | solution.py:655
  60.6 1.4 collective-permute-done.18.refs_1_
  61.9 1.7 %collective-permute-done.20.refs_3_ = bf16[4,32,1536]{2,1,0:T(8,128)(2,1)S(1)} collective-permute-done((bf16[4,32,1536]{2,1,0:T(8,128)(2,1)S(1)}, bf16[4,32,1536]{2,1,0:T(8,128)(2,1)S(1)}, u32[]{:S(2)}, u32[]{:S(2)}) %collective-permute-start.20) | collective-permute-done | bytes 393248 | tf_op jit(solution)/shard_map/ppermute | solution.py:669
  63.7 8.1 %content_down.1 = (bf16[2,512,1536]{2,1,0:T(8,128)(2,1)S(1)}, bf16[2,512,1536]{2,1,0:T(8,128)(2,1)S(1)}, bf16[2,512,1536]{2,1,0:T(8,128)(2,1)S(1)}, f32[512,128]...) custom-call(s32[8,5]{1,0:T(8,128)S(1)} %copy-done, ...), custom_call_target="tpu_custom_call" | custom-call | flops 25165824 | bytes 50331 | tf_op jit(solution)/shard_map/content_down/pallas_call | solution.py:655
  72.0 1.9 %content_sum.1 = (bf16[2,4,16,1536]{3,2,1,0:T(8,128)(2,1)S(1)}, bf16[2,4,16,1536]{3,2,1,0:T(8,128)(2,1)S(1)}, bf16[2,2,4,16,1536]{4,3,2,1,0:T(8,128)(2,1)S(1)}) custom-call(bf16[2,512,512]{2,1,0:T(8,128)(2,1)S(1)} %get-tuple-element.239.normed_ref, bf16[2,512,1536]{2,1,0:T(8,128)(2,1)S(1)} %get-tuple-element.230.grad_ref.content_grad_ref), custom_call_target="tpu_custom_call" | custom-call | flops 25165824 | bytes 50331 | tf_op jit(solution)/shard_map/content_sum/pallas_call | solution.py:655
  74.4 0.6 collective-permute-start.23
  75.0 2.5 %spatial_sum.1.square_ref = f32[512,512]{1,0:T(8,128)S(1)} custom-call(s32[8,5]{1,0:T(8,128)S(1)} %copy-done, bf16[2,512,1536]{2,1,0:T(8,128)(2,1)S(1)} %get-tuple-element.241.grad_mixed_ref, bf16[2,512,1536]{2,1,0:T(8,128)(2,1)S(1)} %get-tuple-element.218.gate_ref), custom_call_target="tpu_custom_call" | custom-call | flops 25165824 | bytes 50331 | tf_op jit(solution)/shard_map/spatial_sum/pallas_call | solution.py:655
  77.6 0.6 collective-permute-start.24
  78.2 6.5 %gate_back.1 = (bf16[2,512,1536]{2,1,0:T(8,128)(2,1)S(1)}, f32[8,16,128]{2,1,0:T(8,128)S(1)}) custom-call(s32[8,5]{1,0:T(8,128)S(1)} %copy-done, bf16[2,512,1536]{2,1,0:T(8,128)(2,1)S(1)} %get-tuple-element.241.grad_mixed_ref, bf16[2,512,1536]{2,1,0:T(8,128)(2,1)S(1)} %get-tuple-element.218.gate_ref, bf16[2,512,1536]{2,1,0:T(8,128)(2,1)S(1)} %get-tuple-element.242.slope_ref, ...), custom_call_target="tpu_custom_call" | custom-call | flops 25165824 | bytes 50331 | tf_op jit(solution)/shard_map/gate_back/pallas_call | solution.py:655
  84.7 1.0 collective-permute-done.23.refs_5_.refs_8_
  85.7 2.0 %gate_sum.1 = (bf16[2,4,16,1024]{3,2,1,0:T(8,128)(2,1)S(1)}, bf16[2,4,16,1024]{3,2,1,0:T(8,128)(2,1)S(1)}, bf16[2,2,4,16,1024]{4,3,2,1,0:T(8,128)(2,1)S(1)}, bf1...) custom-call(bf16[2,512,512]{2,1,0:T(8,128)(2,1)S(1)} %get-tuple-elem, ...), custom_call_target="tpu_custom_call" | custom-call | flops 25165824 | bytes 50331 | tf_op jit(solution)/shard_map/gate_sum/pallas_call | solution.py:655
  87.6 0.9 collective-permute-done.24.refs_2_
  88.6 0.5 collective-permute-start.25
  89.2 1.9 %layer.1 = (bf16[2,128,512]{2,1,0:T(8,128)(2,1)S(1)}, bf16[2,128,512]{2,1,0:T(8,128)(2,1)S(1)}, bf16[2,2,128,512]{3,2,1,0:T(8,128)(2,1)S(1)}) custom-call(bf16[2,512,1536]{2,1,0:T(8,128)(2,1)S(1)} %get-tuple-element.260.gated_ref, bf16[1536,512]{1,0:T(8,128)(2,1)S(1)} %get-tuple-element.261.shrink), custom_call_target="tpu_custom_call" | custom-call | flops 25165824 | bytes 50331 | tf_op jit(solution)/shard_map/layer/pallas_call | solution.py:655
  91.4 1.6 %collective-permute-start.28 = (bf16[2,4,16,1152]{3,2,1,0:T(8,128)(2,1)S(1)}, bf16[2,4,16,1152]{3,2,1,0:T(8,128)(2,1)S(1)}, u32[]{:S(2)}, u32[]{:S(2)}) collective-permute-start(bf16[2,4,16,1152]{3,2,1,0:T(8,128)(2,1)S(1)} %fusion.2), channel_id=1, source_target_pairs={{0,2},{1,3},{2,0},{3,1},{4,6},{5,7},{6,4},{7,5},{8,10},{9,11},{10,... | collective-permute-start | bytes 884744 | tf_op jit(solution)/shard_map/ppermute | solution.py:669
  93.1 0.6 collective-permute-start.27
  94.2 1.5 collective-permute-start.30
  95.6 3.9 %back.1 = (bf16[2,128,512]{2,1,0:T(8,128)(2,1)S(1)}, bf16[2,2,128,512]{3,2,1,0:T(8,128)(2,1)S(1)}, bf16[2,2,2,128,512]{4,3,2,1,0:T(8,128)(2,1)S(1)}) custom-call(bf16[2,512,1536]{2,1,0:T(8,128)(2,1)S(1)} %get-tuple-element.267.grad_ref.gate_grad_ref, bf16[2,512,1536]{2,1,0:T(8,128)(2,1)S(1)} %get-tuple-element.230.grad_ref.content_grad_ref, ...), custom_call_target="tpu_custom_call" | custom-call | flops 25165824 | bytes 50331 | tf_op jit(solution)/shard_map/back/pallas_call | solution.py:655
  99.5 5.2 %collective-permute-done.29.refs_12_ = bf16[4,16,1536]{2,1,0:T(8,128)(2,1)S(1)} collective-permute-done((bf16[4,16,1536]{2,1,0:T(8,128)(2,1)S(1)}, bf16[4,16,1536]{2,1,0:T(8,128)(2,1)S(1)}, u32[]{:S(2)}, u32[]{:S(2)}) %collective-permute-start.29) | collective-permute-done | bytes 196640 | tf_op jit(solution)/shard_map/ppermute | solution.py:669
  104.7 0.7 collective-permute-done.30.refs_14_
  105.5 0.6 collective-permute-start.32
  106.2 0.9 collective-permute-start.31
  107.0 4.1 %collective-permute-done.31.refs_13_ = bf16[4,16,1024]{2,1,0:T(8,128)(2,1)S(1)} collective-permute-done((bf16[4,16,1024]{2,1,0:T(8,128)(2,1)S(1)}, bf16[4,16,1024]{2,1,0:T(8,128)(2,1)S(1)}, u32[]{:S(2)}, u32[]{:S(2)}) %collective-permute-start.31) | collective-permute-done | bytes 131104 | tf_op jit(solution)/shard_map/ppermute | solution.py:669
  111.5 0.9 collective-permute-start.42
  112.4 1.0 collective-permute-start.34
  113.4 1.5 %collective-permute-start.35 = (bf16[16,5248]{1,0:T(8,128)(2,1)S(1)}, bf16[16,5248]{1,0:T(8,128)(2,1)S(1)}, u32[]{:S(2)}, u32[]{:S(2)}) collective-permute-start(bf16[16,5248]{1,0:T(8,128)(2,1)S(1)} %get-tuple-element.285), channel_id=1, source_target_pairs={{0,24},{4,28},{8,16},{12,20},{16,8},{20,12},{24,0},{28,4},{1,25},{... | collective-permute-start | bytes 503816 | tf_op jit(solution)/shard_map/ppermute | solution.py:669
  114.9 1.0 collective-permute-start.33
  115.9 3.2 %fetch.1 = (f32[64,3072]{1,0:T(8,128)S(1)}, f32[64,3072]{1,0:T(8,128)S(1)}, f32[64,3072]{1,0:T(8,128)S(1)}, f32[64,3072]{1,0:T(8,128)S(1)}, f32[192,512]{1,0:T(8...) custom-call(f32[64,3072]{1,0:T(8,128)} %refs_0_, ...), custom_call_target="tpu_custom_call" | custom-call | flops 25165824 | bytes 50331 | tf_op jit(solution)/shard_map/fetch/pallas_call | solution.py:655
  119.1 5.4 %collective-permute-done.34.two_ref = bf16[16,5248]{1,0:T(8,128)(2,1)S(1)} collective-permute-done((bf16[16,5248]{1,0:T(8,128)(2,1)S(1)}, bf16[16,5248]{1,0:T(8,128)(2,1)S(1)}, u32[]{:S(2)}, u32[]{:S(2)}) %collective-permute-start.34) | collective-permute-done | bytes 167968 | tf_op jit(solution)/shard_map/ppermute | solution.py:669
  124.6 1.2 collective-permute-done.33.one_ref
  126.1 0.6 collective-permute-start.41
  126.8 1.2 collective-permute-done.36.refs_1_
  128.0 1.7 %collective-permute-start.37 = (f32[8,128]{1,0:T(8,128)S(1)}, f32[8,128]{1,0:T(8,128)S(1)}, u32[]{:S(2)}, u32[]{:S(2)}) collective-permute-start(f32[8,128]{1,0:T(8,128)S(1)} %add.32.refs_0_), channel_id=1, source_target_pairs={{0,4},{4,0},{8,12},{12,8},{16,20},{20,16},{24,28},{28,24},{1,5},{5... | collective-permute-start | bytes 12296 | tf_op jit(solution)/shard_map/ppermute | solution.py:669
  129.7 1.9 %collective-permute-done.37.refs_1_ = f32[8,128]{1,0:T(8,128)S(1)} collective-permute-done((f32[8,128]{1,0:T(8,128)S(1)}, f32[8,128]{1,0:T(8,128)S(1)}, u32[]{:S(2)}, u32[]{:S(2)}) %collective-permute-start.37) | collective-permute-done | bytes 4128 | tf_op jit(solution)/shard_map/ppermute | solution.py:669
  131.6 2.1 %collective-permute-start.40 = (f32[8,128]{1,0:T(8,128)S(1)}, f32[8,128]{1,0:T(8,128)S(1)}, u32[]{:S(2)}, u32[]{:S(2)}) collective-permute-start(f32[8,128]{1,0:T(8,128)S(1)} %add.33.refs_0_), channel_id=1, source_target_pairs={{0,24},{4,28},{8,16},{12,20},{16,8},{20,12},{24,0},{28,4},{1,25},{... | collective-permute-start | bytes 12296 | tf_op jit(solution)/shard_map/ppermute | solution.py:669
  133.7 2.2 %collective-permute-start.39 = (f32[8,128]{1,0:T(8,128)S(1)}, f32[8,128]{1,0:T(8,128)S(1)}, u32[]{:S(2)}, u32[]{:S(2)}) collective-permute-start(f32[8,128]{1,0:T(8,128)S(1)} %add.33.refs_0_), channel_id=1, source_target_pairs={{0,16},{4,20},{8,24},{12,28},{16,0},{20,4},{24,8},{28,12},{1,17},{... | collective-permute-start | bytes 12296 | tf_op jit(solution)/shard_map/ppermute | solution.py:669
  136.0 1.0 collective-permute-done.40.refs_3_
  137.0 1.2 collective-permute-done.39.refs_2_
  138.2 1.3 collective-permute-done.38.refs_1_
  139.5 0.5 collective-permute-start.44
  140.2 1.5 collective-permute-start.43
  141.7 1.2 collective-permute-done.44.core_ref
  142.9 1.8 %give.1 = (f32[8,128,512]{2,1,0:T(8,128)}, bf16[8,128,512]{2,1,0:T(8,128)(2,1)}) custom-call(bf16[8,128,512]{2,1,0:T(8,128)(2,1)S(1)} %get-tuple-element.312.cots_ref, bf16[8,128,512]{2,1,0:T(8,128)(2,1)S(1)} %get-tuple-element.313.acts_ref, bf16[2,128,512]{2,1,0:T(8,128)(2,1)S(1)} %get-tuple-element.314.grad_own, ...), custom_call_target="tpu_custom_call" | custom-call | flops 25165824 | bytes 50331 | tf_op jit(solution)/shard_map/give/pallas_call | solution.py:655
  144.8 3.7 %adam.1 = (f32[64,3072]{1,0:T(8,128)}, f32[64,3072]{1,0:T(8,128)}, f32[64,3072]{1,0:T(8,128)}, f32[64,3072]{1,0:T(8,128)}, f32[64,3072]{1,0:T(8,128)}, /*index=5...) custom-call(f32[8,128]{1,0:T(8,128)S(1)} %add.35.message_ref, ...), custom_call_target="tpu_custom_call" | custom-call | flops 25165824 | bytes 50331 | tf_op jit(solution)/shard_map/adam/pallas_call | solution.py:655
  (80 shorter events, 4.3 us)
Async XLA Ops:
  3.1 30.9 %collective-permute-start.7 = (bf16[2,2,2,128,512]{4,3,2,1,0:T(8,128)(2,1)S(1)}, bf16[2,2,2,128,512]{4,3,2,1,0:T(8,128)(2,1)S(1)}, u32[]{:S(2)}, u32[]{:S(2)}) collective-permute-start(bf16[2,2,2,128,512]{4,3,2,1,0:T(8,128)(2,1)S(1)} %get-tuple-element.198), channel_id=1, source_target_pairs={{0,2},{1,3},{2,0},{3,1},{4,6},{5,7},{6,4},{7,5},{8,10},{9,11},{10,... | collective-permute-start | bytes 3145736 | tf_op jit(solution)/shard_map/ppermute | solution.py:669
  6.1 16.1 %collective-permute-start.3 = (bf16[2,2,128,512]{3,2,1,0:T(8,128)(2,1)S(1)}, bf16[2,2,128,512]{3,2,1,0:T(8,128)(2,1)S(1)}, u32[]{:S(2)}, u32[]{:S(2)}) collective-permute-start(bf16[2,2,128,512]{3,2,1,0:T(8,128)(2,1)S(1)} %get-tuple-element.197), channel_id=1, source_target_pairs={{0,1},{1,0},{2,3},{3,2},{4,5},{5,4},{6,7},{7,6},{8,9},{9,8},{10,11... | collective-permute-start | bytes 1572872 | tf_op jit(solution)/shard_map/ppermute | solution.py:669
  6.1 8.4 %collective-permute-start.2 = (bf16[32,2176]{1,0:T(8,128)(2,1)S(1)}, bf16[32,2176]{1,0:T(8,128)(2,1)S(1)}, u32[]{:S(2)}, u32[]{:S(2)}) collective-permute-start(bf16[32,2176]{1,0:T(8,128)(2,1)S(1)} %pack_first.1.refs_0_), channel_id=1, source_target_pairs={{0,24},{4,28},{8,16},{12,20},{16,8},{20,12},{24,0},{28,4},{1,25},{... | collective-permute-start | bytes 417800 | tf_op jit(solution)/shard_map/ppermute | solution.py:669
  9.7 12.4 %collective-permute-start.1 = (bf16[32,2176]{1,0:T(8,128)(2,1)S(1)}, bf16[32,2176]{1,0:T(8,128)(2,1)S(1)}, u32[]{:S(2)}, u32[]{:S(2)}) collective-permute-start(bf16[32,2176]{1,0:T(8,128)(2,1)S(1)} %pack_first.1.refs_0_), channel_id=1, source_target_pairs={{0,16},{4,20},{8,24},{12,28},{16,0},{20,4},{24,8},{28,12},{1,17},{... | collective-permute-start | bytes 417800 | tf_op jit(solution)/shard_map/ppermute | solution.py:669
  9.7 12.4 %collective-permute-start = (bf16[32,2176]{1,0:T(8,128)(2,1)S(1)}, bf16[32,2176]{1,0:T(8,128)(2,1)S(1)}, u32[]{:S(2)}, u32[]{:S(2)}) collective-permute-start(bf16[32,2176]{1,0:T(8,128)(2,1)S(1)} %pack_first.1.refs_0_), channel_id=1, source_target_pairs={{0,8},{4,12},{8,0},{12,4},{16,24},{20,28},{24,16},{28,20},{1,9},{5... | collective-permute-start | bytes 417800 | tf_op jit(solution)/shard_map/ppermute | solution.py:669
  22.2 14.3 %collective-permute-start.11 = (bf16[4,32,2176]{2,1,0:T(8,128)(2,1)S(1)}, bf16[4,32,2176]{2,1,0:T(8,128)(2,1)S(1)}, u32[]{:S(2)}, u32[]{:S(2)}) collective-permute-start(bf16[4,32,2176]{2,1,0:T(8,128)(2,1)S(1)} %stack.4.refs_0_.refs_4_), channel_id=1, source_target_pairs={{0,4},{4,0},{8,12},{12,8},{16,20},{20,16},{24,28},{28,24},{1,5},{5... | collective-permute-start | bytes 1671176 | tf_op jit(solution)/shard_map/ppermute | solution.py:669
  23.8 7.6 %collective-permute-start.6 = (bf16[32,1536]{1,0:T(8,128)(2,1)S(1)}, bf16[32,1536]{1,0:T(8,128)(2,1)S(1)}, u32[]{:S(2)}, u32[]{:S(2)}) collective-permute-start(bf16[32,1536]{1,0:T(8,128)(2,1)S(1)} %get-tuple-element.204.refs_0_), channel_id=1, source_target_pairs={{0,24},{4,28},{8,16},{12,20},{16,8},{20,12},{24,0},{28,4},{1,25},{... | collective-permute-start | bytes 294920 | tf_op jit(solution)/shard_map/ppermute | solution.py:669
  26.3 7.7 %collective-permute-start.5 = (bf16[32,1536]{1,0:T(8,128)(2,1)S(1)}, bf16[32,1536]{1,0:T(8,128)(2,1)S(1)}, u32[]{:S(2)}, u32[]{:S(2)}) collective-permute-start(bf16[32,1536]{1,0:T(8,128)(2,1)S(1)} %get-tuple-element.204.refs_0_), channel_id=1, source_target_pairs={{0,16},{4,20},{8,24},{12,28},{16,0},{20,4},{24,8},{28,12},{1,17},{... | collective-permute-start | bytes 294920 | tf_op jit(solution)/shard_map/ppermute | solution.py:669
  26.3 7.7 %collective-permute-start.4 = (bf16[32,1536]{1,0:T(8,128)(2,1)S(1)}, bf16[32,1536]{1,0:T(8,128)(2,1)S(1)}, u32[]{:S(2)}, u32[]{:S(2)}) collective-permute-start(bf16[32,1536]{1,0:T(8,128)(2,1)S(1)} %get-tuple-element.204.refs_0_), channel_id=1, source_target_pairs={{0,8},{4,12},{8,0},{12,4},{16,24},{20,28},{24,16},{28,20},{1,9},{5... | collective-permute-start | bytes 294920 | tf_op jit(solution)/shard_map/ppermute | solution.py:669
  34.0 8.5 %collective-permute-start.13 = (bf16[2,2,2,128,512]{4,3,2,1,0:T(8,128)(2,1)S(1)}, bf16[2,2,2,128,512]{4,3,2,1,0:T(8,128)(2,1)S(1)}, u32[]{:S(2)}, u32[]{:S(2)}) collective-permute-start(bf16[2,2,2,128,512]{4,3,2,1,0:T(8,128)(2,1)S(1)} %collective-permute-done.7.side_ref), channel_id=1, source_target_pairs={{0,1},{1,0},{2,3},{3,2},{4,5},{5,4},{6,7},{7,6},{8,9},{9,8},{10,11... | collective-permute-start | bytes 3145736 | tf_op jit(solution)/shard_map/ppermute | solution.py:669
  34.1 6.5 %collective-permute-start.14 = (bf16[4,32,2176]{2,1,0:T(8,128)(2,1)S(1)}, bf16[4,32,2176]{2,1,0:T(8,128)(2,1)S(1)}, u32[]{:S(2)}, u32[]{:S(2)}) collective-permute-start(bf16[4,32,2176]{2,1,0:T(8,128)(2,1)S(1)} %stack.4.refs_0_.refs_4_), channel_id=1, source_target_pairs={{0,1},{1,0},{2,3},{3,2},{4,5},{5,4},{6,7},{7,6},{8,9},{9,8},{10,11... | collective-permute-start | bytes 1671176 | tf_op jit(solution)/shard_map/ppermute | solution.py:669
  36.5 4.0 %collective-permute-start.15 = (bf16[4,32,2176]{2,1,0:T(8,128)(2,1)S(1)}, bf16[4,32,2176]{2,1,0:T(8,128)(2,1)S(1)}, u32[]{:S(2)}, u32[]{:S(2)}) collective-permute-start(bf16[4,32,2176]{2,1,0:T(8,128)(2,1)S(1)} %collective-permute-done.11.refs_1_.refs_5_), channel_id=1, source_target_pairs={{0,1},{1,0},{2,3},{3,2},{4,5},{5,4},{6,7},{7,6},{8,9},{9,8},{10,11... | collective-permute-start | bytes 1671176 | tf_op jit(solution)/shard_map/ppermute | solution.py:669
  36.6 13.6 %collective-permute-start.12 = (bf16[4,32,1536]{2,1,0:T(8,128)(2,1)S(1)}, bf16[4,32,1536]{2,1,0:T(8,128)(2,1)S(1)}, u32[]{:S(2)}, u32[]{:S(2)}) collective-permute-start(bf16[4,32,1536]{2,1,0:T(8,128)(2,1)S(1)} %stack.5.refs_0_), channel_id=1, source_target_pairs={{0,4},{4,0},{8,12},{12,8},{16,20},{20,16},{24,28},{28,24},{1,5},{5... | collective-permute-start | bytes 1179656 | tf_op jit(solution)/shard_map/ppermute | solution.py:669
  38.0 13.3 %copy-start = (s32[8,5]{1,0:T(8,128)S(1)}, s32[8,5]{1,0:T(8,128)}, u32[]{:S(2)}) copy-start(s32[8,5]{1,0:T(8,128)} %lens_ref.7) | copy-start | bytes 484
  38.0 12.1 %collective-permute-start.10 = (bf16[32,1536]{1,0:T(8,128)(2,1)S(1)}, bf16[32,1536]{1,0:T(8,128)(2,1)S(1)}, u32[]{:S(2)}, u32[]{:S(2)}) collective-permute-start(bf16[32,1536]{1,0:T(8,128)(2,1)S(1)} %get-tuple-element.208.refs_0_), channel_id=1, source_target_pairs={{0,24},{4,28},{8,16},{12,20},{16,8},{20,12},{24,0},{28,4},{1,25},{... | collective-permute-start | bytes 294920 | tf_op jit(solution)/shard_map/ppermute | solution.py:669
  40.5 9.6 %collective-permute-start.9 = (bf16[32,1536]{1,0:T(8,128)(2,1)S(1)}, bf16[32,1536]{1,0:T(8,128)(2,1)S(1)}, u32[]{:S(2)}, u32[]{:S(2)}) collective-permute-start(bf16[32,1536]{1,0:T(8,128)(2,1)S(1)} %get-tuple-element.208.refs_0_), channel_id=1, source_target_pairs={{0,16},{4,20},{8,24},{12,28},{16,0},{20,4},{24,8},{28,12},{1,17},{... | collective-permute-start | bytes 294920 | tf_op jit(solution)/shard_map/ppermute | solution.py:669
  40.5 9.6 %collective-permute-start.8 = (bf16[32,1536]{1,0:T(8,128)(2,1)S(1)}, bf16[32,1536]{1,0:T(8,128)(2,1)S(1)}, u32[]{:S(2)}, u32[]{:S(2)}) collective-permute-start(bf16[32,1536]{1,0:T(8,128)(2,1)S(1)} %get-tuple-element.208.refs_0_), channel_id=1, source_target_pairs={{0,8},{4,12},{8,0},{12,4},{16,24},{20,28},{24,16},{28,20},{1,9},{5... | collective-permute-start | bytes 294920 | tf_op jit(solution)/shard_map/ppermute | solution.py:669
  50.2 3.7 %collective-permute-start.16 = (bf16[4,32,1536]{2,1,0:T(8,128)(2,1)S(1)}, bf16[4,32,1536]{2,1,0:T(8,128)(2,1)S(1)}, u32[]{:S(2)}, u32[]{:S(2)}) collective-permute-start(bf16[4,32,1536]{2,1,0:T(8,128)(2,1)S(1)} %collective-permute-done.12.refs_1_), channel_id=1, source_target_pairs={{0,1},{1,0},{2,3},{3,2},{4,5},{5,4},{6,7},{7,6},{8,9},{9,8},{10,11... | collective-permute-start | bytes 1179656 | tf_op jit(solution)/shard_map/ppermute | solution.py:669
  50.3 3.7 %collective-permute-start.17 = (bf16[4,32,1536]{2,1,0:T(8,128)(2,1)S(1)}, bf16[4,32,1536]{2,1,0:T(8,128)(2,1)S(1)}, u32[]{:S(2)}, u32[]{:S(2)}) collective-permute-start(bf16[4,32,1536]{2,1,0:T(8,128)(2,1)S(1)} %stack.5.refs_0_), channel_id=1, source_target_pairs={{0,1},{1,0},{2,3},{3,2},{4,5},{5,4},{6,7},{7,6},{8,9},{9,8},{10,11... | collective-permute-start | bytes 1179656 | tf_op jit(solution)/shard_map/ppermute | solution.py:669
  50.8 11.2 %collective-permute-start.18 = (bf16[4,32,1536]{2,1,0:T(8,128)(2,1)S(1)}, bf16[4,32,1536]{2,1,0:T(8,128)(2,1)S(1)}, u32[]{:S(2)}, u32[]{:S(2)}) collective-permute-start(bf16[4,32,1536]{2,1,0:T(8,128)(2,1)S(1)} %stack.6.refs_0_), channel_id=1, source_target_pairs={{0,4},{4,0},{8,12},{12,8},{16,20},{20,16},{24,28},{28,24},{1,5},{5... | collective-permute-start | bytes 1179656 | tf_op jit(solution)/shard_map/ppermute | solution.py:669
  51.4 10.6 %collective-permute-start.19 = (bf16[4,32,1536]{2,1,0:T(8,128)(2,1)S(1)}, bf16[4,32,1536]{2,1,0:T(8,128)(2,1)S(1)}, u32[]{:S(2)}, u32[]{:S(2)}) collective-permute-start(bf16[4,32,1536]{2,1,0:T(8,128)(2,1)S(1)} %stack.6.refs_0_), channel_id=1, source_target_pairs={{0,1},{1,0},{2,3},{3,2},{4,5},{5,4},{6,7},{7,6},{8,9},{9,8},{10,11... | collective-permute-start | bytes 1179656 | tf_op jit(solution)/shard_map/ppermute | solution.py:669
  61.9 1.7 %collective-permute-start.20 = (bf16[4,32,1536]{2,1,0:T(8,128)(2,1)S(1)}, bf16[4,32,1536]{2,1,0:T(8,128)(2,1)S(1)}, u32[]{:S(2)}, u32[]{:S(2)}) collective-permute-start(bf16[4,32,1536]{2,1,0:T(8,128)(2,1)S(1)} %collective-permute-done.18.refs_1_), channel_id=1, source_target_pairs={{0,1},{1,0},{2,3},{3,2},{4,5},{5,4},{6,7},{7,6},{8,9},{9,8},{10,11... | collective-permute-start | bytes 1179656 | tf_op jit(solution)/shard_map/ppermute | solution.py:669
  71.7 2.6 %collective-permute-start.21 = (bf16[2,2,4,16,1536]{4,3,2,1,0:T(8,128)(2,1)S(1)}, bf16[2,2,4,16,1536]{4,3,2,1,0:T(8,128)(2,1)S(1)}, u32[]{:S(2)}, u32[]{:S(2)}) collective-permute-start(bf16[2,2,4,16,1536]{4,3,2,1,0:T(8,128)(2,1)S(1)} %get-tuple-element.229), channel_id=1, source_target_pairs={{0,1},{1,0},{2,3},{3,2},{4,5},{5,4},{6,7},{7,6},{8,9},{9,8},{10,11... | collective-permute-start | bytes 2359304 | tf_op jit(solution)/shard_map/ppermute | solution.py:669
  73.9 3.6 %collective-permute-start.22 = (bf16[2,2,4,16,1536]{4,3,2,1,0:T(8,128)(2,1)S(1)}, bf16[2,2,4,16,1536]{4,3,2,1,0:T(8,128)(2,1)S(1)}, u32[]{:S(2)}, u32[]{:S(2)}) collective-permute-start(bf16[2,2,4,16,1536]{4,3,2,1,0:T(8,128)(2,1)S(1)} %get-tuple-element.233), channel_id=1, source_target_pairs={{0,1},{1,0},{2,3},{3,2},{4,5},{5,4},{6,7},{7,6},{8,9},{9,8},{10,11... | collective-permute-start | bytes 2359304 | tf_op jit(solution)/shard_map/ppermute | solution.py:669
  74.4 11.2 %collective-permute-start.23 = (bf16[2,4,16,1536]{3,2,1,0:T(8,128)(2,1)S(1)}, bf16[2,4,16,1536]{3,2,1,0:T(8,128)(2,1)S(1)}, u32[]{:S(2)}, u32[]{:S(2)}) collective-permute-start(bf16[2,4,16,1536]{3,2,1,0:T(8,128)(2,1)S(1)} %fusion.1), channel_id=1, source_target_pairs={{0,2},{1,3},{2,0},{3,1},{4,6},{5,7},{6,4},{7,5},{8,10},{9,11},{10,... | collective-permute-start | bytes 1179656 | tf_op jit(solution)/shard_map/ppermute | solution.py:669
  77.6 11.0 %collective-permute-start.24 = (bf16[2,4,16,1536]{3,2,1,0:T(8,128)(2,1)S(1)}, bf16[2,4,16,1536]{3,2,1,0:T(8,128)(2,1)S(1)}, u32[]{:S(2)}, u32[]{:S(2)}) collective-permute-start(bf16[2,4,16,1536]{3,2,1,0:T(8,128)(2,1)S(1)} %fusion), channel_id=1, source_target_pairs={{0,4},{4,0},{8,12},{12,8},{16,20},{20,16},{24,28},{28,24},{1,5},{5... | collective-permute-start | bytes 1179656 | tf_op jit(solution)/shard_map/ppermute | solution.py:669
  88.5 2.8 %collective-permute-start.26 = (bf16[2,2,4,16,1152]{4,3,2,1,0:T(8,128)(2,1)S(1)}, bf16[2,2,4,16,1152]{4,3,2,1,0:T(8,128)(2,1)S(1)}, u32[]{:S(2)}, u32[]{:S(2)}) collective-permute-start(bf16[2,2,4,16,1152]{4,3,2,1,0:T(8,128)(2,1)S(1)} %get-tuple-element.254), channel_id=1, source_target_pairs={{0,1},{1,0},{2,3},{3,2},{4,5},{5,4},{6,7},{7,6},{8,9},{9,8},{10,11... | collective-permute-start | bytes 1769480 | tf_op jit(solution)/shard_map/ppermute | solution.py:669
  88.6 2.8 %collective-permute-start.25 = (bf16[2,2,4,16,1024]{4,3,2,1,0:T(8,128)(2,1)S(1)}, bf16[2,2,4,16,1024]{4,3,2,1,0:T(8,128)(2,1)S(1)}, u32[]{:S(2)}, u32[]{:S(2)}) collective-permute-start(bf16[2,2,4,16,1024]{4,3,2,1,0:T(8,128)(2,1)S(1)} %get-tuple-element.253), channel_id=1, source_target_pairs={{0,1},{1,0},{2,3},{3,2},{4,5},{5,4},{6,7},{7,6},{8,9},{9,8},{10,11... | collective-permute-start | bytes 1572872 | tf_op jit(solution)/shard_map/ppermute | solution.py:669
  91.4 14.0 %collective-permute-start.28 = (bf16[2,4,16,1152]{3,2,1,0:T(8,128)(2,1)S(1)}, bf16[2,4,16,1152]{3,2,1,0:T(8,128)(2,1)S(1)}, u32[]{:S(2)}, u32[]{:S(2)}) collective-permute-start(bf16[2,4,16,1152]{3,2,1,0:T(8,128)(2,1)S(1)} %fusion.2), channel_id=1, source_target_pairs={{0,2},{1,3},{2,0},{3,1},{4,6},{5,7},{6,4},{7,5},{8,10},{9,11},{10,... | collective-permute-start | bytes 884744 | tf_op jit(solution)/shard_map/ppermute | solution.py:669
  93.1 12.3 %collective-permute-start.27 = (bf16[2,4,16,1024]{3,2,1,0:T(8,128)(2,1)S(1)}, bf16[2,4,16,1024]{3,2,1,0:T(8,128)(2,1)S(1)}, u32[]{:S(2)}, u32[]{:S(2)}) collective-permute-start(bf16[2,4,16,1024]{3,2,1,0:T(8,128)(2,1)S(1)} %fusion.3), channel_id=1, source_target_pairs={{0,4},{4,0},{8,12},{12,8},{16,20},{20,16},{24,28},{28,24},{1,5},{5... | collective-permute-start | bytes 786440 | tf_op jit(solution)/shard_map/ppermute | solution.py:669
  93.7 11.0 %collective-permute-start.29 = (bf16[4,16,1536]{2,1,0:T(8,128)(2,1)S(1)}, bf16[4,16,1536]{2,1,0:T(8,128)(2,1)S(1)}, u32[]{:S(2)}, u32[]{:S(2)}) collective-permute-start(bf16[4,16,1536]{2,1,0:T(8,128)(2,1)S(1)} %get-tuple-element.258), channel_id=1, source_target_pairs={{0,2},{1,3},{2,0},{3,1},{4,6},{5,7},{6,4},{7,5},{8,10},{9,11},{10,... | collective-permute-start | bytes 589832 | tf_op jit(solution)/shard_map/ppermute | solution.py:669
  94.2 11.2 %collective-permute-start.30 = (bf16[4,16,1536]{2,1,0:T(8,128)(2,1)S(1)}, bf16[4,16,1536]{2,1,0:T(8,128)(2,1)S(1)}, u32[]{:S(2)}, u32[]{:S(2)}) collective-permute-start(bf16[4,16,1536]{2,1,0:T(8,128)(2,1)S(1)} %get-tuple-element.259), channel_id=1, source_target_pairs={{0,4},{4,0},{8,12},{12,8},{16,20},{20,16},{24,28},{28,24},{1,5},{5... | collective-permute-start | bytes 589832 | tf_op jit(solution)/shard_map/ppermute | solution.py:669
  105.5 5.6 %collective-permute-start.32 = (bf16[4,16,1152]{2,1,0:T(8,128)(2,1)S(1)}, bf16[4,16,1152]{2,1,0:T(8,128)(2,1)S(1)}, u32[]{:S(2)}, u32[]{:S(2)}) collective-permute-start(bf16[4,16,1152]{2,1,0:T(8,128)(2,1)S(1)} %get-tuple-element.281), channel_id=1, source_target_pairs={{0,4},{4,0},{8,12},{12,8},{16,20},{20,16},{24,28},{28,24},{1,5},{5... | collective-permute-start | bytes 442376 | tf_op jit(solution)/shard_map/ppermute | solution.py:669
  106.2 5.0 %collective-permute-start.31 = (bf16[4,16,1024]{2,1,0:T(8,128)(2,1)S(1)}, bf16[4,16,1024]{2,1,0:T(8,128)(2,1)S(1)}, u32[]{:S(2)}, u32[]{:S(2)}) collective-permute-start(bf16[4,16,1024]{2,1,0:T(8,128)(2,1)S(1)} %get-tuple-element.279), channel_id=1, source_target_pairs={{0,2},{1,3},{2,0},{3,1},{4,6},{5,7},{6,4},{7,5},{8,10},{9,11},{10,... | collective-permute-start | bytes 393224 | tf_op jit(solution)/shard_map/ppermute | solution.py:669
  111.5 28.0 %collective-permute-start.42 = (bf16[2,2,2,128,512]{4,3,2,1,0:T(8,128)(2,1)S(1)}, bf16[2,2,2,128,512]{4,3,2,1,0:T(8,128)(2,1)S(1)}, u32[]{:S(2)}, u32[]{:S(2)}) collective-permute-start(bf16[2,2,2,128,512]{4,3,2,1,0:T(8,128)(2,1)S(1)} %get-tuple-element.308), channel_id=1, source_target_pairs={{0,2},{1,3},{2,0},{3,1},{4,6},{5,7},{6,4},{7,5},{8,10},{9,11},{10,... | collective-permute-start | bytes 3145736 | tf_op jit(solution)/shard_map/ppermute | solution.py:669
  112.4 12.1 %collective-permute-start.34 = (bf16[16,5248]{1,0:T(8,128)(2,1)S(1)}, bf16[16,5248]{1,0:T(8,128)(2,1)S(1)}, u32[]{:S(2)}, u32[]{:S(2)}) collective-permute-start(bf16[16,5248]{1,0:T(8,128)(2,1)S(1)} %get-tuple-element.284), channel_id=1, source_target_pairs={{0,16},{4,20},{8,24},{12,28},{16,0},{20,4},{24,8},{28,12},{1,17},{... | collective-permute-start | bytes 503816 | tf_op jit(solution)/shard_map/ppermute | solution.py:669
  113.4 11.1 %collective-permute-start.35 = (bf16[16,5248]{1,0:T(8,128)(2,1)S(1)}, bf16[16,5248]{1,0:T(8,128)(2,1)S(1)}, u32[]{:S(2)}, u32[]{:S(2)}) collective-permute-start(bf16[16,5248]{1,0:T(8,128)(2,1)S(1)} %get-tuple-element.285), channel_id=1, source_target_pairs={{0,24},{4,28},{8,16},{12,20},{16,8},{20,12},{24,0},{28,4},{1,25},{... | collective-permute-start | bytes 503816 | tf_op jit(solution)/shard_map/ppermute | solution.py:669
  114.9 10.8 %collective-permute-start.33 = (bf16[16,5248]{1,0:T(8,128)(2,1)S(1)}, bf16[16,5248]{1,0:T(8,128)(2,1)S(1)}, u32[]{:S(2)}, u32[]{:S(2)}) collective-permute-start(bf16[16,5248]{1,0:T(8,128)(2,1)S(1)} %get-tuple-element.283), channel_id=1, source_target_pairs={{0,8},{4,12},{8,0},{12,4},{16,24},{20,28},{24,16},{28,20},{1,9},{5... | collective-permute-start | bytes 503816 | tf_op jit(solution)/shard_map/ppermute | solution.py:669
  126.1 13.4 %collective-permute-start.41 = (bf16[16,5248]{1,0:T(8,128)(2,1)S(1)}, bf16[16,5248]{1,0:T(8,128)(2,1)S(1)}, u32[]{:S(2)}, u32[]{:S(2)}) collective-permute-start(bf16[16,5248]{1,0:T(8,128)(2,1)S(1)} %get-tuple-element.306.refs_0_.own_ref), channel_id=1, source_target_pairs={{0,2},{1,3},{2,0},{3,1},{4,6},{5,7},{6,4},{7,5},{8,10},{9,11},{10,... | collective-permute-start | bytes 503816 | tf_op jit(solution)/shard_map/ppermute | solution.py:669
  126.7 18.1 %copy-start.1 = (f32[256]{0:T(256)S(1)}, f32[256]{0:T(256)}, u32[]{:S(2)}) copy-start(f32[256]{0:T(256)} %param.38) | copy-start | bytes 3076
  126.7 18.1 %copy-start.2 = (f32[64]{0:T(128)S(1)}, f32[64]{0:T(128)}, u32[]{:S(2)}) copy-start(f32[64]{0:T(128)} %param.42) | copy-start | bytes 772
  126.7 18.1 %copy-start.3 = (f32[256]{0:T(256)S(1)}, f32[256]{0:T(256)}, u32[]{:S(2)}) copy-start(f32[256]{0:T(256)} %param.39) | copy-start | bytes 3076
  126.7 18.1 %copy-start.4 = (f32[256]{0:T(256)S(1)}, f32[256]{0:T(256)}, u32[]{:S(2)}) copy-start(f32[256]{0:T(256)} %param.40) | copy-start | bytes 3076
  126.7 18.1 %copy-start.5 = (f32[256]{0:T(256)S(1)}, f32[256]{0:T(256)}, u32[]{:S(2)}) copy-start(f32[256]{0:T(256)} %param.41) | copy-start | bytes 3076
  126.7 18.1 %copy-start.6 = (f32[64]{0:T(128)S(1)}, f32[64]{0:T(128)}, u32[]{:S(2)}) copy-start(f32[64]{0:T(128)} %param.43) | copy-start | bytes 772
  126.7 18.1 %copy-start.7 = (f32[64]{0:T(128)S(1)}, f32[64]{0:T(128)}, u32[]{:S(2)}) copy-start(f32[64]{0:T(128)} %param.44) | copy-start | bytes 772
  126.7 18.1 %copy-start.8 = (f32[64]{0:T(128)S(1)}, f32[64]{0:T(128)}, u32[]{:S(2)}) copy-start(f32[64]{0:T(128)} %param.45) | copy-start | bytes 772
  126.7 1.2 collective-permute-start.36
  128.0 3.6 %collective-permute-start.37 = (f32[8,128]{1,0:T(8,128)S(1)}, f32[8,128]{1,0:T(8,128)S(1)}, u32[]{:S(2)}, u32[]{:S(2)}) collective-permute-start(f32[8,128]{1,0:T(8,128)S(1)} %add.32.refs_0_), channel_id=1, source_target_pairs={{0,4},{4,0},{8,12},{12,8},{16,20},{20,16},{24,28},{28,24},{1,5},{5... | collective-permute-start | bytes 12296 | tf_op jit(solution)/shard_map/ppermute | solution.py:669
  131.6 5.4 %collective-permute-start.40 = (f32[8,128]{1,0:T(8,128)S(1)}, f32[8,128]{1,0:T(8,128)S(1)}, u32[]{:S(2)}, u32[]{:S(2)}) collective-permute-start(f32[8,128]{1,0:T(8,128)S(1)} %add.33.refs_0_), channel_id=1, source_target_pairs={{0,24},{4,28},{8,16},{12,20},{16,8},{20,12},{24,0},{28,4},{1,25},{... | collective-permute-start | bytes 12296 | tf_op jit(solution)/shard_map/ppermute | solution.py:669
  133.7 4.5 %collective-permute-start.39 = (f32[8,128]{1,0:T(8,128)S(1)}, f32[8,128]{1,0:T(8,128)S(1)}, u32[]{:S(2)}, u32[]{:S(2)}) collective-permute-start(f32[8,128]{1,0:T(8,128)S(1)} %add.33.refs_0_), channel_id=1, source_target_pairs={{0,16},{4,20},{8,24},{12,28},{16,0},{20,4},{24,8},{28,12},{1,17},{... | collective-permute-start | bytes 12296 | tf_op jit(solution)/shard_map/ppermute | solution.py:669
  135.9 3.6 %collective-permute-start.38 = (f32[8,128]{1,0:T(8,128)S(1)}, f32[8,128]{1,0:T(8,128)S(1)}, u32[]{:S(2)}, u32[]{:S(2)}) collective-permute-start(f32[8,128]{1,0:T(8,128)S(1)} %add.33.refs_0_), channel_id=1, source_target_pairs={{0,8},{4,12},{8,0},{12,4},{16,24},{20,28},{24,16},{28,20},{1,9},{5... | collective-permute-start | bytes 12296 | tf_op jit(solution)/shard_map/ppermute | solution.py:669
  139.5 3.4 %collective-permute-start.45 = (bf16[2,2,2,128,512]{4,3,2,1,0:T(8,128)(2,1)S(1)}, bf16[2,2,2,128,512]{4,3,2,1,0:T(8,128)(2,1)S(1)}, u32[]{:S(2)}, u32[]{:S(2)}) collective-permute-start(bf16[2,2,2,128,512]{4,3,2,1,0:T(8,128)(2,1)S(1)} %collective-permute-done.42.side_ref), channel_id=1, source_target_pairs={{0,1},{1,0},{2,3},{3,2},{4,5},{5,4},{6,7},{7,6},{8,9},{9,8},{10,11... | collective-permute-start | bytes 3145736 | tf_op jit(solution)/shard_map/ppermute | solution.py:669
  139.5 3.4 %collective-permute-start.44 = (bf16[2,2,128,512]{3,2,1,0:T(8,128)(2,1)S(1)}, bf16[2,2,128,512]{3,2,1,0:T(8,128)(2,1)S(1)}, u32[]{:S(2)}, u32[]{:S(2)}) collective-permute-start(bf16[2,2,128,512]{3,2,1,0:T(8,128)(2,1)S(1)} %get-tuple-element.317), channel_id=1, source_target_pairs={{0,1},{1,0},{2,3},{3,2},{4,5},{5,4},{6,7},{7,6},{8,9},{9,8},{10,11... | collective-permute-start | bytes 1572872 | tf_op jit(solution)/shard_map/ppermute | solution.py:669
  140.1 4.7 %collective-permute-start.46 = (bf16[2,16,5248]{2,1,0:T(8,128)(2,1)S(1)}, bf16[2,16,5248]{2,1,0:T(8,128)(2,1)S(1)}, u32[]{:S(2)}, u32[]{:S(2)}) collective-permute-start(bf16[2,16,5248]{2,1,0:T(8,128)(2,1)S(1)} %stack.7), channel_id=1, source_target_pairs={{0,1},{1,0},{2,3},{3,2},{4,5},{5,4},{6,7},{7,6},{8,9},{9,8},{10,11... | collective-permute-start | bytes 1007624 | tf_op jit(solution)/shard_map/ppermute | solution.py:669
  140.2 4.5 %collective-permute-start.43 = (f32[8,128]{1,0:T(8,128)S(1)}, f32[8,128]{1,0:T(8,128)S(1)}, u32[]{:S(2)}, u32[]{:S(2)}) collective-permute-start(f32[8,128]{1,0:T(8,128)S(1)} %add.34.refs_0_), channel_id=1, source_target_pairs={{0,2},{1,3},{2,0},{3,1},{4,6},{5,7},{6,4},{7,5},{8,10},{9,11},{10,... | collective-permute-start | bytes 12296 | tf_op jit(solution)/shard_map/ppermute | solution.py:669

commit v4 on v2

--- a/solution.py
+++ b/solution.py
@@ -30,6 +30,7 @@
 GELU_B = GELU_A * 0.044715
 LANES = 128
 CHUNK = 64
+PIECE = 32
 BLOCK = 16
 VMEM_LIMIT = 16 * 1024 * 1024
 
@@ -224,8 +225,8 @@
         normed = normed_ref[row]
         for c in range(0, HALF, WIDTH):
             hidden = dot(normed, weight[:, c : c + WIDTH])
-            for p in range(0, ROW, CHUNK):
-                here = slice(p, p + CHUNK)
+            for p in range(0, ROW, PIECE):
+                here = slice(p, p + PIECE)
                 values = hidden[here]
                 squares, gate = gelu_gate(values)
                 slope_ref[row, here, c : c + WIDTH] = gelu_slope(values, squares, gate).astype(BF16)
@@ -298,9 +299,9 @@
     def do_channels(k, carry):
         channels = run(k * WIDTH, WIDTH)
         hidden = dot(normed_ref[...].reshape(tokens, D), weight[:, channels])
-        for p in range(0, tokens, CHUNK):
-            r, here = p // ROW, slice(p % ROW, p % ROW + CHUNK)
-            values = hidden[p : p + CHUNK]
+        for p in range(0, tokens, PIECE):
+            r, here = p // ROW, slice(p % ROW, p % ROW + PIECE)
+            values = hidden[p : p + PIECE]
             squares, gate = gelu_gate(values)
             content_ref[r, here, channels] = (values * gate).astype(BF16)
             slope_ref[r, here, channels] = gelu_slope(values, squares, gate).astype(BF16)
@@ -336,9 +337,9 @@
     def do_channels(k, carry):
         channels = run(k * WIDTH, WIDTH)
         grad_gated = dot(cots[...], shrink[channels, :], ((1,), (1,)))
-        for p in range(0, tokens, CHUNK):
-            r, here = p // ROW, slice(p % ROW, p % ROW + CHUNK)
-            grads = grad_gated[p : p + CHUNK]
+        for p in range(0, tokens, PIECE):
+            r, here = p // ROW, slice(p % ROW, p % ROW + PIECE)
+            grads = grad_gated[p : p + PIECE]
             content = content_ref[r, here, channels].astype(F32)
             mixed = mixed_ref[r, here, channels].astype(F32)
             slope = slope_ref[r, here, channels].astype(F32)
@@ -347,7 +348,7 @@
             grad_mixed = (grads * content).astype(BF16)
             grad_mixed_ref[r, here, channels] = grad_mixed
             total = grad_mixed.astype(F32)
-            sums[p : p + CHUNK, :] += total[:, :LANES] + total[:, LANES:]
+            sums[p : p + PIECE, :] += total[:, :LANES] + total[:, LANES:]
         tall_sum[channels, :] = dot(gated_ref[:, :, channels].reshape(tokens, WIDTH), cots[...], ((0,), (0,)))
         return carry
 
@@ -400,13 +401,13 @@
         for c in range(0, HALF, WIDTH):
             grads_all = dot(masked, grad_mixed_ref[row, :, c : c + WIDTH])
             vector = jnp.zeros((8, WIDTH), F32)
-            for p in range(0, ROW, CHUNK):
-                here = slice(p, p + CHUNK)
+            for p in range(0, ROW, PIECE):
+                here = slice(p, p + PIECE)
                 low = grads_all[here].astype(BF16)
                 grad_gate[here, c : c + WIDTH] = low
                 grads = low.astype(F32)
                 products = grads * gate_ref[row, here, c : c + WIDTH].astype(F32)
-                vector = vector + jnp.sum(products.reshape(CHUNK // 8, 8, WIDTH), axis=0)
+                vector = vector + jnp.sum(products.reshape(PIECE // 8, 8, WIDTH), axis=0)
                 scaled = grads * gains_ref[0:1, D + c : D + c + WIDTH]
                 first = scaled[:, :LANES] + scaled[:, LANES:]
                 other = products[:, :LANES] + products[:, LANES:]
@@ -681,8 +682,8 @@
     clipped = clip_scale * gradient
     moment = BETA_FIRST * momentum + (1.0 - BETA_FIRST) * clipped
     square = BETA_SECOND * variance + (1.0 - BETA_SECOND) * clipped * clipped
-    first_hat = moment / (1.0 - BETA_FIRST**STEP)
-    second_hat = square / (1.0 - BETA_SECOND**STEP)
+    first_hat = moment * (1.0 / (1.0 - BETA_FIRST**STEP))
+    second_hat = square * (1.0 / (1.0 - BETA_SECOND**STEP))
     updated = weight - step_rate * (
         first_hat / (jnp.sqrt(second_hat) + ADAM_EPS) + decay_rate * weight
     )

time: 149 us -> 149 us (level)
  no operation moved by 1% of the time
where the time goes in v4:
time: 149 us
  Pallas kernels  57.2 us (38%)
  waiting for transfers between devices  47.8 us (32%)
  starting transfers between devices  42.3 us (28%)
    pallas_call x28, Pallas kernels, call_kernel(): pl.pallas_call(kernel, name=name, in_specs=in_specs, out_specs=specs, out...  57.2 us
    ppermute x47, waiting for transfers between devices, swap_with(): return lax.ppermute(value, axis, [(i, i ^ bit) for i in range(size)])  47.8 us
    ppermute x47, starting transfers between devices, swap_with(): return lax.ppermute(value, axis, [(i, i ^ bit) for i in range(size)])  42.3 us
  transfers between devices with their start and end apart: 47, of which 21 were waited for; matrix products, arithmetic and copies ran while one was open for 0% of the time, Pallas kernels for 28%

profile of v4, /device:TPU:0, one launch (start us, length us, event | category | flops | bytes accessed | tf_op | source)
XLA Modules:
  0.0 149.0 jit_solution(6935615633925412170)
XLA Ops:
  0.7 1.0 pack_first.1.refs_0_
  1.7 1.4 cut.1
  3.1 3.0 %collective-permute-start.7 = (bf16[2,2,2,128,512]{4,3,2,1,0:T(8,128)(2,1)S(1)}, bf16[2,2,2,128,512]{4,3,2,1,0:T(8,128)(2,1)S(1)}, u32[]{:S(2)}, u32[]{:S(2)}) collective-permute-start(bf16[2,2,2,128,512]{4,3,2,1,0:T(8,128)(2,1)S(1)} %get-tuple-element.198), channel_id=1, source_target_pairs={{0,2},{1,3},{2,0},{3,1},{4,6},{5,7},{6,4},{7,5},{8,10},{9,11},{10,... | collective-permute-start | bytes 3145736 | tf_op jit(solution)/shard_map/ppermute | solution.py:669
  6.1 3.6 %collective-permute-start.2 = (bf16[32,2176]{1,0:T(8,128)(2,1)S(1)}, bf16[32,2176]{1,0:T(8,128)(2,1)S(1)}, u32[]{:S(2)}, u32[]{:S(2)}) collective-permute-start(bf16[32,2176]{1,0:T(8,128)(2,1)S(1)} %pack_first.1.refs_0_), channel_id=1, source_target_pairs={{0,24},{4,28},{8,16},{12,20},{16,8},{20,12},{24,0},{28,4},{1,25},{... | collective-permute-start | bytes 417800 | tf_op jit(solution)/shard_map/ppermute | solution.py:669
  9.7 0.8 collective-permute-start
  10.5 1.1 pack_second.1
  11.6 2.9 %collective-permute-done.2.refs_3_ = bf16[32,2176]{1,0:T(8,128)(2,1)S(1)} collective-permute-done((bf16[32,2176]{1,0:T(8,128)(2,1)S(1)}, bf16[32,2176]{1,0:T(8,128)(2,1)S(1)}, u32[]{:S(2)}, u32[]{:S(2)}) %collective-permute-start.2) | collective-permute-done | bytes 139296 | tf_op jit(solution)/shard_map/ppermute | solution.py:669
  14.5 7.7 %collective-permute-done.1.refs_2_ = bf16[32,2176]{1,0:T(8,128)(2,1)S(1)} collective-permute-done((bf16[32,2176]{1,0:T(8,128)(2,1)S(1)}, bf16[32,2176]{1,0:T(8,128)(2,1)S(1)}, u32[]{:S(2)}, u32[]{:S(2)}) %collective-permute-start.1) | collective-permute-done | bytes 139296 | tf_op jit(solution)/shard_map/ppermute | solution.py:669
  22.2 1.6 %collective-permute-start.11 = (bf16[4,32,2176]{2,1,0:T(8,128)(2,1)S(1)}, bf16[4,32,2176]{2,1,0:T(8,128)(2,1)S(1)}, u32[]{:S(2)}, u32[]{:S(2)}) collective-permute-start(bf16[4,32,2176]{2,1,0:T(8,128)(2,1)S(1)} %stack.4.refs_0_.refs_4_), channel_id=1, source_target_pairs={{0,4},{4,0},{8,12},{12,8},{16,20},{20,16},{24,28},{28,24},{1,5},{5... | collective-permute-start | bytes 1671176 | tf_op jit(solution)/shard_map/ppermute | solution.py:669
  23.8 2.5 %collective-permute-start.6 = (bf16[32,1536]{1,0:T(8,128)(2,1)S(1)}, bf16[32,1536]{1,0:T(8,128)(2,1)S(1)}, u32[]{:S(2)}, u32[]{:S(2)}) collective-permute-start(bf16[32,1536]{1,0:T(8,128)(2,1)S(1)} %get-tuple-element.204.refs_0_), channel_id=1, source_target_pairs={{0,24},{4,28},{8,16},{12,20},{16,8},{20,12},{24,0},{28,4},{1,25},{... | collective-permute-start | bytes 294920 | tf_op jit(solution)/shard_map/ppermute | solution.py:669
  26.3 1.9 %collective-permute-start.4 = (bf16[32,1536]{1,0:T(8,128)(2,1)S(1)}, bf16[32,1536]{1,0:T(8,128)(2,1)S(1)}, u32[]{:S(2)}, u32[]{:S(2)}) collective-permute-start(bf16[32,1536]{1,0:T(8,128)(2,1)S(1)} %get-tuple-element.204.refs_0_), channel_id=1, source_target_pairs={{0,8},{4,12},{8,0},{12,4},{16,24},{20,28},{24,16},{28,20},{1,9},{5... | collective-permute-start | bytes 294920 | tf_op jit(solution)/shard_map/ppermute | solution.py:669
  28.2 3.2 %collective-permute-done.6.refs_3_ = bf16[32,1536]{1,0:T(8,128)(2,1)S(1)} collective-permute-done((bf16[32,1536]{1,0:T(8,128)(2,1)S(1)}, bf16[32,1536]{1,0:T(8,128)(2,1)S(1)}, u32[]{:S(2)}, u32[]{:S(2)}) %collective-permute-start.6) | collective-permute-done | bytes 98336 | tf_op jit(solution)/shard_map/ppermute | solution.py:669
  31.4 2.6 %collective-permute-done.5.refs_2_ = bf16[32,1536]{1,0:T(8,128)(2,1)S(1)} collective-permute-done((bf16[32,1536]{1,0:T(8,128)(2,1)S(1)}, bf16[32,1536]{1,0:T(8,128)(2,1)S(1)}, u32[]{:S(2)}, u32[]{:S(2)}) %collective-permute-start.5) | collective-permute-done | bytes 98336 | tf_op jit(solution)/shard_map/ppermute | solution.py:669
  34.6 2.0 %collective-permute-done.11.refs_1_.refs_5_ = bf16[4,32,2176]{2,1,0:T(8,128)(2,1)S(1)} collective-permute-done((bf16[4,32,2176]{2,1,0:T(8,128)(2,1)S(1)}, bf16[4,32,2176]{2,1,0:T(8,128)(2,1)S(1)}, u32[]{:S(2)}, u32[]{:S(2)}) %collective-permute-start.11) | collective-permute-done | bytes 557088 | tf_op jit(solution)/shard_map/ppermute | solution.py:669
  36.6 1.5 %collective-permute-start.12 = (bf16[4,32,1536]{2,1,0:T(8,128)(2,1)S(1)}, bf16[4,32,1536]{2,1,0:T(8,128)(2,1)S(1)}, u32[]{:S(2)}, u32[]{:S(2)}) collective-permute-start(bf16[4,32,1536]{2,1,0:T(8,128)(2,1)S(1)} %stack.5.refs_0_), channel_id=1, source_target_pairs={{0,4},{4,0},{8,12},{12,8},{16,20},{20,16},{24,28},{28,24},{1,5},{5... | collective-permute-start | bytes 1179656 | tf_op jit(solution)/shard_map/ppermute | solution.py:669
  38.0 2.5 %collective-permute-start.10 = (bf16[32,1536]{1,0:T(8,128)(2,1)S(1)}, bf16[32,1536]{1,0:T(8,128)(2,1)S(1)}, u32[]{:S(2)}, u32[]{:S(2)}) collective-permute-start(bf16[32,1536]{1,0:T(8,128)(2,1)S(1)} %get-tuple-element.208.refs_0_), channel_id=1, source_target_pairs={{0,24},{4,28},{8,16},{12,20},{16,8},{20,12},{24,0},{28,4},{1,25},{... | collective-permute-start | bytes 294920 | tf_op jit(solution)/shard_map/ppermute | solution.py:669
  40.5 1.9 %collective-permute-start.8 = (bf16[32,1536]{1,0:T(8,128)(2,1)S(1)}, bf16[32,1536]{1,0:T(8,128)(2,1)S(1)}, u32[]{:S(2)}, u32[]{:S(2)}) collective-permute-start(bf16[32,1536]{1,0:T(8,128)(2,1)S(1)} %get-tuple-element.208.refs_0_), channel_id=1, source_target_pairs={{0,8},{4,12},{8,0},{12,4},{16,24},{20,28},{24,16},{28,20},{1,9},{5... | collective-permute-start | bytes 294920 | tf_op jit(solution)/shard_map/ppermute | solution.py:669
  42.4 7.7 %gating.1 = (bf16[2,512,512]{2,1,0:T(8,128)(2,1)S(1)}, bf16[2,512,512]{2,1,0:T(8,128)(2,1)S(1)}, f32[2,512,128]{2,1,0:T(8,128)S(1)}, bf16[2,512,1536]{2,1,0:T(8,...) custom-call(bf16[8,128,512]{2,1,0:T(8,128)(2,1)} %refs_13_, ...), custom_call_target="tpu_custom_call" | custom-call | flops 25165824 | bytes 50331 | tf_op jit(solution)/shard_map/gating/pallas_call | solution.py:655
  50.8 0.6 collective-permute-start.18
  51.4 2.5 %mixing.1.mixed_ref = bf16[2,512,1536]{2,1,0:T(8,128)(2,1)S(1)} custom-call(s32[8,5]{1,0:T(8,128)S(1)} %copy-done, bf16[512,512]{1,0:T(8,128)(2,1)S(1)} %get-tuple-element.217.spatial_ref, bf16[2,512,1536]{2,1,0:T(8,128)(2,1)S(1)} %get-tuple-element.218.gate_ref, f32[512,128]{1,0:T(8,128)S(1)} %get-tuple-element.223.bias_col), custom_call_target="tpu_custom_call" | custom-call | flops 25165824 | bytes 50331 | tf_op jit(solution)/shard_map/mixing/pallas_call | solution.py:655
  53.9 6.7 %content_up.1 = (bf16[2,512,1536]{2,1,0:T(8,128)(2,1)S(1)}, bf16[2,512,1536]{2,1,0:T(8,128)(2,1)S(1)}, bf16[512,1536]{1,0:T(8,128)(2,1)S(1)}) custom-call(bf16[2,512,512]{2,1,0:T(8,128)(2,1)S(1)} %get-tuple-element.239.normed_ref, bf16[4,32,1536]{2,1,0:T(8,128)(2,1)S(1)} %stack.5.refs_0_, bf16[4,32,1536]{2,1,0:T(8,128)(2,1)S(1)} %collective-permute-done.12.refs_1_, ...), custom_call_target="tpu_custom_call" | custom-call | flops 25165824 | bytes 50331 | tf_op jit(solution)/shard_map/content_up/pallas_call | solution.py:655
  60.6 1.4 collective-permute-done.18.refs_1_
  61.9 1.7 %collective-permute-done.20.refs_3_ = bf16[4,32,1536]{2,1,0:T(8,128)(2,1)S(1)} collective-permute-done((bf16[4,32,1536]{2,1,0:T(8,128)(2,1)S(1)}, bf16[4,32,1536]{2,1,0:T(8,128)(2,1)S(1)}, u32[]{:S(2)}, u32[]{:S(2)}) %collective-permute-start.20) | collective-permute-done | bytes 393248 | tf_op jit(solution)/shard_map/ppermute | solution.py:669
  63.7 8.4 %content_down.1 = (bf16[2,512,1536]{2,1,0:T(8,128)(2,1)S(1)}, bf16[2,512,1536]{2,1,0:T(8,128)(2,1)S(1)}, bf16[2,512,1536]{2,1,0:T(8,128)(2,1)S(1)}, f32[512,128]...) custom-call(s32[8,5]{1,0:T(8,128)S(1)} %copy-done, ...), custom_call_target="tpu_custom_call" | custom-call | flops 25165824 | bytes 50331 | tf_op jit(solution)/shard_map/content_down/pallas_call | solution.py:655
  72.2 1.9 %content_sum.1 = (bf16[2,4,16,1536]{3,2,1,0:T(8,128)(2,1)S(1)}, bf16[2,4,16,1536]{3,2,1,0:T(8,128)(2,1)S(1)}, bf16[2,2,4,16,1536]{4,3,2,1,0:T(8,128)(2,1)S(1)}) custom-call(bf16[2,512,512]{2,1,0:T(8,128)(2,1)S(1)} %get-tuple-element.239.normed_ref, bf16[2,512,1536]{2,1,0:T(8,128)(2,1)S(1)} %get-tuple-element.230.grad_ref.content_grad_ref), custom_call_target="tpu_custom_call" | custom-call | flops 25165824 | bytes 50331 | tf_op jit(solution)/shard_map/content_sum/pallas_call | solution.py:655
  74.7 0.6 collective-permute-start.23
  75.3 2.5 %spatial_sum.1.square_ref = f32[512,512]{1,0:T(8,128)S(1)} custom-call(s32[8,5]{1,0:T(8,128)S(1)} %copy-done, bf16[2,512,1536]{2,1,0:T(8,128)(2,1)S(1)} %get-tuple-element.241.grad_mixed_ref, bf16[2,512,1536]{2,1,0:T(8,128)(2,1)S(1)} %get-tuple-element.218.gate_ref), custom_call_target="tpu_custom_call" | custom-call | flops 25165824 | bytes 50331 | tf_op jit(solution)/shard_map/spatial_sum/pallas_call | solution.py:655
  77.9 0.6 collective-permute-start.24
  78.5 6.6 %gate_back.1 = (bf16[2,512,1536]{2,1,0:T(8,128)(2,1)S(1)}, f32[8,16,128]{2,1,0:T(8,128)S(1)}) custom-call(s32[8,5]{1,0:T(8,128)S(1)} %copy-done, bf16[2,512,1536]{2,1,0:T(8,128)(2,1)S(1)} %get-tuple-element.241.grad_mixed_ref, bf16[2,512,1536]{2,1,0:T(8,128)(2,1)S(1)} %get-tuple-element.218.gate_ref, bf16[2,512,1536]{2,1,0:T(8,128)(2,1)S(1)} %get-tuple-element.242.slope_ref, ...), custom_call_target="tpu_custom_call" | custom-call | flops 25165824 | bytes 50331 | tf_op jit(solution)/shard_map/gate_back/pallas_call | solution.py:655
  85.1 0.8 collective-permute-done.23.refs_5_.refs_8_
  85.9 2.0 %gate_sum.1 = (bf16[2,4,16,1024]{3,2,1,0:T(8,128)(2,1)S(1)}, bf16[2,4,16,1024]{3,2,1,0:T(8,128)(2,1)S(1)}, bf16[2,2,4,16,1024]{4,3,2,1,0:T(8,128)(2,1)S(1)}, bf1...) custom-call(bf16[2,512,512]{2,1,0:T(8,128)(2,1)S(1)} %get-tuple-elem, ...), custom_call_target="tpu_custom_call" | custom-call | flops 25165824 | bytes 50331 | tf_op jit(solution)/shard_map/gate_sum/pallas_call | solution.py:655
  87.9 0.9 collective-permute-done.24.refs_2_
  88.8 0.5 collective-permute-start.25
  89.5 1.9 %layer.1 = (bf16[2,128,512]{2,1,0:T(8,128)(2,1)S(1)}, bf16[2,128,512]{2,1,0:T(8,128)(2,1)S(1)}, bf16[2,2,128,512]{3,2,1,0:T(8,128)(2,1)S(1)}) custom-call(bf16[2,512,1536]{2,1,0:T(8,128)(2,1)S(1)} %get-tuple-element.260.gated_ref, bf16[1536,512]{1,0:T(8,128)(2,1)S(1)} %get-tuple-element.261.shrink), custom_call_target="tpu_custom_call" | custom-call | flops 25165824 | bytes 50331 | tf_op jit(solution)/shard_map/layer/pallas_call | solution.py:655
  91.7 1.6 %collective-permute-start.28 = (bf16[2,4,16,1152]{3,2,1,0:T(8,128)(2,1)S(1)}, bf16[2,4,16,1152]{3,2,1,0:T(8,128)(2,1)S(1)}, u32[]{:S(2)}, u32[]{:S(2)}) collective-permute-start(bf16[2,4,16,1152]{3,2,1,0:T(8,128)(2,1)S(1)} %fusion.2), channel_id=1, source_target_pairs={{0,2},{1,3},{2,0},{3,1},{4,6},{5,7},{6,4},{7,5},{8,10},{9,11},{10,... | collective-permute-start | bytes 884744 | tf_op jit(solution)/shard_map/ppermute | solution.py:669
  93.3 0.7 collective-permute-start.27
  94.5 1.4 collective-permute-start.30
  95.9 3.9 %back.1 = (bf16[2,128,512]{2,1,0:T(8,128)(2,1)S(1)}, bf16[2,2,128,512]{3,2,1,0:T(8,128)(2,1)S(1)}, bf16[2,2,2,128,512]{4,3,2,1,0:T(8,128)(2,1)S(1)}) custom-call(bf16[2,512,1536]{2,1,0:T(8,128)(2,1)S(1)} %get-tuple-element.267.grad_ref.gate_grad_ref, bf16[2,512,1536]{2,1,0:T(8,128)(2,1)S(1)} %get-tuple-element.230.grad_ref.content_grad_ref, ...), custom_call_target="tpu_custom_call" | custom-call | flops 25165824 | bytes 50331 | tf_op jit(solution)/shard_map/back/pallas_call | solution.py:655
  99.8 5.2 %collective-permute-done.29.refs_12_ = bf16[4,16,1536]{2,1,0:T(8,128)(2,1)S(1)} collective-permute-done((bf16[4,16,1536]{2,1,0:T(8,128)(2,1)S(1)}, bf16[4,16,1536]{2,1,0:T(8,128)(2,1)S(1)}, u32[]{:S(2)}, u32[]{:S(2)}) %collective-permute-start.29) | collective-permute-done | bytes 196640 | tf_op jit(solution)/shard_map/ppermute | solution.py:669
  105.0 0.7 collective-permute-done.30.refs_14_
  105.8 0.7 collective-permute-start.32
  106.4 0.9 collective-permute-start.31
  107.3 4.1 %collective-permute-done.31.refs_13_ = bf16[4,16,1024]{2,1,0:T(8,128)(2,1)S(1)} collective-permute-done((bf16[4,16,1024]{2,1,0:T(8,128)(2,1)S(1)}, bf16[4,16,1024]{2,1,0:T(8,128)(2,1)S(1)}, u32[]{:S(2)}, u32[]{:S(2)}) %collective-permute-start.31) | collective-permute-done | bytes 131104 | tf_op jit(solution)/shard_map/ppermute | solution.py:669
  111.8 0.9 collective-permute-start.42
  112.7 1.0 collective-permute-start.34
  113.7 1.5 %collective-permute-start.35 = (bf16[16,5248]{1,0:T(8,128)(2,1)S(1)}, bf16[16,5248]{1,0:T(8,128)(2,1)S(1)}, u32[]{:S(2)}, u32[]{:S(2)}) collective-permute-start(bf16[16,5248]{1,0:T(8,128)(2,1)S(1)} %get-tuple-element.285), channel_id=1, source_target_pairs={{0,24},{4,28},{8,16},{12,20},{16,8},{20,12},{24,0},{28,4},{1,25},{... | collective-permute-start | bytes 503816 | tf_op jit(solution)/shard_map/ppermute | solution.py:669
  115.2 1.0 collective-permute-start.33
  116.2 3.2 %fetch.1 = (f32[64,3072]{1,0:T(8,128)S(1)}, f32[64,3072]{1,0:T(8,128)S(1)}, f32[64,3072]{1,0:T(8,128)S(1)}, f32[64,3072]{1,0:T(8,128)S(1)}, f32[192,512]{1,0:T(8...) custom-call(f32[64,3072]{1,0:T(8,128)} %refs_0_, ...), custom_call_target="tpu_custom_call" | custom-call | flops 25165824 | bytes 50331 | tf_op jit(solution)/shard_map/fetch/pallas_call | solution.py:655
  119.4 5.4 %collective-permute-done.34.two_ref = bf16[16,5248]{1,0:T(8,128)(2,1)S(1)} collective-permute-done((bf16[16,5248]{1,0:T(8,128)(2,1)S(1)}, bf16[16,5248]{1,0:T(8,128)(2,1)S(1)}, u32[]{:S(2)}, u32[]{:S(2)}) %collective-permute-start.34) | collective-permute-done | bytes 167968 | tf_op jit(solution)/shard_map/ppermute | solution.py:669
  124.8 1.2 collective-permute-done.33.one_ref
  126.3 0.6 collective-permute-start.41
  127.1 1.2 collective-permute-done.36.refs_1_
  128.3 1.7 %collective-permute-start.37 = (f32[8,128]{1,0:T(8,128)S(1)}, f32[8,128]{1,0:T(8,128)S(1)}, u32[]{:S(2)}, u32[]{:S(2)}) collective-permute-start(f32[8,128]{1,0:T(8,128)S(1)} %add.32.refs_0_), channel_id=1, source_target_pairs={{0,4},{4,0},{8,12},{12,8},{16,20},{20,16},{24,28},{28,24},{1,5},{5... | collective-permute-start | bytes 12296 | tf_op jit(solution)/shard_map/ppermute | solution.py:669
  130.0 1.9 %collective-permute-done.37.refs_1_ = f32[8,128]{1,0:T(8,128)S(1)} collective-permute-done((f32[8,128]{1,0:T(8,128)S(1)}, f32[8,128]{1,0:T(8,128)S(1)}, u32[]{:S(2)}, u32[]{:S(2)}) %collective-permute-start.37) | collective-permute-done | bytes 4128 | tf_op jit(solution)/shard_map/ppermute | solution.py:669
  131.9 2.1 %collective-permute-start.40 = (f32[8,128]{1,0:T(8,128)S(1)}, f32[8,128]{1,0:T(8,128)S(1)}, u32[]{:S(2)}, u32[]{:S(2)}) collective-permute-start(f32[8,128]{1,0:T(8,128)S(1)} %add.33.refs_0_), channel_id=1, source_target_pairs={{0,24},{4,28},{8,16},{12,20},{16,8},{20,12},{24,0},{28,4},{1,25},{... | collective-permute-start | bytes 12296 | tf_op jit(solution)/shard_map/ppermute | solution.py:669
  134.0 2.2 %collective-permute-start.39 = (f32[8,128]{1,0:T(8,128)S(1)}, f32[8,128]{1,0:T(8,128)S(1)}, u32[]{:S(2)}, u32[]{:S(2)}) collective-permute-start(f32[8,128]{1,0:T(8,128)S(1)} %add.33.refs_0_), channel_id=1, source_target_pairs={{0,16},{4,20},{8,24},{12,28},{16,0},{20,4},{24,8},{28,12},{1,17},{... | collective-permute-start | bytes 12296 | tf_op jit(solution)/shard_map/ppermute | solution.py:669
  136.3 1.0 collective-permute-done.40.refs_3_
  137.3 1.2 collective-permute-done.39.refs_2_
  138.5 1.3 collective-permute-done.38.refs_1_
  139.8 0.5 collective-permute-start.44
  140.5 1.5 collective-permute-start.43
  142.0 1.2 collective-permute-done.44.core_ref
  143.2 1.8 %give.1 = (f32[8,128,512]{2,1,0:T(8,128)}, bf16[8,128,512]{2,1,0:T(8,128)(2,1)}) custom-call(bf16[8,128,512]{2,1,0:T(8,128)(2,1)S(1)} %get-tuple-element.312.cots_ref, bf16[8,128,512]{2,1,0:T(8,128)(2,1)S(1)} %get-tuple-element.313.acts_ref, bf16[2,128,512]{2,1,0:T(8,128)(2,1)S(1)} %get-tuple-element.314.grad_own, ...), custom_call_target="tpu_custom_call" | custom-call | flops 25165824 | bytes 50331 | tf_op jit(solution)/shard_map/give/pallas_call | solution.py:655
  145.1 3.7 %adam.1 = (f32[64,3072]{1,0:T(8,128)}, f32[64,3072]{1,0:T(8,128)}, f32[64,3072]{1,0:T(8,128)}, f32[64,3072]{1,0:T(8,128)}, f32[64,3072]{1,0:T(8,128)}, /*index=5...) custom-call(f32[8,128]{1,0:T(8,128)S(1)} %add.35.message_ref, ...), custom_call_target="tpu_custom_call" | custom-call | flops 25165824 | bytes 50331 | tf_op jit(solution)/shard_map/adam/pallas_call | solution.py:655
  (80 shorter events, 4.3 us)
Async XLA Ops:
  3.1 30.9 %collective-permute-start.7 = (bf16[2,2,2,128,512]{4,3,2,1,0:T(8,128)(2,1)S(1)}, bf16[2,2,2,128,512]{4,3,2,1,0:T(8,128)(2,1)S(1)}, u32[]{:S(2)}, u32[]{:S(2)}) collective-permute-start(bf16[2,2,2,128,512]{4,3,2,1,0:T(8,128)(2,1)S(1)} %get-tuple-element.198), channel_id=1, source_target_pairs={{0,2},{1,3},{2,0},{3,1},{4,6},{5,7},{6,4},{7,5},{8,10},{9,11},{10,... | collective-permute-start | bytes 3145736 | tf_op jit(solution)/shard_map/ppermute | solution.py:669
  6.1 16.1 %collective-permute-start.3 = (bf16[2,2,128,512]{3,2,1,0:T(8,128)(2,1)S(1)}, bf16[2,2,128,512]{3,2,1,0:T(8,128)(2,1)S(1)}, u32[]{:S(2)}, u32[]{:S(2)}) collective-permute-start(bf16[2,2,128,512]{3,2,1,0:T(8,128)(2,1)S(1)} %get-tuple-element.197), channel_id=1, source_target_pairs={{0,1},{1,0},{2,3},{3,2},{4,5},{5,4},{6,7},{7,6},{8,9},{9,8},{10,11... | collective-permute-start | bytes 1572872 | tf_op jit(solution)/shard_map/ppermute | solution.py:669
  6.1 8.4 %collective-permute-start.2 = (bf16[32,2176]{1,0:T(8,128)(2,1)S(1)}, bf16[32,2176]{1,0:T(8,128)(2,1)S(1)}, u32[]{:S(2)}, u32[]{:S(2)}) collective-permute-start(bf16[32,2176]{1,0:T(8,128)(2,1)S(1)} %pack_first.1.refs_0_), channel_id=1, source_target_pairs={{0,24},{4,28},{8,16},{12,20},{16,8},{20,12},{24,0},{28,4},{1,25},{... | collective-permute-start | bytes 417800 | tf_op jit(solution)/shard_map/ppermute | solution.py:669
  9.7 12.4 %collective-permute-start.1 = (bf16[32,2176]{1,0:T(8,128)(2,1)S(1)}, bf16[32,2176]{1,0:T(8,128)(2,1)S(1)}, u32[]{:S(2)}, u32[]{:S(2)}) collective-permute-start(bf16[32,2176]{1,0:T(8,128)(2,1)S(1)} %pack_first.1.refs_0_), channel_id=1, source_target_pairs={{0,16},{4,20},{8,24},{12,28},{16,0},{20,4},{24,8},{28,12},{1,17},{... | collective-permute-start | bytes 417800 | tf_op jit(solution)/shard_map/ppermute | solution.py:669
  9.7 12.4 %collective-permute-start = (bf16[32,2176]{1,0:T(8,128)(2,1)S(1)}, bf16[32,2176]{1,0:T(8,128)(2,1)S(1)}, u32[]{:S(2)}, u32[]{:S(2)}) collective-permute-start(bf16[32,2176]{1,0:T(8,128)(2,1)S(1)} %pack_first.1.refs_0_), channel_id=1, source_target_pairs={{0,8},{4,12},{8,0},{12,4},{16,24},{20,28},{24,16},{28,20},{1,9},{5... | collective-permute-start | bytes 417800 | tf_op jit(solution)/shard_map/ppermute | solution.py:669
  22.2 14.3 %collective-permute-start.11 = (bf16[4,32,2176]{2,1,0:T(8,128)(2,1)S(1)}, bf16[4,32,2176]{2,1,0:T(8,128)(2,1)S(1)}, u32[]{:S(2)}, u32[]{:S(2)}) collective-permute-start(bf16[4,32,2176]{2,1,0:T(8,128)(2,1)S(1)} %stack.4.refs_0_.refs_4_), channel_id=1, source_target_pairs={{0,4},{4,0},{8,12},{12,8},{16,20},{20,16},{24,28},{28,24},{1,5},{5... | collective-permute-start | bytes 1671176 | tf_op jit(solution)/shard_map/ppermute | solution.py:669
  23.8 7.6 %collective-permute-start.6 = (bf16[32,1536]{1,0:T(8,128)(2,1)S(1)}, bf16[32,1536]{1,0:T(8,128)(2,1)S(1)}, u32[]{:S(2)}, u32[]{:S(2)}) collective-permute-start(bf16[32,1536]{1,0:T(8,128)(2,1)S(1)} %get-tuple-element.204.refs_0_), channel_id=1, source_target_pairs={{0,24},{4,28},{8,16},{12,20},{16,8},{20,12},{24,0},{28,4},{1,25},{... | collective-permute-start | bytes 294920 | tf_op jit(solution)/shard_map/ppermute | solution.py:669
  26.3 7.7 %collective-permute-start.5 = (bf16[32,1536]{1,0:T(8,128)(2,1)S(1)}, bf16[32,1536]{1,0:T(8,128)(2,1)S(1)}, u32[]{:S(2)}, u32[]{:S(2)}) collective-permute-start(bf16[32,1536]{1,0:T(8,128)(2,1)S(1)} %get-tuple-element.204.refs_0_), channel_id=1, source_target_pairs={{0,16},{4,20},{8,24},{12,28},{16,0},{20,4},{24,8},{28,12},{1,17},{... | collective-permute-start | bytes 294920 | tf_op jit(solution)/shard_map/ppermute | solution.py:669
  26.3 7.7 %collective-permute-start.4 = (bf16[32,1536]{1,0:T(8,128)(2,1)S(1)}, bf16[32,1536]{1,0:T(8,128)(2,1)S(1)}, u32[]{:S(2)}, u32[]{:S(2)}) collective-permute-start(bf16[32,1536]{1,0:T(8,128)(2,1)S(1)} %get-tuple-element.204.refs_0_), channel_id=1, source_target_pairs={{0,8},{4,12},{8,0},{12,4},{16,24},{20,28},{24,16},{28,20},{1,9},{5... | collective-permute-start | bytes 294920 | tf_op jit(solution)/shard_map/ppermute | solution.py:669
  34.0 8.5 %collective-permute-start.13 = (bf16[2,2,2,128,512]{4,3,2,1,0:T(8,128)(2,1)S(1)}, bf16[2,2,2,128,512]{4,3,2,1,0:T(8,128)(2,1)S(1)}, u32[]{:S(2)}, u32[]{:S(2)}) collective-permute-start(bf16[2,2,2,128,512]{4,3,2,1,0:T(8,128)(2,1)S(1)} %collective-permute-done.7.side_ref), channel_id=1, source_target_pairs={{0,1},{1,0},{2,3},{3,2},{4,5},{5,4},{6,7},{7,6},{8,9},{9,8},{10,11... | collective-permute-start | bytes 3145736 | tf_op jit(solution)/shard_map/ppermute | solution.py:669
  34.1 6.5 %collective-permute-start.14 = (bf16[4,32,2176]{2,1,0:T(8,128)(2,1)S(1)}, bf16[4,32,2176]{2,1,0:T(8,128)(2,1)S(1)}, u32[]{:S(2)}, u32[]{:S(2)}) collective-permute-start(bf16[4,32,2176]{2,1,0:T(8,128)(2,1)S(1)} %stack.4.refs_0_.refs_4_), channel_id=1, source_target_pairs={{0,1},{1,0},{2,3},{3,2},{4,5},{5,4},{6,7},{7,6},{8,9},{9,8},{10,11... | collective-permute-start | bytes 1671176 | tf_op jit(solution)/shard_map/ppermute | solution.py:669
  36.5 4.0 %collective-permute-start.15 = (bf16[4,32,2176]{2,1,0:T(8,128)(2,1)S(1)}, bf16[4,32,2176]{2,1,0:T(8,128)(2,1)S(1)}, u32[]{:S(2)}, u32[]{:S(2)}) collective-permute-start(bf16[4,32,2176]{2,1,0:T(8,128)(2,1)S(1)} %collective-permute-done.11.refs_1_.refs_5_), channel_id=1, source_target_pairs={{0,1},{1,0},{2,3},{3,2},{4,5},{5,4},{6,7},{7,6},{8,9},{9,8},{10,11... | collective-permute-start | bytes 1671176 | tf_op jit(solution)/shard_map/ppermute | solution.py:669
  36.6 13.6 %collective-permute-start.12 = (bf16[4,32,1536]{2,1,0:T(8,128)(2,1)S(1)}, bf16[4,32,1536]{2,1,0:T(8,128)(2,1)S(1)}, u32[]{:S(2)}, u32[]{:S(2)}) collective-permute-start(bf16[4,32,1536]{2,1,0:T(8,128)(2,1)S(1)} %stack.5.refs_0_), channel_id=1, source_target_pairs={{0,4},{4,0},{8,12},{12,8},{16,20},{20,16},{24,28},{28,24},{1,5},{5... | collective-permute-start | bytes 1179656 | tf_op jit(solution)/shard_map/ppermute | solution.py:669
  38.0 13.3 %copy-start = (s32[8,5]{1,0:T(8,128)S(1)}, s32[8,5]{1,0:T(8,128)}, u32[]{:S(2)}) copy-start(s32[8,5]{1,0:T(8,128)} %lens_ref.7) | copy-start | bytes 484
  38.0 12.1 %collective-permute-start.10 = (bf16[32,1536]{1,0:T(8,128)(2,1)S(1)}, bf16[32,1536]{1,0:T(8,128)(2,1)S(1)}, u32[]{:S(2)}, u32[]{:S(2)}) collective-permute-start(bf16[32,1536]{1,0:T(8,128)(2,1)S(1)} %get-tuple-element.208.refs_0_), channel_id=1, source_target_pairs={{0,24},{4,28},{8,16},{12,20},{16,8},{20,12},{24,0},{28,4},{1,25},{... | collective-permute-start | bytes 294920 | tf_op jit(solution)/shard_map/ppermute | solution.py:669
  40.5 9.6 %collective-permute-start.9 = (bf16[32,1536]{1,0:T(8,128)(2,1)S(1)}, bf16[32,1536]{1,0:T(8,128)(2,1)S(1)}, u32[]{:S(2)}, u32[]{:S(2)}) collective-permute-start(bf16[32,1536]{1,0:T(8,128)(2,1)S(1)} %get-tuple-element.208.refs_0_), channel_id=1, source_target_pairs={{0,16},{4,20},{8,24},{12,28},{16,0},{20,4},{24,8},{28,12},{1,17},{... | collective-permute-start | bytes 294920 | tf_op jit(solution)/shard_map/ppermute | solution.py:669
  40.5 9.6 %collective-permute-start.8 = (bf16[32,1536]{1,0:T(8,128)(2,1)S(1)}, bf16[32,1536]{1,0:T(8,128)(2,1)S(1)}, u32[]{:S(2)}, u32[]{:S(2)}) collective-permute-start(bf16[32,1536]{1,0:T(8,128)(2,1)S(1)} %get-tuple-element.208.refs_0_), channel_id=1, source_target_pairs={{0,8},{4,12},{8,0},{12,4},{16,24},{20,28},{24,16},{28,20},{1,9},{5... | collective-permute-start | bytes 294920 | tf_op jit(solution)/shard_map/ppermute | solution.py:669
  50.2 3.7 %collective-permute-start.16 = (bf16[4,32,1536]{2,1,0:T(8,128)(2,1)S(1)}, bf16[4,32,1536]{2,1,0:T(8,128)(2,1)S(1)}, u32[]{:S(2)}, u32[]{:S(2)}) collective-permute-start(bf16[4,32,1536]{2,1,0:T(8,128)(2,1)S(1)} %collective-permute-done.12.refs_1_), channel_id=1, source_target_pairs={{0,1},{1,0},{2,3},{3,2},{4,5},{5,4},{6,7},{7,6},{8,9},{9,8},{10,11... | collective-permute-start | bytes 1179656 | tf_op jit(solution)/shard_map/ppermute | solution.py:669
  50.3 3.7 %collective-permute-start.17 = (bf16[4,32,1536]{2,1,0:T(8,128)(2,1)S(1)}, bf16[4,32,1536]{2,1,0:T(8,128)(2,1)S(1)}, u32[]{:S(2)}, u32[]{:S(2)}) collective-permute-start(bf16[4,32,1536]{2,1,0:T(8,128)(2,1)S(1)} %stack.5.refs_0_), channel_id=1, source_target_pairs={{0,1},{1,0},{2,3},{3,2},{4,5},{5,4},{6,7},{7,6},{8,9},{9,8},{10,11... | collective-permute-start | bytes 1179656 | tf_op jit(solution)/shard_map/ppermute | solution.py:669
  50.8 11.2 %collective-permute-start.18 = (bf16[4,32,1536]{2,1,0:T(8,128)(2,1)S(1)}, bf16[4,32,1536]{2,1,0:T(8,128)(2,1)S(1)}, u32[]{:S(2)}, u32[]{:S(2)}) collective-permute-start(bf16[4,32,1536]{2,1,0:T(8,128)(2,1)S(1)} %stack.6.refs_0_), channel_id=1, source_target_pairs={{0,4},{4,0},{8,12},{12,8},{16,20},{20,16},{24,28},{28,24},{1,5},{5... | collective-permute-start | bytes 1179656 | tf_op jit(solution)/shard_map/ppermute | solution.py:669
  51.4 10.6 %collective-permute-start.19 = (bf16[4,32,1536]{2,1,0:T(8,128)(2,1)S(1)}, bf16[4,32,1536]{2,1,0:T(8,128)(2,1)S(1)}, u32[]{:S(2)}, u32[]{:S(2)}) collective-permute-start(bf16[4,32,1536]{2,1,0:T(8,128)(2,1)S(1)} %stack.6.refs_0_), channel_id=1, source_target_pairs={{0,1},{1,0},{2,3},{3,2},{4,5},{5,4},{6,7},{7,6},{8,9},{9,8},{10,11... | collective-permute-start | bytes 1179656 | tf_op jit(solution)/shard_map/ppermute | solution.py:669
  61.9 1.7 %collective-permute-start.20 = (bf16[4,32,1536]{2,1,0:T(8,128)(2,1)S(1)}, bf16[4,32,1536]{2,1,0:T(8,128)(2,1)S(1)}, u32[]{:S(2)}, u32[]{:S(2)}) collective-permute-start(bf16[4,32,1536]{2,1,0:T(8,128)(2,1)S(1)} %collective-permute-done.18.refs_1_), channel_id=1, source_target_pairs={{0,1},{1,0},{2,3},{3,2},{4,5},{5,4},{6,7},{7,6},{8,9},{9,8},{10,11... | collective-permute-start | bytes 1179656 | tf_op jit(solution)/shard_map/ppermute | solution.py:669
  72.0 2.6 %collective-permute-start.21 = (bf16[2,2,4,16,1536]{4,3,2,1,0:T(8,128)(2,1)S(1)}, bf16[2,2,4,16,1536]{4,3,2,1,0:T(8,128)(2,1)S(1)}, u32[]{:S(2)}, u32[]{:S(2)}) collective-permute-start(bf16[2,2,4,16,1536]{4,3,2,1,0:T(8,128)(2,1)S(1)} %get-tuple-element.229), channel_id=1, source_target_pairs={{0,1},{1,0},{2,3},{3,2},{4,5},{5,4},{6,7},{7,6},{8,9},{9,8},{10,11... | collective-permute-start | bytes 2359304 | tf_op jit(solution)/shard_map/ppermute | solution.py:669
  74.2 3.6 %collective-permute-start.22 = (bf16[2,2,4,16,1536]{4,3,2,1,0:T(8,128)(2,1)S(1)}, bf16[2,2,4,16,1536]{4,3,2,1,0:T(8,128)(2,1)S(1)}, u32[]{:S(2)}, u32[]{:S(2)}) collective-permute-start(bf16[2,2,4,16,1536]{4,3,2,1,0:T(8,128)(2,1)S(1)} %get-tuple-element.233), channel_id=1, source_target_pairs={{0,1},{1,0},{2,3},{3,2},{4,5},{5,4},{6,7},{7,6},{8,9},{9,8},{10,11... | collective-permute-start | bytes 2359304 | tf_op jit(solution)/shard_map/ppermute | solution.py:669
  74.7 11.2 %collective-permute-start.23 = (bf16[2,4,16,1536]{3,2,1,0:T(8,128)(2,1)S(1)}, bf16[2,4,16,1536]{3,2,1,0:T(8,128)(2,1)S(1)}, u32[]{:S(2)}, u32[]{:S(2)}) collective-permute-start(bf16[2,4,16,1536]{3,2,1,0:T(8,128)(2,1)S(1)} %fusion.1), channel_id=1, source_target_pairs={{0,2},{1,3},{2,0},{3,1},{4,6},{5,7},{6,4},{7,5},{8,10},{9,11},{10,... | collective-permute-start | bytes 1179656 | tf_op jit(solution)/shard_map/ppermute | solution.py:669
  77.9 10.9 %collective-permute-start.24 = (bf16[2,4,16,1536]{3,2,1,0:T(8,128)(2,1)S(1)}, bf16[2,4,16,1536]{3,2,1,0:T(8,128)(2,1)S(1)}, u32[]{:S(2)}, u32[]{:S(2)}) collective-permute-start(bf16[2,4,16,1536]{3,2,1,0:T(8,128)(2,1)S(1)} %fusion), channel_id=1, source_target_pairs={{0,4},{4,0},{8,12},{12,8},{16,20},{20,16},{24,28},{28,24},{1,5},{5... | collective-permute-start | bytes 1179656 | tf_op jit(solution)/shard_map/ppermute | solution.py:669
  88.8 2.8 %collective-permute-start.26 = (bf16[2,2,4,16,1152]{4,3,2,1,0:T(8,128)(2,1)S(1)}, bf16[2,2,4,16,1152]{4,3,2,1,0:T(8,128)(2,1)S(1)}, u32[]{:S(2)}, u32[]{:S(2)}) collective-permute-start(bf16[2,2,4,16,1152]{4,3,2,1,0:T(8,128)(2,1)S(1)} %get-tuple-element.254), channel_id=1, source_target_pairs={{0,1},{1,0},{2,3},{3,2},{4,5},{5,4},{6,7},{7,6},{8,9},{9,8},{10,11... | collective-permute-start | bytes 1769480 | tf_op jit(solution)/shard_map/ppermute | solution.py:669
  88.8 2.8 %collective-permute-start.25 = (bf16[2,2,4,16,1024]{4,3,2,1,0:T(8,128)(2,1)S(1)}, bf16[2,2,4,16,1024]{4,3,2,1,0:T(8,128)(2,1)S(1)}, u32[]{:S(2)}, u32[]{:S(2)}) collective-permute-start(bf16[2,2,4,16,1024]{4,3,2,1,0:T(8,128)(2,1)S(1)} %get-tuple-element.253), channel_id=1, source_target_pairs={{0,1},{1,0},{2,3},{3,2},{4,5},{5,4},{6,7},{7,6},{8,9},{9,8},{10,11... | collective-permute-start | bytes 1572872 | tf_op jit(solution)/shard_map/ppermute | solution.py:669
  91.7 14.0 %collective-permute-start.28 = (bf16[2,4,16,1152]{3,2,1,0:T(8,128)(2,1)S(1)}, bf16[2,4,16,1152]{3,2,1,0:T(8,128)(2,1)S(1)}, u32[]{:S(2)}, u32[]{:S(2)}) collective-permute-start(bf16[2,4,16,1152]{3,2,1,0:T(8,128)(2,1)S(1)} %fusion.2), channel_id=1, source_target_pairs={{0,2},{1,3},{2,0},{3,1},{4,6},{5,7},{6,4},{7,5},{8,10},{9,11},{10,... | collective-permute-start | bytes 884744 | tf_op jit(solution)/shard_map/ppermute | solution.py:669
  93.3 12.3 %collective-permute-start.27 = (bf16[2,4,16,1024]{3,2,1,0:T(8,128)(2,1)S(1)}, bf16[2,4,16,1024]{3,2,1,0:T(8,128)(2,1)S(1)}, u32[]{:S(2)}, u32[]{:S(2)}) collective-permute-start(bf16[2,4,16,1024]{3,2,1,0:T(8,128)(2,1)S(1)} %fusion.3), channel_id=1, source_target_pairs={{0,4},{4,0},{8,12},{12,8},{16,20},{20,16},{24,28},{28,24},{1,5},{5... | collective-permute-start | bytes 786440 | tf_op jit(solution)/shard_map/ppermute | solution.py:669
  94.0 11.0 %collective-permute-start.29 = (bf16[4,16,1536]{2,1,0:T(8,128)(2,1)S(1)}, bf16[4,16,1536]{2,1,0:T(8,128)(2,1)S(1)}, u32[]{:S(2)}, u32[]{:S(2)}) collective-permute-start(bf16[4,16,1536]{2,1,0:T(8,128)(2,1)S(1)} %get-tuple-element.258), channel_id=1, source_target_pairs={{0,2},{1,3},{2,0},{3,1},{4,6},{5,7},{6,4},{7,5},{8,10},{9,11},{10,... | collective-permute-start | bytes 589832 | tf_op jit(solution)/shard_map/ppermute | solution.py:669
  94.5 11.2 %collective-permute-start.30 = (bf16[4,16,1536]{2,1,0:T(8,128)(2,1)S(1)}, bf16[4,16,1536]{2,1,0:T(8,128)(2,1)S(1)}, u32[]{:S(2)}, u32[]{:S(2)}) collective-permute-start(bf16[4,16,1536]{2,1,0:T(8,128)(2,1)S(1)} %get-tuple-element.259), channel_id=1, source_target_pairs={{0,4},{4,0},{8,12},{12,8},{16,20},{20,16},{24,28},{28,24},{1,5},{5... | collective-permute-start | bytes 589832 | tf_op jit(solution)/shard_map/ppermute | solution.py:669
  105.8 5.6 %collective-permute-start.32 = (bf16[4,16,1152]{2,1,0:T(8,128)(2,1)S(1)}, bf16[4,16,1152]{2,1,0:T(8,128)(2,1)S(1)}, u32[]{:S(2)}, u32[]{:S(2)}) collective-permute-start(bf16[4,16,1152]{2,1,0:T(8,128)(2,1)S(1)} %get-tuple-element.281), channel_id=1, source_target_pairs={{0,4},{4,0},{8,12},{12,8},{16,20},{20,16},{24,28},{28,24},{1,5},{5... | collective-permute-start | bytes 442376 | tf_op jit(solution)/shard_map/ppermute | solution.py:669
  106.4 5.0 %collective-permute-start.31 = (bf16[4,16,1024]{2,1,0:T(8,128)(2,1)S(1)}, bf16[4,16,1024]{2,1,0:T(8,128)(2,1)S(1)}, u32[]{:S(2)}, u32[]{:S(2)}) collective-permute-start(bf16[4,16,1024]{2,1,0:T(8,128)(2,1)S(1)} %get-tuple-element.279), channel_id=1, source_target_pairs={{0,2},{1,3},{2,0},{3,1},{4,6},{5,7},{6,4},{7,5},{8,10},{9,11},{10,... | collective-permute-start | bytes 393224 | tf_op jit(solution)/shard_map/ppermute | solution.py:669
  111.8 28.0 %collective-permute-start.42 = (bf16[2,2,2,128,512]{4,3,2,1,0:T(8,128)(2,1)S(1)}, bf16[2,2,2,128,512]{4,3,2,1,0:T(8,128)(2,1)S(1)}, u32[]{:S(2)}, u32[]{:S(2)}) collective-permute-start(bf16[2,2,2,128,512]{4,3,2,1,0:T(8,128)(2,1)S(1)} %get-tuple-element.308), channel_id=1, source_target_pairs={{0,2},{1,3},{2,0},{3,1},{4,6},{5,7},{6,4},{7,5},{8,10},{9,11},{10,... | collective-permute-start | bytes 3145736 | tf_op jit(solution)/shard_map/ppermute | solution.py:669
  112.7 12.1 %collective-permute-start.34 = (bf16[16,5248]{1,0:T(8,128)(2,1)S(1)}, bf16[16,5248]{1,0:T(8,128)(2,1)S(1)}, u32[]{:S(2)}, u32[]{:S(2)}) collective-permute-start(bf16[16,5248]{1,0:T(8,128)(2,1)S(1)} %get-tuple-element.284), channel_id=1, source_target_pairs={{0,16},{4,20},{8,24},{12,28},{16,0},{20,4},{24,8},{28,12},{1,17},{... | collective-permute-start | bytes 503816 | tf_op jit(solution)/shard_map/ppermute | solution.py:669
  113.7 11.1 %collective-permute-start.35 = (bf16[16,5248]{1,0:T(8,128)(2,1)S(1)}, bf16[16,5248]{1,0:T(8,128)(2,1)S(1)}, u32[]{:S(2)}, u32[]{:S(2)}) collective-permute-start(bf16[16,5248]{1,0:T(8,128)(2,1)S(1)} %get-tuple-element.285), channel_id=1, source_target_pairs={{0,24},{4,28},{8,16},{12,20},{16,8},{20,12},{24,0},{28,4},{1,25},{... | collective-permute-start | bytes 503816 | tf_op jit(solution)/shard_map/ppermute | solution.py:669
  115.2 10.8 %collective-permute-start.33 = (bf16[16,5248]{1,0:T(8,128)(2,1)S(1)}, bf16[16,5248]{1,0:T(8,128)(2,1)S(1)}, u32[]{:S(2)}, u32[]{:S(2)}) collective-permute-start(bf16[16,5248]{1,0:T(8,128)(2,1)S(1)} %get-tuple-element.283), channel_id=1, source_target_pairs={{0,8},{4,12},{8,0},{12,4},{16,24},{20,28},{24,16},{28,20},{1,9},{5... | collective-permute-start | bytes 503816 | tf_op jit(solution)/shard_map/ppermute | solution.py:669
  126.3 13.4 %collective-permute-start.41 = (bf16[16,5248]{1,0:T(8,128)(2,1)S(1)}, bf16[16,5248]{1,0:T(8,128)(2,1)S(1)}, u32[]{:S(2)}, u32[]{:S(2)}) collective-permute-start(bf16[16,5248]{1,0:T(8,128)(2,1)S(1)} %get-tuple-element.306.refs_0_.own_ref), channel_id=1, source_target_pairs={{0,2},{1,3},{2,0},{3,1},{4,6},{5,7},{6,4},{7,5},{8,10},{9,11},{10,... | collective-permute-start | bytes 503816 | tf_op jit(solution)/shard_map/ppermute | solution.py:669
  127.0 18.1 %copy-start.1 = (f32[256]{0:T(256)S(1)}, f32[256]{0:T(256)}, u32[]{:S(2)}) copy-start(f32[256]{0:T(256)} %param.38) | copy-start | bytes 3076
  127.0 18.1 %copy-start.2 = (f32[64]{0:T(128)S(1)}, f32[64]{0:T(128)}, u32[]{:S(2)}) copy-start(f32[64]{0:T(128)} %param.42) | copy-start | bytes 772
  127.0 18.1 %copy-start.3 = (f32[256]{0:T(256)S(1)}, f32[256]{0:T(256)}, u32[]{:S(2)}) copy-start(f32[256]{0:T(256)} %param.39) | copy-start | bytes 3076
  127.0 18.1 %copy-start.4 = (f32[256]{0:T(256)S(1)}, f32[256]{0:T(256)}, u32[]{:S(2)}) copy-start(f32[256]{0:T(256)} %param.40) | copy-start | bytes 3076
  127.0 18.1 %copy-start.5 = (f32[256]{0:T(256)S(1)}, f32[256]{0:T(256)}, u32[]{:S(2)}) copy-start(f32[256]{0:T(256)} %param.41) | copy-start | bytes 3076
  127.0 18.1 %copy-start.6 = (f32[64]{0:T(128)S(1)}, f32[64]{0:T(128)}, u32[]{:S(2)}) copy-start(f32[64]{0:T(128)} %param.43) | copy-start | bytes 772
  127.0 18.1 %copy-start.7 = (f32[64]{0:T(128)S(1)}, f32[64]{0:T(128)}, u32[]{:S(2)}) copy-start(f32[64]{0:T(128)} %param.44) | copy-start | bytes 772
  127.0 18.1 %copy-start.8 = (f32[64]{0:T(128)S(1)}, f32[64]{0:T(128)}, u32[]{:S(2)}) copy-start(f32[64]{0:T(128)} %param.45) | copy-start | bytes 772
  127.0 1.2 collective-permute-start.36
  128.3 3.6 %collective-permute-start.37 = (f32[8,128]{1,0:T(8,128)S(1)}, f32[8,128]{1,0:T(8,128)S(1)}, u32[]{:S(2)}, u32[]{:S(2)}) collective-permute-start(f32[8,128]{1,0:T(8,128)S(1)} %add.32.refs_0_), channel_id=1, source_target_pairs={{0,4},{4,0},{8,12},{12,8},{16,20},{20,16},{24,28},{28,24},{1,5},{5... | collective-permute-start | bytes 12296 | tf_op jit(solution)/shard_map/ppermute | solution.py:669
  131.9 5.4 %collective-permute-start.40 = (f32[8,128]{1,0:T(8,128)S(1)}, f32[8,128]{1,0:T(8,128)S(1)}, u32[]{:S(2)}, u32[]{:S(2)}) collective-permute-start(f32[8,128]{1,0:T(8,128)S(1)} %add.33.refs_0_), channel_id=1, source_target_pairs={{0,24},{4,28},{8,16},{12,20},{16,8},{20,12},{24,0},{28,4},{1,25},{... | collective-permute-start | bytes 12296 | tf_op jit(solution)/shard_map/ppermute | solution.py:669
  134.0 4.5 %collective-permute-start.39 = (f32[8,128]{1,0:T(8,128)S(1)}, f32[8,128]{1,0:T(8,128)S(1)}, u32[]{:S(2)}, u32[]{:S(2)}) collective-permute-start(f32[8,128]{1,0:T(8,128)S(1)} %add.33.refs_0_), channel_id=1, source_target_pairs={{0,16},{4,20},{8,24},{12,28},{16,0},{20,4},{24,8},{28,12},{1,17},{... | collective-permute-start | bytes 12296 | tf_op jit(solution)/shard_map/ppermute | solution.py:669
  136.2 3.6 %collective-permute-start.38 = (f32[8,128]{1,0:T(8,128)S(1)}, f32[8,128]{1,0:T(8,128)S(1)}, u32[]{:S(2)}, u32[]{:S(2)}) collective-permute-start(f32[8,128]{1,0:T(8,128)S(1)} %add.33.refs_0_), channel_id=1, source_target_pairs={{0,8},{4,12},{8,0},{12,4},{16,24},{20,28},{24,16},{28,20},{1,9},{5... | collective-permute-start | bytes 12296 | tf_op jit(solution)/shard_map/ppermute | solution.py:669
  139.8 3.4 %collective-permute-start.45 = (bf16[2,2,2,128,512]{4,3,2,1,0:T(8,128)(2,1)S(1)}, bf16[2,2,2,128,512]{4,3,2,1,0:T(8,128)(2,1)S(1)}, u32[]{:S(2)}, u32[]{:S(2)}) collective-permute-start(bf16[2,2,2,128,512]{4,3,2,1,0:T(8,128)(2,1)S(1)} %collective-permute-done.42.side_ref), channel_id=1, source_target_pairs={{0,1},{1,0},{2,3},{3,2},{4,5},{5,4},{6,7},{7,6},{8,9},{9,8},{10,11... | collective-permute-start | bytes 3145736 | tf_op jit(solution)/shard_map/ppermute | solution.py:669
  139.8 3.4 %collective-permute-start.44 = (bf16[2,2,128,512]{3,2,1,0:T(8,128)(2,1)S(1)}, bf16[2,2,128,512]{3,2,1,0:T(8,128)(2,1)S(1)}, u32[]{:S(2)}, u32[]{:S(2)}) collective-permute-start(bf16[2,2,128,512]{3,2,1,0:T(8,128)(2,1)S(1)} %get-tuple-element.317), channel_id=1, source_target_pairs={{0,1},{1,0},{2,3},{3,2},{4,5},{5,4},{6,7},{7,6},{8,9},{9,8},{10,11... | collective-permute-start | bytes 1572872 | tf_op jit(solution)/shard_map/ppermute | solution.py:669
  140.3 4.7 %collective-permute-start.46 = (bf16[2,16,5248]{2,1,0:T(8,128)(2,1)S(1)}, bf16[2,16,5248]{2,1,0:T(8,128)(2,1)S(1)}, u32[]{:S(2)}, u32[]{:S(2)}) collective-permute-start(bf16[2,16,5248]{2,1,0:T(8,128)(2,1)S(1)} %stack.7), channel_id=1, source_target_pairs={{0,1},{1,0},{2,3},{3,2},{4,5},{5,4},{6,7},{7,6},{8,9},{9,8},{10,11... | collective-permute-start | bytes 1007624 | tf_op jit(solution)/shard_map/ppermute | solution.py:669
  140.5 4.5 %collective-permute-start.43 = (f32[8,128]{1,0:T(8,128)S(1)}, f32[8,128]{1,0:T(8,128)S(1)}, u32[]{:S(2)}, u32[]{:S(2)}) collective-permute-start(f32[8,128]{1,0:T(8,128)S(1)} %add.34.refs_0_), channel_id=1, source_target_pairs={{0,2},{1,3},{2,0},{3,1},{4,6},{5,7},{6,4},{7,5},{8,10},{9,11},{10,... | collective-permute-start | bytes 12296 | tf_op jit(solution)/shard_map/ppermute | solution.py:669

commit v5 on v4

--- a/solution.py
+++ b/solution.py
@@ -287,14 +287,22 @@
     return read
 
 
-def content_up_kernel(tree, normed_ref, *refs):
-    sources, (content_ref, slope_ref, weight, sem) = refs[:-4], refs[-4:]
-    tokens = normed_ref.shape[0] * normed_ref.shape[1]
-    if tree:
-        fetch_weights(sources, [(0, 0, HALF, weight, 64, 32, 0, sem)], tree)
+def content_up_kernel(tree, members, normed_ref, own_ref, core_ref, side_ref, forward_ref, *refs):
+    parts = [core_ref.at[1], side_ref.at[0, 1], forward_ref.at[1, 1]]
+    sources, (content_ref, slope_ref, weight, cots_turned, cots, sems) = refs[:-6], refs[-6:]
+    narrow = lax.axis_index("narrow")
+    rows_here, quarter = core_ref.shape[1:3]
+    tokens = rows_here * ROW
+    if tree:
+        fetch_weights(sources, [(0, 0, HALF, weight, 64, 32, 0, sems.at[0])], tree)
     else:
-        pltpu.make_async_copy(sources[0], weight, sem).start()
-    wait_weights([(weight, sem)])
+        pltpu.make_async_copy(sources[0], weight, sems.at[0]).start()
+    for r in range(rows_here):
+        for j in range(members):
+            source = own_ref.at[narrow * rows_here + r] if j == 0 else parts[j - 1].at[r]
+            place = run(r * ROW + (narrow ^ j) * quarter, quarter)
+            pltpu.make_async_copy(source, cots.at[place, :], sems.at[1]).start()
+    wait_weights([(weight, sems.at[0])])
 
     def do_channels(k, carry):
         channels = run(k * WIDTH, WIDTH)
@@ -308,31 +316,25 @@
         return carry
 
     lax.fori_loop(0, HALF // WIDTH, do_channels, 0)
-
-
-def content_down_kernel(
-    tree, count, members, lens_ref, content_ref, slope_ref, mixed_ref, own_ref, core_ref, side_ref, forward_ref, *refs
-):
-    parts = [core_ref.at[1], side_ref.at[0, 1], forward_ref.at[1, 1]]
+    wait_weights([(cots, sems.at[1])])
+    cots_turned[...] = cots[...].T
+
+
+def content_down_kernel(tree, count, lens_ref, content_ref, slope_ref, mixed_ref, cots, cots_turned, *refs):
     sources = refs[:count]
     gated_ref, grad_ref, grad_mixed_ref, bias_ref, shrink = refs[count : count + 5]
     raws = refs[count + 5 : count + (8 if tree else 6)]
-    cots, sums, tall_sum, sems = refs[count + 5 + len(raws) :]
+    sums, tall_sum, sem = refs[count + 5 + len(raws) :]
     narrow = lax.axis_index("narrow")
-    rows_here, quarter = core_ref.shape[1:3]
+    rows_here = content_ref.shape[0]
     tokens = rows_here * ROW
 
     if tree:
-        fetch_weights(sources, [(0, k * D, D, shrink, 192, 96, k * 32, sems.at[0]) for k in range(3)], tree)
+        fetch_weights(sources, [(0, k * D, D, shrink, 192, 96, k * 32, sem) for k in range(3)], tree)
     else:
-        pltpu.make_async_copy(sources[0], shrink, sems.at[0]).start()
-    for r in range(rows_here):
-        for j in range(members):
-            source = own_ref.at[narrow * rows_here + r] if j == 0 else parts[j - 1].at[r]
-            place = run(r * ROW + (narrow ^ j) * quarter, quarter)
-            pltpu.make_async_copy(source, cots.at[place, :], sems.at[1]).start()
+        pltpu.make_async_copy(sources[0], shrink, sem).start()
     sums[...] = jnp.zeros_like(sums)
-    wait_weights([(shrink, sems.at[0]), (cots, sems.at[1])])
+    wait_weights([(shrink, sem)])
 
     def do_channels(k, carry):
         channels = run(k * WIDTH, WIDTH)
@@ -349,7 +351,11 @@
             grad_mixed_ref[r, here, channels] = grad_mixed
             total = grad_mixed.astype(F32)
             sums[p : p + PIECE, :] += total[:, :LANES] + total[:, LANES:]
-        tall_sum[channels, :] = dot(gated_ref[:, :, channels].reshape(tokens, WIDTH), cots[...], ((0,), (0,)))
+        product = dot(cots_turned[...], gated_ref[:, :, channels].reshape(tokens, WIDTH))
+        if tree:
+            tall_sum[channels, :] = product.astype(BF16).T
+        else:
+            raws[0][channels, :] = product.T
         return carry
 
     lax.fori_loop(0, HALF // WIDTH, do_channels, 0)
@@ -360,8 +366,6 @@
     if tree:
         for j in range(3):
             emit_blocks("y", reader(tall_sum, 192, 48, j * BLOCK, slice(0, D)), D, j * D, *raws)
-    else:
-        raws[0][...] = tall_sum[...]
 
 
 def content_sum_kernel(tree, normed_ref, grad_ref, *refs):
@@ -858,13 +862,13 @@
     normed_late = normed
     if tree:
         expand_pieces[3], normed_late, _ = lax.optimization_barrier((expand_pieces[3], normed, mixed))
-    content, content_slope, content_weight = call_kernel(
-        functools.partial(content_up_kernel, tree),
+    content, content_slope, content_weight, cots_turned, cots = call_kernel(
+        functools.partial(content_up_kernel, tree, narrow_size),
         "content_up",
-        [normed_late, *expand_pieces],
-        [None] + [anywhere] * len(expand_pieces),
-        [low_half, low_half, weight_type],
-        [dma(())],
+        [normed_late, cotangent, core_came, side_came, forward_came, *expand_pieces],
+        [None, stored] + [anywhere] * (narrow_size - 1 + len(expand_pieces)),
+        [low_half, low_half, weight_type, shape((D, tokens), BF16), shape((tokens, D), BF16)],
+        [dma((2,))],
         product // 64,
     )
     if tree:
@@ -881,18 +885,13 @@
         return [shape(size, F32) for size in plain]
 
     gated, content_grad, grad_mixed, bias_part, shrink_low, *shrink_raws = call_kernel(
-        functools.partial(content_down_kernel, tree, len(shrink_pieces), narrow_size),
+        functools.partial(content_down_kernel, tree, len(shrink_pieces)),
         "content_down",
-        [doc_lengths, content, content_slope, mixed, cotangent, core_came, side_came, forward_came, *shrink_pieces],
-        [smem, None, None, None, stored] + [anywhere] * (narrow_size - 1 + len(shrink_pieces)),
+        [doc_lengths, content, content_slope, mixed, cots, cots_turned, *shrink_pieces],
+        [smem] + [None] * 5 + [anywhere] * len(shrink_pieces),
         [low_half, low_half, low_half, shape((ROW, 128), F32), shape((HALF, D), BF16)]
         + raw_outputs((HALF,), ((HALF, D),)),
-        [
-            pltpu.VMEM((tokens, D), BF16),
-            pltpu.VMEM((tokens, 128), F32),
-            pltpu.VMEM((HALF, D), F32),
-            dma((2,)),
-        ],
+        [pltpu.VMEM((tokens, 128), F32), pltpu.VMEM((HALF, D), BF16), dma(())],
         product // 64,
     )
     if tree:

time: 149 us -> 150 us (level)
  transfers between devices with their start and end apart: 47 -> 47, of which waited for: 21 -> 20; matrix products, arithmetic and copies ran while one was open for 0% -> 0% of each run, Pallas kernels for 28% -> 29%
where the time goes in v5:
time: 150 us; the launch traced here: 149 us
  Pallas kernels  57.3 us (38%)
  waiting for transfers between devices  47.2 us (31%)
  starting transfers between devices  43.3 us (29%)
    pallas_call x28, Pallas kernels, call_kernel(): pl.pallas_call(kernel, name=name, in_specs=in_specs, out_specs=specs, out...  57.3 us
    ppermute x47, waiting for transfers between devices, swap_with(): return lax.ppermute(value, axis, [(i, i ^ bit) for i in range(size)])  47.2 us
    ppermute x47, starting transfers between devices, swap_with(): return lax.ppermute(value, axis, [(i, i ^ bit) for i in range(size)])  43.3 us
  transfers between devices with their start and end apart: 47, of which 20 were waited for; matrix products, arithmetic and copies ran while one was open for 0% of the time, Pallas kernels for 29%

profile of v5, /device:TPU:0, one launch (start us, length us, event | category | flops | bytes accessed | tf_op | source)
XLA Modules:
  0.0 149.4 jit_solution(3152789901534791804)
XLA Ops:
  0.7 1.0 pack_first.1.refs_0_
  1.7 1.4 cut.1
  3.1 3.0 %collective-permute-start.7 = (bf16[2,2,2,128,512]{4,3,2,1,0:T(8,128)(2,1)S(1)}, bf16[2,2,2,128,512]{4,3,2,1,0:T(8,128)(2,1)S(1)}, u32[]{:S(2)}, u32[]{:S(2)}) collective-permute-start(bf16[2,2,2,128,512]{4,3,2,1,0:T(8,128)(2,1)S(1)} %get-tuple-element.200), channel_id=1, source_target_pairs={{0,2},{1,3},{2,0},{3,1},{4,6},{5,7},{6,4},{7,5},{8,10},{9,11},{10,... | collective-permute-start | bytes 3145736 | tf_op jit(solution)/shard_map/ppermute | solution.py:673
  6.1 3.6 %collective-permute-start.2 = (bf16[32,2176]{1,0:T(8,128)(2,1)S(1)}, bf16[32,2176]{1,0:T(8,128)(2,1)S(1)}, u32[]{:S(2)}, u32[]{:S(2)}) collective-permute-start(bf16[32,2176]{1,0:T(8,128)(2,1)S(1)} %pack_first.1.refs_0_), channel_id=1, source_target_pairs={{0,24},{4,28},{8,16},{12,20},{16,8},{20,12},{24,0},{28,4},{1,25},{... | collective-permute-start | bytes 417800 | tf_op jit(solution)/shard_map/ppermute | solution.py:673
  9.7 0.8 collective-permute-start
  10.5 1.1 pack_second.1
  11.6 2.9 %collective-permute-done.2.refs_3_ = bf16[32,2176]{1,0:T(8,128)(2,1)S(1)} collective-permute-done((bf16[32,2176]{1,0:T(8,128)(2,1)S(1)}, bf16[32,2176]{1,0:T(8,128)(2,1)S(1)}, u32[]{:S(2)}, u32[]{:S(2)}) %collective-permute-start.2) | collective-permute-done | bytes 139296 | tf_op jit(solution)/shard_map/ppermute | solution.py:673
  14.5 7.7 %collective-permute-done.1.refs_2_ = bf16[32,2176]{1,0:T(8,128)(2,1)S(1)} collective-permute-done((bf16[32,2176]{1,0:T(8,128)(2,1)S(1)}, bf16[32,2176]{1,0:T(8,128)(2,1)S(1)}, u32[]{:S(2)}, u32[]{:S(2)}) %collective-permute-start.1) | collective-permute-done | bytes 139296 | tf_op jit(solution)/shard_map/ppermute | solution.py:673
  22.2 1.6 %collective-permute-start.11 = (bf16[4,32,2176]{2,1,0:T(8,128)(2,1)S(1)}, bf16[4,32,2176]{2,1,0:T(8,128)(2,1)S(1)}, u32[]{:S(2)}, u32[]{:S(2)}) collective-permute-start(bf16[4,32,2176]{2,1,0:T(8,128)(2,1)S(1)} %stack.4.refs_0_.refs_4_), channel_id=1, source_target_pairs={{0,4},{4,0},{8,12},{12,8},{16,20},{20,16},{24,28},{28,24},{1,5},{5... | collective-permute-start | bytes 1671176 | tf_op jit(solution)/shard_map/ppermute | solution.py:673
  23.8 2.5 %collective-permute-start.6 = (bf16[32,1536]{1,0:T(8,128)(2,1)S(1)}, bf16[32,1536]{1,0:T(8,128)(2,1)S(1)}, u32[]{:S(2)}, u32[]{:S(2)}) collective-permute-start(bf16[32,1536]{1,0:T(8,128)(2,1)S(1)} %get-tuple-element.206.refs_0_), channel_id=1, source_target_pairs={{0,24},{4,28},{8,16},{12,20},{16,8},{20,12},{24,0},{28,4},{1,25},{... | collective-permute-start | bytes 294920 | tf_op jit(solution)/shard_map/ppermute | solution.py:673
  26.3 1.9 %collective-permute-start.4 = (bf16[32,1536]{1,0:T(8,128)(2,1)S(1)}, bf16[32,1536]{1,0:T(8,128)(2,1)S(1)}, u32[]{:S(2)}, u32[]{:S(2)}) collective-permute-start(bf16[32,1536]{1,0:T(8,128)(2,1)S(1)} %get-tuple-element.206.refs_0_), channel_id=1, source_target_pairs={{0,8},{4,12},{8,0},{12,4},{16,24},{20,28},{24,16},{28,20},{1,9},{5... | collective-permute-start | bytes 294920 | tf_op jit(solution)/shard_map/ppermute | solution.py:673
  28.2 3.2 %collective-permute-done.6.refs_3_ = bf16[32,1536]{1,0:T(8,128)(2,1)S(1)} collective-permute-done((bf16[32,1536]{1,0:T(8,128)(2,1)S(1)}, bf16[32,1536]{1,0:T(8,128)(2,1)S(1)}, u32[]{:S(2)}, u32[]{:S(2)}) %collective-permute-start.6) | collective-permute-done | bytes 98336 | tf_op jit(solution)/shard_map/ppermute | solution.py:673
  31.4 2.6 %collective-permute-done.5.refs_2_ = bf16[32,1536]{1,0:T(8,128)(2,1)S(1)} collective-permute-done((bf16[32,1536]{1,0:T(8,128)(2,1)S(1)}, bf16[32,1536]{1,0:T(8,128)(2,1)S(1)}, u32[]{:S(2)}, u32[]{:S(2)}) %collective-permute-start.5) | collective-permute-done | bytes 98336 | tf_op jit(solution)/shard_map/ppermute | solution.py:673
  34.1 0.5 collective-permute-start.14
  34.6 2.0 %collective-permute-done.11.refs_1_.refs_5_ = bf16[4,32,2176]{2,1,0:T(8,128)(2,1)S(1)} collective-permute-done((bf16[4,32,2176]{2,1,0:T(8,128)(2,1)S(1)}, bf16[4,32,2176]{2,1,0:T(8,128)(2,1)S(1)}, u32[]{:S(2)}, u32[]{:S(2)}) %collective-permute-start.11) | collective-permute-done | bytes 557088 | tf_op jit(solution)/shard_map/ppermute | solution.py:673
  36.6 1.5 collective-permute-start.12
  38.0 2.5 %collective-permute-start.10 = (bf16[32,1536]{1,0:T(8,128)(2,1)S(1)}, bf16[32,1536]{1,0:T(8,128)(2,1)S(1)}, u32[]{:S(2)}, u32[]{:S(2)}) collective-permute-start(bf16[32,1536]{1,0:T(8,128)(2,1)S(1)} %get-tuple-element.210.refs_0_), channel_id=1, source_target_pairs={{0,24},{4,28},{8,16},{12,20},{16,8},{20,12},{24,0},{28,4},{1,25},{... | collective-permute-start | bytes 294920 | tf_op jit(solution)/shard_map/ppermute | solution.py:673
  40.5 1.9 %collective-permute-start.8 = (bf16[32,1536]{1,0:T(8,128)(2,1)S(1)}, bf16[32,1536]{1,0:T(8,128)(2,1)S(1)}, u32[]{:S(2)}, u32[]{:S(2)}) collective-permute-start(bf16[32,1536]{1,0:T(8,128)(2,1)S(1)} %get-tuple-element.210.refs_0_), channel_id=1, source_target_pairs={{0,8},{4,12},{8,0},{12,4},{16,24},{20,28},{24,16},{28,20},{1,9},{5... | collective-permute-start | bytes 294920 | tf_op jit(solution)/shard_map/ppermute | solution.py:673
  42.4 7.7 %gating.1 = (bf16[2,512,512]{2,1,0:T(8,128)(2,1)S(1)}, bf16[2,512,512]{2,1,0:T(8,128)(2,1)S(1)}, f32[2,512,128]{2,1,0:T(8,128)S(1)}, bf16[2,512,1536]{2,1,0:T(8,...) custom-call(bf16[8,128,512]{2,1,0:T(8,128)(2,1)} %refs_13_, ...), custom_call_target="tpu_custom_call" | custom-call | flops 25165824 | bytes 50331 | tf_op jit(solution)/shard_map/gating/pallas_call | solution.py:659
  50.8 0.6 collective-permute-start.18
  51.4 2.5 %mixing.1.mixed_ref = bf16[2,512,1536]{2,1,0:T(8,128)(2,1)S(1)} custom-call(s32[8,5]{1,0:T(8,128)S(1)} %copy-done, bf16[512,512]{1,0:T(8,128)(2,1)S(1)} %get-tuple-element.219.spatial_ref, bf16[2,512,1536]{2,1,0:T(8,128)(2,1)S(1)} %get-tuple-element.220.gate_ref, f32[512,128]{1,0:T(8,128)S(1)} %get-tuple-element.225.bias_col), custom_call_target="tpu_custom_call" | custom-call | flops 25165824 | bytes 50331 | tf_op jit(solution)/shard_map/mixing/pallas_call | solution.py:659
  53.9 8.2 %content_up.1 = (bf16[2,512,1536]{2,1,0:T(8,128)(2,1)S(1)}, bf16[2,512,1536]{2,1,0:T(8,128)(2,1)S(1)}, bf16[512,1536]{1,0:T(8,128)(2,1)S(1)}, bf16[512,1024]{1,0:T(8,128)(2,1)S(1)}, bf16[1024,512]{1,0:T(8,128)(2,1)S(1)}) custom-call(bf16[2,512,512]{2,1,0:T(8,128)(2,1)S(1)} %get-tuple-element.243.normed_ref, bf16[8,128,512]{2,1,0:T(8,128)(2,1)} %refs_12_, ...), custom_call_target="tpu_custom_call" | custom-call | flops 25165824 | bytes 50331 | tf_op jit(solution)/shard_map/content_up/pallas_call | solution.py:659
  62.1 0.6 collective-permute-start.20
  62.7 1.3 collective-permute-done.20.refs_3_
  64.0 7.0 %content_down.1 = (bf16[2,512,1536]{2,1,0:T(8,128)(2,1)S(1)}, bf16[2,512,1536]{2,1,0:T(8,128)(2,1)S(1)}, bf16[2,512,1536]{2,1,0:T(8,128)(2,1)S(1)}, f32[512,128]...) custom-call(s32[8,5]{1,0:T(8,128)S(1)} %copy-done, ...), custom_call_target="tpu_custom_call" | custom-call | flops 25165824 | bytes 50331 | tf_op jit(solution)/shard_map/content_down/pallas_call | solution.py:659
  71.4 1.9 %content_sum.1 = (bf16[2,4,16,1536]{3,2,1,0:T(8,128)(2,1)S(1)}, bf16[2,4,16,1536]{3,2,1,0:T(8,128)(2,1)S(1)}, bf16[2,2,4,16,1536]{4,3,2,1,0:T(8,128)(2,1)S(1)}) custom-call(bf16[2,512,512]{2,1,0:T(8,128)(2,1)S(1)} %get-tuple-element.243.normed_ref, bf16[2,512,1536]{2,1,0:T(8,128)(2,1)S(1)} %get-tuple-element.234.grad_ref.content_grad_ref), custom_call_target="tpu_custom_call" | custom-call | flops 25165824 | bytes 50331 | tf_op jit(solution)/shard_map/content_sum/pallas_call | solution.py:659
  73.7 0.6 collective-permute-start.23
  74.2 2.5 %spatial_sum.1.square_ref = f32[512,512]{1,0:T(8,128)S(1)} custom-call(s32[8,5]{1,0:T(8,128)S(1)} %copy-done, bf16[2,512,1536]{2,1,0:T(8,128)(2,1)S(1)} %get-tuple-element.245.grad_mixed_ref, bf16[2,512,1536]{2,1,0:T(8,128)(2,1)S(1)} %get-tuple-element.220.gate_ref), custom_call_target="tpu_custom_call" | custom-call | flops 25165824 | bytes 50331 | tf_op jit(solution)/shard_map/spatial_sum/pallas_call | solution.py:659
  76.9 1.6 %collective-permute-start.24 = (bf16[2,4,16,1536]{3,2,1,0:T(8,128)(2,1)S(1)}, bf16[2,4,16,1536]{3,2,1,0:T(8,128)(2,1)S(1)}, u32[]{:S(2)}, u32[]{:S(2)}) collective-permute-start(bf16[2,4,16,1536]{3,2,1,0:T(8,128)(2,1)S(1)} %fusion), channel_id=1, source_target_pairs={{0,4},{4,0},{8,12},{12,8},{16,20},{20,16},{24,28},{28,24},{1,5},{5... | collective-permute-start | bytes 1179656 | tf_op jit(solution)/shard_map/ppermute | solution.py:673
  78.4 6.6 %gate_back.1 = (bf16[2,512,1536]{2,1,0:T(8,128)(2,1)S(1)}, f32[8,16,128]{2,1,0:T(8,128)S(1)}) custom-call(s32[8,5]{1,0:T(8,128)S(1)} %copy-done, bf16[2,512,1536]{2,1,0:T(8,128)(2,1)S(1)} %get-tuple-element.245.grad_mixed_ref, bf16[2,512,1536]{2,1,0:T(8,128)(2,1)S(1)} %get-tuple-element.220.gate_ref, bf16[2,512,1536]{2,1,0:T(8,128)(2,1)S(1)} %get-tuple-element.246.slope_ref, ...), custom_call_target="tpu_custom_call" | custom-call | flops 25165824 | bytes 50331 | tf_op jit(solution)/shard_map/gate_back/pallas_call | solution.py:659
  85.1 2.0 %gate_sum.1 = (bf16[2,4,16,1024]{3,2,1,0:T(8,128)(2,1)S(1)}, bf16[2,4,16,1024]{3,2,1,0:T(8,128)(2,1)S(1)}, bf16[2,2,4,16,1024]{4,3,2,1,0:T(8,128)(2,1)S(1)}, bf1...) custom-call(bf16[2,512,512]{2,1,0:T(8,128)(2,1)S(1)} %get-tuple-elem, ...), custom_call_target="tpu_custom_call" | custom-call | flops 25165824 | bytes 50331 | tf_op jit(solution)/shard_map/gate_sum/pallas_call | solution.py:659
  87.1 0.9 collective-permute-done.24.refs_2_
  88.0 0.5 collective-permute-start.25
  88.7 1.9 %layer.1 = (bf16[2,128,512]{2,1,0:T(8,128)(2,1)S(1)}, bf16[2,128,512]{2,1,0:T(8,128)(2,1)S(1)}, bf16[2,2,128,512]{3,2,1,0:T(8,128)(2,1)S(1)}) custom-call(bf16[2,512,1536]{2,1,0:T(8,128)(2,1)S(1)} %get-tuple-element.264.gated_ref, bf16[1536,512]{1,0:T(8,128)(2,1)S(1)} %get-tuple-element.265.shrink), custom_call_target="tpu_custom_call" | custom-call | flops 25165824 | bytes 50331 | tf_op jit(solution)/shard_map/layer/pallas_call | solution.py:659
  90.9 1.6 %collective-permute-start.28 = (bf16[2,4,16,1152]{3,2,1,0:T(8,128)(2,1)S(1)}, bf16[2,4,16,1152]{3,2,1,0:T(8,128)(2,1)S(1)}, u32[]{:S(2)}, u32[]{:S(2)}) collective-permute-start(bf16[2,4,16,1152]{3,2,1,0:T(8,128)(2,1)S(1)} %fusion.2), channel_id=1, source_target_pairs={{0,2},{1,3},{2,0},{3,1},{4,6},{5,7},{6,4},{7,5},{8,10},{9,11},{10,... | collective-permute-start | bytes 884744 | tf_op jit(solution)/shard_map/ppermute | solution.py:673
  92.5 1.6 %collective-permute-start.27 = (bf16[2,4,16,1024]{3,2,1,0:T(8,128)(2,1)S(1)}, bf16[2,4,16,1024]{3,2,1,0:T(8,128)(2,1)S(1)}, u32[]{:S(2)}, u32[]{:S(2)}) collective-permute-start(bf16[2,4,16,1024]{3,2,1,0:T(8,128)(2,1)S(1)} %fusion.3), channel_id=1, source_target_pairs={{0,4},{4,0},{8,12},{12,8},{16,20},{20,16},{24,28},{28,24},{1,5},{5... | collective-permute-start | bytes 786440 | tf_op jit(solution)/shard_map/ppermute | solution.py:673
  94.1 0.5 collective-permute-start.29
  94.6 0.5 collective-permute-start.30
  95.1 3.9 %back.1 = (bf16[2,128,512]{2,1,0:T(8,128)(2,1)S(1)}, bf16[2,2,128,512]{3,2,1,0:T(8,128)(2,1)S(1)}, bf16[2,2,2,128,512]{4,3,2,1,0:T(8,128)(2,1)S(1)}) custom-call(bf16[2,512,1536]{2,1,0:T(8,128)(2,1)S(1)} %get-tuple-element.271.grad_ref.gate_grad_ref, bf16[2,512,1536]{2,1,0:T(8,128)(2,1)S(1)} %get-tuple-element.234.grad_ref.content_grad_ref, ...), custom_call_target="tpu_custom_call" | custom-call | flops 25165824 | bytes 50331 | tf_op jit(solution)/shard_map/back/pallas_call | solution.py:659
  99.0 5.2 %collective-permute-done.29.refs_12_ = bf16[4,16,1536]{2,1,0:T(8,128)(2,1)S(1)} collective-permute-done((bf16[4,16,1536]{2,1,0:T(8,128)(2,1)S(1)}, bf16[4,16,1536]{2,1,0:T(8,128)(2,1)S(1)}, u32[]{:S(2)}, u32[]{:S(2)}) %collective-permute-start.29) | collective-permute-done | bytes 196640 | tf_op jit(solution)/shard_map/ppermute | solution.py:673
  104.2 0.7 collective-permute-done.30.refs_14_
  105.0 1.6 %collective-permute-start.32 = (bf16[4,16,1152]{2,1,0:T(8,128)(2,1)S(1)}, bf16[4,16,1152]{2,1,0:T(8,128)(2,1)S(1)}, u32[]{:S(2)}, u32[]{:S(2)}) collective-permute-start(bf16[4,16,1152]{2,1,0:T(8,128)(2,1)S(1)} %get-tuple-element.285), channel_id=1, source_target_pairs={{0,4},{4,0},{8,12},{12,8},{16,20},{20,16},{24,28},{28,24},{1,5},{5... | collective-permute-start | bytes 442376 | tf_op jit(solution)/shard_map/ppermute | solution.py:673
  106.6 0.9 collective-permute-start.31
  107.4 4.1 %collective-permute-done.31.refs_13_ = bf16[4,16,1024]{2,1,0:T(8,128)(2,1)S(1)} collective-permute-done((bf16[4,16,1024]{2,1,0:T(8,128)(2,1)S(1)}, bf16[4,16,1024]{2,1,0:T(8,128)(2,1)S(1)}, u32[]{:S(2)}, u32[]{:S(2)}) %collective-permute-start.31) | collective-permute-done | bytes 131104 | tf_op jit(solution)/shard_map/ppermute | solution.py:673
  111.9 0.9 collective-permute-start.42
  112.8 1.0 collective-permute-start.34
  113.8 1.5 %collective-permute-start.35 = (bf16[16,5248]{1,0:T(8,128)(2,1)S(1)}, bf16[16,5248]{1,0:T(8,128)(2,1)S(1)}, u32[]{:S(2)}, u32[]{:S(2)}) collective-permute-start(bf16[16,5248]{1,0:T(8,128)(2,1)S(1)} %get-tuple-element.289), channel_id=1, source_target_pairs={{0,24},{4,28},{8,16},{12,20},{16,8},{20,12},{24,0},{28,4},{1,25},{... | collective-permute-start | bytes 503816 | tf_op jit(solution)/shard_map/ppermute | solution.py:673
  115.3 1.0 collective-permute-start.33
  116.3 3.2 %fetch.1 = (f32[64,3072]{1,0:T(8,128)S(1)}, f32[64,3072]{1,0:T(8,128)S(1)}, f32[64,3072]{1,0:T(8,128)S(1)}, f32[64,3072]{1,0:T(8,128)S(1)}, f32[192,512]{1,0:T(8...) custom-call(f32[64,3072]{1,0:T(8,128)} %refs_0_, ...), custom_call_target="tpu_custom_call" | custom-call | flops 25165824 | bytes 50331 | tf_op jit(solution)/shard_map/fetch/pallas_call | solution.py:659
  119.5 5.4 %collective-permute-done.34.two_ref = bf16[16,5248]{1,0:T(8,128)(2,1)S(1)} collective-permute-done((bf16[16,5248]{1,0:T(8,128)(2,1)S(1)}, bf16[16,5248]{1,0:T(8,128)(2,1)S(1)}, u32[]{:S(2)}, u32[]{:S(2)}) %collective-permute-start.34) | collective-permute-done | bytes 167968 | tf_op jit(solution)/shard_map/ppermute | solution.py:673
  125.0 1.2 collective-permute-done.33.one_ref
  126.5 0.9 collective-permute-start.41
  127.5 1.2 collective-permute-done.36.refs_1_
  128.9 3.4 %collective-permute-done.37.refs_1_ = f32[8,128]{1,0:T(8,128)S(1)} collective-permute-done((f32[8,128]{1,0:T(8,128)S(1)}, f32[8,128]{1,0:T(8,128)S(1)}, u32[]{:S(2)}, u32[]{:S(2)}) %collective-permute-start.37) | collective-permute-done | bytes 4128 | tf_op jit(solution)/shard_map/ppermute | solution.py:673
  132.3 2.1 %collective-permute-start.40 = (f32[8,128]{1,0:T(8,128)S(1)}, f32[8,128]{1,0:T(8,128)S(1)}, u32[]{:S(2)}, u32[]{:S(2)}) collective-permute-start(f32[8,128]{1,0:T(8,128)S(1)} %add.33.refs_0_), channel_id=1, source_target_pairs={{0,24},{4,28},{8,16},{12,20},{16,8},{20,12},{24,0},{28,4},{1,25},{... | collective-permute-start | bytes 12296 | tf_op jit(solution)/shard_map/ppermute | solution.py:673
  134.4 2.2 %collective-permute-start.39 = (f32[8,128]{1,0:T(8,128)S(1)}, f32[8,128]{1,0:T(8,128)S(1)}, u32[]{:S(2)}, u32[]{:S(2)}) collective-permute-start(f32[8,128]{1,0:T(8,128)S(1)} %add.33.refs_0_), channel_id=1, source_target_pairs={{0,16},{4,20},{8,24},{12,28},{16,0},{20,4},{24,8},{28,12},{1,17},{... | collective-permute-start | bytes 12296 | tf_op jit(solution)/shard_map/ppermute | solution.py:673
  136.7 1.0 collective-permute-done.40.refs_3_
  137.7 1.2 collective-permute-done.39.refs_2_
  138.9 1.3 collective-permute-done.38.refs_1_
  140.2 0.5 collective-permute-start.44
  140.9 1.2 collective-permute-start.43
  142.1 1.5 %collective-permute-done.44.core_ref = bf16[2,2,128,512]{3,2,1,0:T(8,128)(2,1)S(1)} collective-permute-done((bf16[2,2,128,512]{3,2,1,0:T(8,128)(2,1)S(1)}, bf16[2,2,128,512]{3,2,1,0:T(8,128)(2,1)S(1)}, u32[]{:S(2)}, u32[]{:S(2)}) %collective-permute-start.44) | collective-permute-done | bytes 524320 | tf_op jit(solution)/shard_map/ppermute | solution.py:673
  143.6 1.8 %give.1 = (f32[8,128,512]{2,1,0:T(8,128)}, bf16[8,128,512]{2,1,0:T(8,128)(2,1)}) custom-call(bf16[8,128,512]{2,1,0:T(8,128)(2,1)S(1)} %get-tuple-element.316.cots_ref, bf16[8,128,512]{2,1,0:T(8,128)(2,1)S(1)} %get-tuple-element.317.acts_ref, bf16[2,128,512]{2,1,0:T(8,128)(2,1)S(1)} %get-tuple-element.318.grad_own, ...), custom_call_target="tpu_custom_call" | custom-call | flops 25165824 | bytes 50331 | tf_op jit(solution)/shard_map/give/pallas_call | solution.py:659
  145.5 3.7 %adam.1 = (f32[64,3072]{1,0:T(8,128)}, f32[64,3072]{1,0:T(8,128)}, f32[64,3072]{1,0:T(8,128)}, f32[64,3072]{1,0:T(8,128)}, f32[64,3072]{1,0:T(8,128)}, /*index=5...) custom-call(f32[8,128]{1,0:T(8,128)S(1)} %add.35.message_ref, ...), custom_call_target="tpu_custom_call" | custom-call | flops 25165824 | bytes 50331 | tf_op jit(solution)/shard_map/adam/pallas_call | solution.py:659
  (80 shorter events, 3.6 us)
Async XLA Ops:
  3.1 30.9 %collective-permute-start.7 = (bf16[2,2,2,128,512]{4,3,2,1,0:T(8,128)(2,1)S(1)}, bf16[2,2,2,128,512]{4,3,2,1,0:T(8,128)(2,1)S(1)}, u32[]{:S(2)}, u32[]{:S(2)}) collective-permute-start(bf16[2,2,2,128,512]{4,3,2,1,0:T(8,128)(2,1)S(1)} %get-tuple-element.200), channel_id=1, source_target_pairs={{0,2},{1,3},{2,0},{3,1},{4,6},{5,7},{6,4},{7,5},{8,10},{9,11},{10,... | collective-permute-start | bytes 3145736 | tf_op jit(solution)/shard_map/ppermute | solution.py:673
  6.1 16.1 %collective-permute-start.3 = (bf16[2,2,128,512]{3,2,1,0:T(8,128)(2,1)S(1)}, bf16[2,2,128,512]{3,2,1,0:T(8,128)(2,1)S(1)}, u32[]{:S(2)}, u32[]{:S(2)}) collective-permute-start(bf16[2,2,128,512]{3,2,1,0:T(8,128)(2,1)S(1)} %get-tuple-element.199), channel_id=1, source_target_pairs={{0,1},{1,0},{2,3},{3,2},{4,5},{5,4},{6,7},{7,6},{8,9},{9,8},{10,11... | collective-permute-start | bytes 1572872 | tf_op jit(solution)/shard_map/ppermute | solution.py:673
  6.1 8.4 %collective-permute-start.2 = (bf16[32,2176]{1,0:T(8,128)(2,1)S(1)}, bf16[32,2176]{1,0:T(8,128)(2,1)S(1)}, u32[]{:S(2)}, u32[]{:S(2)}) collective-permute-start(bf16[32,2176]{1,0:T(8,128)(2,1)S(1)} %pack_first.1.refs_0_), channel_id=1, source_target_pairs={{0,24},{4,28},{8,16},{12,20},{16,8},{20,12},{24,0},{28,4},{1,25},{... | collective-permute-start | bytes 417800 | tf_op jit(solution)/shard_map/ppermute | solution.py:673
  9.7 12.4 %collective-permute-start.1 = (bf16[32,2176]{1,0:T(8,128)(2,1)S(1)}, bf16[32,2176]{1,0:T(8,128)(2,1)S(1)}, u32[]{:S(2)}, u32[]{:S(2)}) collective-permute-start(bf16[32,2176]{1,0:T(8,128)(2,1)S(1)} %pack_first.1.refs_0_), channel_id=1, source_target_pairs={{0,16},{4,20},{8,24},{12,28},{16,0},{20,4},{24,8},{28,12},{1,17},{... | collective-permute-start | bytes 417800 | tf_op jit(solution)/shard_map/ppermute | solution.py:673
  9.7 12.4 %collective-permute-start = (bf16[32,2176]{1,0:T(8,128)(2,1)S(1)}, bf16[32,2176]{1,0:T(8,128)(2,1)S(1)}, u32[]{:S(2)}, u32[]{:S(2)}) collective-permute-start(bf16[32,2176]{1,0:T(8,128)(2,1)S(1)} %pack_first.1.refs_0_), channel_id=1, source_target_pairs={{0,8},{4,12},{8,0},{12,4},{16,24},{20,28},{24,16},{28,20},{1,9},{5... | collective-permute-start | bytes 417800 | tf_op jit(solution)/shard_map/ppermute | solution.py:673
  22.2 14.3 %collective-permute-start.11 = (bf16[4,32,2176]{2,1,0:T(8,128)(2,1)S(1)}, bf16[4,32,2176]{2,1,0:T(8,128)(2,1)S(1)}, u32[]{:S(2)}, u32[]{:S(2)}) collective-permute-start(bf16[4,32,2176]{2,1,0:T(8,128)(2,1)S(1)} %stack.4.refs_0_.refs_4_), channel_id=1, source_target_pairs={{0,4},{4,0},{8,12},{12,8},{16,20},{20,16},{24,28},{28,24},{1,5},{5... | collective-permute-start | bytes 1671176 | tf_op jit(solution)/shard_map/ppermute | solution.py:673
  23.8 7.6 %collective-permute-start.6 = (bf16[32,1536]{1,0:T(8,128)(2,1)S(1)}, bf16[32,1536]{1,0:T(8,128)(2,1)S(1)}, u32[]{:S(2)}, u32[]{:S(2)}) collective-permute-start(bf16[32,1536]{1,0:T(8,128)(2,1)S(1)} %get-tuple-element.206.refs_0_), channel_id=1, source_target_pairs={{0,24},{4,28},{8,16},{12,20},{16,8},{20,12},{24,0},{28,4},{1,25},{... | collective-permute-start | bytes 294920 | tf_op jit(solution)/shard_map/ppermute | solution.py:673
  26.3 7.7 %collective-permute-start.5 = (bf16[32,1536]{1,0:T(8,128)(2,1)S(1)}, bf16[32,1536]{1,0:T(8,128)(2,1)S(1)}, u32[]{:S(2)}, u32[]{:S(2)}) collective-permute-start(bf16[32,1536]{1,0:T(8,128)(2,1)S(1)} %get-tuple-element.206.refs_0_), channel_id=1, source_target_pairs={{0,16},{4,20},{8,24},{12,28},{16,0},{20,4},{24,8},{28,12},{1,17},{... | collective-permute-start | bytes 294920 | tf_op jit(solution)/shard_map/ppermute | solution.py:673
  26.3 7.7 %collective-permute-start.4 = (bf16[32,1536]{1,0:T(8,128)(2,1)S(1)}, bf16[32,1536]{1,0:T(8,128)(2,1)S(1)}, u32[]{:S(2)}, u32[]{:S(2)}) collective-permute-start(bf16[32,1536]{1,0:T(8,128)(2,1)S(1)} %get-tuple-element.206.refs_0_), channel_id=1, source_target_pairs={{0,8},{4,12},{8,0},{12,4},{16,24},{20,28},{24,16},{28,20},{1,9},{5... | collective-permute-start | bytes 294920 | tf_op jit(solution)/shard_map/ppermute | solution.py:673
  34.0 8.5 %collective-permute-start.13 = (bf16[2,2,2,128,512]{4,3,2,1,0:T(8,128)(2,1)S(1)}, bf16[2,2,2,128,512]{4,3,2,1,0:T(8,128)(2,1)S(1)}, u32[]{:S(2)}, u32[]{:S(2)}) collective-permute-start(bf16[2,2,2,128,512]{4,3,2,1,0:T(8,128)(2,1)S(1)} %collective-permute-done.7.side_ref), channel_id=1, source_target_pairs={{0,1},{1,0},{2,3},{3,2},{4,5},{5,4},{6,7},{7,6},{8,9},{9,8},{10,11... | collective-permute-start | bytes 3145736 | tf_op jit(solution)/shard_map/ppermute | solution.py:673
  34.1 6.5 %collective-permute-start.14 = (bf16[4,32,2176]{2,1,0:T(8,128)(2,1)S(1)}, bf16[4,32,2176]{2,1,0:T(8,128)(2,1)S(1)}, u32[]{:S(2)}, u32[]{:S(2)}) collective-permute-start(bf16[4,32,2176]{2,1,0:T(8,128)(2,1)S(1)} %stack.4.refs_0_.refs_4_), channel_id=1, source_target_pairs={{0,1},{1,0},{2,3},{3,2},{4,5},{5,4},{6,7},{7,6},{8,9},{9,8},{10,11... | collective-permute-start | bytes 1671176 | tf_op jit(solution)/shard_map/ppermute | solution.py:673
  36.5 4.0 %collective-permute-start.15 = (bf16[4,32,2176]{2,1,0:T(8,128)(2,1)S(1)}, bf16[4,32,2176]{2,1,0:T(8,128)(2,1)S(1)}, u32[]{:S(2)}, u32[]{:S(2)}) collective-permute-start(bf16[4,32,2176]{2,1,0:T(8,128)(2,1)S(1)} %collective-permute-done.11.refs_1_.refs_5_), channel_id=1, source_target_pairs={{0,1},{1,0},{2,3},{3,2},{4,5},{5,4},{6,7},{7,6},{8,9},{9,8},{10,11... | collective-permute-start | bytes 1671176 | tf_op jit(solution)/shard_map/ppermute | solution.py:673
  36.6 13.6 %collective-permute-start.12 = (bf16[4,32,1536]{2,1,0:T(8,128)(2,1)S(1)}, bf16[4,32,1536]{2,1,0:T(8,128)(2,1)S(1)}, u32[]{:S(2)}, u32[]{:S(2)}) collective-permute-start(bf16[4,32,1536]{2,1,0:T(8,128)(2,1)S(1)} %stack.5.refs_0_), channel_id=1, source_target_pairs={{0,4},{4,0},{8,12},{12,8},{16,20},{20,16},{24,28},{28,24},{1,5},{5... | collective-permute-start | bytes 1179656 | tf_op jit(solution)/shard_map/ppermute | solution.py:673
  38.0 13.3 %copy-start = (s32[8,5]{1,0:T(8,128)S(1)}, s32[8,5]{1,0:T(8,128)}, u32[]{:S(2)}) copy-start(s32[8,5]{1,0:T(8,128)} %lens_ref.7) | copy-start | bytes 484
  38.0 12.1 %collective-permute-start.10 = (bf16[32,1536]{1,0:T(8,128)(2,1)S(1)}, bf16[32,1536]{1,0:T(8,128)(2,1)S(1)}, u32[]{:S(2)}, u32[]{:S(2)}) collective-permute-start(bf16[32,1536]{1,0:T(8,128)(2,1)S(1)} %get-tuple-element.210.refs_0_), channel_id=1, source_target_pairs={{0,24},{4,28},{8,16},{12,20},{16,8},{20,12},{24,0},{28,4},{1,25},{... | collective-permute-start | bytes 294920 | tf_op jit(solution)/shard_map/ppermute | solution.py:673
  40.5 9.6 %collective-permute-start.9 = (bf16[32,1536]{1,0:T(8,128)(2,1)S(1)}, bf16[32,1536]{1,0:T(8,128)(2,1)S(1)}, u32[]{:S(2)}, u32[]{:S(2)}) collective-permute-start(bf16[32,1536]{1,0:T(8,128)(2,1)S(1)} %get-tuple-element.210.refs_0_), channel_id=1, source_target_pairs={{0,16},{4,20},{8,24},{12,28},{16,0},{20,4},{24,8},{28,12},{1,17},{... | collective-permute-start | bytes 294920 | tf_op jit(solution)/shard_map/ppermute | solution.py:673
  40.5 9.6 %collective-permute-start.8 = (bf16[32,1536]{1,0:T(8,128)(2,1)S(1)}, bf16[32,1536]{1,0:T(8,128)(2,1)S(1)}, u32[]{:S(2)}, u32[]{:S(2)}) collective-permute-start(bf16[32,1536]{1,0:T(8,128)(2,1)S(1)} %get-tuple-element.210.refs_0_), channel_id=1, source_target_pairs={{0,8},{4,12},{8,0},{12,4},{16,24},{20,28},{24,16},{28,20},{1,9},{5... | collective-permute-start | bytes 294920 | tf_op jit(solution)/shard_map/ppermute | solution.py:673
  50.2 3.7 %collective-permute-start.16 = (bf16[4,32,1536]{2,1,0:T(8,128)(2,1)S(1)}, bf16[4,32,1536]{2,1,0:T(8,128)(2,1)S(1)}, u32[]{:S(2)}, u32[]{:S(2)}) collective-permute-start(bf16[4,32,1536]{2,1,0:T(8,128)(2,1)S(1)} %collective-permute-done.12.refs_1_), channel_id=1, source_target_pairs={{0,1},{1,0},{2,3},{3,2},{4,5},{5,4},{6,7},{7,6},{8,9},{9,8},{10,11... | collective-permute-start | bytes 1179656 | tf_op jit(solution)/shard_map/ppermute | solution.py:673
  50.2 3.6 %collective-permute-start.17 = (bf16[4,32,1536]{2,1,0:T(8,128)(2,1)S(1)}, bf16[4,32,1536]{2,1,0:T(8,128)(2,1)S(1)}, u32[]{:S(2)}, u32[]{:S(2)}) collective-permute-start(bf16[4,32,1536]{2,1,0:T(8,128)(2,1)S(1)} %stack.5.refs_0_), channel_id=1, source_target_pairs={{0,1},{1,0},{2,3},{3,2},{4,5},{5,4},{6,7},{7,6},{8,9},{9,8},{10,11... | collective-permute-start | bytes 1179656 | tf_op jit(solution)/shard_map/ppermute | solution.py:673
  50.8 11.3 %collective-permute-start.18 = (bf16[4,32,1536]{2,1,0:T(8,128)(2,1)S(1)}, bf16[4,32,1536]{2,1,0:T(8,128)(2,1)S(1)}, u32[]{:S(2)}, u32[]{:S(2)}) collective-permute-start(bf16[4,32,1536]{2,1,0:T(8,128)(2,1)S(1)} %stack.6.refs_0_), channel_id=1, source_target_pairs={{0,4},{4,0},{8,12},{12,8},{16,20},{20,16},{24,28},{28,24},{1,5},{5... | collective-permute-start | bytes 1179656 | tf_op jit(solution)/shard_map/ppermute | solution.py:673
  51.4 11.3 %collective-permute-start.19 = (bf16[4,32,1536]{2,1,0:T(8,128)(2,1)S(1)}, bf16[4,32,1536]{2,1,0:T(8,128)(2,1)S(1)}, u32[]{:S(2)}, u32[]{:S(2)}) collective-permute-start(bf16[4,32,1536]{2,1,0:T(8,128)(2,1)S(1)} %stack.6.refs_0_), channel_id=1, source_target_pairs={{0,1},{1,0},{2,3},{3,2},{4,5},{5,4},{6,7},{7,6},{8,9},{9,8},{10,11... | collective-permute-start | bytes 1179656 | tf_op jit(solution)/shard_map/ppermute | solution.py:673
  62.1 1.9 %collective-permute-start.20 = (bf16[4,32,1536]{2,1,0:T(8,128)(2,1)S(1)}, bf16[4,32,1536]{2,1,0:T(8,128)(2,1)S(1)}, u32[]{:S(2)}, u32[]{:S(2)}) collective-permute-start(bf16[4,32,1536]{2,1,0:T(8,128)(2,1)S(1)} %collective-permute-done.18.refs_1_), channel_id=1, source_target_pairs={{0,1},{1,0},{2,3},{3,2},{4,5},{5,4},{6,7},{7,6},{8,9},{9,8},{10,11... | collective-permute-start | bytes 1179656 | tf_op jit(solution)/shard_map/ppermute | solution.py:673
  71.0 2.6 %collective-permute-start.21 = (bf16[2,2,4,16,1536]{4,3,2,1,0:T(8,128)(2,1)S(1)}, bf16[2,2,4,16,1536]{4,3,2,1,0:T(8,128)(2,1)S(1)}, u32[]{:S(2)}, u32[]{:S(2)}) collective-permute-start(bf16[2,2,4,16,1536]{4,3,2,1,0:T(8,128)(2,1)S(1)} %get-tuple-element.233), channel_id=1, source_target_pairs={{0,1},{1,0},{2,3},{3,2},{4,5},{5,4},{6,7},{7,6},{8,9},{9,8},{10,11... | collective-permute-start | bytes 2359304 | tf_op jit(solution)/shard_map/ppermute | solution.py:673
  73.4 3.4 %collective-permute-start.22 = (bf16[2,2,4,16,1536]{4,3,2,1,0:T(8,128)(2,1)S(1)}, bf16[2,2,4,16,1536]{4,3,2,1,0:T(8,128)(2,1)S(1)}, u32[]{:S(2)}, u32[]{:S(2)}) collective-permute-start(bf16[2,2,4,16,1536]{4,3,2,1,0:T(8,128)(2,1)S(1)} %get-tuple-element.237), channel_id=1, source_target_pairs={{0,1},{1,0},{2,3},{3,2},{4,5},{5,4},{6,7},{7,6},{8,9},{9,8},{10,11... | collective-permute-start | bytes 2359304 | tf_op jit(solution)/shard_map/ppermute | solution.py:673
  73.7 11.5 %collective-permute-start.23 = (bf16[2,4,16,1536]{3,2,1,0:T(8,128)(2,1)S(1)}, bf16[2,4,16,1536]{3,2,1,0:T(8,128)(2,1)S(1)}, u32[]{:S(2)}, u32[]{:S(2)}) collective-permute-start(bf16[2,4,16,1536]{3,2,1,0:T(8,128)(2,1)S(1)} %fusion.1), channel_id=1, source_target_pairs={{0,2},{1,3},{2,0},{3,1},{4,6},{5,7},{6,4},{7,5},{8,10},{9,11},{10,... | collective-permute-start | bytes 1179656 | tf_op jit(solution)/shard_map/ppermute | solution.py:673
  76.9 11.2 %collective-permute-start.24 = (bf16[2,4,16,1536]{3,2,1,0:T(8,128)(2,1)S(1)}, bf16[2,4,16,1536]{3,2,1,0:T(8,128)(2,1)S(1)}, u32[]{:S(2)}, u32[]{:S(2)}) collective-permute-start(bf16[2,4,16,1536]{3,2,1,0:T(8,128)(2,1)S(1)} %fusion), channel_id=1, source_target_pairs={{0,4},{4,0},{8,12},{12,8},{16,20},{20,16},{24,28},{28,24},{1,5},{5... | collective-permute-start | bytes 1179656 | tf_op jit(solution)/shard_map/ppermute | solution.py:673
  88.0 2.8 %collective-permute-start.26 = (bf16[2,2,4,16,1152]{4,3,2,1,0:T(8,128)(2,1)S(1)}, bf16[2,2,4,16,1152]{4,3,2,1,0:T(8,128)(2,1)S(1)}, u32[]{:S(2)}, u32[]{:S(2)}) collective-permute-start(bf16[2,2,4,16,1152]{4,3,2,1,0:T(8,128)(2,1)S(1)} %get-tuple-element.258), channel_id=1, source_target_pairs={{0,1},{1,0},{2,3},{3,2},{4,5},{5,4},{6,7},{7,6},{8,9},{9,8},{10,11... | collective-permute-start | bytes 1769480 | tf_op jit(solution)/shard_map/ppermute | solution.py:673
  88.0 2.8 %collective-permute-start.25 = (bf16[2,2,4,16,1024]{4,3,2,1,0:T(8,128)(2,1)S(1)}, bf16[2,2,4,16,1024]{4,3,2,1,0:T(8,128)(2,1)S(1)}, u32[]{:S(2)}, u32[]{:S(2)}) collective-permute-start(bf16[2,2,4,16,1024]{4,3,2,1,0:T(8,128)(2,1)S(1)} %get-tuple-element.257), channel_id=1, source_target_pairs={{0,1},{1,0},{2,3},{3,2},{4,5},{5,4},{6,7},{7,6},{8,9},{9,8},{10,11... | collective-permute-start | bytes 1572872 | tf_op jit(solution)/shard_map/ppermute | solution.py:673
  90.9 14.0 %collective-permute-start.28 = (bf16[2,4,16,1152]{3,2,1,0:T(8,128)(2,1)S(1)}, bf16[2,4,16,1152]{3,2,1,0:T(8,128)(2,1)S(1)}, u32[]{:S(2)}, u32[]{:S(2)}) collective-permute-start(bf16[2,4,16,1152]{3,2,1,0:T(8,128)(2,1)S(1)} %fusion.2), channel_id=1, source_target_pairs={{0,2},{1,3},{2,0},{3,1},{4,6},{5,7},{6,4},{7,5},{8,10},{9,11},{10,... | collective-permute-start | bytes 884744 | tf_op jit(solution)/shard_map/ppermute | solution.py:673
  92.5 12.3 %collective-permute-start.27 = (bf16[2,4,16,1024]{3,2,1,0:T(8,128)(2,1)S(1)}, bf16[2,4,16,1024]{3,2,1,0:T(8,128)(2,1)S(1)}, u32[]{:S(2)}, u32[]{:S(2)}) collective-permute-start(bf16[2,4,16,1024]{3,2,1,0:T(8,128)(2,1)S(1)} %fusion.3), channel_id=1, source_target_pairs={{0,4},{4,0},{8,12},{12,8},{16,20},{20,16},{24,28},{28,24},{1,5},{5... | collective-permute-start | bytes 786440 | tf_op jit(solution)/shard_map/ppermute | solution.py:673
  94.1 10.1 %collective-permute-start.29 = (bf16[4,16,1536]{2,1,0:T(8,128)(2,1)S(1)}, bf16[4,16,1536]{2,1,0:T(8,128)(2,1)S(1)}, u32[]{:S(2)}, u32[]{:S(2)}) collective-permute-start(bf16[4,16,1536]{2,1,0:T(8,128)(2,1)S(1)} %get-tuple-element.262), channel_id=1, source_target_pairs={{0,2},{1,3},{2,0},{3,1},{4,6},{5,7},{6,4},{7,5},{8,10},{9,11},{10,... | collective-permute-start | bytes 589832 | tf_op jit(solution)/shard_map/ppermute | solution.py:673
  94.6 10.3 %collective-permute-start.30 = (bf16[4,16,1536]{2,1,0:T(8,128)(2,1)S(1)}, bf16[4,16,1536]{2,1,0:T(8,128)(2,1)S(1)}, u32[]{:S(2)}, u32[]{:S(2)}) collective-permute-start(bf16[4,16,1536]{2,1,0:T(8,128)(2,1)S(1)} %get-tuple-element.263), channel_id=1, source_target_pairs={{0,4},{4,0},{8,12},{12,8},{16,20},{20,16},{24,28},{28,24},{1,5},{5... | collective-permute-start | bytes 589832 | tf_op jit(solution)/shard_map/ppermute | solution.py:673
  105.0 6.5 %collective-permute-start.32 = (bf16[4,16,1152]{2,1,0:T(8,128)(2,1)S(1)}, bf16[4,16,1152]{2,1,0:T(8,128)(2,1)S(1)}, u32[]{:S(2)}, u32[]{:S(2)}) collective-permute-start(bf16[4,16,1152]{2,1,0:T(8,128)(2,1)S(1)} %get-tuple-element.285), channel_id=1, source_target_pairs={{0,4},{4,0},{8,12},{12,8},{16,20},{20,16},{24,28},{28,24},{1,5},{5... | collective-permute-start | bytes 442376 | tf_op jit(solution)/shard_map/ppermute | solution.py:673
  106.6 5.0 %collective-permute-start.31 = (bf16[4,16,1024]{2,1,0:T(8,128)(2,1)S(1)}, bf16[4,16,1024]{2,1,0:T(8,128)(2,1)S(1)}, u32[]{:S(2)}, u32[]{:S(2)}) collective-permute-start(bf16[4,16,1024]{2,1,0:T(8,128)(2,1)S(1)} %get-tuple-element.283), channel_id=1, source_target_pairs={{0,2},{1,3},{2,0},{3,1},{4,6},{5,7},{6,4},{7,5},{8,10},{9,11},{10,... | collective-permute-start | bytes 393224 | tf_op jit(solution)/shard_map/ppermute | solution.py:673
  111.9 28.3 %collective-permute-start.42 = (bf16[2,2,2,128,512]{4,3,2,1,0:T(8,128)(2,1)S(1)}, bf16[2,2,2,128,512]{4,3,2,1,0:T(8,128)(2,1)S(1)}, u32[]{:S(2)}, u32[]{:S(2)}) collective-permute-start(bf16[2,2,2,128,512]{4,3,2,1,0:T(8,128)(2,1)S(1)} %get-tuple-element.312), channel_id=1, source_target_pairs={{0,2},{1,3},{2,0},{3,1},{4,6},{5,7},{6,4},{7,5},{8,10},{9,11},{10,... | collective-permute-start | bytes 3145736 | tf_op jit(solution)/shard_map/ppermute | solution.py:673
  112.8 12.1 %collective-permute-start.34 = (bf16[16,5248]{1,0:T(8,128)(2,1)S(1)}, bf16[16,5248]{1,0:T(8,128)(2,1)S(1)}, u32[]{:S(2)}, u32[]{:S(2)}) collective-permute-start(bf16[16,5248]{1,0:T(8,128)(2,1)S(1)} %get-tuple-element.288), channel_id=1, source_target_pairs={{0,16},{4,20},{8,24},{12,28},{16,0},{20,4},{24,8},{28,12},{1,17},{... | collective-permute-start | bytes 503816 | tf_op jit(solution)/shard_map/ppermute | solution.py:673
  113.8 11.1 %collective-permute-start.35 = (bf16[16,5248]{1,0:T(8,128)(2,1)S(1)}, bf16[16,5248]{1,0:T(8,128)(2,1)S(1)}, u32[]{:S(2)}, u32[]{:S(2)}) collective-permute-start(bf16[16,5248]{1,0:T(8,128)(2,1)S(1)} %get-tuple-element.289), channel_id=1, source_target_pairs={{0,24},{4,28},{8,16},{12,20},{16,8},{20,12},{24,0},{28,4},{1,25},{... | collective-permute-start | bytes 503816 | tf_op jit(solution)/shard_map/ppermute | solution.py:673
  115.3 10.8 %collective-permute-start.33 = (bf16[16,5248]{1,0:T(8,128)(2,1)S(1)}, bf16[16,5248]{1,0:T(8,128)(2,1)S(1)}, u32[]{:S(2)}, u32[]{:S(2)}) collective-permute-start(bf16[16,5248]{1,0:T(8,128)(2,1)S(1)} %get-tuple-element.287), channel_id=1, source_target_pairs={{0,8},{4,12},{8,0},{12,4},{16,24},{20,28},{24,16},{28,20},{1,9},{5... | collective-permute-start | bytes 503816 | tf_op jit(solution)/shard_map/ppermute | solution.py:673
  126.5 13.7 %collective-permute-start.41 = (bf16[16,5248]{1,0:T(8,128)(2,1)S(1)}, bf16[16,5248]{1,0:T(8,128)(2,1)S(1)}, u32[]{:S(2)}, u32[]{:S(2)}) collective-permute-start(bf16[16,5248]{1,0:T(8,128)(2,1)S(1)} %get-tuple-element.310.refs_0_.own_ref), channel_id=1, source_target_pairs={{0,2},{1,3},{2,0},{3,1},{4,6},{5,7},{6,4},{7,5},{8,10},{9,11},{10,... | collective-permute-start | bytes 503816 | tf_op jit(solution)/shard_map/ppermute | solution.py:673
  127.4 18.1 %copy-start.1 = (f32[256]{0:T(256)S(1)}, f32[256]{0:T(256)}, u32[]{:S(2)}) copy-start(f32[256]{0:T(256)} %param.38) | copy-start | bytes 3076
  127.4 18.1 %copy-start.2 = (f32[64]{0:T(128)S(1)}, f32[64]{0:T(128)}, u32[]{:S(2)}) copy-start(f32[64]{0:T(128)} %param.42) | copy-start | bytes 772
  127.4 18.1 %copy-start.3 = (f32[256]{0:T(256)S(1)}, f32[256]{0:T(256)}, u32[]{:S(2)}) copy-start(f32[256]{0:T(256)} %param.39) | copy-start | bytes 3076
  127.4 18.1 %copy-start.4 = (f32[256]{0:T(256)S(1)}, f32[256]{0:T(256)}, u32[]{:S(2)}) copy-start(f32[256]{0:T(256)} %param.40) | copy-start | bytes 3076
  127.4 18.1 %copy-start.5 = (f32[256]{0:T(256)S(1)}, f32[256]{0:T(256)}, u32[]{:S(2)}) copy-start(f32[256]{0:T(256)} %param.41) | copy-start | bytes 3076
  127.4 18.1 %copy-start.6 = (f32[64]{0:T(128)S(1)}, f32[64]{0:T(128)}, u32[]{:S(2)}) copy-start(f32[64]{0:T(128)} %param.43) | copy-start | bytes 772
  127.4 18.1 %copy-start.7 = (f32[64]{0:T(128)S(1)}, f32[64]{0:T(128)}, u32[]{:S(2)}) copy-start(f32[64]{0:T(128)} %param.44) | copy-start | bytes 772
  127.4 18.1 %copy-start.8 = (f32[64]{0:T(128)S(1)}, f32[64]{0:T(128)}, u32[]{:S(2)}) copy-start(f32[64]{0:T(128)} %param.45) | copy-start | bytes 772
  127.4 1.2 collective-permute-start.36
  128.7 3.6 %collective-permute-start.37 = (f32[8,128]{1,0:T(8,128)S(1)}, f32[8,128]{1,0:T(8,128)S(1)}, u32[]{:S(2)}, u32[]{:S(2)}) collective-permute-start(f32[8,128]{1,0:T(8,128)S(1)} %add.32.refs_0_), channel_id=1, source_target_pairs={{0,4},{4,0},{8,12},{12,8},{16,20},{20,16},{24,28},{28,24},{1,5},{5... | collective-permute-start | bytes 12296 | tf_op jit(solution)/shard_map/ppermute | solution.py:673
  132.3 5.4 %collective-permute-start.40 = (f32[8,128]{1,0:T(8,128)S(1)}, f32[8,128]{1,0:T(8,128)S(1)}, u32[]{:S(2)}, u32[]{:S(2)}) collective-permute-start(f32[8,128]{1,0:T(8,128)S(1)} %add.33.refs_0_), channel_id=1, source_target_pairs={{0,24},{4,28},{8,16},{12,20},{16,8},{20,12},{24,0},{28,4},{1,25},{... | collective-permute-start | bytes 12296 | tf_op jit(solution)/shard_map/ppermute | solution.py:673
  134.4 4.5 %collective-permute-start.39 = (f32[8,128]{1,0:T(8,128)S(1)}, f32[8,128]{1,0:T(8,128)S(1)}, u32[]{:S(2)}, u32[]{:S(2)}) collective-permute-start(f32[8,128]{1,0:T(8,128)S(1)} %add.33.refs_0_), channel_id=1, source_target_pairs={{0,16},{4,20},{8,24},{12,28},{16,0},{20,4},{24,8},{28,12},{1,17},{... | collective-permute-start | bytes 12296 | tf_op jit(solution)/shard_map/ppermute | solution.py:673
  136.6 3.6 %collective-permute-start.38 = (f32[8,128]{1,0:T(8,128)S(1)}, f32[8,128]{1,0:T(8,128)S(1)}, u32[]{:S(2)}, u32[]{:S(2)}) collective-permute-start(f32[8,128]{1,0:T(8,128)S(1)} %add.33.refs_0_), channel_id=1, source_target_pairs={{0,8},{4,12},{8,0},{12,4},{16,24},{20,28},{24,16},{28,20},{1,9},{5... | collective-permute-start | bytes 12296 | tf_op jit(solution)/shard_map/ppermute | solution.py:673
  140.2 3.4 %collective-permute-start.45 = (bf16[2,2,2,128,512]{4,3,2,1,0:T(8,128)(2,1)S(1)}, bf16[2,2,2,128,512]{4,3,2,1,0:T(8,128)(2,1)S(1)}, u32[]{:S(2)}, u32[]{:S(2)}) collective-permute-start(bf16[2,2,2,128,512]{4,3,2,1,0:T(8,128)(2,1)S(1)} %collective-permute-done.42.side_ref), channel_id=1, source_target_pairs={{0,1},{1,0},{2,3},{3,2},{4,5},{5,4},{6,7},{7,6},{8,9},{9,8},{10,11... | collective-permute-start | bytes 3145736 | tf_op jit(solution)/shard_map/ppermute | solution.py:673
  140.2 3.4 %collective-permute-start.44 = (bf16[2,2,128,512]{3,2,1,0:T(8,128)(2,1)S(1)}, bf16[2,2,128,512]{3,2,1,0:T(8,128)(2,1)S(1)}, u32[]{:S(2)}, u32[]{:S(2)}) collective-permute-start(bf16[2,2,128,512]{3,2,1,0:T(8,128)(2,1)S(1)} %get-tuple-element.321), channel_id=1, source_target_pairs={{0,1},{1,0},{2,3},{3,2},{4,5},{5,4},{6,7},{7,6},{8,9},{9,8},{10,11... | collective-permute-start | bytes 1572872 | tf_op jit(solution)/shard_map/ppermute | solution.py:673
  140.7 4.7 %collective-permute-start.46 = (bf16[2,16,5248]{2,1,0:T(8,128)(2,1)S(1)}, bf16[2,16,5248]{2,1,0:T(8,128)(2,1)S(1)}, u32[]{:S(2)}, u32[]{:S(2)}) collective-permute-start(bf16[2,16,5248]{2,1,0:T(8,128)(2,1)S(1)} %stack.7), channel_id=1, source_target_pairs={{0,1},{1,0},{2,3},{3,2},{4,5},{5,4},{6,7},{7,6},{8,9},{9,8},{10,11... | collective-permute-start | bytes 1007624 | tf_op jit(solution)/shard_map/ppermute | solution.py:673
  140.9 4.5 %collective-permute-start.43 = (f32[8,128]{1,0:T(8,128)S(1)}, f32[8,128]{1,0:T(8,128)S(1)}, u32[]{:S(2)}, u32[]{:S(2)}) collective-permute-start(f32[8,128]{1,0:T(8,128)S(1)} %add.34.refs_0_), channel_id=1, source_target_pairs={{0,2},{1,3},{2,0},{3,1},{4,6},{5,7},{6,4},{7,5},{8,10},{9,11},{10,... | collective-permute-start | bytes 12296 | tf_op jit(solution)/shard_map/ppermute | solution.py:673

commit v6 on v5

--- a/solution.py
+++ b/solution.py
@@ -94,7 +94,7 @@
         pltpu.make_async_copy(target, target, sem).wait()
 
 
-def cut_kernel(acts_ref, cots_ref, core_out, pair_out, sems):
+def cut_copies(acts_ref, cots_ref, core_out, pair_out, sems):
     rows_here = core_out.shape[1]
     narrow = lax.axis_index("narrow")
     copies = []
@@ -102,13 +102,21 @@
         for j, target in ((1, core_out.at[i]), (2, pair_out.at[0, i]), (3, pair_out.at[1, i])):
             source = ref.at[pl.ds((narrow ^ j) * rows_here, rows_here)]
             copies.append(pltpu.make_async_copy(source, target, sems.at[len(copies)]))
+    return copies
+
+
+def cut_kernel(acts_ref, cots_ref, core_out, pair_out, sems):
+    copies = cut_copies(acts_ref, cots_ref, core_out, pair_out, sems)
     for copy in copies:
         copy.start()
     for copy in copies:
         copy.wait()
 
 
-def pack_first_kernel(expand_ref, spatial_ref, gains_ref, bias_ref, out_ref, expand, spatial, gains, bias, sems):
+def open_kernel(
+    acts_ref, cots_ref, expand_ref, spatial_ref, gains_ref, bias_ref, core_out, pair_out, out_ref,
+    expand, spatial, gains, bias, sems, cut_sems,
+):
     rows = run((lax.axis_index("narrow") & 1) * 32, 32)
     copies = [
         pltpu.make_async_copy(expand_ref.at[rows, pl.ds(HALF, HALF)], expand, sems.at[0]),
@@ -116,7 +124,8 @@
         pltpu.make_async_copy(gains_ref, gains, sems.at[2]),
         pltpu.make_async_copy(bias_ref, bias, sems.at[3]),
     ]
-    for copy in copies:
+    cuts = cut_copies(acts_ref, cots_ref, core_out, pair_out, cut_sems)
+    for copy in copies + cuts:
         copy.start()
     for copy in copies:
         copy.wait()
@@ -131,6 +140,8 @@
     out_ref[:, HALF + ROW :] = vectors.astype(BF16)
     out_ref[:, :HALF] = expand[...].astype(BF16)
     out_ref[:, HALF : HALF + ROW] = spatial[...].astype(BF16)
+    for copy in cuts:
+        copy.wait()
 
 
 def pack_second_kernel(expand_ref, shrink_ref, expand_out, shrink_out, expand, shrink, sems):
@@ -751,31 +762,27 @@
 
     pair = shape((2, *part.shape), BF16)
 
-    def cut(acts, cots):
-        return call_kernel(
-            cut_kernel,
-            "cut",
-            [acts, cots],
-            [stored] * 2,
-            [(pair, stored), (shape((2, *pair.shape), BF16), stored)],
-            [dma((6,))],
+    cut_types = [(pair, stored), (shape((2, *pair.shape), BF16), stored)]
+    if tree:
+        core_cut, pair_cut, first_own = call_kernel(
+            open_kernel,
+            "open",
+            [
+                activations,
+                cotangent,
+                expand_weight,
+                spatial_weight,
+                norm_gains.reshape(2, LANES),
+                spatial_bias.reshape(1, 64),
+            ],
+            [stored] * 6,
+            cut_types + [shape((32, HALF + ROW + VECTOR_LANES), BF16)],
+            [pltpu.VMEM((32, HALF), F32), pltpu.VMEM((32, ROW), F32), pltpu.VMEM((2, LANES), F32)]
+            + [pltpu.VMEM((1, 64), F32), dma((4,)), dma((6,))],
             product // 64,
         )
-
-    if tree:
-        first_own = call_kernel(
-            pack_first_kernel,
-            "pack_first",
-            [expand_weight, spatial_weight, norm_gains.reshape(2, LANES), spatial_bias.reshape(1, 64)],
-            [stored] * 4,
-            [shape((32, HALF + ROW + VECTOR_LANES), BF16)],
-            [pltpu.VMEM((32, HALF), F32), pltpu.VMEM((32, ROW), F32), pltpu.VMEM((2, LANES), F32)]
-            + [pltpu.VMEM((1, 64), F32), dma((4,))],
-            product // 64,
-        )[0]
         over_z = lambda own: [swap_with(own, "wide", wide_size, 2 * s) for s in range(1, 4)]
         came_z = over_z(first_own)
-        core_cut, pair_cut = cut(after(activations, first_own), cotangent)
         side_came = cross_y(pair_cut)
         expand_own, shrink_own = call_kernel(
             pack_second_kernel,
@@ -819,7 +826,10 @@
         first_pieces = [expand_low[:, HALF:], gather(spatial_weight)]
         small_pieces = [small, small]
         expand_pieces, shrink_pieces = [expand_low[:, :HALF]], [gather(shrink_weight)]
-        core_came, side_came, forward_came = trade(*cut(activations, cotangent))
+        core_cut, pair_cut = call_kernel(
+            cut_kernel, "cut", [activations, cotangent], [stored] * 2, cut_types, [dma((6,))], product // 64
+        )
+        core_came, side_came, forward_came = trade(core_cut, pair_cut)
         count = 2
 
     low_d, low_half = shape((rows, ROW, D), BF16), shape((rows, ROW, HALF), BF16)

time: 150 us -> 149 us (level)
    pallas_call x28 -> x27, Pallas kernels: 57.3 us -> 56.4 us  [call_kernel(): pl.pallas_call(kernel, name=name, in_specs=in_specs, out_specs=specs, out...]
where the time goes in v6:
time: 149 us
  Pallas kernels  56.4 us (38%)
  waiting for transfers between devices  47.2 us (32%)
  starting transfers between devices  43.3 us (29%)
    pallas_call x27, Pallas kernels, call_kernel(): pl.pallas_call(kernel, name=name, in_specs=in_specs, out_specs=specs, out...  56.4 us
    ppermute x47, waiting for transfers between devices, swap_with(): return lax.ppermute(value, axis, [(i, i ^ bit) for i in range(size)])  47.2 us
    ppermute x47, starting transfers between devices, swap_with(): return lax.ppermute(value, axis, [(i, i ^ bit) for i in range(size)])  43.3 us
  transfers between devices with their start and end apart: 47, of which 20 were waited for; matrix products, arithmetic and copies ran while one was open for 0% of the time, Pallas kernels for 29%

profile of v6, /device:TPU:0, one launch (start us, length us, event | category | flops | bytes accessed | tf_op | source)
XLA Modules:
  0.0 148.5 jit_solution(6364959817996758849)
XLA Ops:
  0.7 1.5 %open.1 = (bf16[2,2,128,512]{3,2,1,0:T(8,128)(2,1)S(1)}, bf16[2,2,2,128,512]{4,3,2,1,0:T(8,128)(2,1)S(1)}, bf16[32,2176]{1,0:T(8,128)(2,1)S(1)}) custom-call(bf16[8,128,512]{2,1,0:T(8,128)(2,1)} %refs_13_, bf16[8,128,512]{2,1,0:T(8,128)(2,1)} %refs_12_, f32[64,3072]{1,0:T(8,128)} %refs_0_, f32[64,512]{1,0:T(8,128)} %refs_8_, f32[2,128]{1,0:T(2,128)} %bitcast.31, ...), custom_call_target="tpu_custom_call" | custom-call | flops 25165824 | bytes 50331 | tf_op jit(solution)/shard_map/open/pallas_call | solution.py:670
  2.2 3.0 %collective-permute-start.7 = (bf16[2,2,2,128,512]{4,3,2,1,0:T(8,128)(2,1)S(1)}, bf16[2,2,2,128,512]{4,3,2,1,0:T(8,128)(2,1)S(1)}, u32[]{:S(2)}, u32[]{:S(2)}) collective-permute-start(bf16[2,2,2,128,512]{4,3,2,1,0:T(8,128)(2,1)S(1)} %get-tuple-element.200), channel_id=1, source_target_pairs={{0,2},{1,3},{2,0},{3,1},{4,6},{5,7},{6,4},{7,5},{8,10},{9,11},{10,... | collective-permute-start | bytes 3145736 | tf_op jit(solution)/shard_map/ppermute | solution.py:684
  5.3 3.6 %collective-permute-start.2 = (bf16[32,2176]{1,0:T(8,128)(2,1)S(1)}, bf16[32,2176]{1,0:T(8,128)(2,1)S(1)}, u32[]{:S(2)}, u32[]{:S(2)}) collective-permute-start(bf16[32,2176]{1,0:T(8,128)(2,1)S(1)} %get-tuple-element.198.refs_0_), channel_id=1, source_target_pairs={{0,24},{4,28},{8,16},{12,20},{16,8},{20,12},{24,0},{28,4},{1,25},{... | collective-permute-start | bytes 417800 | tf_op jit(solution)/shard_map/ppermute | solution.py:684
  8.9 0.8 collective-permute-start
  9.6 1.1 pack_second.1
  10.7 2.9 %collective-permute-done.2.refs_3_ = bf16[32,2176]{1,0:T(8,128)(2,1)S(1)} collective-permute-done((bf16[32,2176]{1,0:T(8,128)(2,1)S(1)}, bf16[32,2176]{1,0:T(8,128)(2,1)S(1)}, u32[]{:S(2)}, u32[]{:S(2)}) %collective-permute-start.2) | collective-permute-done | bytes 139296 | tf_op jit(solution)/shard_map/ppermute | solution.py:684
  13.6 7.7 %collective-permute-done.1.refs_2_ = bf16[32,2176]{1,0:T(8,128)(2,1)S(1)} collective-permute-done((bf16[32,2176]{1,0:T(8,128)(2,1)S(1)}, bf16[32,2176]{1,0:T(8,128)(2,1)S(1)}, u32[]{:S(2)}, u32[]{:S(2)}) %collective-permute-start.1) | collective-permute-done | bytes 139296 | tf_op jit(solution)/shard_map/ppermute | solution.py:684
  21.4 1.6 %collective-permute-start.11 = (bf16[4,32,2176]{2,1,0:T(8,128)(2,1)S(1)}, bf16[4,32,2176]{2,1,0:T(8,128)(2,1)S(1)}, u32[]{:S(2)}, u32[]{:S(2)}) collective-permute-start(bf16[4,32,2176]{2,1,0:T(8,128)(2,1)S(1)} %stack.4.refs_0_.refs_4_), channel_id=1, source_target_pairs={{0,4},{4,0},{8,12},{12,8},{16,20},{20,16},{24,28},{28,24},{1,5},{5... | collective-permute-start | bytes 1671176 | tf_op jit(solution)/shard_map/ppermute | solution.py:684
  22.9 2.5 %collective-permute-start.6 = (bf16[32,1536]{1,0:T(8,128)(2,1)S(1)}, bf16[32,1536]{1,0:T(8,128)(2,1)S(1)}, u32[]{:S(2)}, u32[]{:S(2)}) collective-permute-start(bf16[32,1536]{1,0:T(8,128)(2,1)S(1)} %get-tuple-element.206.refs_0_), channel_id=1, source_target_pairs={{0,24},{4,28},{8,16},{12,20},{16,8},{20,12},{24,0},{28,4},{1,25},{... | collective-permute-start | bytes 294920 | tf_op jit(solution)/shard_map/ppermute | solution.py:684
  25.4 1.9 %collective-permute-start.4 = (bf16[32,1536]{1,0:T(8,128)(2,1)S(1)}, bf16[32,1536]{1,0:T(8,128)(2,1)S(1)}, u32[]{:S(2)}, u32[]{:S(2)}) collective-permute-start(bf16[32,1536]{1,0:T(8,128)(2,1)S(1)} %get-tuple-element.206.refs_0_), channel_id=1, source_target_pairs={{0,8},{4,12},{8,0},{12,4},{16,24},{20,28},{24,16},{28,20},{1,9},{5... | collective-permute-start | bytes 294920 | tf_op jit(solution)/shard_map/ppermute | solution.py:684
  27.3 3.2 %collective-permute-done.6.refs_3_ = bf16[32,1536]{1,0:T(8,128)(2,1)S(1)} collective-permute-done((bf16[32,1536]{1,0:T(8,128)(2,1)S(1)}, bf16[32,1536]{1,0:T(8,128)(2,1)S(1)}, u32[]{:S(2)}, u32[]{:S(2)}) %collective-permute-start.6) | collective-permute-done | bytes 98336 | tf_op jit(solution)/shard_map/ppermute | solution.py:684
  30.5 2.6 %collective-permute-done.5.refs_2_ = bf16[32,1536]{1,0:T(8,128)(2,1)S(1)} collective-permute-done((bf16[32,1536]{1,0:T(8,128)(2,1)S(1)}, bf16[32,1536]{1,0:T(8,128)(2,1)S(1)}, u32[]{:S(2)}, u32[]{:S(2)}) %collective-permute-start.5) | collective-permute-done | bytes 98336 | tf_op jit(solution)/shard_map/ppermute | solution.py:684
  33.2 0.5 collective-permute-start.14
  33.7 2.0 %collective-permute-done.11.refs_1_.refs_5_ = bf16[4,32,2176]{2,1,0:T(8,128)(2,1)S(1)} collective-permute-done((bf16[4,32,2176]{2,1,0:T(8,128)(2,1)S(1)}, bf16[4,32,2176]{2,1,0:T(8,128)(2,1)S(1)}, u32[]{:S(2)}, u32[]{:S(2)}) %collective-permute-start.11) | collective-permute-done | bytes 557088 | tf_op jit(solution)/shard_map/ppermute | solution.py:684
  35.7 1.5 %collective-permute-start.12 = (bf16[4,32,1536]{2,1,0:T(8,128)(2,1)S(1)}, bf16[4,32,1536]{2,1,0:T(8,128)(2,1)S(1)}, u32[]{:S(2)}, u32[]{:S(2)}) collective-permute-start(bf16[4,32,1536]{2,1,0:T(8,128)(2,1)S(1)} %stack.5.refs_0_), channel_id=1, source_target_pairs={{0,4},{4,0},{8,12},{12,8},{16,20},{20,16},{24,28},{28,24},{1,5},{5... | collective-permute-start | bytes 1179656 | tf_op jit(solution)/shard_map/ppermute | solution.py:684
  37.2 2.5 %collective-permute-start.10 = (bf16[32,1536]{1,0:T(8,128)(2,1)S(1)}, bf16[32,1536]{1,0:T(8,128)(2,1)S(1)}, u32[]{:S(2)}, u32[]{:S(2)}) collective-permute-start(bf16[32,1536]{1,0:T(8,128)(2,1)S(1)} %get-tuple-element.210.refs_0_), channel_id=1, source_target_pairs={{0,24},{4,28},{8,16},{12,20},{16,8},{20,12},{24,0},{28,4},{1,25},{... | collective-permute-start | bytes 294920 | tf_op jit(solution)/shard_map/ppermute | solution.py:684
  39.7 1.9 %collective-permute-start.8 = (bf16[32,1536]{1,0:T(8,128)(2,1)S(1)}, bf16[32,1536]{1,0:T(8,128)(2,1)S(1)}, u32[]{:S(2)}, u32[]{:S(2)}) collective-permute-start(bf16[32,1536]{1,0:T(8,128)(2,1)S(1)} %get-tuple-element.210.refs_0_), channel_id=1, source_target_pairs={{0,8},{4,12},{8,0},{12,4},{16,24},{20,28},{24,16},{28,20},{1,9},{5... | collective-permute-start | bytes 294920 | tf_op jit(solution)/shard_map/ppermute | solution.py:684
  41.6 7.7 %gating.1 = (bf16[2,512,512]{2,1,0:T(8,128)(2,1)S(1)}, bf16[2,512,512]{2,1,0:T(8,128)(2,1)S(1)}, f32[2,512,128]{2,1,0:T(8,128)S(1)}, bf16[2,512,1536]{2,1,0:T(8,...) custom-call(bf16[8,128,512]{2,1,0:T(8,128)(2,1)} %refs_13_, ...), custom_call_target="tpu_custom_call" | custom-call | flops 25165824 | bytes 50331 | tf_op jit(solution)/shard_map/gating/pallas_call | solution.py:670
  49.4 0.5 collective-permute-start.17
  49.9 0.6 collective-permute-start.18
  50.5 2.5 %mixing.1.mixed_ref = bf16[2,512,1536]{2,1,0:T(8,128)(2,1)S(1)} custom-call(s32[8,5]{1,0:T(8,128)S(1)} %copy-done, bf16[512,512]{1,0:T(8,128)(2,1)S(1)} %get-tuple-element.219.spatial_ref, bf16[2,512,1536]{2,1,0:T(8,128)(2,1)S(1)} %get-tuple-element.220.gate_ref, f32[512,128]{1,0:T(8,128)S(1)} %get-tuple-element.225.bias_col), custom_call_target="tpu_custom_call" | custom-call | flops 25165824 | bytes 50331 | tf_op jit(solution)/shard_map/mixing/pallas_call | solution.py:670
  53.0 8.2 %content_up.1 = (bf16[2,512,1536]{2,1,0:T(8,128)(2,1)S(1)}, bf16[2,512,1536]{2,1,0:T(8,128)(2,1)S(1)}, bf16[512,1536]{1,0:T(8,128)(2,1)S(1)}, bf16[512,1024]{1,0:T(8,128)(2,1)S(1)}, bf16[1024,512]{1,0:T(8,128)(2,1)S(1)}) custom-call(bf16[2,512,512]{2,1,0:T(8,128)(2,1)S(1)} %get-tuple-element.243.normed_ref, bf16[8,128,512]{2,1,0:T(8,128)(2,1)} %refs_12_, ...), custom_call_target="tpu_custom_call" | custom-call | flops 25165824 | bytes 50331 | tf_op jit(solution)/shard_map/content_up/pallas_call | solution.py:670
  61.2 0.6 collective-permute-start.20
  61.8 1.3 collective-permute-done.20.refs_3_
  63.1 7.0 %content_down.1 = (bf16[2,512,1536]{2,1,0:T(8,128)(2,1)S(1)}, bf16[2,512,1536]{2,1,0:T(8,128)(2,1)S(1)}, bf16[2,512,1536]{2,1,0:T(8,128)(2,1)S(1)}, f32[512,128]...) custom-call(s32[8,5]{1,0:T(8,128)S(1)} %copy-done, ...), custom_call_target="tpu_custom_call" | custom-call | flops 25165824 | bytes 50331 | tf_op jit(solution)/shard_map/content_down/pallas_call | solution.py:670
  70.5 1.9 %content_sum.1 = (bf16[2,4,16,1536]{3,2,1,0:T(8,128)(2,1)S(1)}, bf16[2,4,16,1536]{3,2,1,0:T(8,128)(2,1)S(1)}, bf16[2,2,4,16,1536]{4,3,2,1,0:T(8,128)(2,1)S(1)}) custom-call(bf16[2,512,512]{2,1,0:T(8,128)(2,1)S(1)} %get-tuple-element.243.normed_ref, bf16[2,512,1536]{2,1,0:T(8,128)(2,1)S(1)} %get-tuple-element.234.grad_ref.content_grad_ref), custom_call_target="tpu_custom_call" | custom-call | flops 25165824 | bytes 50331 | tf_op jit(solution)/shard_map/content_sum/pallas_call | solution.py:670
  72.8 0.6 collective-permute-start.23
  73.4 2.5 %spatial_sum.1.square_ref = f32[512,512]{1,0:T(8,128)S(1)} custom-call(s32[8,5]{1,0:T(8,128)S(1)} %copy-done, bf16[2,512,1536]{2,1,0:T(8,128)(2,1)S(1)} %get-tuple-element.245.grad_mixed_ref, bf16[2,512,1536]{2,1,0:T(8,128)(2,1)S(1)} %get-tuple-element.220.gate_ref), custom_call_target="tpu_custom_call" | custom-call | flops 25165824 | bytes 50331 | tf_op jit(solution)/shard_map/spatial_sum/pallas_call | solution.py:670
  76.0 1.6 %collective-permute-start.24 = (bf16[2,4,16,1536]{3,2,1,0:T(8,128)(2,1)S(1)}, bf16[2,4,16,1536]{3,2,1,0:T(8,128)(2,1)S(1)}, u32[]{:S(2)}, u32[]{:S(2)}) collective-permute-start(bf16[2,4,16,1536]{3,2,1,0:T(8,128)(2,1)S(1)} %fusion), channel_id=1, source_target_pairs={{0,4},{4,0},{8,12},{12,8},{16,20},{20,16},{24,28},{28,24},{1,5},{5... | collective-permute-start | bytes 1179656 | tf_op jit(solution)/shard_map/ppermute | solution.py:684
  77.5 6.6 %gate_back.1 = (bf16[2,512,1536]{2,1,0:T(8,128)(2,1)S(1)}, f32[8,16,128]{2,1,0:T(8,128)S(1)}) custom-call(s32[8,5]{1,0:T(8,128)S(1)} %copy-done, bf16[2,512,1536]{2,1,0:T(8,128)(2,1)S(1)} %get-tuple-element.245.grad_mixed_ref, bf16[2,512,1536]{2,1,0:T(8,128)(2,1)S(1)} %get-tuple-element.220.gate_ref, bf16[2,512,1536]{2,1,0:T(8,128)(2,1)S(1)} %get-tuple-element.246.slope_ref, ...), custom_call_target="tpu_custom_call" | custom-call | flops 25165824 | bytes 50331 | tf_op jit(solution)/shard_map/gate_back/pallas_call | solution.py:670
  84.2 2.0 %gate_sum.1 = (bf16[2,4,16,1024]{3,2,1,0:T(8,128)(2,1)S(1)}, bf16[2,4,16,1024]{3,2,1,0:T(8,128)(2,1)S(1)}, bf16[2,2,4,16,1024]{4,3,2,1,0:T(8,128)(2,1)S(1)}, bf1...) custom-call(bf16[2,512,512]{2,1,0:T(8,128)(2,1)S(1)} %get-tuple-elem, ...), custom_call_target="tpu_custom_call" | custom-call | flops 25165824 | bytes 50331 | tf_op jit(solution)/shard_map/gate_sum/pallas_call | solution.py:670
  86.2 0.9 collective-permute-done.24.refs_2_
  87.2 0.5 collective-permute-start.25
  87.8 1.9 %layer.1 = (bf16[2,128,512]{2,1,0:T(8,128)(2,1)S(1)}, bf16[2,128,512]{2,1,0:T(8,128)(2,1)S(1)}, bf16[2,2,128,512]{3,2,1,0:T(8,128)(2,1)S(1)}) custom-call(bf16[2,512,1536]{2,1,0:T(8,128)(2,1)S(1)} %get-tuple-element.264.gated_ref, bf16[1536,512]{1,0:T(8,128)(2,1)S(1)} %get-tuple-element.265.shrink), custom_call_target="tpu_custom_call" | custom-call | flops 25165824 | bytes 50331 | tf_op jit(solution)/shard_map/layer/pallas_call | solution.py:670
  90.0 1.6 %collective-permute-start.28 = (bf16[2,4,16,1152]{3,2,1,0:T(8,128)(2,1)S(1)}, bf16[2,4,16,1152]{3,2,1,0:T(8,128)(2,1)S(1)}, u32[]{:S(2)}, u32[]{:S(2)}) collective-permute-start(bf16[2,4,16,1152]{3,2,1,0:T(8,128)(2,1)S(1)} %fusion.2), channel_id=1, source_target_pairs={{0,2},{1,3},{2,0},{3,1},{4,6},{5,7},{6,4},{7,5},{8,10},{9,11},{10,... | collective-permute-start | bytes 884744 | tf_op jit(solution)/shard_map/ppermute | solution.py:684
  91.6 1.6 %collective-permute-start.27 = (bf16[2,4,16,1024]{3,2,1,0:T(8,128)(2,1)S(1)}, bf16[2,4,16,1024]{3,2,1,0:T(8,128)(2,1)S(1)}, u32[]{:S(2)}, u32[]{:S(2)}) collective-permute-start(bf16[2,4,16,1024]{3,2,1,0:T(8,128)(2,1)S(1)} %fusion.3), channel_id=1, source_target_pairs={{0,4},{4,0},{8,12},{12,8},{16,20},{20,16},{24,28},{28,24},{1,5},{5... | collective-permute-start | bytes 786440 | tf_op jit(solution)/shard_map/ppermute | solution.py:684
  93.2 0.5 collective-permute-start.29
  93.7 0.5 collective-permute-start.30
  94.3 3.9 %back.1 = (bf16[2,128,512]{2,1,0:T(8,128)(2,1)S(1)}, bf16[2,2,128,512]{3,2,1,0:T(8,128)(2,1)S(1)}, bf16[2,2,2,128,512]{4,3,2,1,0:T(8,128)(2,1)S(1)}) custom-call(bf16[2,512,1536]{2,1,0:T(8,128)(2,1)S(1)} %get-tuple-element.271.grad_ref.gate_grad_ref, bf16[2,512,1536]{2,1,0:T(8,128)(2,1)S(1)} %get-tuple-element.234.grad_ref.content_grad_ref, ...), custom_call_target="tpu_custom_call" | custom-call | flops 25165824 | bytes 50331 | tf_op jit(solution)/shard_map/back/pallas_call | solution.py:670
  98.1 5.2 %collective-permute-done.29.refs_12_ = bf16[4,16,1536]{2,1,0:T(8,128)(2,1)S(1)} collective-permute-done((bf16[4,16,1536]{2,1,0:T(8,128)(2,1)S(1)}, bf16[4,16,1536]{2,1,0:T(8,128)(2,1)S(1)}, u32[]{:S(2)}, u32[]{:S(2)}) %collective-permute-start.29) | collective-permute-done | bytes 196640 | tf_op jit(solution)/shard_map/ppermute | solution.py:684
  103.3 0.7 collective-permute-done.30.refs_14_
  104.1 1.6 %collective-permute-start.32 = (bf16[4,16,1152]{2,1,0:T(8,128)(2,1)S(1)}, bf16[4,16,1152]{2,1,0:T(8,128)(2,1)S(1)}, u32[]{:S(2)}, u32[]{:S(2)}) collective-permute-start(bf16[4,16,1152]{2,1,0:T(8,128)(2,1)S(1)} %get-tuple-element.285), channel_id=1, source_target_pairs={{0,4},{4,0},{8,12},{12,8},{16,20},{20,16},{24,28},{28,24},{1,5},{5... | collective-permute-start | bytes 442376 | tf_op jit(solution)/shard_map/ppermute | solution.py:684
  105.7 0.9 collective-permute-start.31
  106.5 4.1 %collective-permute-done.31.refs_13_ = bf16[4,16,1024]{2,1,0:T(8,128)(2,1)S(1)} collective-permute-done((bf16[4,16,1024]{2,1,0:T(8,128)(2,1)S(1)}, bf16[4,16,1024]{2,1,0:T(8,128)(2,1)S(1)}, u32[]{:S(2)}, u32[]{:S(2)}) %collective-permute-start.31) | collective-permute-done | bytes 131104 | tf_op jit(solution)/shard_map/ppermute | solution.py:684
  111.0 0.9 collective-permute-start.42
  111.9 1.0 collective-permute-start.34
  113.0 1.5 %collective-permute-start.35 = (bf16[16,5248]{1,0:T(8,128)(2,1)S(1)}, bf16[16,5248]{1,0:T(8,128)(2,1)S(1)}, u32[]{:S(2)}, u32[]{:S(2)}) collective-permute-start(bf16[16,5248]{1,0:T(8,128)(2,1)S(1)} %get-tuple-element.289), channel_id=1, source_target_pairs={{0,24},{4,28},{8,16},{12,20},{16,8},{20,12},{24,0},{28,4},{1,25},{... | collective-permute-start | bytes 503816 | tf_op jit(solution)/shard_map/ppermute | solution.py:684
  114.5 0.9 collective-permute-start.33
  115.4 3.2 %fetch.1 = (f32[64,3072]{1,0:T(8,128)S(1)}, f32[64,3072]{1,0:T(8,128)S(1)}, f32[64,3072]{1,0:T(8,128)S(1)}, f32[64,3072]{1,0:T(8,128)S(1)}, f32[192,512]{1,0:T(8...) custom-call(f32[64,3072]{1,0:T(8,128)} %refs_0_, ...), custom_call_target="tpu_custom_call" | custom-call | flops 25165824 | bytes 50331 | tf_op jit(solution)/shard_map/fetch/pallas_call | solution.py:670
  118.7 5.4 %collective-permute-done.34.two_ref = bf16[16,5248]{1,0:T(8,128)(2,1)S(1)} collective-permute-done((bf16[16,5248]{1,0:T(8,128)(2,1)S(1)}, bf16[16,5248]{1,0:T(8,128)(2,1)S(1)}, u32[]{:S(2)}, u32[]{:S(2)}) %collective-permute-start.34) | collective-permute-done | bytes 167968 | tf_op jit(solution)/shard_map/ppermute | solution.py:684
  124.1 1.2 collective-permute-done.33.one_ref
  125.6 0.9 collective-permute-start.41
  126.6 1.2 collective-permute-done.36.refs_1_
  128.0 3.4 %collective-permute-done.37.refs_1_ = f32[8,128]{1,0:T(8,128)S(1)} collective-permute-done((f32[8,128]{1,0:T(8,128)S(1)}, f32[8,128]{1,0:T(8,128)S(1)}, u32[]{:S(2)}, u32[]{:S(2)}) %collective-permute-start.37) | collective-permute-done | bytes 4128 | tf_op jit(solution)/shard_map/ppermute | solution.py:684
  131.4 2.1 %collective-permute-start.40 = (f32[8,128]{1,0:T(8,128)S(1)}, f32[8,128]{1,0:T(8,128)S(1)}, u32[]{:S(2)}, u32[]{:S(2)}) collective-permute-start(f32[8,128]{1,0:T(8,128)S(1)} %add.33.refs_0_), channel_id=1, source_target_pairs={{0,24},{4,28},{8,16},{12,20},{16,8},{20,12},{24,0},{28,4},{1,25},{... | collective-permute-start | bytes 12296 | tf_op jit(solution)/shard_map/ppermute | solution.py:684
  133.5 2.2 %collective-permute-start.39 = (f32[8,128]{1,0:T(8,128)S(1)}, f32[8,128]{1,0:T(8,128)S(1)}, u32[]{:S(2)}, u32[]{:S(2)}) collective-permute-start(f32[8,128]{1,0:T(8,128)S(1)} %add.33.refs_0_), channel_id=1, source_target_pairs={{0,16},{4,20},{8,24},{12,28},{16,0},{20,4},{24,8},{28,12},{1,17},{... | collective-permute-start | bytes 12296 | tf_op jit(solution)/shard_map/ppermute | solution.py:684
  135.8 1.0 collective-permute-done.40.refs_3_
  136.8 1.2 collective-permute-done.39.refs_2_
  138.0 1.3 collective-permute-done.38.refs_1_
  139.3 0.5 collective-permute-start.44
  140.0 1.2 collective-permute-start.43
  141.2 1.5 %collective-permute-done.44.core_ref = bf16[2,2,128,512]{3,2,1,0:T(8,128)(2,1)S(1)} collective-permute-done((bf16[2,2,128,512]{3,2,1,0:T(8,128)(2,1)S(1)}, bf16[2,2,128,512]{3,2,1,0:T(8,128)(2,1)S(1)}, u32[]{:S(2)}, u32[]{:S(2)}) %collective-permute-start.44) | collective-permute-done | bytes 524320 | tf_op jit(solution)/shard_map/ppermute | solution.py:684
  142.7 1.8 %give.1 = (f32[8,128,512]{2,1,0:T(8,128)}, bf16[8,128,512]{2,1,0:T(8,128)(2,1)}) custom-call(bf16[8,128,512]{2,1,0:T(8,128)(2,1)S(1)} %get-tuple-element.316.cots_ref, bf16[8,128,512]{2,1,0:T(8,128)(2,1)S(1)} %get-tuple-element.317.acts_ref, bf16[2,128,512]{2,1,0:T(8,128)(2,1)S(1)} %get-tuple-element.318.grad_own, ...), custom_call_target="tpu_custom_call" | custom-call | flops 25165824 | bytes 50331 | tf_op jit(solution)/shard_map/give/pallas_call | solution.py:670
  144.7 3.7 %adam.1 = (f32[64,3072]{1,0:T(8,128)}, f32[64,3072]{1,0:T(8,128)}, f32[64,3072]{1,0:T(8,128)}, f32[64,3072]{1,0:T(8,128)}, f32[64,3072]{1,0:T(8,128)}, /*index=5...) custom-call(f32[8,128]{1,0:T(8,128)S(1)} %add.35.message_ref, ...), custom_call_target="tpu_custom_call" | custom-call | flops 25165824 | bytes 50331 | tf_op jit(solution)/shard_map/adam/pallas_call | solution.py:670
  (79 shorter events, 3.1 us)
Async XLA Ops:
  2.2 30.9 %collective-permute-start.7 = (bf16[2,2,2,128,512]{4,3,2,1,0:T(8,128)(2,1)S(1)}, bf16[2,2,2,128,512]{4,3,2,1,0:T(8,128)(2,1)S(1)}, u32[]{:S(2)}, u32[]{:S(2)}) collective-permute-start(bf16[2,2,2,128,512]{4,3,2,1,0:T(8,128)(2,1)S(1)} %get-tuple-element.200), channel_id=1, source_target_pairs={{0,2},{1,3},{2,0},{3,1},{4,6},{5,7},{6,4},{7,5},{8,10},{9,11},{10,... | collective-permute-start | bytes 3145736 | tf_op jit(solution)/shard_map/ppermute | solution.py:684
  5.3 16.1 %collective-permute-start.3 = (bf16[2,2,128,512]{3,2,1,0:T(8,128)(2,1)S(1)}, bf16[2,2,128,512]{3,2,1,0:T(8,128)(2,1)S(1)}, u32[]{:S(2)}, u32[]{:S(2)}) collective-permute-start(bf16[2,2,128,512]{3,2,1,0:T(8,128)(2,1)S(1)} %get-tuple-element.199), channel_id=1, source_target_pairs={{0,1},{1,0},{2,3},{3,2},{4,5},{5,4},{6,7},{7,6},{8,9},{9,8},{10,11... | collective-permute-start | bytes 1572872 | tf_op jit(solution)/shard_map/ppermute | solution.py:684
  5.3 8.4 %collective-permute-start.2 = (bf16[32,2176]{1,0:T(8,128)(2,1)S(1)}, bf16[32,2176]{1,0:T(8,128)(2,1)S(1)}, u32[]{:S(2)}, u32[]{:S(2)}) collective-permute-start(bf16[32,2176]{1,0:T(8,128)(2,1)S(1)} %get-tuple-element.198.refs_0_), channel_id=1, source_target_pairs={{0,24},{4,28},{8,16},{12,20},{16,8},{20,12},{24,0},{28,4},{1,25},{... | collective-permute-start | bytes 417800 | tf_op jit(solution)/shard_map/ppermute | solution.py:684
  8.9 12.4 %collective-permute-start.1 = (bf16[32,2176]{1,0:T(8,128)(2,1)S(1)}, bf16[32,2176]{1,0:T(8,128)(2,1)S(1)}, u32[]{:S(2)}, u32[]{:S(2)}) collective-permute-start(bf16[32,2176]{1,0:T(8,128)(2,1)S(1)} %get-tuple-element.198.refs_0_), channel_id=1, source_target_pairs={{0,16},{4,20},{8,24},{12,28},{16,0},{20,4},{24,8},{28,12},{1,17},{... | collective-permute-start | bytes 417800 | tf_op jit(solution)/shard_map/ppermute | solution.py:684
  8.9 12.4 %collective-permute-start = (bf16[32,2176]{1,0:T(8,128)(2,1)S(1)}, bf16[32,2176]{1,0:T(8,128)(2,1)S(1)}, u32[]{:S(2)}, u32[]{:S(2)}) collective-permute-start(bf16[32,2176]{1,0:T(8,128)(2,1)S(1)} %get-tuple-element.198.refs_0_), channel_id=1, source_target_pairs={{0,8},{4,12},{8,0},{12,4},{16,24},{20,28},{24,16},{28,20},{1,9},{5... | collective-permute-start | bytes 417800 | tf_op jit(solution)/shard_map/ppermute | solution.py:684
  21.4 14.3 %collective-permute-start.11 = (bf16[4,32,2176]{2,1,0:T(8,128)(2,1)S(1)}, bf16[4,32,2176]{2,1,0:T(8,128)(2,1)S(1)}, u32[]{:S(2)}, u32[]{:S(2)}) collective-permute-start(bf16[4,32,2176]{2,1,0:T(8,128)(2,1)S(1)} %stack.4.refs_0_.refs_4_), channel_id=1, source_target_pairs={{0,4},{4,0},{8,12},{12,8},{16,20},{20,16},{24,28},{28,24},{1,5},{5... | collective-permute-start | bytes 1671176 | tf_op jit(solution)/shard_map/ppermute | solution.py:684
  22.9 7.6 %collective-permute-start.6 = (bf16[32,1536]{1,0:T(8,128)(2,1)S(1)}, bf16[32,1536]{1,0:T(8,128)(2,1)S(1)}, u32[]{:S(2)}, u32[]{:S(2)}) collective-permute-start(bf16[32,1536]{1,0:T(8,128)(2,1)S(1)} %get-tuple-element.206.refs_0_), channel_id=1, source_target_pairs={{0,24},{4,28},{8,16},{12,20},{16,8},{20,12},{24,0},{28,4},{1,25},{... | collective-permute-start | bytes 294920 | tf_op jit(solution)/shard_map/ppermute | solution.py:684
  25.4 7.7 %collective-permute-start.5 = (bf16[32,1536]{1,0:T(8,128)(2,1)S(1)}, bf16[32,1536]{1,0:T(8,128)(2,1)S(1)}, u32[]{:S(2)}, u32[]{:S(2)}) collective-permute-start(bf16[32,1536]{1,0:T(8,128)(2,1)S(1)} %get-tuple-element.206.refs_0_), channel_id=1, source_target_pairs={{0,16},{4,20},{8,24},{12,28},{16,0},{20,4},{24,8},{28,12},{1,17},{... | collective-permute-start | bytes 294920 | tf_op jit(solution)/shard_map/ppermute | solution.py:684
  25.4 7.7 %collective-permute-start.4 = (bf16[32,1536]{1,0:T(8,128)(2,1)S(1)}, bf16[32,1536]{1,0:T(8,128)(2,1)S(1)}, u32[]{:S(2)}, u32[]{:S(2)}) collective-permute-start(bf16[32,1536]{1,0:T(8,128)(2,1)S(1)} %get-tuple-element.206.refs_0_), channel_id=1, source_target_pairs={{0,8},{4,12},{8,0},{12,4},{16,24},{20,28},{24,16},{28,20},{1,9},{5... | collective-permute-start | bytes 294920 | tf_op jit(solution)/shard_map/ppermute | solution.py:684
  33.1 8.5 %collective-permute-start.13 = (bf16[2,2,2,128,512]{4,3,2,1,0:T(8,128)(2,1)S(1)}, bf16[2,2,2,128,512]{4,3,2,1,0:T(8,128)(2,1)S(1)}, u32[]{:S(2)}, u32[]{:S(2)}) collective-permute-start(bf16[2,2,2,128,512]{4,3,2,1,0:T(8,128)(2,1)S(1)} %collective-permute-done.7.side_ref), channel_id=1, source_target_pairs={{0,1},{1,0},{2,3},{3,2},{4,5},{5,4},{6,7},{7,6},{8,9},{9,8},{10,11... | collective-permute-start | bytes 3145736 | tf_op jit(solution)/shard_map/ppermute | solution.py:684
  33.2 6.5 %collective-permute-start.14 = (bf16[4,32,2176]{2,1,0:T(8,128)(2,1)S(1)}, bf16[4,32,2176]{2,1,0:T(8,128)(2,1)S(1)}, u32[]{:S(2)}, u32[]{:S(2)}) collective-permute-start(bf16[4,32,2176]{2,1,0:T(8,128)(2,1)S(1)} %stack.4.refs_0_.refs_4_), channel_id=1, source_target_pairs={{0,1},{1,0},{2,3},{3,2},{4,5},{5,4},{6,7},{7,6},{8,9},{9,8},{10,11... | collective-permute-start | bytes 1671176 | tf_op jit(solution)/shard_map/ppermute | solution.py:684
  35.7 4.0 %collective-permute-start.15 = (bf16[4,32,2176]{2,1,0:T(8,128)(2,1)S(1)}, bf16[4,32,2176]{2,1,0:T(8,128)(2,1)S(1)}, u32[]{:S(2)}, u32[]{:S(2)}) collective-permute-start(bf16[4,32,2176]{2,1,0:T(8,128)(2,1)S(1)} %collective-permute-done.11.refs_1_.refs_5_), channel_id=1, source_target_pairs={{0,1},{1,0},{2,3},{3,2},{4,5},{5,4},{6,7},{7,6},{8,9},{9,8},{10,11... | collective-permute-start | bytes 1671176 | tf_op jit(solution)/shard_map/ppermute | solution.py:684
  35.7 13.6 %collective-permute-start.12 = (bf16[4,32,1536]{2,1,0:T(8,128)(2,1)S(1)}, bf16[4,32,1536]{2,1,0:T(8,128)(2,1)S(1)}, u32[]{:S(2)}, u32[]{:S(2)}) collective-permute-start(bf16[4,32,1536]{2,1,0:T(8,128)(2,1)S(1)} %stack.5.refs_0_), channel_id=1, source_target_pairs={{0,4},{4,0},{8,12},{12,8},{16,20},{20,16},{24,28},{28,24},{1,5},{5... | collective-permute-start | bytes 1179656 | tf_op jit(solution)/shard_map/ppermute | solution.py:684
  37.2 13.3 %copy-start = (s32[8,5]{1,0:T(8,128)S(1)}, s32[8,5]{1,0:T(8,128)}, u32[]{:S(2)}) copy-start(s32[8,5]{1,0:T(8,128)} %lens_ref.7) | copy-start | bytes 484
  37.2 12.1 %collective-permute-start.10 = (bf16[32,1536]{1,0:T(8,128)(2,1)S(1)}, bf16[32,1536]{1,0:T(8,128)(2,1)S(1)}, u32[]{:S(2)}, u32[]{:S(2)}) collective-permute-start(bf16[32,1536]{1,0:T(8,128)(2,1)S(1)} %get-tuple-element.210.refs_0_), channel_id=1, source_target_pairs={{0,24},{4,28},{8,16},{12,20},{16,8},{20,12},{24,0},{28,4},{1,25},{... | collective-permute-start | bytes 294920 | tf_op jit(solution)/shard_map/ppermute | solution.py:684
  39.7 9.6 %collective-permute-start.9 = (bf16[32,1536]{1,0:T(8,128)(2,1)S(1)}, bf16[32,1536]{1,0:T(8,128)(2,1)S(1)}, u32[]{:S(2)}, u32[]{:S(2)}) collective-permute-start(bf16[32,1536]{1,0:T(8,128)(2,1)S(1)} %get-tuple-element.210.refs_0_), channel_id=1, source_target_pairs={{0,16},{4,20},{8,24},{12,28},{16,0},{20,4},{24,8},{28,12},{1,17},{... | collective-permute-start | bytes 294920 | tf_op jit(solution)/shard_map/ppermute | solution.py:684
  39.7 9.6 %collective-permute-start.8 = (bf16[32,1536]{1,0:T(8,128)(2,1)S(1)}, bf16[32,1536]{1,0:T(8,128)(2,1)S(1)}, u32[]{:S(2)}, u32[]{:S(2)}) collective-permute-start(bf16[32,1536]{1,0:T(8,128)(2,1)S(1)} %get-tuple-element.210.refs_0_), channel_id=1, source_target_pairs={{0,8},{4,12},{8,0},{12,4},{16,24},{20,28},{24,16},{28,20},{1,9},{5... | collective-permute-start | bytes 294920 | tf_op jit(solution)/shard_map/ppermute | solution.py:684
  49.3 3.7 %collective-permute-start.16 = (bf16[4,32,1536]{2,1,0:T(8,128)(2,1)S(1)}, bf16[4,32,1536]{2,1,0:T(8,128)(2,1)S(1)}, u32[]{:S(2)}, u32[]{:S(2)}) collective-permute-start(bf16[4,32,1536]{2,1,0:T(8,128)(2,1)S(1)} %collective-permute-done.12.refs_1_), channel_id=1, source_target_pairs={{0,1},{1,0},{2,3},{3,2},{4,5},{5,4},{6,7},{7,6},{8,9},{9,8},{10,11... | collective-permute-start | bytes 1179656 | tf_op jit(solution)/shard_map/ppermute | solution.py:684
  49.4 3.6 %collective-permute-start.17 = (bf16[4,32,1536]{2,1,0:T(8,128)(2,1)S(1)}, bf16[4,32,1536]{2,1,0:T(8,128)(2,1)S(1)}, u32[]{:S(2)}, u32[]{:S(2)}) collective-permute-start(bf16[4,32,1536]{2,1,0:T(8,128)(2,1)S(1)} %stack.5.refs_0_), channel_id=1, source_target_pairs={{0,1},{1,0},{2,3},{3,2},{4,5},{5,4},{6,7},{7,6},{8,9},{9,8},{10,11... | collective-permute-start | bytes 1179656 | tf_op jit(solution)/shard_map/ppermute | solution.py:684
  49.9 11.3 %collective-permute-start.18 = (bf16[4,32,1536]{2,1,0:T(8,128)(2,1)S(1)}, bf16[4,32,1536]{2,1,0:T(8,128)(2,1)S(1)}, u32[]{:S(2)}, u32[]{:S(2)}) collective-permute-start(bf16[4,32,1536]{2,1,0:T(8,128)(2,1)S(1)} %stack.6.refs_0_), channel_id=1, source_target_pairs={{0,4},{4,0},{8,12},{12,8},{16,20},{20,16},{24,28},{28,24},{1,5},{5... | collective-permute-start | bytes 1179656 | tf_op jit(solution)/shard_map/ppermute | solution.py:684
  50.5 11.3 %collective-permute-start.19 = (bf16[4,32,1536]{2,1,0:T(8,128)(2,1)S(1)}, bf16[4,32,1536]{2,1,0:T(8,128)(2,1)S(1)}, u32[]{:S(2)}, u32[]{:S(2)}) collective-permute-start(bf16[4,32,1536]{2,1,0:T(8,128)(2,1)S(1)} %stack.6.refs_0_), channel_id=1, source_target_pairs={{0,1},{1,0},{2,3},{3,2},{4,5},{5,4},{6,7},{7,6},{8,9},{9,8},{10,11... | collective-permute-start | bytes 1179656 | tf_op jit(solution)/shard_map/ppermute | solution.py:684
  61.2 1.9 %collective-permute-start.20 = (bf16[4,32,1536]{2,1,0:T(8,128)(2,1)S(1)}, bf16[4,32,1536]{2,1,0:T(8,128)(2,1)S(1)}, u32[]{:S(2)}, u32[]{:S(2)}) collective-permute-start(bf16[4,32,1536]{2,1,0:T(8,128)(2,1)S(1)} %collective-permute-done.18.refs_1_), channel_id=1, source_target_pairs={{0,1},{1,0},{2,3},{3,2},{4,5},{5,4},{6,7},{7,6},{8,9},{9,8},{10,11... | collective-permute-start | bytes 1179656 | tf_op jit(solution)/shard_map/ppermute | solution.py:684
  70.1 2.6 %collective-permute-start.21 = (bf16[2,2,4,16,1536]{4,3,2,1,0:T(8,128)(2,1)S(1)}, bf16[2,2,4,16,1536]{4,3,2,1,0:T(8,128)(2,1)S(1)}, u32[]{:S(2)}, u32[]{:S(2)}) collective-permute-start(bf16[2,2,4,16,1536]{4,3,2,1,0:T(8,128)(2,1)S(1)} %get-tuple-element.233), channel_id=1, source_target_pairs={{0,1},{1,0},{2,3},{3,2},{4,5},{5,4},{6,7},{7,6},{8,9},{9,8},{10,11... | collective-permute-start | bytes 2359304 | tf_op jit(solution)/shard_map/ppermute | solution.py:684
  72.5 3.4 %collective-permute-start.22 = (bf16[2,2,4,16,1536]{4,3,2,1,0:T(8,128)(2,1)S(1)}, bf16[2,2,4,16,1536]{4,3,2,1,0:T(8,128)(2,1)S(1)}, u32[]{:S(2)}, u32[]{:S(2)}) collective-permute-start(bf16[2,2,4,16,1536]{4,3,2,1,0:T(8,128)(2,1)S(1)} %get-tuple-element.237), channel_id=1, source_target_pairs={{0,1},{1,0},{2,3},{3,2},{4,5},{5,4},{6,7},{7,6},{8,9},{9,8},{10,11... | collective-permute-start | bytes 2359304 | tf_op jit(solution)/shard_map/ppermute | solution.py:684
  72.8 11.5 %collective-permute-start.23 = (bf16[2,4,16,1536]{3,2,1,0:T(8,128)(2,1)S(1)}, bf16[2,4,16,1536]{3,2,1,0:T(8,128)(2,1)S(1)}, u32[]{:S(2)}, u32[]{:S(2)}) collective-permute-start(bf16[2,4,16,1536]{3,2,1,0:T(8,128)(2,1)S(1)} %fusion.1), channel_id=1, source_target_pairs={{0,2},{1,3},{2,0},{3,1},{4,6},{5,7},{6,4},{7,5},{8,10},{9,11},{10,... | collective-permute-start | bytes 1179656 | tf_op jit(solution)/shard_map/ppermute | solution.py:684
  76.0 11.2 %collective-permute-start.24 = (bf16[2,4,16,1536]{3,2,1,0:T(8,128)(2,1)S(1)}, bf16[2,4,16,1536]{3,2,1,0:T(8,128)(2,1)S(1)}, u32[]{:S(2)}, u32[]{:S(2)}) collective-permute-start(bf16[2,4,16,1536]{3,2,1,0:T(8,128)(2,1)S(1)} %fusion), channel_id=1, source_target_pairs={{0,4},{4,0},{8,12},{12,8},{16,20},{20,16},{24,28},{28,24},{1,5},{5... | collective-permute-start | bytes 1179656 | tf_op jit(solution)/shard_map/ppermute | solution.py:684
  87.2 2.8 %collective-permute-start.26 = (bf16[2,2,4,16,1152]{4,3,2,1,0:T(8,128)(2,1)S(1)}, bf16[2,2,4,16,1152]{4,3,2,1,0:T(8,128)(2,1)S(1)}, u32[]{:S(2)}, u32[]{:S(2)}) collective-permute-start(bf16[2,2,4,16,1152]{4,3,2,1,0:T(8,128)(2,1)S(1)} %get-tuple-element.258), channel_id=1, source_target_pairs={{0,1},{1,0},{2,3},{3,2},{4,5},{5,4},{6,7},{7,6},{8,9},{9,8},{10,11... | collective-permute-start | bytes 1769480 | tf_op jit(solution)/shard_map/ppermute | solution.py:684
  87.2 2.8 %collective-permute-start.25 = (bf16[2,2,4,16,1024]{4,3,2,1,0:T(8,128)(2,1)S(1)}, bf16[2,2,4,16,1024]{4,3,2,1,0:T(8,128)(2,1)S(1)}, u32[]{:S(2)}, u32[]{:S(2)}) collective-permute-start(bf16[2,2,4,16,1024]{4,3,2,1,0:T(8,128)(2,1)S(1)} %get-tuple-element.257), channel_id=1, source_target_pairs={{0,1},{1,0},{2,3},{3,2},{4,5},{5,4},{6,7},{7,6},{8,9},{9,8},{10,11... | collective-permute-start | bytes 1572872 | tf_op jit(solution)/shard_map/ppermute | solution.py:684
  90.0 14.0 %collective-permute-start.28 = (bf16[2,4,16,1152]{3,2,1,0:T(8,128)(2,1)S(1)}, bf16[2,4,16,1152]{3,2,1,0:T(8,128)(2,1)S(1)}, u32[]{:S(2)}, u32[]{:S(2)}) collective-permute-start(bf16[2,4,16,1152]{3,2,1,0:T(8,128)(2,1)S(1)} %fusion.2), channel_id=1, source_target_pairs={{0,2},{1,3},{2,0},{3,1},{4,6},{5,7},{6,4},{7,5},{8,10},{9,11},{10,... | collective-permute-start | bytes 884744 | tf_op jit(solution)/shard_map/ppermute | solution.py:684
  91.6 12.3 %collective-permute-start.27 = (bf16[2,4,16,1024]{3,2,1,0:T(8,128)(2,1)S(1)}, bf16[2,4,16,1024]{3,2,1,0:T(8,128)(2,1)S(1)}, u32[]{:S(2)}, u32[]{:S(2)}) collective-permute-start(bf16[2,4,16,1024]{3,2,1,0:T(8,128)(2,1)S(1)} %fusion.3), channel_id=1, source_target_pairs={{0,4},{4,0},{8,12},{12,8},{16,20},{20,16},{24,28},{28,24},{1,5},{5... | collective-permute-start | bytes 786440 | tf_op jit(solution)/shard_map/ppermute | solution.py:684
  93.2 10.1 %collective-permute-start.29 = (bf16[4,16,1536]{2,1,0:T(8,128)(2,1)S(1)}, bf16[4,16,1536]{2,1,0:T(8,128)(2,1)S(1)}, u32[]{:S(2)}, u32[]{:S(2)}) collective-permute-start(bf16[4,16,1536]{2,1,0:T(8,128)(2,1)S(1)} %get-tuple-element.262), channel_id=1, source_target_pairs={{0,2},{1,3},{2,0},{3,1},{4,6},{5,7},{6,4},{7,5},{8,10},{9,11},{10,... | collective-permute-start | bytes 589832 | tf_op jit(solution)/shard_map/ppermute | solution.py:684
  93.7 10.3 %collective-permute-start.30 = (bf16[4,16,1536]{2,1,0:T(8,128)(2,1)S(1)}, bf16[4,16,1536]{2,1,0:T(8,128)(2,1)S(1)}, u32[]{:S(2)}, u32[]{:S(2)}) collective-permute-start(bf16[4,16,1536]{2,1,0:T(8,128)(2,1)S(1)} %get-tuple-element.263), channel_id=1, source_target_pairs={{0,4},{4,0},{8,12},{12,8},{16,20},{20,16},{24,28},{28,24},{1,5},{5... | collective-permute-start | bytes 589832 | tf_op jit(solution)/shard_map/ppermute | solution.py:684
  104.1 6.5 %collective-permute-start.32 = (bf16[4,16,1152]{2,1,0:T(8,128)(2,1)S(1)}, bf16[4,16,1152]{2,1,0:T(8,128)(2,1)S(1)}, u32[]{:S(2)}, u32[]{:S(2)}) collective-permute-start(bf16[4,16,1152]{2,1,0:T(8,128)(2,1)S(1)} %get-tuple-element.285), channel_id=1, source_target_pairs={{0,4},{4,0},{8,12},{12,8},{16,20},{20,16},{24,28},{28,24},{1,5},{5... | collective-permute-start | bytes 442376 | tf_op jit(solution)/shard_map/ppermute | solution.py:684
  105.7 5.0 %collective-permute-start.31 = (bf16[4,16,1024]{2,1,0:T(8,128)(2,1)S(1)}, bf16[4,16,1024]{2,1,0:T(8,128)(2,1)S(1)}, u32[]{:S(2)}, u32[]{:S(2)}) collective-permute-start(bf16[4,16,1024]{2,1,0:T(8,128)(2,1)S(1)} %get-tuple-element.283), channel_id=1, source_target_pairs={{0,2},{1,3},{2,0},{3,1},{4,6},{5,7},{6,4},{7,5},{8,10},{9,11},{10,... | collective-permute-start | bytes 393224 | tf_op jit(solution)/shard_map/ppermute | solution.py:684
  111.0 28.3 %collective-permute-start.42 = (bf16[2,2,2,128,512]{4,3,2,1,0:T(8,128)(2,1)S(1)}, bf16[2,2,2,128,512]{4,3,2,1,0:T(8,128)(2,1)S(1)}, u32[]{:S(2)}, u32[]{:S(2)}) collective-permute-start(bf16[2,2,2,128,512]{4,3,2,1,0:T(8,128)(2,1)S(1)} %get-tuple-element.312), channel_id=1, source_target_pairs={{0,2},{1,3},{2,0},{3,1},{4,6},{5,7},{6,4},{7,5},{8,10},{9,11},{10,... | collective-permute-start | bytes 3145736 | tf_op jit(solution)/shard_map/ppermute | solution.py:684
  111.9 12.1 %collective-permute-start.34 = (bf16[16,5248]{1,0:T(8,128)(2,1)S(1)}, bf16[16,5248]{1,0:T(8,128)(2,1)S(1)}, u32[]{:S(2)}, u32[]{:S(2)}) collective-permute-start(bf16[16,5248]{1,0:T(8,128)(2,1)S(1)} %get-tuple-element.288), channel_id=1, source_target_pairs={{0,16},{4,20},{8,24},{12,28},{16,0},{20,4},{24,8},{28,12},{1,17},{... | collective-permute-start | bytes 503816 | tf_op jit(solution)/shard_map/ppermute | solution.py:684
  113.0 11.1 %collective-permute-start.35 = (bf16[16,5248]{1,0:T(8,128)(2,1)S(1)}, bf16[16,5248]{1,0:T(8,128)(2,1)S(1)}, u32[]{:S(2)}, u32[]{:S(2)}) collective-permute-start(bf16[16,5248]{1,0:T(8,128)(2,1)S(1)} %get-tuple-element.289), channel_id=1, source_target_pairs={{0,24},{4,28},{8,16},{12,20},{16,8},{20,12},{24,0},{28,4},{1,25},{... | collective-permute-start | bytes 503816 | tf_op jit(solution)/shard_map/ppermute | solution.py:684
  114.5 10.8 %collective-permute-start.33 = (bf16[16,5248]{1,0:T(8,128)(2,1)S(1)}, bf16[16,5248]{1,0:T(8,128)(2,1)S(1)}, u32[]{:S(2)}, u32[]{:S(2)}) collective-permute-start(bf16[16,5248]{1,0:T(8,128)(2,1)S(1)} %get-tuple-element.287), channel_id=1, source_target_pairs={{0,8},{4,12},{8,0},{12,4},{16,24},{20,28},{24,16},{28,20},{1,9},{5... | collective-permute-start | bytes 503816 | tf_op jit(solution)/shard_map/ppermute | solution.py:684
  125.6 13.7 %collective-permute-start.41 = (bf16[16,5248]{1,0:T(8,128)(2,1)S(1)}, bf16[16,5248]{1,0:T(8,128)(2,1)S(1)}, u32[]{:S(2)}, u32[]{:S(2)}) collective-permute-start(bf16[16,5248]{1,0:T(8,128)(2,1)S(1)} %get-tuple-element.310.refs_0_.own_ref), channel_id=1, source_target_pairs={{0,2},{1,3},{2,0},{3,1},{4,6},{5,7},{6,4},{7,5},{8,10},{9,11},{10,... | collective-permute-start | bytes 503816 | tf_op jit(solution)/shard_map/ppermute | solution.py:684
  126.5 18.1 %copy-start.1 = (f32[256]{0:T(256)S(1)}, f32[256]{0:T(256)}, u32[]{:S(2)}) copy-start(f32[256]{0:T(256)} %param.38) | copy-start | bytes 3076
  126.5 18.1 %copy-start.2 = (f32[64]{0:T(128)S(1)}, f32[64]{0:T(128)}, u32[]{:S(2)}) copy-start(f32[64]{0:T(128)} %param.42) | copy-start | bytes 772
  126.5 18.1 %copy-start.3 = (f32[256]{0:T(256)S(1)}, f32[256]{0:T(256)}, u32[]{:S(2)}) copy-start(f32[256]{0:T(256)} %param.39) | copy-start | bytes 3076
  126.5 18.1 %copy-start.4 = (f32[256]{0:T(256)S(1)}, f32[256]{0:T(256)}, u32[]{:S(2)}) copy-start(f32[256]{0:T(256)} %param.40) | copy-start | bytes 3076
  126.5 18.1 %copy-start.5 = (f32[256]{0:T(256)S(1)}, f32[256]{0:T(256)}, u32[]{:S(2)}) copy-start(f32[256]{0:T(256)} %param.41) | copy-start | bytes 3076
  126.5 18.1 %copy-start.6 = (f32[64]{0:T(128)S(1)}, f32[64]{0:T(128)}, u32[]{:S(2)}) copy-start(f32[64]{0:T(128)} %param.43) | copy-start | bytes 772
  126.5 18.1 %copy-start.7 = (f32[64]{0:T(128)S(1)}, f32[64]{0:T(128)}, u32[]{:S(2)}) copy-start(f32[64]{0:T(128)} %param.44) | copy-start | bytes 772
  126.6 18.1 %copy-start.8 = (f32[64]{0:T(128)S(1)}, f32[64]{0:T(128)}, u32[]{:S(2)}) copy-start(f32[64]{0:T(128)} %param.45) | copy-start | bytes 772
  126.6 1.2 collective-permute-start.36
  127.8 3.6 %collective-permute-start.37 = (f32[8,128]{1,0:T(8,128)S(1)}, f32[8,128]{1,0:T(8,128)S(1)}, u32[]{:S(2)}, u32[]{:S(2)}) collective-permute-start(f32[8,128]{1,0:T(8,128)S(1)} %add.32.refs_0_), channel_id=1, source_target_pairs={{0,4},{4,0},{8,12},{12,8},{16,20},{20,16},{24,28},{28,24},{1,5},{5... | collective-permute-start | bytes 12296 | tf_op jit(solution)/shard_map/ppermute | solution.py:684
  131.4 5.4 %collective-permute-start.40 = (f32[8,128]{1,0:T(8,128)S(1)}, f32[8,128]{1,0:T(8,128)S(1)}, u32[]{:S(2)}, u32[]{:S(2)}) collective-permute-start(f32[8,128]{1,0:T(8,128)S(1)} %add.33.refs_0_), channel_id=1, source_target_pairs={{0,24},{4,28},{8,16},{12,20},{16,8},{20,12},{24,0},{28,4},{1,25},{... | collective-permute-start | bytes 12296 | tf_op jit(solution)/shard_map/ppermute | solution.py:684
  133.5 4.5 %collective-permute-start.39 = (f32[8,128]{1,0:T(8,128)S(1)}, f32[8,128]{1,0:T(8,128)S(1)}, u32[]{:S(2)}, u32[]{:S(2)}) collective-permute-start(f32[8,128]{1,0:T(8,128)S(1)} %add.33.refs_0_), channel_id=1, source_target_pairs={{0,16},{4,20},{8,24},{12,28},{16,0},{20,4},{24,8},{28,12},{1,17},{... | collective-permute-start | bytes 12296 | tf_op jit(solution)/shard_map/ppermute | solution.py:684
  135.7 3.6 %collective-permute-start.38 = (f32[8,128]{1,0:T(8,128)S(1)}, f32[8,128]{1,0:T(8,128)S(1)}, u32[]{:S(2)}, u32[]{:S(2)}) collective-permute-start(f32[8,128]{1,0:T(8,128)S(1)} %add.33.refs_0_), channel_id=1, source_target_pairs={{0,8},{4,12},{8,0},{12,4},{16,24},{20,28},{24,16},{28,20},{1,9},{5... | collective-permute-start | bytes 12296 | tf_op jit(solution)/shard_map/ppermute | solution.py:684
  139.3 3.4 %collective-permute-start.45 = (bf16[2,2,2,128,512]{4,3,2,1,0:T(8,128)(2,1)S(1)}, bf16[2,2,2,128,512]{4,3,2,1,0:T(8,128)(2,1)S(1)}, u32[]{:S(2)}, u32[]{:S(2)}) collective-permute-start(bf16[2,2,2,128,512]{4,3,2,1,0:T(8,128)(2,1)S(1)} %collective-permute-done.42.side_ref), channel_id=1, source_target_pairs={{0,1},{1,0},{2,3},{3,2},{4,5},{5,4},{6,7},{7,6},{8,9},{9,8},{10,11... | collective-permute-start | bytes 3145736 | tf_op jit(solution)/shard_map/ppermute | solution.py:684
  139.3 3.4 %collective-permute-start.44 = (bf16[2,2,128,512]{3,2,1,0:T(8,128)(2,1)S(1)}, bf16[2,2,128,512]{3,2,1,0:T(8,128)(2,1)S(1)}, u32[]{:S(2)}, u32[]{:S(2)}) collective-permute-start(bf16[2,2,128,512]{3,2,1,0:T(8,128)(2,1)S(1)} %get-tuple-element.321), channel_id=1, source_target_pairs={{0,1},{1,0},{2,3},{3,2},{4,5},{5,4},{6,7},{7,6},{8,9},{9,8},{10,11... | collective-permute-start | bytes 1572872 | tf_op jit(solution)/shard_map/ppermute | solution.py:684
  139.9 4.7 %collective-permute-start.46 = (bf16[2,16,5248]{2,1,0:T(8,128)(2,1)S(1)}, bf16[2,16,5248]{2,1,0:T(8,128)(2,1)S(1)}, u32[]{:S(2)}, u32[]{:S(2)}) collective-permute-start(bf16[2,16,5248]{2,1,0:T(8,128)(2,1)S(1)} %stack.7), channel_id=1, source_target_pairs={{0,1},{1,0},{2,3},{3,2},{4,5},{5,4},{6,7},{7,6},{8,9},{9,8},{10,11... | collective-permute-start | bytes 1007624 | tf_op jit(solution)/shard_map/ppermute | solution.py:684
  140.0 4.5 %collective-permute-start.43 = (f32[8,128]{1,0:T(8,128)S(1)}, f32[8,128]{1,0:T(8,128)S(1)}, u32[]{:S(2)}, u32[]{:S(2)}) collective-permute-start(f32[8,128]{1,0:T(8,128)S(1)} %add.34.refs_0_), channel_id=1, source_target_pairs={{0,2},{1,3},{2,0},{3,1},{4,6},{5,7},{6,4},{7,5},{8,10},{9,11},{10,... | collective-permute-start | bytes 12296 | tf_op jit(solution)/shard_map/ppermute | solution.py:684
